TPU v7x, 32 devices: a whole 2x2x4 slice. The times are simulated.
32 devices in a mesh: groups: 2 (over y), dp: 4 (over z), seq: 4 (over x, core).
Axes of the slice: x: 2, y: 2, z: 4, core: 2. Of those that a mesh axis runs over, the one named last changes fastest.
Arguments:
- query_rows: bfloat16 [8, 1024, 8192], P(('groups', 'dp'), 'seq'), parts along dimension 0, may hold values from -60 to 60
- key_rows: bfloat16 [8, 1024, 1024], P(('groups', 'dp'), 'seq'), parts along dimension 0, may hold values from -4 to 4
- placed_value_rows: bfloat16 [8, 1024, 1024], P(('groups', 'dp'), 'seq'), parts along dimension 0, may hold values from -4 to 4
- doc_lengths: int32 [8, 8], P(('groups', 'dp')), parts along dimension 0, may hold values from 1 to 512, 1024 in all within a row
- span_order: int32 [8, 8], P(('groups', 'dp')), parts along dimension 0, may hold values from 0 to 7, each once within a row
- out_weight: bfloat16 [8192, 8192], P('dp', 'seq'), may hold values from -0.25 to 0.25
Outputs:
- whitened: float32 [32, 512, 8192], P(('groups', 'seq'), None, 'dp'), parts along dimension 0
There are 2 independent parts, one for each index of `groups`. A program takes and returns all parts, laid end to end along the dimension named above; an argument that names none is the same for every part. Nothing has to cross between parts.
All inputs are finite; a program needn't handle non-finite values.
Results may differ from a plain program's by a relative error of at most 0.00073.
Values may be sent and summed in bfloat16 or wider, within the bound.
No kernel may reach another device: no remote copies, remote signals or barrier semaphores. Data moves between devices by JAX's collectives and lax.ppermute only.
A program may use at most 128 MiB of HBM per device.

v0:
```python
import functools
import math

import jax
import jax.numpy as jnp
from jax import lax
from jax.experimental import pallas as pl
from jax.experimental.pallas import tpu as pltpu
from jax.sharding import PartitionSpec as P

QUERY_HEADS = 64
KEY_VALUE_HEADS = 8
HEAD_SIZE = 128
BLOCK_W = 512
NB = 16
SPAN = 128
GROUP = QUERY_HEADS // KEY_VALUE_HEADS
BLOCK_HEADS = BLOCK_W // HEAD_SIZE
KV_BLOCKS = GROUP // BLOCK_HEADS
PANELS = BLOCK_W // SPAN
STARTS = [sum(BLOCK_W - SPAN * j for j in range(k)) for k in range(PANELS)]
PACKED = sum(BLOCK_W - SPAN * j for j in range(PANELS))
VMEM_BYTES = 50 * 1024 * 1024
F32 = jnp.float32
BF16 = jnp.bfloat16
NT = (((1,), (1,)), ((), ()))
TN = (((0,), (0,)), ((), ()))


def params(limit=VMEM_BYTES):
    return pltpu.CompilerParams(vmem_limit_bytes=limit)


def cost(flops, moved, trans=0):
    return pl.CostEstimate(flops=int(flops), bytes_accessed=int(moved), transcendentals=int(trans))


def encode(value, exponent):
    scaled = value * jnp.exp2(15.0 - exponent)
    power = scaled * scaled
    power = power * power
    power = power * power
    return jnp.where(scaled < 0.0, -power, power)


def decode(code, exponent):
    code = code.astype(F32)
    root = jnp.exp2(jnp.log(jnp.maximum(jnp.abs(code), 1e-37)) * (0.125 / math.log(2.0)) + (exponent - 15.0))
    return jnp.where(code < 0.0, -root, root)


def marker():
    rows = lax.broadcasted_iota(jnp.int32, (SPAN, SPAN), 0)
    columns = lax.broadcasted_iota(jnp.int32, (SPAN, SPAN), 1)
    return (rows == SPAN - 1) & (columns == 0)


def exponent_of(largest):
    return jnp.ceil(jnp.log(jnp.maximum(largest, 1e-30)) * (1.0 / math.log(2.0)) + 0.001)


def write_coded(panels, out, largest):
    exponent = exponent_of(largest)
    at = 0
    for k, panel in enumerate(panels):
        coded = encode(panel, exponent)
        if k == 0:
            first = jnp.where(marker(), jnp.broadcast_to(exponent, (SPAN, SPAN)), coded[:, :SPAN])
            coded = jnp.concatenate([first, coded[:, SPAN:]], axis=1)
        out[:, at : at + panel.shape[1]] = coded.astype(BF16)
        at += panel.shape[1]


def read_coded(ref):
    exponent = ref[SPAN - 16 : SPAN, :SPAN].astype(F32)[15:16, 0:1]
    return decode(ref[...], exponent)


def split(value):
    high = value.astype(BF16)
    return high, (value - high.astype(F32)).astype(BF16)


def cut_kernel(meta, *refs, targets, given):
    outs = refs[-targets:]
    for number, out in enumerate(outs):
        at = 0
        for ref in refs[number * given : (number + 1) * given]:
            out[:, at : at + ref.shape[1]] = ref[...]
            at += ref.shape[1]


def turn_kernel(w_ref, *refs):
    refs[-1][...] = w_ref[...].T


def attention_kernel(meta, *refs, chips, spans, all_spans, documents, most, sets):
    sources = 2 * chips
    near = sources + 4
    query_refs, near_refs = refs[:sources], refs[sources:near]
    far_refs = refs[near : near + sets * (sources - 2)]
    out, queries, keys, values, slots, limits, left, right, total = refs[near + sets * (sources - 2) :]
    own = meta[0]
    chip, core = own // 2, lax.rem(own, 2)
    lengths = 4
    order = lengths + documents

    for r in range(all_spans):
        device = r // spans
        distance = lax.rem(chip - device // 2 + chips, chips)
        cross = lax.rem(core + device % 2, 2)
        slots[meta[order + r]] = (distance * 2 + cross) * spans + r % spans

    def place_kv(source, key_part, value_part):
        for t in range(spans):
            rows = slice(t * SPAN, (t + 1) * SPAN)
            keys[source * spans + t] = key_part[rows]
            values[source * spans + t] = value_part[rows].astype(F32).T.astype(BF16)

    place_kv(0, near_refs[0], near_refs[1])
    place_kv(1, near_refs[2], near_refs[3])
    for which in range(sets):

        @pl.when(meta[3] == which)
        def _(which=which):
            for source in range(2, sources):
                ref = far_refs[which * (sources - 2) + source - 2]
                place_kv(source, ref[:, :HEAD_SIZE], ref[:, HEAD_SIZE:])

    for source in range(sources):
        for t in range(spans):
            for h in range(BLOCK_HEADS):
                queries[source * spans + t, h * SPAN : (h + 1) * SPAN] = query_refs[source][
                    t * SPAN : (t + 1) * SPAN, h * HEAD_SIZE : (h + 1) * HEAD_SIZE
                ]

    factor = HEAD_SIZE ** (-0.5) / math.log(2.0)

    def one_span(q, carry):
        source = q // spans
        distance, cross = source // 2, lax.rem(source, 2)
        device = lax.rem(chip - distance + chips, chips) * 2 + lax.rem(core + cross, 2)
        position = meta[order + device * spans + lax.rem(q, spans)]
        first_row = position * SPAN
        begin = jnp.int32(0)
        at = jnp.int32(0)
        query_pos = lax.broadcasted_iota(jnp.int32, (1, SPAN), 1) + first_row
        query_begin = jnp.zeros((1, SPAN), jnp.int32)
        for d in range(documents):
            begin = jnp.where(at <= first_row, at, begin)
            query_begin = jnp.where(query_pos >= at, at, query_begin)
            at = at + meta[lengths + d]
        count = position - begin // SPAN + 1
        lanes = pl.ds(pl.multiple_of(q * SPAN, SPAN), SPAN)

        for n in range(1, most + 1):

            @pl.when(count == n)
            def _(n=n):
                held = [slots[position - n + 1 + i] for i in range(n)]
                for i in range(n):
                    key_pos = lax.broadcasted_iota(jnp.int32, (SPAN, SPAN), 0) + (position - n + 1 + i) * SPAN
                    seen = (key_pos <= query_pos) & (key_pos >= query_begin)
                    limits[i * SPAN : (i + 1) * SPAN] = jnp.where(seen, 3e38, -1e30)
                key_part = jnp.concatenate([keys[slot] for slot in held], axis=0)
                value_part = jnp.concatenate([values[slot] for slot in held], axis=1)
                scores = lax.dot_general(key_part, queries[q], NT, preferred_element_type=F32)
                limit = limits[: n * SPAN]
                scores = jnp.minimum(scores, jnp.concatenate([limit] * BLOCK_HEADS, axis=1))
                largest = jnp.max(scores, axis=0, keepdims=True)
                lifted = jnp.exp2((scores - largest) * factor)
                summed = jnp.sum(lifted, axis=0, keepdims=True)
                weights = (lifted * (1.0 / summed)).astype(BF16)
                mixed = jnp.dot(value_part, weights, preferred_element_type=F32)
                for h in range(BLOCK_HEADS):
                    one_head = mixed[:, h * SPAN : (h + 1) * SPAN]
                    columns = slice(h * HEAD_SIZE, (h + 1) * HEAD_SIZE)
                    high, low = split(one_head)
                    left[0, columns, lanes] = high
                    left[1, columns, lanes] = low
                    high, low = split(one_head.T)
                    right[0, lanes, columns] = high
                    right[1, lanes, columns] = low

        return carry

    lax.fori_loop(0, all_spans, one_span, 0)

    half = BLOCK_W // 2
    total[...] = jnp.zeros_like(total)

    def one_pass(i, carry):
        a, b = lax.rem(i, 2), i // 2
        total[:half] += jnp.dot(left[a, :half], right[b], preferred_element_type=F32)
        total[half:, half:] += jnp.dot(left[a, half:], right[b, :, half:], preferred_element_type=F32)
        return carry

    lax.fori_loop(0, 3, one_pass, 0)
    for i, packed in enumerate(fold(total)):
        out[:, i * BLOCK_W : (i + 1) * BLOCK_W] = packed


def tile_of(ref, i, j):
    return ref[i * SPAN : (i + 1) * SPAN, j * SPAN : (j + 1) * SPAN]


def diagonal_masks():
    rows = lax.broadcasted_iota(jnp.int32, (SPAN, SPAN), 0)
    columns = lax.broadcasted_iota(jnp.int32, (SPAN, SPAN), 1)
    return rows <= columns, rows == columns


def fold(ref):
    upper, equal = diagonal_masks()
    for off, (a, b) in ((((0, 1), (0, 2), (0, 3)), (0, 1)), (((1, 2), (1, 3), (2, 3)), (2, 3))):
        second = tile_of(ref, b, b)
        square = jnp.where(upper, tile_of(ref, a, a), second)
        line = jnp.sum(jnp.where(equal, second, 0.0), axis=0, keepdims=True)
        body = jnp.concatenate([tile_of(ref, *where) for where in off] + [square], axis=1)
        tail = jnp.concatenate([jnp.zeros((8, 3 * SPAN), F32), jnp.broadcast_to(line, (8, SPAN))], axis=1)
        yield jnp.concatenate([body, tail], axis=0)


def unfold(packs, work):
    upper, equal = diagonal_masks()
    trace = jnp.zeros((1, 1), F32)
    squares = []
    for pack, off, (a, b) in zip(
        packs, (((0, 1), (0, 2), (0, 3)), ((1, 2), (1, 3), (2, 3))), ((0, 1), (2, 3))
    ):
        for i, (row, column) in enumerate(off):
            work[row * SPAN : (row + 1) * SPAN, column * SPAN : (column + 1) * SPAN] = pack[:SPAN, i * SPAN : (i + 1) * SPAN]
        square = pack[:SPAN, 3 * SPAN :]
        turned = square.T
        line = jnp.broadcast_to(pack[SPAN : SPAN + 1, 3 * SPAN :], (SPAN, SPAN))
        squares.append((a, jnp.where(upper, square, turned)))
        squares.append((b, jnp.where(equal, line, jnp.where(upper, turned, square))))
    for _, square in squares:
        trace = trace + jnp.sum(jnp.where(equal, square, 0.0), axis=(0, 1), keepdims=True)
    damping = trace * (0.1 / BLOCK_W)
    for a, square in squares:
        work[a * SPAN : (a + 1) * SPAN, a * SPAN : (a + 1) * SPAN] = jnp.where(equal, square + damping, square)


def factor_kernel(*refs, start, stop, received):
    width = BLOCK_W - start
    panels = width // SPAN
    step = 32
    groups = step // 8
    per_tile = SPAN // step
    last = stop == BLOCK_W
    given, refs = (refs[:received], refs[received:])
    out, refs = refs[0], refs[1:]
    if not last:
        rest, refs = refs[0], refs[1:]
    work, previous, upper = refs
    if start == 0:
        work[...] = jnp.zeros_like(work)
        total = given[0][...] + given[1][...] if received == 2 else given[0][...]
        unfold((total[:, :BLOCK_W], total[:, BLOCK_W:]), work)
    else:
        work[...] = given[0][...]
    previous[...] = jnp.zeros_like(previous)

    def triple(value, first):
        high, low = split(value)
        return jnp.concatenate((high, low, high) if first else (high, high, low), axis=0)

    def superpanel(g, carry):
        row = pl.multiple_of(g * step, step)
        tile_index = g // per_tile
        tile = pl.ds(pl.multiple_of(tile_index * SPAN, SPAN), SPAN)
        turn = lax.rem(SPAN - lax.rem(g, per_tile) * step, SPAN)
        before = previous[...]
        right = triple(before, False)
        near = pltpu.roll(previous[:, tile], turn, 1)
        fresh = lax.dot_general(triple(near, True), right, TN, preferred_element_type=F32)[:step]
        current = work[pl.ds(row, step), :] - fresh
        work[...] = work[...] - lax.dot_general(triple(before, True), right, TN, preferred_element_type=F32)

        square = current[:, :SPAN]
        for k in range(1, panels):
            square = jnp.where(tile_index == k, current[:, k * SPAN : (k + 1) * SPAN], square)
        square = pltpu.roll(square, turn, 1)
        line = lax.broadcasted_iota(jnp.int32, (8, SPAN), 0)
        held = [
            {q: jnp.broadcast_to(square[8 * q : 8 * q + 8, j : j + 1], (8, SPAN)) for q in range(j // 8, groups)}
            for j in range(step)
        ]
        body = [[current[8 * q : 8 * q + 8, k * SPAN : (k + 1) * SPAN] for k in range(panels)] for q in range(groups)]
        scales = [jnp.zeros((8, SPAN), F32) for _ in range(groups)]

        def spread(value, i):
            return jnp.broadcast_to(value[i % 8 : i % 8 + 1], (8, SPAN))

        for i in range(0, step, 2):
            at = i // 8
            first, cross, second = spread(held[i][at], i), spread(held[i][at], i + 1), spread(held[i + 1][at], i + 1)
            determinant = first * second - cross * cross
            inverse = 1.0 / determinant
            first_root = lax.rsqrt(first)
            first_inverse = first_root * first_root
            scales[at] = jnp.where(line == i % 8, first_root, scales[at])
            scales[at] = jnp.where(line == i % 8 + 1, lax.rsqrt(determinant * first_inverse), scales[at])
            ratios = {}
            for q in range(at, groups):
                x, y = held[i][q], held[i + 1][q]
                ratios[q] = ((x * second - y * cross) * inverse, (y * first - x * cross) * inverse)
            ratios[at] = tuple(jnp.where(line > i % 8 + 1, ratio, 0.0) for ratio in ratios[at])
            for j in range(i + 2, step):
                x, y = spread(held[i][j // 8], j), spread(held[i + 1][j // 8], j)
                for q in range(j // 8, groups):
                    held[j][q] = held[j][q] - (ratios[q][0] * x + ratios[q][1] * y)
            between = jnp.where(line == i % 8 + 1, cross * first_inverse, 0.0)
            for k in range(panels):
                x, y = spread(body[at][k], i), spread(body[at][k], i + 1)
                for q in range(at, groups):
                    body[q][k] = body[q][k] - (ratios[q][0] * x + ratios[q][1] * y)
                body[at][k] = body[at][k] - between * x
        result = jnp.concatenate(
            [jnp.concatenate([body[q][k] * scales[q] for k in range(panels)], axis=1) for q in range(groups)], axis=0
        )
        across = lax.broadcasted_iota(jnp.int32, (step, width), 1)
        down = lax.broadcasted_iota(jnp.int32, (step, width), 0)
        result = jnp.where(across >= down + row, result, 0.0)
        previous[...] = result
        upper[pl.ds(row, step), :] = result
        return carry

    lax.fori_loop(0, (stop - start) // step, superpanel, 0)
    if not last:
        done = stop - start
        before = previous[...]
        final = lax.dot_general(
            triple(before[:, done:], True), triple(before[:, done:], False), TN, preferred_element_type=F32
        )
        rest[...] = work[done:, done:] - final
    ready = [upper[k * SPAN : (k + 1) * SPAN, k * SPAN :] for k in range((stop - start) // SPAN)]
    largest = functools.reduce(jnp.maximum, [jnp.max(jnp.abs(p), axis=(0, 1), keepdims=True) for p in ready])
    write_coded(ready, out, largest)


def whiten_kernel(order, *refs, blocks, start, first, chunks, aliased):
    u_refs, w_refs, refs = refs[:blocks], refs[blocks : blocks + chunks], refs[blocks + chunks + aliased :]
    out, left, ready, sems = refs
    width = BLOCK_W - start
    half = BLOCK_W // 2
    chunk = ready.shape[2] // chunks
    step = pl.program_id(0)
    for which in range(blocks):

        @pl.when(step == which)
        def _(which=which):
            upper = read_coded(u_refs[which])
            rows = lax.broadcasted_iota(jnp.int32, (SPAN, SPAN), 0)
            columns = lax.broadcasted_iota(jnp.int32, (SPAN, SPAN), 1)
            at = 0
            for k in range(half // SPAN):
                panel = upper[:, at : at + width - SPAN * k]
                at += width - SPAN * k
                pieces = [jnp.zeros((SPAN, SPAN * k), F32)] if k else []
                pieces += [jnp.where(rows > columns, 0.0, panel[:, :SPAN]), panel[:, SPAN:]]
                high, low = split(jnp.concatenate([p for p in pieces if p.shape[1]], axis=1))
                left[k * SPAN : (k + 1) * SPAN] = high
                left[half + k * SPAN : half + (k + 1) * SPAN] = low

    def copy(number, c):
        slot = lax.rem(number, 2)
        columns = pl.ds(c * chunk, chunk)
        return pltpu.make_async_copy(
            ready.at[slot, :, columns],
            out.at[order[first + number], pl.ds(start, half), columns],
            sems.at[slot, c],
        )

    for c in range(chunks):

        @pl.when(step >= 2)
        def _(c=c):
            copy(step - 2, c).wait()

        product = jnp.dot(left[...], w_refs[c][...], preferred_element_type=F32)
        ready[lax.rem(step, 2), :, c * chunk : (c + 1) * chunk] = product[:half] + product[half:]
        copy(step, c).start()

    @pl.when(step == blocks - 1)
    def _():
        for c in range(chunks):
            if blocks > 1:
                copy(step - 1, c).wait()
            copy(step, c).wait()


def shards(query_rows, key_rows, placed_value_rows, doc_lengths, span_order, out_weight):
    tokens = query_rows.shape[1]
    features = out_weight.shape[0]
    seq = lax.axis_size("seq")
    ring = lax.axis_size("dp")
    chips = seq // 2
    spans = tokens // SPAN
    all_spans = spans * seq
    documents = doc_lengths.shape[1]
    per = KEY_VALUE_HEADS // seq
    blocks = NB // seq
    own = lax.axis_index("seq").astype(jnp.int32)
    place = lax.axis_index("dp").astype(jnp.int32)
    query, key, value = query_rows[0], key_rows[0], placed_value_rows[0]
    vmem = pl.BlockSpec(memory_space=pltpu.VMEM)
    anywhere = pl.BlockSpec(memory_space=pl.ANY)
    in_ring = blocks == ring

    if in_ring:
        turns = [lax.rem(place + 2 * ring - 1 - t, ring) for t in range(blocks)]
    else:
        turns = [jnp.int32(t) for t in range(blocks)]
    first_kv = turns[0] // KV_BLOCKS

    def moved(distance, cross):
        return [
            (x * 2 + c, (x + distance) % chips * 2 + (1 - c if cross else c)) for x in range(chips) for c in range(2)
        ]

    def cut(targets, columns, scalars, name, after=()):
        specs, arrays = [], []
        for target in targets:
            for array, size, index in columns:
                specs.append(
                    pl.BlockSpec((tokens, size), lambda i, meta, target=target, index=index: (0, index(target(meta), meta)))
                )
                arrays.append(array)
        width = sum(size for _, size, _ in columns)
        return pl.pallas_call(
            functools.partial(cut_kernel, targets=len(targets), given=len(columns)),
            out_shape=[jax.ShapeDtypeStruct((tokens, width), BF16)] * len(targets),
            grid_spec=pltpu.PrefetchScalarGridSpec(
                num_scalar_prefetch=1,
                grid=(1,),
                in_specs=specs + [anywhere] * len(after),
                out_specs=[pl.BlockSpec((tokens, width), lambda i, meta: (0, 0))] * len(targets),
            ),
            compiler_params=params(),
            cost_estimate=cost(0, 2**21),
            name=name,
        )(scalars, *arrays, *after)

    tile = 512

    def turn(first, count, *before):
        return pl.pallas_call(
            turn_kernel,
            out_shape=jax.ShapeDtypeStruct((blocks * BLOCK_W, features), BF16),
            grid=(count, features // tile),
            in_specs=[pl.BlockSpec((tile, BLOCK_W), lambda b, o: (o, first + b))] + [anywhere] * len(before),
            out_specs=pl.BlockSpec((BLOCK_W, tile), lambda b, o: (first + b, o)),
            input_output_aliases={1: 0} if before else {},
            compiler_params=params(),
            cost_estimate=cost(3.5e9 * count, 2**20),
            name="turn_weight",
        )(out_weight, *before)

    def target_at(distance, cross):
        return lambda meta: lax.rem(meta[0] // 2 + distance, chips) * 2 + lax.rem(lax.rem(meta[0], 2) + cross, 2)

    far = [(distance, cross) for distance in range(1, chips) for cross in range(2)]
    pieces = []

    most = all_spans // 2 + 1

    def grams_of(t, peer):
        kv = turns[t] // KV_BLOCKS
        carriers = pieces[: min(t + 1, per)]
        which = jnp.where(kv == first_kv, 0, 1).astype(jnp.int32)
        meta = jnp.concatenate([jnp.stack([own, turns[t], kv, which]), doc_lengths[0], span_order[0]])
        folded = jax.ShapeDtypeStruct((SPAN + 8, 2 * BLOCK_W), F32)
        peer_kv = blocks * BLOCK_W // HEAD_SIZE
        return pl.pallas_call(
            functools.partial(
                attention_kernel,
                chips=chips, spans=spans, all_spans=all_spans, documents=documents, most=most, sets=len(carriers),
            ),
            out_shape=folded,
            grid_spec=pltpu.PrefetchScalarGridSpec(
                num_scalar_prefetch=1,
                grid=(1,),
                in_specs=[
                    pl.BlockSpec((tokens, BLOCK_W), lambda i, meta: (0, meta[0] * blocks + meta[1])),
                    pl.BlockSpec((tokens, BLOCK_W), lambda i, meta: (0, meta[1])),
                ]
                + [pl.BlockSpec((tokens, BLOCK_W), lambda i, meta: (0, 0))] * len(far)
                + [pl.BlockSpec((tokens, HEAD_SIZE), lambda i, meta: (0, meta[0] * per + meta[2]))] * 2
                + [
                    pl.BlockSpec((tokens, HEAD_SIZE), lambda i, meta: (0, peer_kv + meta[2])),
                    pl.BlockSpec((tokens, HEAD_SIZE), lambda i, meta: (0, peer_kv + per + meta[2])),
                ]
                + [pl.BlockSpec((tokens, 2 * HEAD_SIZE), lambda i, meta: (0, BLOCK_W // (2 * HEAD_SIZE)))]
                * (len(carriers) * len(far)),
                out_specs=pl.BlockSpec((SPAN + 8, 2 * BLOCK_W), lambda i, meta: (0, 0)),
                scratch_shapes=[
                    pltpu.VMEM((all_spans, BLOCK_HEADS * SPAN, HEAD_SIZE), BF16),
                    pltpu.VMEM((all_spans, SPAN, HEAD_SIZE), BF16),
                    pltpu.VMEM((all_spans, HEAD_SIZE, SPAN), BF16),
                    pltpu.SMEM((all_spans,), jnp.int32),
                    pltpu.VMEM((most * SPAN, SPAN), F32),
                    pltpu.VMEM((2, BLOCK_W, all_spans * SPAN), BF16),
                    pltpu.VMEM((2, all_spans * SPAN, BLOCK_W), BF16),
                    pltpu.VMEM((BLOCK_W, BLOCK_W), F32),
                ],
            ),
            compiler_params=params(),
            cost_estimate=cost(1.4e10, 2**20),
            name="attention_outer_products",
        )(meta, query, peer, *pieces[t], key, value, peer, peer, *[array for carrier in carriers for array in carrier])

    grams = []
    for t in range(blocks):
        kv = first_kv if t == 0 else per - 1 - first_kv
        columns = [(query, BLOCK_W, lambda target, meta: target * blocks + meta[1])]
        if t < per:
            columns += [(array, HEAD_SIZE, lambda target, meta: target * per + meta[2]) for array in (key, value)]
        scalars = jnp.stack([own, turns[t], kv])
        after = [] if t == 0 else [peer, turned] if t == 1 else [grams[t - 2]]
        parts = cut([target_at(*where) for where in far], columns, scalars, "cut_piece", after)
        pieces.append([lax.ppermute(part, "seq", moved(*where)) for part, where in zip(parts, far)])
        if t == 0:
            columns = [(query, blocks * BLOCK_W, lambda target, meta: target)]
            columns += [(array, per * HEAD_SIZE, lambda target, meta: target) for array in (key, value)]
            peer = lax.ppermute(cut([target_at(0, 1)], columns, own[None], "cut_peer", parts)[0], "seq", moved(0, 1))
            turned = turn(0, blocks // 2)
        grams.append(grams_of(t, peer))

    half = BLOCK_W // 2
    top_width, bottom_width = STARTS[2], PACKED - STARTS[2]
    scratch = lambda width: [pltpu.VMEM((width, width), F32), pltpu.VMEM((32, width), F32), pltpu.VMEM((half, width), F32)]

    def factor_top(*given):
        return pl.pallas_call(
            functools.partial(factor_kernel, start=0, stop=half, received=len(given)),
            out_shape=[
                jax.ShapeDtypeStruct((SPAN, top_width), BF16),
                jax.ShapeDtypeStruct((half, half), F32),
            ],
            in_specs=[vmem] * len(given),
            out_specs=[vmem] * 2,
            scratch_shapes=scratch(BLOCK_W),
            compiler_params=params(),
            cost_estimate=cost(1.0e10, 2**20),
            name="factor_top",
        )(*given)

    def factor_bottom(rest):
        return pl.pallas_call(
            functools.partial(factor_kernel, start=half, stop=BLOCK_W, received=1),
            out_shape=jax.ShapeDtypeStruct((SPAN, bottom_width), BF16),
            in_specs=[vmem],
            out_specs=vmem,
            scratch_shapes=scratch(half),
            compiler_params=params(),
            cost_estimate=cost(0.9e10, 2**20),
            name="factor_bottom",
        )(rest)

    if in_ring:
        carried = None
        for t in range(ring - 1):
            partial = grams[t] if carried is None else grams[t] + carried
            carried = lax.ppermute(partial, "dp", [(z, (z + 1) % ring) for z in range(ring)])
        top, rest = factor_top(grams[ring - 1], carried)

        def shared(array):
            return [array] + [
                lax.ppermute(array, "dp", [(z, (z + d) % ring) for z in range(ring)]) for d in range(1, ring)
            ]

        tops = shared(top)
        bottom = factor_bottom(rest)
        bottoms = shared(bottom)
        order = jnp.stack([lax.rem(place - d + ring, ring) for d in range(ring)])
    else:
        halves = [factor_top(lax.psum(grams[t], "dp")) for t in range(blocks)]
        tops = [top for top, _ in halves]
        bottoms = [factor_bottom(rest) for _, rest in halves]
        bottom = bottoms[0]
        order = jnp.arange(blocks, dtype=jnp.int32)

    turned = turn(blocks // 2, blocks - blocks // 2, turned, bottom)

    def whiten(uppers, first, start, result):
        more = [] if result is None else [result]
        depth = BLOCK_W - start
        chunks = features // tile
        weights = [
            pl.BlockSpec(
                (depth, tile),
                lambda b, order, c=c: (order[first + b] * (BLOCK_W // depth) + start // depth, c),
            )
            for c in range(chunks)
        ]
        return pl.pallas_call(
            functools.partial(
                whiten_kernel, blocks=len(uppers), start=start, first=first, chunks=chunks, aliased=len(more)
            ),
            out_shape=jax.ShapeDtypeStruct((blocks, BLOCK_W, features), F32),
            grid_spec=pltpu.PrefetchScalarGridSpec(
                num_scalar_prefetch=1,
                grid=(len(uppers),),
                in_specs=[vmem] * len(uppers) + weights + [anywhere] * len(more),
                out_specs=anywhere,
                scratch_shapes=[
                    pltpu.VMEM((2 * half, depth), BF16),
                    pltpu.VMEM((2, half, features), F32),
                    pltpu.SemaphoreType.DMA((2, chunks)),
                ],
            ),
            input_output_aliases={1 + len(uppers) + chunks: 0} if more else {},
            compiler_params=params(),
            cost_estimate=cost(2.0e9 * len(uppers), 2**20),
            name="whiten_bottom" if start else "whiten_top",
        )(order, *uppers, *[turned] * chunks, *more)

    result = whiten(tops[:1], 0, 0, None)
    result = whiten(bottoms[:1], 0, half, result)
    result = whiten(tops[1:], 1, 0, result)
    return whiten(bottoms[1:], 1, half, result)


def solution(mesh):
    in_specs = (
        P(("groups", "dp"), "seq", None),
        P(("groups", "dp"), "seq", None),
        P(("groups", "dp"), "seq", None),
        P(("groups", "dp"), None),
        P(("groups", "dp"), None),
        P("dp", "seq"),
    )
    out_specs = P(("groups", "seq"), None, "dp")
    return jax.shard_map(shards, mesh=mesh, in_specs=in_specs, out_specs=out_specs, check_vma=False)
```

profile of v0, /device:TPU:0, one launch (start us, length us, event | category | flops | bytes accessed | tf_op | source)
XLA Modules:
  0.0 149.1 jit_solution(3323698015426731845)
XLA Ops:
  0.1 1.0 copy-done
  1.1 1.0 copy-done.2
  2.2 1.7 %cut_piece.4 = (bf16[256,768]{1,0:T(8,128)(2,1)S(1)}, bf16[256,768]{1,0:T(8,128)(2,1)S(1)}) custom-call(s32[3]{0:T(128)S(1)} %pad_add_fusion.1.meta, bf16[256,8192]{1,0:T(8,128)(2,1)} %bitcast.39, bf16[256,1024]{1,0:T(8,128)(2,1)S(1)} %bitcast.21, bf16[256,1024]{1,0:T(8,128)(2,1)S(1)} %bitcast.30, bf16[256,8192]{1,0:T(8,128)(2,1)} %bitcast.40, ...), custom_call_target="tpu_custom_call" | custom-call | bytes 2097152 | tf_op jit(solution)/shard_map/cut_piece/pallas_call | solution.py:432
  3.9 2.4 %cut_peer.1 = bf16[256,2560]{1,0:T(8,128)(2,1)} custom-call(s32[1]{0:T(128)} %bitcast.4.meta, bf16[256,8192]{1,0:T(8,128)(2,1)} %bitcast.41, bf16[256,1024]{1,0:T(8,128)(2,1)S(1)} %bitcast.23, bf16[256,1024]{1,0:T(8,128)(2,1)S(1)} %bitcast.32, bf16[256,768]{1,0:T(8,128)(2,1)S(1)} %get-tuple-element.15.refs_3_, bf16[256,768]{1,0:T(8,128)(2,1)S(1)} %get-tuple-element.16.refs_4_), custom_call_target="tpu_custom_call" | custom-call | bytes 2097152 | tf_op jit(solution)/shard_map/cut_peer/pallas_call | solution.py:432
  6.7 2.5 %collective-permute-start.3 = (bf16[256,768]{1,0:T(8,128)(2,1)S(1)}, bf16[256,768]{1,0:T(8,128)(2,1)S(1)}, u32[]{:S(2)}, u32[]{:S(2)}) collective-permute-start(bf16[256,768]{1,0:T(8,128)(2,1)S(1)} %get-tuple-element.15.refs_3_), channel_id=1, source_target_pairs={{0,2},{1,3},{2,0},{3,1},{4,6},{5,7},{6,4},{7,5},{8,10},{9,11},{10,... | collective-permute-start | bytes 1179656 | tf_op jit(solution)/shard_map/ppermute | solution.py:523
  11.3 7.3 %turn_weight.2.refs_7_.refs_0_ = bf16[2048,2048]{1,0:T(8,128)(2,1)} custom-call(bf16[2048,2048]{1,0:T(8,128)(2,1)} %w_ref.3), custom_call_target="tpu_custom_call" | custom-call | flops 7000000000 | bytes 1048576 | tf_op jit(solution)/shard_map/turn_weight/pallas_call | solution.py:449
  18.6 1.7 %cut_piece.5 = (bf16[256,768]{1,0:T(8,128)(2,1)S(1)}, bf16[256,768]{1,0:T(8,128)(2,1)S(1)}) custom-call(s32[3]{0:T(128)S(1)} %add_add_fusion.1.meta, bf16[256,8192]{1,0:T(8,128)(2,1)} %bitcast.42, bf16[256,1024]{1,0:T(8,128)(2,1)S(1)} %bitcast.24, bf16[256,1024]{1,0:T(8,128)(2,1)S(1)} %bitcast.33, bf16[256,8192]{1,0:T(8,128)(2,1)} %bitcast.43, ...), custom_call_target="tpu_custom_call" | custom-call | bytes 2097152 | tf_op jit(solution)/shard_map/cut_piece/pallas_call | solution.py:432
  20.3 1.8 %collective-permute-start.1 = (bf16[256,768]{1,0:T(8,128)(2,1)S(1)}, bf16[256,768]{1,0:T(8,128)(2,1)S(1)}, u32[]{:S(2)}, u32[]{:S(2)}) collective-permute-start(bf16[256,768]{1,0:T(8,128)(2,1)S(1)} %get-tuple-element.17), channel_id=1, source_target_pairs={{0,2},{1,3},{2,0},{3,1},{4,6},{5,7},{6,4},{7,5},{8,10},{9,11},{10,... | collective-permute-start | bytes 1179656 | tf_op jit(solution)/shard_map/ppermute | solution.py:523
  22.1 5.3 %collective-permute-done.4.refs_9_.refs_3_ = bf16[256,768]{1,0:T(8,128)(2,1)} collective-permute-done((bf16[256,768]{1,0:T(8,128)(2,1)S(1)}, bf16[256,768]{1,0:T(8,128)(2,1)}, u32[]{:S(2)}, u32[]{:S(2)}) %collective-permute-start.4) | collective-permute-done | bytes 393248 | tf_op jit(solution)/shard_map/ppermute | solution.py:523
  27.3 10.0 %attention_outer_products.6.refs_2_ = f32[136,1024]{1,0:T(8,128)S(1)} custom-call(s32[20]{0:T(128)S(1)} %concatenate.15.meta, bf16[256,8192]{1,0:T(8,128)(2,1)} %bitcast.44, bf16[256,2560]{1,0:T(8,128)(2,1)S(1)} %collective-permute-done.refs_6_.refs_1_.refs_7_, bf16[256,768]{1,0:T(8,128)(2,1)S(1)} %collective-permute-done.3.refs_8_.refs_2_, ...), custom_call_target="tpu_custom_call" | custom-call | flops 14000000000 | bytes 1048576 | tf_op jit(solution)/shard_map/attention_outer_products/pallas_call | solution.py:476
  37.3 1.7 %collective-permute-start.9 = (f32[136,1024]{1,0:T(8,128)S(1)}, f32[136,1024]{1,0:T(8,128)S(1)}, u32[]{:S(2)}, u32[]{:S(2)}) collective-permute-start(f32[136,1024]{1,0:T(8,128)S(1)} %attention_outer_products.6.refs_2_), channel_id=1, source_target_pairs={{0,4},{4,8},{8,12},{12,0},{1,5},{5,9},{9,13},{13,1},{2,6},{6,10},{... | collective-permute-start | bytes 1671176 | tf_op jit(solution)/shard_map/ppermute | solution.py:566
  39.0 1.6 %cut_piece.7 = (bf16[256,512]{1,0:T(8,128)(2,1)S(1)}, bf16[256,512]{1,0:T(8,128)(2,1)S(1)}) custom-call(s32[3]{0:T(128)S(1)} %add_add_fusion.2.meta, bf16[256,8192]{1,0:T(8,128)(2,1)} %bitcast.45, bf16[256,8192]{1,0:T(8,128)(2,1)} %bitcast.46, f32[136,1024]{1,0:T(8,128)S(1)} %attention_outer_products.6.refs_2_), custom_call_target="tpu_custom_call" | custom-call | bytes 2097152 | tf_op jit(solution)/shard_map/cut_piece/pallas_call | solution.py:432
  40.6 1.6 %collective-permute-start.7 = (bf16[256,512]{1,0:T(8,128)(2,1)S(1)}, bf16[256,512]{1,0:T(8,128)(2,1)S(1)}, u32[]{:S(2)}, u32[]{:S(2)}) collective-permute-start(bf16[256,512]{1,0:T(8,128)(2,1)S(1)} %get-tuple-element.21), channel_id=1, source_target_pairs={{0,2},{1,3},{2,0},{3,1},{4,6},{5,7},{6,4},{7,5},{8,10},{9,11},{10,... | collective-permute-start | bytes 786440 | tf_op jit(solution)/shard_map/ppermute | solution.py:523
  42.3 1.7 %collective-permute-done.2.refs_3_.refs_11_ = bf16[256,768]{1,0:T(8,128)(2,1)S(1)} collective-permute-done((bf16[256,768]{1,0:T(8,128)(2,1)S(1)}, bf16[256,768]{1,0:T(8,128)(2,1)S(1)}, u32[]{:S(2)}, u32[]{:S(2)}) %collective-permute-start.2) | collective-permute-done | bytes 393248 | tf_op jit(solution)/shard_map/ppermute | solution.py:523
  44.1 10.0 %attention_outer_products.4.refs_2_ = f32[136,1024]{1,0:T(8,128)S(1)} custom-call(s32[20]{0:T(128)S(1)} %concatenate.13.meta, bf16[256,8192]{1,0:T(8,128)(2,1)} %bitcast.47, bf16[256,2560]{1,0:T(8,128)(2,1)} %copy-done.4, bf16[256,768]{1,0:T(8,128)(2,1)S(1)} %collective-permute-done.1.refs_2_.refs_10_, ...), custom_call_target="tpu_custom_call" | custom-call | flops 14000000000 | bytes 1048576 | tf_op jit(solution)/shard_map/attention_outer_products/pallas_call | solution.py:476
  54.1 1.6 %cut_piece.6 = (bf16[256,512]{1,0:T(8,128)(2,1)S(1)}, bf16[256,512]{1,0:T(8,128)(2,1)S(1)}) custom-call(s32[3]{0:T(128)S(1)} %add_add_fusion.meta, bf16[256,8192]{1,0:T(8,128)(2,1)} %bitcast.48, bf16[256,8192]{1,0:T(8,128)(2,1)} %bitcast.49, f32[136,1024]{1,0:T(8,128)S(1)} %attention_outer_products.4.refs_2_), custom_call_target="tpu_custom_call" | custom-call | bytes 2097152 | tf_op jit(solution)/shard_map/cut_piece/pallas_call | solution.py:432
  55.7 1.6 %collective-permute-start.5 = (bf16[256,512]{1,0:T(8,128)(2,1)S(1)}, bf16[256,512]{1,0:T(8,128)(2,1)S(1)}, u32[]{:S(2)}, u32[]{:S(2)}) collective-permute-start(bf16[256,512]{1,0:T(8,128)(2,1)S(1)} %get-tuple-element.19), channel_id=1, source_target_pairs={{0,2},{1,3},{2,0},{3,1},{4,6},{5,7},{6,4},{7,5},{8,10},{9,11},{10,... | collective-permute-start | bytes 786440 | tf_op jit(solution)/shard_map/ppermute | solution.py:523
  58.0 1.8 %collective-permute-start.10 = (f32[136,1024]{1,0:T(8,128)S(1)}, f32[136,1024]{1,0:T(8,128)S(1)}, u32[]{:S(2)}, u32[]{:S(2)}) collective-permute-start(f32[136,1024]{1,0:T(8,128)S(1)} %add.51), channel_id=1, source_target_pairs={{0,4},{4,8},{8,12},{12,0},{1,5},{5,9},{9,13},{13,1},{2,6},{6,10},{... | collective-permute-start | bytes 1671176 | tf_op jit(solution)/shard_map/ppermute | solution.py:566
  59.8 10.2 %attention_outer_products.7 = f32[136,1024]{1,0:T(8,128)S(1)} custom-call(s32[20]{0:T(128)S(1)} %concatenate.14.meta, bf16[256,8192]{1,0:T(8,128)(2,1)} %bitcast.50, bf16[256,2560]{1,0:T(8,128)(2,1)} %copy-done.4, bf16[256,512]{1,0:T(8,128)(2,1)S(1)} %collective-permute-done.7.refs_2_, bf16[256,512]{1,0:T(8,128)(2,1)S(1)} %collective-permute-done.8.refs_3_, ...), custom_call_target="tpu_custom_call" | custom-call | flops 14000000000 | bytes 1048576 | tf_op jit(solution)/shard_map/attention_outer_products/pallas_call | solution.py:476
  70.0 4.4 %collective-permute-done.10 = f32[136,1024]{1,0:T(8,128)S(1)} collective-permute-done((f32[136,1024]{1,0:T(8,128)S(1)}, f32[136,1024]{1,0:T(8,128)S(1)}, u32[]{:S(2)}, u32[]{:S(2)}) %collective-permute-start.10) | collective-permute-done | bytes 557088 | tf_op jit(solution)/shard_map/ppermute | solution.py:566
  74.6 10.0 %attention_outer_products.5.refs_0_ = f32[136,1024]{1,0:T(8,128)S(1)} custom-call(s32[20]{0:T(128)S(1)} %concatenate.12.meta, bf16[256,8192]{1,0:T(8,128)(2,1)} %bitcast.51, bf16[256,2560]{1,0:T(8,128)(2,1)} %copy-done.4, bf16[256,512]{1,0:T(8,128)(2,1)S(1)} %collective-permute-done.5.refs_2_, bf16[256,512]{1,0:T(8,128)(2,1)S(1)} %collective-permute-done.6.refs_3_, ...), custom_call_target="tpu_custom_call" | custom-call | flops 14000000000 | bytes 1048576 | tf_op jit(solution)/shard_map/attention_outer_products/pallas_call | solution.py:476
  84.7 5.5 %collective-permute-done.11.refs_1_ = f32[136,1024]{1,0:T(8,128)S(1)} collective-permute-done((f32[136,1024]{1,0:T(8,128)S(1)}, f32[136,1024]{1,0:T(8,128)S(1)}, u32[]{:S(2)}, u32[]{:S(2)}) %collective-permute-start.11) | collective-permute-done | bytes 557088 | tf_op jit(solution)/shard_map/ppermute | solution.py:566
  90.1 10.0 %factor_top.1 = (bf16[128,896]{1,0:T(8,128)(2,1)S(1)}, f32[256,256]{1,0:T(8,128)S(1)}) custom-call(f32[136,1024]{1,0:T(8,128)S(1)} %attention_outer_products.5.refs_0_, f32[136,1024]{1,0:T(8,128)S(1)} %collective-permute-done.11.refs_1_), custom_call_target="tpu_custom_call" | custom-call | flops 10000000000 | bytes 1048576 | tf_op jit(solution)/shard_map/factor_top/pallas_call | solution.py:536
  100.3 3.7 %collective-permute-start.17 = (bf16[128,896]{1,0:T(8,128)(2,1)S(1)}, bf16[128,896]{1,0:T(8,128)(2,1)S(1)}, u32[]{:S(2)}, u32[]{:S(2)}) collective-permute-start(bf16[128,896]{1,0:T(8,128)(2,1)S(1)} %get-tuple-element.24.refs_0_), channel_id=1, source_target_pairs={{0,12},{4,0},{8,4},{12,8},{1,13},{5,1},{9,5},{13,9},{2,14},{6,2},{... | collective-permute-start | bytes 688136 | tf_op jit(solution)/shard_map/ppermute | solution.py:571
  104.1 8.4 %factor_bottom.1.refs_1_.refs_0_ = bf16[128,384]{1,0:T(8,128)(2,1)S(1)} custom-call(f32[256,256]{1,0:T(8,128)S(1)} %get-tuple-element.23.refs_0_), custom_call_target="tpu_custom_call" | custom-call | flops 8999999488 | bytes 1048576 | tf_op jit(solution)/shard_map/factor_bottom/pallas_call | solution.py:551
  112.4 7.3 %turn_weight.3.refs_1_.refs_2_.refs_3_.refs_4_.refs_5_.refs_6_ = bf16[2048,2048]{1,0:T(8,128)(2,1)} custom-call(bf16[2048,2048]{1,0:T(8,128)(2,1)} %w_ref.3, bf16[2048,2048]{1,0:T(8,128)(2,1)} %turn_weight.2.refs_7_.refs_0_, bf16[128,384]{1,0:T(8,128)(2,1)S(1)} %factor_bottom.1.refs_1_.refs_0_), custom_call_target="tpu_custom_call", output_to_operand_aliasing={{}: (1, {})} | custom-call | flops 7000000000 | bytes 1048576 | tf_op jit(solution)/shard_map/turn_weight/pallas_call | solution.py:449
  120.3 1.5 collective-permute-start.13
  121.8 4.3 %whiten_top.2.refs_5_ = f32[4,512,2048]{2,1,0:T(8,128)} custom-call(s32[4]{0:T(128)S(1)} %pad_add_fusion.order, bf16[128,896]{1,0:T(8,128)(2,1)S(1)} %get-tuple-element.24.refs_0_, bf16[2048,2048]{1,0:T(8,128)(2,1)} %turn_weight.3.refs_1_.refs_2_.refs_3_.refs_4_.refs_5_.refs_6_, ...), custom_call_target="tpu_custom_call" | custom-call | flops 2000000000 | bytes 1048576 | tf_op jit(solution)/shard_map/whiten_top/pallas_call | solution.py:598
  126.0 3.5 %whiten_bottom.2.refs_7_ = f32[4,512,2048]{2,1,0:T(8,128)} custom-call(s32[4]{0:T(128)S(1)} %pad_add_fusion.order, bf16[128,384]{1,0:T(8,128)(2,1)S(1)} %factor_bottom.1.refs_1_.refs_0_, bf16[2048,2048]{1,0:T(8,128)(2,1)} %turn_weight.3.refs_1_.refs_2_.refs_3_.refs_4_.refs_5_.refs_6_, ...), custom_call_target="tpu_custom_call", output_to_operand_aliasing={{}: (6, {})} | custom-call | flops 2000000000 | bytes 1048576 | tf_op jit(solution)/shard_map/whiten_bottom/pallas_call | solution.py:598
  129.5 3.2 %collective-permute-start.14 = (bf16[128,384]{1,0:T(8,128)(2,1)S(1)}, bf16[128,384]{1,0:T(8,128)(2,1)S(1)}, u32[]{:S(2)}, u32[]{:S(2)}) collective-permute-start(bf16[128,384]{1,0:T(8,128)(2,1)S(1)} %factor_bottom.1.refs_1_.refs_0_), channel_id=1, source_target_pairs={{0,12},{4,0},{8,4},{12,8},{1,13},{5,1},{9,5},{13,9},{2,14},{6,2},{... | collective-permute-start | bytes 294920 | tf_op jit(solution)/shard_map/ppermute | solution.py:571
  132.7 9.4 %whiten_top.3.refs_7_ = f32[4,512,2048]{2,1,0:T(8,128)} custom-call(s32[4]{0:T(128)S(1)} %pad_add_fusion.order, bf16[128,896]{1,0:T(8,128)(2,1)S(1)} %collective-permute-done.15.refs_0_, bf16[128,896]{1,0:T(8,128)(2,1)S(1)} %collective-permute-done.16.refs_1_, bf16[128,896]{1,0:T(8,128)(2,1)S(1)} %collective-permute-done.17.refs_2_, ...), custom_call_target="tpu_custom_call", output_to_operand_aliasing={{}: (8, {})} | custom-call | flops 6000000000 | bytes 1048576 | tf_op jit(solution)/shard_map/whiten_top/pallas_call | solution.py:598
  142.2 6.8 %whiten_bottom.3 = f32[4,512,2048]{2,1,0:T(8,128)} custom-call(s32[4]{0:T(128)S(1)} %pad_add_fusion.order, bf16[128,384]{1,0:T(8,128)(2,1)S(1)} %collective-permute-done.12.refs_0_, bf16[128,384]{1,0:T(8,128)(2,1)S(1)} %collective-permute-done.13.refs_1_, bf16[128,384]{1,0:T(8,128)(2,1)S(1)} %collective-permute-done.14.refs_2_, ...), custom_call_target="tpu_custom_call", output_to_operand_aliasing={{}: (8, {})} | custom-call | flops 6000000000 | bytes 1048576 | tf_op jit(solution)/shard_map/whiten_bottom/pallas_call | solution.py:598
  (46 shorter events, 4.4 us)
Async XLA Ops:
  0.1 1.0 copy-start
  1.1 1.0 copy-start.2
  2.2 1.7 %copy-start.1 = (bf16[1,256,1024]{2,1,0:T(8,128)(2,1)S(1)}, bf16[1,256,1024]{2,1,0:T(8,128)(2,1)}, u32[]{:S(2)}) copy-start(bf16[1,256,1024]{2,1,0:T(8,128)(2,1)} %param.7) | copy-start | bytes 1572868
  2.2 1.7 %copy-start.3 = (bf16[1,256,1024]{2,1,0:T(8,128)(2,1)S(1)}, bf16[1,256,1024]{2,1,0:T(8,128)(2,1)}, u32[]{:S(2)}) copy-start(bf16[1,256,1024]{2,1,0:T(8,128)(2,1)} %param.8) | copy-start | bytes 1572868
  2.2 7.2 %copy-start.5 = (s32[1,8]{1,0:T(1,128)S(1)}, s32[1,8]{1,0:T(1,128)}, u32[]{:S(2)}) copy-start(s32[1,8]{1,0:T(1,128)} %param.9) | copy-start | bytes 100
  2.2 7.2 %copy-start.6 = (s32[1,8]{1,0:T(1,128)S(1)}, s32[1,8]{1,0:T(1,128)}, u32[]{:S(2)}) copy-start(s32[1,8]{1,0:T(1,128)} %param.10) | copy-start | bytes 100
  6.3 12.3 %collective-permute-start = (bf16[256,2560]{1,0:T(8,128)(2,1)}, bf16[256,2560]{1,0:T(8,128)(2,1)S(1)}, u32[]{:S(2)}, u32[]{:S(2)}) collective-permute-start(bf16[256,2560]{1,0:T(8,128)(2,1)} %cut_peer.1), channel_id=1, source_target_pairs={{0,1},{1,0},{2,3},{3,2},{4,5},{5,4},{6,7},{7,6},{8,9},{9,8},{10,11... | collective-permute-start | bytes 3932168 | tf_op jit(solution)/shard_map/ppermute | solution.py:527
  6.7 15.3 %collective-permute-start.3 = (bf16[256,768]{1,0:T(8,128)(2,1)S(1)}, bf16[256,768]{1,0:T(8,128)(2,1)S(1)}, u32[]{:S(2)}, u32[]{:S(2)}) collective-permute-start(bf16[256,768]{1,0:T(8,128)(2,1)S(1)} %get-tuple-element.15.refs_3_), channel_id=1, source_target_pairs={{0,2},{1,3},{2,0},{3,1},{4,6},{5,7},{6,4},{7,5},{8,10},{9,11},{10,... | collective-permute-start | bytes 1179656 | tf_op jit(solution)/shard_map/ppermute | solution.py:523
  9.2 18.1 %collective-permute-start.4 = (bf16[256,768]{1,0:T(8,128)(2,1)S(1)}, bf16[256,768]{1,0:T(8,128)(2,1)}, u32[]{:S(2)}, u32[]{:S(2)}) collective-permute-start(bf16[256,768]{1,0:T(8,128)(2,1)S(1)} %get-tuple-element.16.refs_4_), channel_id=1, source_target_pairs={{0,3},{1,2},{2,1},{3,0},{4,7},{5,6},{6,5},{7,4},{8,11},{9,10},{10,... | collective-permute-start | bytes 1179656 | tf_op jit(solution)/shard_map/ppermute | solution.py:523
  18.6 8.8 %copy-start.4 = (bf16[256,2560]{1,0:T(8,128)(2,1)}, bf16[256,2560]{1,0:T(8,128)(2,1)S(1)}, u32[]{:S(2)}) copy-start(bf16[256,2560]{1,0:T(8,128)(2,1)S(1)} %collective-permute-done.refs_6_.refs_1_.refs_7_) | copy-start | bytes 3932164
  20.3 22.1 %collective-permute-start.1 = (bf16[256,768]{1,0:T(8,128)(2,1)S(1)}, bf16[256,768]{1,0:T(8,128)(2,1)S(1)}, u32[]{:S(2)}, u32[]{:S(2)}) collective-permute-start(bf16[256,768]{1,0:T(8,128)(2,1)S(1)} %get-tuple-element.17), channel_id=1, source_target_pairs={{0,2},{1,3},{2,0},{3,1},{4,6},{5,7},{6,4},{7,5},{8,10},{9,11},{10,... | collective-permute-start | bytes 1179656 | tf_op jit(solution)/shard_map/ppermute | solution.py:523
  22.0 22.0 %collective-permute-start.2 = (bf16[256,768]{1,0:T(8,128)(2,1)S(1)}, bf16[256,768]{1,0:T(8,128)(2,1)S(1)}, u32[]{:S(2)}, u32[]{:S(2)}) collective-permute-start(bf16[256,768]{1,0:T(8,128)(2,1)S(1)} %get-tuple-element.18), channel_id=1, source_target_pairs={{0,3},{1,2},{2,1},{3,0},{4,7},{5,6},{6,5},{7,4},{8,11},{9,10},{10,... | collective-permute-start | bytes 1179656 | tf_op jit(solution)/shard_map/ppermute | solution.py:523
  37.3 20.6 %collective-permute-start.9 = (f32[136,1024]{1,0:T(8,128)S(1)}, f32[136,1024]{1,0:T(8,128)S(1)}, u32[]{:S(2)}, u32[]{:S(2)}) collective-permute-start(f32[136,1024]{1,0:T(8,128)S(1)} %attention_outer_products.6.refs_2_), channel_id=1, source_target_pairs={{0,4},{4,8},{8,12},{12,0},{1,5},{5,9},{9,13},{13,1},{2,6},{6,10},{... | collective-permute-start | bytes 1671176 | tf_op jit(solution)/shard_map/ppermute | solution.py:566
  40.6 19.2 %collective-permute-start.7 = (bf16[256,512]{1,0:T(8,128)(2,1)S(1)}, bf16[256,512]{1,0:T(8,128)(2,1)S(1)}, u32[]{:S(2)}, u32[]{:S(2)}) collective-permute-start(bf16[256,512]{1,0:T(8,128)(2,1)S(1)} %get-tuple-element.21), channel_id=1, source_target_pairs={{0,2},{1,3},{2,0},{3,1},{4,6},{5,7},{6,4},{7,5},{8,10},{9,11},{10,... | collective-permute-start | bytes 786440 | tf_op jit(solution)/shard_map/ppermute | solution.py:523
  42.2 17.7 %collective-permute-start.8 = (bf16[256,512]{1,0:T(8,128)(2,1)S(1)}, bf16[256,512]{1,0:T(8,128)(2,1)S(1)}, u32[]{:S(2)}, u32[]{:S(2)}) collective-permute-start(bf16[256,512]{1,0:T(8,128)(2,1)S(1)} %get-tuple-element.22), channel_id=1, source_target_pairs={{0,3},{1,2},{2,1},{3,0},{4,7},{5,6},{6,5},{7,4},{8,11},{9,10},{10,... | collective-permute-start | bytes 786440 | tf_op jit(solution)/shard_map/ppermute | solution.py:523
  55.7 18.9 %collective-permute-start.5 = (bf16[256,512]{1,0:T(8,128)(2,1)S(1)}, bf16[256,512]{1,0:T(8,128)(2,1)S(1)}, u32[]{:S(2)}, u32[]{:S(2)}) collective-permute-start(bf16[256,512]{1,0:T(8,128)(2,1)S(1)} %get-tuple-element.19), channel_id=1, source_target_pairs={{0,2},{1,3},{2,0},{3,1},{4,6},{5,7},{6,4},{7,5},{8,10},{9,11},{10,... | collective-permute-start | bytes 786440 | tf_op jit(solution)/shard_map/ppermute | solution.py:523
  57.4 17.3 %collective-permute-start.6 = (bf16[256,512]{1,0:T(8,128)(2,1)S(1)}, bf16[256,512]{1,0:T(8,128)(2,1)S(1)}, u32[]{:S(2)}, u32[]{:S(2)}) collective-permute-start(bf16[256,512]{1,0:T(8,128)(2,1)S(1)} %get-tuple-element.20), channel_id=1, source_target_pairs={{0,3},{1,2},{2,1},{3,0},{4,7},{5,6},{6,5},{7,4},{8,11},{9,10},{10,... | collective-permute-start | bytes 786440 | tf_op jit(solution)/shard_map/ppermute | solution.py:523
  58.0 16.4 %collective-permute-start.10 = (f32[136,1024]{1,0:T(8,128)S(1)}, f32[136,1024]{1,0:T(8,128)S(1)}, u32[]{:S(2)}, u32[]{:S(2)}) collective-permute-start(f32[136,1024]{1,0:T(8,128)S(1)} %add.51), channel_id=1, source_target_pairs={{0,4},{4,8},{8,12},{12,0},{1,5},{5,9},{9,13},{13,1},{2,6},{6,10},{... | collective-permute-start | bytes 1671176 | tf_op jit(solution)/shard_map/ppermute | solution.py:566
  74.5 15.6 %collective-permute-start.11 = (f32[136,1024]{1,0:T(8,128)S(1)}, f32[136,1024]{1,0:T(8,128)S(1)}, u32[]{:S(2)}, u32[]{:S(2)}) collective-permute-start(f32[136,1024]{1,0:T(8,128)S(1)} %add.52), channel_id=1, source_target_pairs={{0,4},{4,8},{8,12},{12,0},{1,5},{5,9},{9,13},{13,1},{2,6},{6,10},{... | collective-permute-start | bytes 1671176 | tf_op jit(solution)/shard_map/ppermute | solution.py:566
  100.2 29.3 %collective-permute-start.15 = (bf16[128,896]{1,0:T(8,128)(2,1)S(1)}, bf16[128,896]{1,0:T(8,128)(2,1)S(1)}, u32[]{:S(2)}, u32[]{:S(2)}) collective-permute-start(bf16[128,896]{1,0:T(8,128)(2,1)S(1)} %get-tuple-element.24.refs_0_), channel_id=1, source_target_pairs={{0,4},{4,8},{8,12},{12,0},{1,5},{5,9},{9,13},{13,1},{2,6},{6,10},{... | collective-permute-start | bytes 688136 | tf_op jit(solution)/shard_map/ppermute | solution.py:571
  100.2 32.5 %collective-permute-start.16 = (bf16[128,896]{1,0:T(8,128)(2,1)S(1)}, bf16[128,896]{1,0:T(8,128)(2,1)S(1)}, u32[]{:S(2)}, u32[]{:S(2)}) collective-permute-start(bf16[128,896]{1,0:T(8,128)(2,1)S(1)} %get-tuple-element.24.refs_0_), channel_id=1, source_target_pairs={{0,8},{4,12},{8,0},{12,4},{1,9},{5,13},{9,1},{13,5},{2,10},{6,14},... | collective-permute-start | bytes 688136 | tf_op jit(solution)/shard_map/ppermute | solution.py:571
  100.3 32.4 %collective-permute-start.17 = (bf16[128,896]{1,0:T(8,128)(2,1)S(1)}, bf16[128,896]{1,0:T(8,128)(2,1)S(1)}, u32[]{:S(2)}, u32[]{:S(2)}) collective-permute-start(bf16[128,896]{1,0:T(8,128)(2,1)S(1)} %get-tuple-element.24.refs_0_), channel_id=1, source_target_pairs={{0,12},{4,0},{8,4},{12,8},{1,13},{5,1},{9,5},{13,9},{2,14},{6,2},{... | collective-permute-start | bytes 688136 | tf_op jit(solution)/shard_map/ppermute | solution.py:571
  119.7 22.4 %collective-permute-start.12 = (bf16[128,384]{1,0:T(8,128)(2,1)S(1)}, bf16[128,384]{1,0:T(8,128)(2,1)S(1)}, u32[]{:S(2)}, u32[]{:S(2)}) collective-permute-start(bf16[128,384]{1,0:T(8,128)(2,1)S(1)} %factor_bottom.1.refs_1_.refs_0_), channel_id=1, source_target_pairs={{0,4},{4,8},{8,12},{12,0},{1,5},{5,9},{9,13},{13,1},{2,6},{6,10},{... | collective-permute-start | bytes 294920 | tf_op jit(solution)/shard_map/ppermute | solution.py:571
  120.3 21.9 %collective-permute-start.13 = (bf16[128,384]{1,0:T(8,128)(2,1)S(1)}, bf16[128,384]{1,0:T(8,128)(2,1)S(1)}, u32[]{:S(2)}, u32[]{:S(2)}) collective-permute-start(bf16[128,384]{1,0:T(8,128)(2,1)S(1)} %factor_bottom.1.refs_1_.refs_0_), channel_id=1, source_target_pairs={{0,8},{4,12},{8,0},{12,4},{1,9},{5,13},{9,1},{13,5},{2,10},{6,14},... | collective-permute-start | bytes 294920 | tf_op jit(solution)/shard_map/ppermute | solution.py:571
  129.5 12.6 %collective-permute-start.14 = (bf16[128,384]{1,0:T(8,128)(2,1)S(1)}, bf16[128,384]{1,0:T(8,128)(2,1)S(1)}, u32[]{:S(2)}, u32[]{:S(2)}) collective-permute-start(bf16[128,384]{1,0:T(8,128)(2,1)S(1)} %factor_bottom.1.refs_1_.refs_0_), channel_id=1, source_target_pairs={{0,12},{4,0},{8,4},{12,8},{1,13},{5,1},{9,5},{13,9},{2,14},{6,2},{... | collective-permute-start | bytes 294920 | tf_op jit(solution)/shard_map/ppermute | solution.py:571
where the time goes:
time: 150 us; the launch traced here: 149 us
  Pallas kernels  106 us (71%)
  starting transfers between devices  21.5 us (14%)
  waiting for transfers between devices  16.9 us (11%)
  local copies, waits for them, and re-layouts  3.76 us (3%)
    pallas_call x4, Pallas kernels, grams_of(): pl.pallas_call(functools.partial(attention_kernel, chips=chips, spans=spa...  40.2 us
    pallas_call x4, Pallas kernels, whiten(): pl.pallas_call(functools.partial(whiten_kernel, blocks=len(uppers), start...  23.9 us
    pallas_call x2, Pallas kernels, turn(): pl.pallas_call(turn_kernel, out_shape=jax.ShapeDtypeStruct((blocks * BLOC...  14.6 us
    pallas_call x1, Pallas kernels, factor_top(): pl.pallas_call(functools.partial(factor_kernel, start=0, stop=half, recei...  10 us
    ppermute x3, waiting for transfers between devices, shards(): lax.ppermute(partial, 'dp', [(z, (z + 1) % ring) for z in range(ring)])  9.88 us
    ppermute x6, starting transfers between devices, shared(): lax.ppermute(array, 'dp', [(z, (z + d) % ring) for z in range(ring)])  9.09 us
    pallas_call x5, Pallas kernels, cut(): pl.pallas_call(functools.partial(cut_kernel, targets=len(targets), given=...  8.97 us
    pallas_call x1, Pallas kernels, factor_bottom(): pl.pallas_call(functools.partial(factor_kernel, start=half, stop=BLOCK_W,...  8.36 us
  transfers between devices with their start and end apart: 18, of which 4 were waited for; matrix products, arithmetic and copies ran while one was open for 1% of the time, Pallas kernels for 57%

commit v1 on v0

--- a/solution.py
+++ b/solution.py
@@ -94,12 +94,12 @@
     refs[-1][...] = w_ref[...].T
 
 
-def attention_kernel(meta, *refs, chips, spans, all_spans, documents, most, sets):
+def attention_kernel(meta, *refs, chips, spans, all_spans, documents, most, sets, waited):
     sources = 2 * chips
     near = sources + 4
     query_refs, near_refs = refs[:sources], refs[sources:near]
     far_refs = refs[near : near + sets * (sources - 2)]
-    out, queries, keys, values, slots, limits, left, right, total = refs[near + sets * (sources - 2) :]
+    out, queries, keys, values, slots, limits, left, right, total = refs[near + sets * (sources - 2) + waited :]
     own = meta[0]
     chip, core = own // 2, lax.rem(own, 2)
     lengths = 4
@@ -293,30 +293,21 @@
         def spread(value, i):
             return jnp.broadcast_to(value[i % 8 : i % 8 + 1], (8, SPAN))
 
-        for i in range(0, step, 2):
+        for i in range(step):
             at = i // 8
-            first, cross, second = spread(held[i][at], i), spread(held[i][at], i + 1), spread(held[i + 1][at], i + 1)
-            determinant = first * second - cross * cross
-            inverse = 1.0 / determinant
-            first_root = lax.rsqrt(first)
-            first_inverse = first_root * first_root
-            scales[at] = jnp.where(line == i % 8, first_root, scales[at])
-            scales[at] = jnp.where(line == i % 8 + 1, lax.rsqrt(determinant * first_inverse), scales[at])
-            ratios = {}
-            for q in range(at, groups):
-                x, y = held[i][q], held[i + 1][q]
-                ratios[q] = ((x * second - y * cross) * inverse, (y * first - x * cross) * inverse)
-            ratios[at] = tuple(jnp.where(line > i % 8 + 1, ratio, 0.0) for ratio in ratios[at])
-            for j in range(i + 2, step):
-                x, y = spread(held[i][j // 8], j), spread(held[i + 1][j // 8], j)
+            root = lax.rsqrt(spread(held[i][at], i))
+            inverse = root * root
+            scales[at] = jnp.where(line == i % 8, root, scales[at])
+            ratio = {q: held[i][q] * inverse for q in range(at, groups)}
+            ratio[at] = jnp.where(line > i % 8, ratio[at], 0.0)
+            for j in range(i + 1, step):
+                entry = spread(held[i][j // 8], j)
                 for q in range(j // 8, groups):
-                    held[j][q] = held[j][q] - (ratios[q][0] * x + ratios[q][1] * y)
-            between = jnp.where(line == i % 8 + 1, cross * first_inverse, 0.0)
+                    held[j][q] = held[j][q] - ratio[q] * entry
             for k in range(panels):
-                x, y = spread(body[at][k], i), spread(body[at][k], i + 1)
+                pivot_row = spread(body[at][k], i)
                 for q in range(at, groups):
-                    body[q][k] = body[q][k] - (ratios[q][0] * x + ratios[q][1] * y)
-                body[at][k] = body[at][k] - between * x
+                    body[q][k] = body[q][k] - ratio[q] * pivot_row
         result = jnp.concatenate(
             [jnp.concatenate([body[q][k] * scales[q] for k in range(panels)], axis=1) for q in range(groups)], axis=0
         )
@@ -340,55 +331,72 @@
     write_coded(ready, out, largest)
 
 
-def whiten_kernel(order, *refs, blocks, start, first, chunks, aliased):
-    u_refs, w_refs, refs = refs[:blocks], refs[blocks : blocks + chunks], refs[blocks + chunks + aliased :]
+def whiten_kernel(order, *refs, blocks, starts, first, chunks, aliased):
+    count = len(starts)
+    u_refs, refs = refs[: blocks * count], refs[blocks * count :]
+    w_refs, refs = refs[:chunks], refs[chunks + aliased :]
     out, left, ready, sems = refs
-    width = BLOCK_W - start
     half = BLOCK_W // 2
     chunk = ready.shape[2] // chunks
     step = pl.program_id(0)
-    for which in range(blocks):
-
-        @pl.when(step == which)
-        def _(which=which):
-            upper = read_coded(u_refs[which])
-            rows = lax.broadcasted_iota(jnp.int32, (SPAN, SPAN), 0)
-            columns = lax.broadcasted_iota(jnp.int32, (SPAN, SPAN), 1)
-            at = 0
-            for k in range(half // SPAN):
-                panel = upper[:, at : at + width - SPAN * k]
-                at += width - SPAN * k
-                pieces = [jnp.zeros((SPAN, SPAN * k), F32)] if k else []
-                pieces += [jnp.where(rows > columns, 0.0, panel[:, :SPAN]), panel[:, SPAN:]]
-                high, low = split(jnp.concatenate([p for p in pieces if p.shape[1]], axis=1))
-                left[k * SPAN : (k + 1) * SPAN] = high
-                left[half + k * SPAN : half + (k + 1) * SPAN] = low
-
-    def copy(number, c):
-        slot = lax.rem(number, 2)
+    lowest = starts[0]
+
+    def copy(number, which, c):
+        slot = lax.rem(number * count + which, 2)
         columns = pl.ds(c * chunk, chunk)
         return pltpu.make_async_copy(
             ready.at[slot, :, columns],
-            out.at[order[first + number], pl.ds(start, half), columns],
+            out.at[order[first + number], pl.ds(starts[which], half), columns],
             sems.at[slot, c],
         )
 
-    for c in range(chunks):
-
-        @pl.when(step >= 2)
-        def _(c=c):
-            copy(step - 2, c).wait()
-
-        product = jnp.dot(left[...], w_refs[c][...], preferred_element_type=F32)
-        ready[lax.rem(step, 2), :, c * chunk : (c + 1) * chunk] = product[:half] + product[half:]
-        copy(step, c).start()
+    for which, start in enumerate(starts):
+        width = BLOCK_W - start
+        for b in range(blocks):
+
+            @pl.when(step == b)
+            def _(b=b):
+                upper = read_coded(u_refs[b * count + which])
+                rows = lax.broadcasted_iota(jnp.int32, (SPAN, SPAN), 0)
+                columns = lax.broadcasted_iota(jnp.int32, (SPAN, SPAN), 1)
+                at = 0
+                for k in range(half // SPAN):
+                    panel = upper[:, at : at + width - SPAN * k]
+                    at += width - SPAN * k
+                    pieces = [jnp.zeros((SPAN, SPAN * k), F32)] if k else []
+                    pieces += [jnp.where(rows > columns, 0.0, panel[:, :SPAN]), panel[:, SPAN:]]
+                    high, low = split(jnp.concatenate([p for p in pieces if p.shape[1]], axis=1))
+                    left[k * SPAN : (k + 1) * SPAN, :width] = high
+                    left[k * SPAN : (k + 1) * SPAN, width : 2 * width] = low
+
+        for c in range(chunks):
+            if count == 1:
+
+                @pl.when(step >= 2)
+                def _(c=c):
+                    copy(step - 2, which, c).wait()
+
+            elif blocks > 1:
+
+                @pl.when(step >= 1)
+                def _(c=c):
+                    copy(step - 1, which, c).wait()
+
+            weight = w_refs[c][start - lowest :]
+            product = jnp.dot(
+                left[:, : 2 * width], jnp.concatenate([weight, weight], axis=0), preferred_element_type=F32
+            )
+            ready[lax.rem(step * count + which, 2), :, c * chunk : (c + 1) * chunk] = product
+            copy(step, which, c).start()
 
     @pl.when(step == blocks - 1)
     def _():
         for c in range(chunks):
-            if blocks > 1:
-                copy(step - 1, c).wait()
-            copy(step, c).wait()
+            if count > 1:
+                copy(step, 0, c).wait()
+            elif blocks > 1:
+                copy(step - 1, 0, c).wait()
+            copy(step, count - 1, c).wait()
 
 
 def shards(query_rows, key_rows, placed_value_rows, doc_lengths, span_order, out_weight):
@@ -420,7 +428,7 @@
             (x * 2 + c, (x + distance) % chips * 2 + (1 - c if cross else c)) for x in range(chips) for c in range(2)
         ]
 
-    def cut(targets, columns, scalars, name, after=()):
+    def cut(targets, columns, scalars, name, after=(), limit=VMEM_BYTES):
         specs, arrays = [], []
         for target in targets:
             for array, size, index in columns:
@@ -438,7 +446,7 @@
                 in_specs=specs + [anywhere] * len(after),
                 out_specs=[pl.BlockSpec((tokens, width), lambda i, meta: (0, 0))] * len(targets),
             ),
-            compiler_params=params(),
+            compiler_params=params(limit),
             cost_estimate=cost(0, 2**21),
             name=name,
         )(scalars, *arrays, *after)
@@ -452,9 +460,9 @@
             grid=(count, features // tile),
             in_specs=[pl.BlockSpec((tile, BLOCK_W), lambda b, o: (o, first + b))] + [anywhere] * len(before),
             out_specs=pl.BlockSpec((BLOCK_W, tile), lambda b, o: (first + b, o)),
-            input_output_aliases={1: 0} if before else {},
+            input_output_aliases={1: 0} if first else {},
             compiler_params=params(),
-            cost_estimate=cost(3.5e9 * count, 2**20),
+            cost_estimate=cost(1.0e9 * count, 2**20),
             name="turn_weight",
         )(out_weight, *before)
 
@@ -466,7 +474,7 @@
 
     most = all_spans // 2 + 1
 
-    def grams_of(t, peer):
+    def grams_of(t, peer, after):
         kv = turns[t] // KV_BLOCKS
         carriers = pieces[: min(t + 1, per)]
         which = jnp.where(kv == first_kv, 0, 1).astype(jnp.int32)
@@ -477,6 +485,7 @@
             functools.partial(
                 attention_kernel,
                 chips=chips, spans=spans, all_spans=all_spans, documents=documents, most=most, sets=len(carriers),
+                waited=len(after),
             ),
             out_shape=folded,
             grid_spec=pltpu.PrefetchScalarGridSpec(
@@ -493,7 +502,8 @@
                     pl.BlockSpec((tokens, HEAD_SIZE), lambda i, meta: (0, peer_kv + per + meta[2])),
                 ]
                 + [pl.BlockSpec((tokens, 2 * HEAD_SIZE), lambda i, meta: (0, BLOCK_W // (2 * HEAD_SIZE)))]
-                * (len(carriers) * len(far)),
+                * (len(carriers) * len(far))
+                + [anywhere] * len(after),
                 out_specs=pl.BlockSpec((SPAN + 8, 2 * BLOCK_W), lambda i, meta: (0, 0)),
                 scratch_shapes=[
                     pltpu.VMEM((all_spans, BLOCK_HEADS * SPAN, HEAD_SIZE), BF16),
@@ -509,24 +519,44 @@
             compiler_params=params(),
             cost_estimate=cost(1.4e10, 2**20),
             name="attention_outer_products",
-        )(meta, query, peer, *pieces[t], key, value, peer, peer, *[array for carrier in carriers for array in carrier])
+        )(meta, query, peer, *pieces[t], key, value, peer, peer, *[array for carrier in carriers for array in carrier], *after)
 
     grams = []
-    for t in range(blocks):
-        kv = first_kv if t == 0 else per - 1 - first_kv
-        columns = [(query, BLOCK_W, lambda target, meta: target * blocks + meta[1])]
-        if t < per:
-            columns += [(array, HEAD_SIZE, lambda target, meta: target * per + meta[2]) for array in (key, value)]
-        scalars = jnp.stack([own, turns[t], kv])
-        after = [] if t == 0 else [peer, turned] if t == 1 else [grams[t - 2]]
-        parts = cut([target_at(*where) for where in far], columns, scalars, "cut_piece", after)
-        pieces.append([lax.ppermute(part, "seq", moved(*where)) for part, where in zip(parts, far)])
+    held = []
+    for t in range(blocks + 1):
+        if t < blocks:
+            kv = first_kv if t == 0 else per - 1 - first_kv
+            columns = [(query, BLOCK_W, lambda target, meta: target * blocks + meta[1])]
+            if t < per:
+                columns += [(array, HEAD_SIZE, lambda target, meta: target * per + meta[2]) for array in (key, value)]
+            scalars = jnp.stack([own, turns[t], kv])
+            after = [] if t == 0 else [peer, turned] if t == 1 else [held[t - 2]]
+            parts = cut(
+                [target_at(*where) for where in far], columns, scalars, "cut_piece", after,
+                VMEM_BYTES if t else 63 * 2**20,
+            )
+            pieces.append([lax.ppermute(part, "seq", moved(*where)) for part, where in zip(parts, far)])
         if t == 0:
             columns = [(query, blocks * BLOCK_W, lambda target, meta: target)]
             columns += [(array, per * HEAD_SIZE, lambda target, meta: target) for array in (key, value)]
-            peer = lax.ppermute(cut([target_at(0, 1)], columns, own[None], "cut_peer", parts)[0], "seq", moved(0, 1))
-            turned = turn(0, blocks // 2)
-        grams.append(grams_of(t, peer))
+            peer = cut([target_at(0, 1)], columns, own[None], "cut_peer", parts)[0]
+            turned = turn(0, 1, peer)
+            peer = lax.ppermute(peer, "seq", moved(0, 1))
+            turned = turn(1, 1, turned)
+            continue
+        if t == 1:
+            for b in range(2, blocks - 1):
+                turned = turn(b, 1, turned, parts[0])
+        done = t - 1
+        grams.append(grams_of(done, peer, [turned] if t == 1 else []))
+        if done == 0 or not in_ring:
+            held.append(grams[done])
+        else:
+            held.append(grams[done] + carried if done < ring - 1 else None)
+        if in_ring and done < ring - 1:
+            carried = lax.ppermute(held[done], "dp", [(z, (z + 1) % ring) for z in range(ring)])
+    if blocks > 2:
+        turned = turn(blocks - 1, 1, turned, grams[-1])
 
     half = BLOCK_W // 2
     top_width, bottom_width = STARTS[2], PACKED - STARTS[2]
@@ -560,10 +590,6 @@
         )(rest)
 
     if in_ring:
-        carried = None
-        for t in range(ring - 1):
-            partial = grams[t] if carried is None else grams[t] + carried
-            carried = lax.ppermute(partial, "dp", [(z, (z + 1) % ring) for z in range(ring)])
         top, rest = factor_top(grams[ring - 1], carried)
 
         def shared(array):
@@ -582,31 +608,31 @@
         bottom = bottoms[0]
         order = jnp.arange(blocks, dtype=jnp.int32)
 
-    turned = turn(blocks // 2, blocks - blocks // 2, turned, bottom)
-
-    def whiten(uppers, first, start, result):
+
+    def whiten(uppers, first, starts, result):
         more = [] if result is None else [result]
-        depth = BLOCK_W - start
+        depth = BLOCK_W - starts[0]
         chunks = features // tile
+        count = len(uppers) // len(starts)
         weights = [
             pl.BlockSpec(
                 (depth, tile),
-                lambda b, order, c=c: (order[first + b] * (BLOCK_W // depth) + start // depth, c),
+                lambda b, order, c=c: (order[first + b] * (BLOCK_W // depth) + starts[0] // depth, c),
             )
             for c in range(chunks)
         ]
         return pl.pallas_call(
             functools.partial(
-                whiten_kernel, blocks=len(uppers), start=start, first=first, chunks=chunks, aliased=len(more)
+                whiten_kernel, blocks=count, starts=starts, first=first, chunks=chunks, aliased=len(more)
             ),
             out_shape=jax.ShapeDtypeStruct((blocks, BLOCK_W, features), F32),
             grid_spec=pltpu.PrefetchScalarGridSpec(
                 num_scalar_prefetch=1,
-                grid=(len(uppers),),
+                grid=(count,),
                 in_specs=[vmem] * len(uppers) + weights + [anywhere] * len(more),
                 out_specs=anywhere,
                 scratch_shapes=[
-                    pltpu.VMEM((2 * half, depth), BF16),
+                    pltpu.VMEM((half, 2 * depth), BF16),
                     pltpu.VMEM((2, half, features), F32),
                     pltpu.SemaphoreType.DMA((2, chunks)),
                 ],
@@ -614,13 +640,12 @@
             input_output_aliases={1 + len(uppers) + chunks: 0} if more else {},
             compiler_params=params(),
             cost_estimate=cost(2.0e9 * len(uppers), 2**20),
-            name="whiten_bottom" if start else "whiten_top",
+            name="whiten_bottom" if starts[0] else "whiten_top",
         )(order, *uppers, *[turned] * chunks, *more)
 
-    result = whiten(tops[:1], 0, 0, None)
-    result = whiten(bottoms[:1], 0, half, result)
-    result = whiten(tops[1:], 1, 0, result)
-    return whiten(bottoms[1:], 1, half, result)
+    result = whiten([tops[0], bottoms[0]], 0, (0, half), None)
+    result = whiten(tops[1:], 1, (0,), result)
+    return whiten(bottoms[1:], 1, (half,), result)
 
 
 def solution(mesh):

time: 150 us -> 139 us (0.927)
  the two profiles are of different devices: /device:TPU:0 before, /device:TPU:14 now
where the time goes in v1:
time: 139 us
  Pallas kernels  103 us (74%)
  starting transfers between devices  23.3 us (17%)
  waiting for transfers between devices  9.79 us (7%)
    pallas_call x4, Pallas kernels, grams_of(): pl.pallas_call(functools.partial(attention_kernel, chips=chips, spans=spa...  38.1 us
    pallas_call x3, Pallas kernels, whiten(): pl.pallas_call(functools.partial(whiten_kernel, blocks=count, starts=star...  21.2 us
    pallas_call x4, Pallas kernels, turn(): pl.pallas_call(turn_kernel, out_shape=jax.ShapeDtypeStruct((blocks * BLOC...  16.8 us
    ppermute x6, starting transfers between devices, shared(): lax.ppermute(array, 'dp', [(z, (z + d) % ring) for z in range(ring)])  9.46 us
    pallas_call x1, Pallas kernels, factor_top(): pl.pallas_call(functools.partial(factor_kernel, start=0, stop=half, recei...  9.36 us
    pallas_call x5, Pallas kernels, cut(): pl.pallas_call(functools.partial(cut_kernel, targets=len(targets), given=...  9.02 us
    pallas_call x1, Pallas kernels, factor_bottom(): pl.pallas_call(functools.partial(factor_kernel, start=half, stop=BLOCK_W,...  8.24 us
    ppermute x8, starting transfers between devices, shards(): lax.ppermute(part, 'seq', moved(*where))  7.67 us
  transfers between devices with their start and end apart: 18, of which 5 were waited for; matrix products, arithmetic and copies ran while one was open for 1% of the time, Pallas kernels for 59%

profile of v1, /device:TPU:14, one launch (start us, length us, event | category | flops | bytes accessed | tf_op | source)
XLA Modules:
  0.0 138.7 jit_solution(7737832973780075265)
XLA Ops:
  0.6 2.8 %cut_piece.4 = (bf16[256,768]{1,0:T(8,128)(2,1)}, bf16[256,768]{1,0:T(8,128)(2,1)}) custom-call(s32[3]{0:T(128)} %pad_add_fusion.1.meta, bf16[256,8192]{1,0:T(8,128)(2,1)} %bitcast.39, bf16[256,1024]{1,0:T(8,128)(2,1)} %bitcast.21, bf16[256,1024]{1,0:T(8,128)(2,1)} %bitcast.30, bf16[256,8192]{1,0:T(8,128)(2,1)} %bitcast.40, bf16[256,1024]{1,0:T(8,128)(2,1)} %bitcast.22, ...), custom_call_target="tpu_custom_call" | custom-call | bytes 2097152 | tf_op jit(solution)/shard_map/cut_piece/pallas_call | solution.py:440
  4.5 1.3 cut_peer.1.refs_0_
  6.5 1.2 collective-permute-start.4
  8.1 4.2 %turn_weight.4.refs_0_ = bf16[2048,2048]{1,0:T(8,128)(2,1)} custom-call(bf16[2048,2048]{1,0:T(8,128)(2,1)} %w_ref.7, bf16[256,2560]{1,0:T(8,128)(2,1)S(1)} %cut_peer.1.refs_0_), custom_call_target="tpu_custom_call" | custom-call | flops 1000000000 | bytes 1048576 | tf_op jit(solution)/shard_map/turn_weight/pallas_call | solution.py:457
  12.4 4.2 %turn_weight.5.refs_7_.refs_0_ = bf16[2048,2048]{1,0:T(8,128)(2,1)} custom-call(bf16[2048,2048]{1,0:T(8,128)(2,1)} %w_ref.7, bf16[2048,2048]{1,0:T(8,128)(2,1)} %turn_weight.4.refs_0_), custom_call_target="tpu_custom_call", output_to_operand_aliasing={{}: (1, {})} | custom-call | flops 1000000000 | bytes 1048576 | tf_op jit(solution)/shard_map/turn_weight/pallas_call | solution.py:457
  16.8 1.7 %cut_piece.5 = (bf16[256,768]{1,0:T(8,128)(2,1)S(1)}, bf16[256,768]{1,0:T(8,128)(2,1)S(1)}) custom-call(s32[3]{0:T(128)S(1)} %add_add_fusion.1.meta, bf16[256,8192]{1,0:T(8,128)(2,1)} %bitcast.42, bf16[256,1024]{1,0:T(8,128)(2,1)S(1)} %bitcast.24, bf16[256,1024]{1,0:T(8,128)(2,1)S(1)} %bitcast.33, bf16[256,8192]{1,0:T(8,128)(2,1)} %bitcast.43, ...), custom_call_target="tpu_custom_call" | custom-call | bytes 2097152 | tf_op jit(solution)/shard_map/cut_piece/pallas_call | solution.py:440
  20.3 4.2 %turn_weight.6.refs_10_.refs_0_ = bf16[2048,2048]{1,0:T(8,128)(2,1)} custom-call(bf16[2048,2048]{1,0:T(8,128)(2,1)} %w_ref.7, bf16[2048,2048]{1,0:T(8,128)(2,1)} %turn_weight.5.refs_7_.refs_0_, bf16[256,768]{1,0:T(8,128)(2,1)S(1)} %get-tuple-element.17.refs_1_), custom_call_target="tpu_custom_call", output_to_operand_aliasing={{}: (1, {})} | custom-call | flops 1000000000 | bytes 1048576 | tf_op jit(solution)/shard_map/turn_weight/pallas_call | solution.py:457
  24.4 1.1 collective-permute-done.4.refs_9_.refs_3_
  25.6 9.5 %attention_outer_products.5.refs_2_ = f32[136,1024]{1,0:T(8,128)S(1)} custom-call(s32[20]{0:T(128)S(1)} %concatenate.14.meta, bf16[256,8192]{1,0:T(8,128)(2,1)} %bitcast.44, bf16[256,2560]{1,0:T(8,128)(2,1)} %collective-permute-done.refs_6_.refs_1_.refs_7_, bf16[256,768]{1,0:T(8,128)(2,1)S(1)} %collective-permute-done.3.refs_8_.refs_2_, ...), custom_call_target="tpu_custom_call" | custom-call | flops 14000000000 | bytes 1048576 | tf_op jit(solution)/shard_map/attention_outer_products/pallas_call | solution.py:484
  35.0 2.1 %collective-permute-start.5 = (f32[136,1024]{1,0:T(8,128)S(1)}, f32[136,1024]{1,0:T(8,128)S(1)}, u32[]{:S(2)}, u32[]{:S(2)}) collective-permute-start(f32[136,1024]{1,0:T(8,128)S(1)} %attention_outer_products.5.refs_2_), channel_id=1, source_target_pairs={{0,4},{4,8},{8,12},{12,0},{1,5},{5,9},{9,13},{13,1},{2,6},{6,10},{... | collective-permute-start | bytes 1671176 | tf_op jit(solution)/shard_map/ppermute | solution.py:557
  37.1 1.6 %cut_piece.7 = (bf16[256,512]{1,0:T(8,128)(2,1)S(1)}, bf16[256,512]{1,0:T(8,128)(2,1)S(1)}) custom-call(s32[3]{0:T(128)S(1)} %add_add_fusion.2.meta, bf16[256,8192]{1,0:T(8,128)(2,1)} %bitcast.45, bf16[256,8192]{1,0:T(8,128)(2,1)} %bitcast.46, f32[136,1024]{1,0:T(8,128)S(1)} %attention_outer_products.5.refs_2_), custom_call_target="tpu_custom_call" | custom-call | bytes 2097152 | tf_op jit(solution)/shard_map/cut_piece/pallas_call | solution.py:440
  39.4 1.2 collective-permute-start.9
  40.6 1.8 %collective-permute-done.2.refs_3_.refs_11_ = bf16[256,768]{1,0:T(8,128)(2,1)S(1)} collective-permute-done((bf16[256,768]{1,0:T(8,128)(2,1)S(1)}, bf16[256,768]{1,0:T(8,128)(2,1)S(1)}, u32[]{:S(2)}, u32[]{:S(2)}) %collective-permute-start.2) | collective-permute-done | bytes 393248 | tf_op jit(solution)/shard_map/ppermute | solution.py:538
  42.4 9.5 %attention_outer_products.4 = f32[136,1024]{1,0:T(8,128)S(1)} custom-call(s32[20]{0:T(128)S(1)} %concatenate.13.meta, bf16[256,8192]{1,0:T(8,128)(2,1)} %bitcast.47, bf16[256,2560]{1,0:T(8,128)(2,1)} %collective-permute-done.refs_6_.refs_1_.refs_7_, bf16[256,768]{1,0:T(8,128)(2,1)S(1)} %collective-permute-done.1.refs_2_.refs_10_, ...), custom_call_target="tpu_custom_call" | custom-call | flops 14000000000 | bytes 1048576 | tf_op jit(solution)/shard_map/attention_outer_products/pallas_call | solution.py:484
  52.0 2.1 %collective-permute-start.10 = (f32[136,1024]{1,0:T(8,128)S(1)}, f32[136,1024]{1,0:T(8,128)S(1)}, u32[]{:S(2)}, u32[]{:S(2)}) collective-permute-start(f32[136,1024]{1,0:T(8,128)S(1)} %add.51.refs_2_), channel_id=1, source_target_pairs={{0,4},{4,8},{8,12},{12,0},{1,5},{5,9},{9,13},{13,1},{2,6},{6,10},{... | collective-permute-start | bytes 1671176 | tf_op jit(solution)/shard_map/ppermute | solution.py:557
  54.1 1.6 %cut_piece.6 = (bf16[256,512]{1,0:T(8,128)(2,1)S(1)}, bf16[256,512]{1,0:T(8,128)(2,1)S(1)}) custom-call(s32[3]{0:T(128)S(1)} %add_add_fusion.meta, bf16[256,8192]{1,0:T(8,128)(2,1)} %bitcast.48, bf16[256,8192]{1,0:T(8,128)(2,1)} %bitcast.49, f32[136,1024]{1,0:T(8,128)S(1)} %add.51.refs_2_), custom_call_target="tpu_custom_call" | custom-call | bytes 2097152 | tf_op jit(solution)/shard_map/cut_piece/pallas_call | solution.py:440
  56.3 1.6 %collective-permute-start.7 = (bf16[256,512]{1,0:T(8,128)(2,1)S(1)}, bf16[256,512]{1,0:T(8,128)(2,1)S(1)}, u32[]{:S(2)}, u32[]{:S(2)}) collective-permute-start(bf16[256,512]{1,0:T(8,128)(2,1)S(1)} %get-tuple-element.20), channel_id=1, source_target_pairs={{0,3},{1,2},{2,1},{3,0},{4,7},{5,6},{6,5},{7,4},{8,11},{9,10},{10,... | collective-permute-start | bytes 786440 | tf_op jit(solution)/shard_map/ppermute | solution.py:538
  57.9 9.7 %attention_outer_products.7 = f32[136,1024]{1,0:T(8,128)S(1)} custom-call(s32[20]{0:T(128)S(1)} %concatenate.15.meta, bf16[256,8192]{1,0:T(8,128)(2,1)} %bitcast.50, bf16[256,2560]{1,0:T(8,128)(2,1)} %collective-permute-done.refs_6_.refs_1_.refs_7_, bf16[256,512]{1,0:T(8,128)(2,1)S(1)} %collective-permute-done.8.refs_2_, ...), custom_call_target="tpu_custom_call" | custom-call | flops 14000000000 | bytes 1048576 | tf_op jit(solution)/shard_map/attention_outer_products/pallas_call | solution.py:484
  67.7 2.0 %collective-permute-start.11 = (f32[136,1024]{1,0:T(8,128)S(1)}, f32[136,1024]{1,0:T(8,128)S(1)}, u32[]{:S(2)}, u32[]{:S(2)}) collective-permute-start(f32[136,1024]{1,0:T(8,128)S(1)} %add.52), channel_id=1, source_target_pairs={{0,4},{4,8},{8,12},{12,0},{1,5},{5,9},{9,13},{13,1},{2,6},{6,10},{... | collective-permute-start | bytes 1671176 | tf_op jit(solution)/shard_map/ppermute | solution.py:557
  70.1 9.5 %attention_outer_products.6.refs_0_.refs_1_ = f32[136,1024]{1,0:T(8,128)S(1)} custom-call(s32[20]{0:T(128)S(1)} %concatenate.12.meta, bf16[256,8192]{1,0:T(8,128)(2,1)} %bitcast.51, bf16[256,2560]{1,0:T(8,128)(2,1)} %collective-permute-done.refs_6_.refs_1_.refs_7_, bf16[256,512]{1,0:T(8,128)(2,1)S(1)} %collective-permute-done.6.refs_2_, ...), custom_call_target="tpu_custom_call" | custom-call | flops 14000000000 | bytes 1048576 | tf_op jit(solution)/shard_map/attention_outer_products/pallas_call | solution.py:484
  79.6 4.2 %turn_weight.7.refs_2_.refs_3_.refs_4_.refs_5_.refs_6_ = bf16[2048,2048]{1,0:T(8,128)(2,1)} custom-call(bf16[2048,2048]{1,0:T(8,128)(2,1)} %w_ref.7, bf16[2048,2048]{1,0:T(8,128)(2,1)} %turn_weight.6.refs_10_.refs_0_, f32[136,1024]{1,0:T(8,128)S(1)} %attention_outer_products.6.refs_0_.refs_1_), custom_call_target="tpu_custom_call", output_to_operand_aliasing={{}: (1, {})} | custom-call | flops 1000000000 | bytes 1048576 | tf_op jit(solution)/shard_map/turn_weight/pallas_call | solution.py:457
  83.8 9.4 %factor_top.1 = (bf16[128,896]{1,0:T(8,128)(2,1)S(1)}, f32[256,256]{1,0:T(8,128)S(1)}) custom-call(f32[136,1024]{1,0:T(8,128)S(1)} %attention_outer_products.6.refs_0_.refs_1_, f32[136,1024]{1,0:T(8,128)S(1)} %collective-permute-done.11.refs_1_), custom_call_target="tpu_custom_call" | custom-call | flops 10000000000 | bytes 1048576 | tf_op jit(solution)/shard_map/factor_top/pallas_call | solution.py:566
  93.2 2.0 %collective-permute-start.15 = (bf16[128,896]{1,0:T(8,128)(2,1)S(1)}, bf16[128,896]{1,0:T(8,128)(2,1)S(1)}, u32[]{:S(2)}, u32[]{:S(2)}) collective-permute-start(bf16[128,896]{1,0:T(8,128)(2,1)S(1)} %get-tuple-element.24.refs_0_), channel_id=1, source_target_pairs={{0,4},{4,8},{8,12},{12,0},{1,5},{5,9},{9,13},{13,1},{2,6},{6,10},{... | collective-permute-start | bytes 688136 | tf_op jit(solution)/shard_map/ppermute | solution.py:597
  95.2 3.3 %collective-permute-start.16 = (bf16[128,896]{1,0:T(8,128)(2,1)S(1)}, bf16[128,896]{1,0:T(8,128)(2,1)S(1)}, u32[]{:S(2)}, u32[]{:S(2)}) collective-permute-start(bf16[128,896]{1,0:T(8,128)(2,1)S(1)} %get-tuple-element.24.refs_0_), channel_id=1, source_target_pairs={{0,8},{4,12},{8,0},{12,4},{1,9},{5,13},{9,1},{13,5},{2,10},{6,14},... | collective-permute-start | bytes 688136 | tf_op jit(solution)/shard_map/ppermute | solution.py:597
  98.5 8.2 %factor_bottom.1.refs_1_ = bf16[128,384]{1,0:T(8,128)(2,1)S(1)} custom-call(f32[256,256]{1,0:T(8,128)S(1)} %get-tuple-element.23.refs_0_), custom_call_target="tpu_custom_call" | custom-call | flops 8999999488 | bytes 1048576 | tf_op jit(solution)/shard_map/factor_bottom/pallas_call | solution.py:581
  106.7 2.1 %collective-permute-start.12 = (bf16[128,384]{1,0:T(8,128)(2,1)S(1)}, bf16[128,384]{1,0:T(8,128)(2,1)S(1)}, u32[]{:S(2)}, u32[]{:S(2)}) collective-permute-start(bf16[128,384]{1,0:T(8,128)(2,1)S(1)} %factor_bottom.1.refs_1_), channel_id=1, source_target_pairs={{0,4},{4,8},{8,12},{12,0},{1,5},{5,9},{9,13},{13,1},{2,6},{6,10},{... | collective-permute-start | bytes 294920 | tf_op jit(solution)/shard_map/ppermute | solution.py:597
  108.8 1.8 %collective-permute-start.13 = (bf16[128,384]{1,0:T(8,128)(2,1)S(1)}, bf16[128,384]{1,0:T(8,128)(2,1)S(1)}, u32[]{:S(2)}, u32[]{:S(2)}) collective-permute-start(bf16[128,384]{1,0:T(8,128)(2,1)S(1)} %factor_bottom.1.refs_1_), channel_id=1, source_target_pairs={{0,8},{4,12},{8,0},{12,4},{1,9},{5,13},{9,1},{13,5},{2,10},{6,14},... | collective-permute-start | bytes 294920 | tf_op jit(solution)/shard_map/ppermute | solution.py:597
  110.6 5.0 %whiten_top.2.refs_7_ = f32[4,512,2048]{2,1,0:T(8,128)} custom-call(s32[4]{0:T(128)S(1)} %pad_add_fusion.order, bf16[128,896]{1,0:T(8,128)(2,1)S(1)} %get-tuple-element.24.refs_0_, bf16[128,384]{1,0:T(8,128)(2,1)S(1)} %factor_bottom.1.refs_1_, bf16[2048,2048]{1,0:T(8,128)(2,1)} %turn_weight.7.refs_2_.refs_3_.refs_4_.refs_5_.refs_6_, ...), custom_call_target="tpu_custom_call" | custom-call | flops 4000000000 | bytes 1048576 | tf_op jit(solution)/shard_map/whiten_top/pallas_call | solution.py:624
  115.9 3.3 %collective-permute-done.16.refs_1_ = bf16[128,896]{1,0:T(8,128)(2,1)S(1)} collective-permute-done((bf16[128,896]{1,0:T(8,128)(2,1)S(1)}, bf16[128,896]{1,0:T(8,128)(2,1)S(1)}, u32[]{:S(2)}, u32[]{:S(2)}) %collective-permute-start.16) | collective-permute-done | bytes 229408 | tf_op jit(solution)/shard_map/ppermute | solution.py:597
  119.2 3.0 %collective-permute-done.17.refs_2_ = bf16[128,896]{1,0:T(8,128)(2,1)S(1)} collective-permute-done((bf16[128,896]{1,0:T(8,128)(2,1)S(1)}, bf16[128,896]{1,0:T(8,128)(2,1)S(1)}, u32[]{:S(2)}, u32[]{:S(2)}) %collective-permute-start.17) | collective-permute-done | bytes 229408 | tf_op jit(solution)/shard_map/ppermute | solution.py:597
  122.2 9.4 %whiten_top.3.refs_7_ = f32[4,512,2048]{2,1,0:T(8,128)} custom-call(s32[4]{0:T(128)S(1)} %pad_add_fusion.order, bf16[128,896]{1,0:T(8,128)(2,1)S(1)} %collective-permute-done.15.refs_0_, bf16[128,896]{1,0:T(8,128)(2,1)S(1)} %collective-permute-done.16.refs_1_, bf16[128,896]{1,0:T(8,128)(2,1)S(1)} %collective-permute-done.17.refs_2_, ...), custom_call_target="tpu_custom_call", output_to_operand_aliasing={{}: (8, {})} | custom-call | flops 6000000000 | bytes 1048576 | tf_op jit(solution)/shard_map/whiten_top/pallas_call | solution.py:624
  131.6 6.8 %whiten_bottom.1 = f32[4,512,2048]{2,1,0:T(8,128)} custom-call(s32[4]{0:T(128)S(1)} %pad_add_fusion.order, bf16[128,384]{1,0:T(8,128)(2,1)S(1)} %collective-permute-done.12.refs_0_, bf16[128,384]{1,0:T(8,128)(2,1)S(1)} %collective-permute-done.13.refs_1_, bf16[128,384]{1,0:T(8,128)(2,1)S(1)} %collective-permute-done.14.refs_2_, ...), custom_call_target="tpu_custom_call", output_to_operand_aliasing={{}: (8, {})} | custom-call | flops 6000000000 | bytes 1048576 | tf_op jit(solution)/shard_map/whiten_bottom/pallas_call | solution.py:624
  (43 shorter events, 6.9 us)
Async XLA Ops:
  0.0 3.4 %copy-start = (bf16[1,256,1024]{2,1,0:T(8,128)(2,1)S(1)}, bf16[1,256,1024]{2,1,0:T(8,128)(2,1)}, u32[]{:S(2)}) copy-start(bf16[1,256,1024]{2,1,0:T(8,128)(2,1)} %param.7) | copy-start | bytes 1572868
  0.6 7.1 %copy-start.3 = (s32[1,8]{1,0:T(1,128)S(1)}, s32[1,8]{1,0:T(1,128)}, u32[]{:S(2)}) copy-start(s32[1,8]{1,0:T(1,128)} %param.9) | copy-start | bytes 100
  0.6 7.1 %copy-start.4 = (s32[1,8]{1,0:T(1,128)S(1)}, s32[1,8]{1,0:T(1,128)}, u32[]{:S(2)}) copy-start(s32[1,8]{1,0:T(1,128)} %param.10) | copy-start | bytes 100
  3.4 1.0 copy-start.1
  5.8 11.0 %collective-permute-start = (bf16[256,2560]{1,0:T(8,128)(2,1)S(1)}, bf16[256,2560]{1,0:T(8,128)(2,1)}, u32[]{:S(2)}, u32[]{:S(2)}) collective-permute-start(bf16[256,2560]{1,0:T(8,128)(2,1)S(1)} %cut_peer.1.refs_0_), channel_id=1, source_target_pairs={{0,1},{1,0},{2,3},{3,2},{4,5},{5,4},{6,7},{7,6},{8,9},{9,8},{10,11... | collective-permute-start | bytes 3932168 | tf_op jit(solution)/shard_map/ppermute | solution.py:544
  5.9 18.6 %collective-permute-start.3 = (bf16[256,768]{1,0:T(8,128)(2,1)}, bf16[256,768]{1,0:T(8,128)(2,1)S(1)}, u32[]{:S(2)}, u32[]{:S(2)}) collective-permute-start(bf16[256,768]{1,0:T(8,128)(2,1)} %get-tuple-element.15.refs_3_), channel_id=1, source_target_pairs={{0,2},{1,3},{2,0},{3,1},{4,6},{5,7},{6,4},{7,5},{8,10},{9,11},{10,... | collective-permute-start | bytes 1179656 | tf_op jit(solution)/shard_map/ppermute | solution.py:538
  6.5 19.1 %collective-permute-start.4 = (bf16[256,768]{1,0:T(8,128)(2,1)}, bf16[256,768]{1,0:T(8,128)(2,1)S(1)}, u32[]{:S(2)}, u32[]{:S(2)}) collective-permute-start(bf16[256,768]{1,0:T(8,128)(2,1)} %get-tuple-element.16.refs_4_), channel_id=1, source_target_pairs={{0,3},{1,2},{2,1},{3,0},{4,7},{5,6},{6,5},{7,4},{8,11},{9,10},{10,... | collective-permute-start | bytes 1179656 | tf_op jit(solution)/shard_map/ppermute | solution.py:538
  12.4 4.4 %copy-start.2 = (bf16[1,256,1024]{2,1,0:T(8,128)(2,1)S(1)}, bf16[1,256,1024]{2,1,0:T(8,128)(2,1)}, u32[]{:S(2)}) copy-start(bf16[1,256,1024]{2,1,0:T(8,128)(2,1)} %param.8) | copy-start | bytes 1572868
  18.5 22.1 %collective-permute-start.1 = (bf16[256,768]{1,0:T(8,128)(2,1)S(1)}, bf16[256,768]{1,0:T(8,128)(2,1)S(1)}, u32[]{:S(2)}, u32[]{:S(2)}) collective-permute-start(bf16[256,768]{1,0:T(8,128)(2,1)S(1)} %get-tuple-element.17.refs_1_), channel_id=1, source_target_pairs={{0,2},{1,3},{2,0},{3,1},{4,6},{5,7},{6,4},{7,5},{8,10},{9,11},{10,... | collective-permute-start | bytes 1179656 | tf_op jit(solution)/shard_map/ppermute | solution.py:538
  19.1 23.3 %collective-permute-start.2 = (bf16[256,768]{1,0:T(8,128)(2,1)S(1)}, bf16[256,768]{1,0:T(8,128)(2,1)S(1)}, u32[]{:S(2)}, u32[]{:S(2)}) collective-permute-start(bf16[256,768]{1,0:T(8,128)(2,1)S(1)} %get-tuple-element.18), channel_id=1, source_target_pairs={{0,3},{1,2},{2,1},{3,0},{4,7},{5,6},{6,5},{7,4},{8,11},{9,10},{10,... | collective-permute-start | bytes 1179656 | tf_op jit(solution)/shard_map/ppermute | solution.py:538
  35.0 16.9 %collective-permute-start.5 = (f32[136,1024]{1,0:T(8,128)S(1)}, f32[136,1024]{1,0:T(8,128)S(1)}, u32[]{:S(2)}, u32[]{:S(2)}) collective-permute-start(f32[136,1024]{1,0:T(8,128)S(1)} %attention_outer_products.5.refs_2_), channel_id=1, source_target_pairs={{0,4},{4,8},{8,12},{12,0},{1,5},{5,9},{9,13},{13,1},{2,6},{6,10},{... | collective-permute-start | bytes 1671176 | tf_op jit(solution)/shard_map/ppermute | solution.py:557
  38.7 19.1 %collective-permute-start.8 = (bf16[256,512]{1,0:T(8,128)(2,1)S(1)}, bf16[256,512]{1,0:T(8,128)(2,1)S(1)}, u32[]{:S(2)}, u32[]{:S(2)}) collective-permute-start(bf16[256,512]{1,0:T(8,128)(2,1)S(1)} %get-tuple-element.21), channel_id=1, source_target_pairs={{0,2},{1,3},{2,0},{3,1},{4,6},{5,7},{6,4},{7,5},{8,10},{9,11},{10,... | collective-permute-start | bytes 786440 | tf_op jit(solution)/shard_map/ppermute | solution.py:538
  39.4 18.5 %collective-permute-start.9 = (bf16[256,512]{1,0:T(8,128)(2,1)S(1)}, bf16[256,512]{1,0:T(8,128)(2,1)S(1)}, u32[]{:S(2)}, u32[]{:S(2)}) collective-permute-start(bf16[256,512]{1,0:T(8,128)(2,1)S(1)} %get-tuple-element.22), channel_id=1, source_target_pairs={{0,3},{1,2},{2,1},{3,0},{4,7},{5,6},{6,5},{7,4},{8,11},{9,10},{10,... | collective-permute-start | bytes 786440 | tf_op jit(solution)/shard_map/ppermute | solution.py:538
  52.0 15.6 %collective-permute-start.10 = (f32[136,1024]{1,0:T(8,128)S(1)}, f32[136,1024]{1,0:T(8,128)S(1)}, u32[]{:S(2)}, u32[]{:S(2)}) collective-permute-start(f32[136,1024]{1,0:T(8,128)S(1)} %add.51.refs_2_), channel_id=1, source_target_pairs={{0,4},{4,8},{8,12},{12,0},{1,5},{5,9},{9,13},{13,1},{2,6},{6,10},{... | collective-permute-start | bytes 1671176 | tf_op jit(solution)/shard_map/ppermute | solution.py:557
  55.7 14.0 %collective-permute-start.6 = (bf16[256,512]{1,0:T(8,128)(2,1)S(1)}, bf16[256,512]{1,0:T(8,128)(2,1)S(1)}, u32[]{:S(2)}, u32[]{:S(2)}) collective-permute-start(bf16[256,512]{1,0:T(8,128)(2,1)S(1)} %get-tuple-element.19), channel_id=1, source_target_pairs={{0,2},{1,3},{2,0},{3,1},{4,6},{5,7},{6,4},{7,5},{8,10},{9,11},{10,... | collective-permute-start | bytes 786440 | tf_op jit(solution)/shard_map/ppermute | solution.py:538
  56.3 13.8 %collective-permute-start.7 = (bf16[256,512]{1,0:T(8,128)(2,1)S(1)}, bf16[256,512]{1,0:T(8,128)(2,1)S(1)}, u32[]{:S(2)}, u32[]{:S(2)}) collective-permute-start(bf16[256,512]{1,0:T(8,128)(2,1)S(1)} %get-tuple-element.20), channel_id=1, source_target_pairs={{0,3},{1,2},{2,1},{3,0},{4,7},{5,6},{6,5},{7,4},{8,11},{9,10},{10,... | collective-permute-start | bytes 786440 | tf_op jit(solution)/shard_map/ppermute | solution.py:538
  67.7 16.1 %collective-permute-start.11 = (f32[136,1024]{1,0:T(8,128)S(1)}, f32[136,1024]{1,0:T(8,128)S(1)}, u32[]{:S(2)}, u32[]{:S(2)}) collective-permute-start(f32[136,1024]{1,0:T(8,128)S(1)} %add.52), channel_id=1, source_target_pairs={{0,4},{4,8},{8,12},{12,0},{1,5},{5,9},{9,13},{13,1},{2,6},{6,10},{... | collective-permute-start | bytes 1671176 | tf_op jit(solution)/shard_map/ppermute | solution.py:557
  93.2 22.4 %collective-permute-start.15 = (bf16[128,896]{1,0:T(8,128)(2,1)S(1)}, bf16[128,896]{1,0:T(8,128)(2,1)S(1)}, u32[]{:S(2)}, u32[]{:S(2)}) collective-permute-start(bf16[128,896]{1,0:T(8,128)(2,1)S(1)} %get-tuple-element.24.refs_0_), channel_id=1, source_target_pairs={{0,4},{4,8},{8,12},{12,0},{1,5},{5,9},{9,13},{13,1},{2,6},{6,10},{... | collective-permute-start | bytes 688136 | tf_op jit(solution)/shard_map/ppermute | solution.py:597
  95.2 24.0 %collective-permute-start.16 = (bf16[128,896]{1,0:T(8,128)(2,1)S(1)}, bf16[128,896]{1,0:T(8,128)(2,1)S(1)}, u32[]{:S(2)}, u32[]{:S(2)}) collective-permute-start(bf16[128,896]{1,0:T(8,128)(2,1)S(1)} %get-tuple-element.24.refs_0_), channel_id=1, source_target_pairs={{0,8},{4,12},{8,0},{12,4},{1,9},{5,13},{9,1},{13,5},{2,10},{6,14},... | collective-permute-start | bytes 688136 | tf_op jit(solution)/shard_map/ppermute | solution.py:597
  98.5 23.7 %collective-permute-start.17 = (bf16[128,896]{1,0:T(8,128)(2,1)S(1)}, bf16[128,896]{1,0:T(8,128)(2,1)S(1)}, u32[]{:S(2)}, u32[]{:S(2)}) collective-permute-start(bf16[128,896]{1,0:T(8,128)(2,1)S(1)} %get-tuple-element.24.refs_0_), channel_id=1, source_target_pairs={{0,12},{4,0},{8,4},{12,8},{1,13},{5,1},{9,5},{13,9},{2,14},{6,2},{... | collective-permute-start | bytes 688136 | tf_op jit(solution)/shard_map/ppermute | solution.py:597
  106.7 24.9 %collective-permute-start.12 = (bf16[128,384]{1,0:T(8,128)(2,1)S(1)}, bf16[128,384]{1,0:T(8,128)(2,1)S(1)}, u32[]{:S(2)}, u32[]{:S(2)}) collective-permute-start(bf16[128,384]{1,0:T(8,128)(2,1)S(1)} %factor_bottom.1.refs_1_), channel_id=1, source_target_pairs={{0,4},{4,8},{8,12},{12,0},{1,5},{5,9},{9,13},{13,1},{2,6},{6,10},{... | collective-permute-start | bytes 294920 | tf_op jit(solution)/shard_map/ppermute | solution.py:597
  108.8 22.8 %collective-permute-start.13 = (bf16[128,384]{1,0:T(8,128)(2,1)S(1)}, bf16[128,384]{1,0:T(8,128)(2,1)S(1)}, u32[]{:S(2)}, u32[]{:S(2)}) collective-permute-start(bf16[128,384]{1,0:T(8,128)(2,1)S(1)} %factor_bottom.1.refs_1_), channel_id=1, source_target_pairs={{0,8},{4,12},{8,0},{12,4},{1,9},{5,13},{9,1},{13,5},{2,10},{6,14},... | collective-permute-start | bytes 294920 | tf_op jit(solution)/shard_map/ppermute | solution.py:597
  115.6 16.1 %collective-permute-start.14 = (bf16[128,384]{1,0:T(8,128)(2,1)S(1)}, bf16[128,384]{1,0:T(8,128)(2,1)S(1)}, u32[]{:S(2)}, u32[]{:S(2)}) collective-permute-start(bf16[128,384]{1,0:T(8,128)(2,1)S(1)} %factor_bottom.1.refs_1_), channel_id=1, source_target_pairs={{0,12},{4,0},{8,4},{12,8},{1,13},{5,1},{9,5},{13,9},{2,14},{6,2},{... | collective-permute-start | bytes 294920 | tf_op jit(solution)/shard_map/ppermute | solution.py:597

commit v2 on v1

--- a/solution.py
+++ b/solution.py
@@ -18,16 +18,20 @@
 BLOCK_HEADS = BLOCK_W // HEAD_SIZE
 KV_BLOCKS = GROUP // BLOCK_HEADS
 PANELS = BLOCK_W // SPAN
-STARTS = [sum(BLOCK_W - SPAN * j for j in range(k)) for k in range(PANELS)]
-PACKED = sum(BLOCK_W - SPAN * j for j in range(PANELS))
-VMEM_BYTES = 50 * 1024 * 1024
+SUM_ROWS = SPAN * (PANELS * (PANELS - 1) // 2 + PANELS // 2) + 8
+VMEM_BYTES = 50 * 2**20
+FULL_VMEM = 63 * 2**20
+TURN_VMEM = 50 * 2**20
+ATTENTION_VMEM = 44 * 2**20
+WHITEN_VMEM = 44 * 2**20
+OTHER_VMEM = 44 * 2**20
 F32 = jnp.float32
 BF16 = jnp.bfloat16
 NT = (((1,), (1,)), ((), ()))
 TN = (((0,), (0,)), ((), ()))
 
 
-def params(limit=VMEM_BYTES):
+def params(limit=OTHER_VMEM):
     return pltpu.CompilerParams(vmem_limit_bytes=limit)
 
 
@@ -49,31 +53,32 @@
     return jnp.where(code < 0.0, -root, root)
 
 
-def marker():
-    rows = lax.broadcasted_iota(jnp.int32, (SPAN, SPAN), 0)
-    columns = lax.broadcasted_iota(jnp.int32, (SPAN, SPAN), 1)
-    return (rows == SPAN - 1) & (columns == 0)
-
-
 def exponent_of(largest):
     return jnp.ceil(jnp.log(jnp.maximum(largest, 1e-30)) * (1.0 / math.log(2.0)) + 0.001)
 
 
-def write_coded(panels, out, largest):
+def write_coded(tiles, out):
+    off, pairs = tile_order(tiles.rows, tiles.columns)
+    places = off + [(i, i) for i in range(tiles.rows)]
+    largest = functools.reduce(jnp.maximum, [jnp.max(jnp.abs(tiles(*p)), axis=(0, 1), keepdims=True) for p in places])
     exponent = exponent_of(largest)
-    at = 0
-    for k, panel in enumerate(panels):
-        coded = encode(panel, exponent)
-        if k == 0:
-            first = jnp.where(marker(), jnp.broadcast_to(exponent, (SPAN, SPAN)), coded[:, :SPAN])
-            coded = jnp.concatenate([first, coded[:, SPAN:]], axis=1)
-        out[:, at : at + panel.shape[1]] = coded.astype(BF16)
-        at += panel.shape[1]
-
-
-def read_coded(ref):
-    exponent = ref[SPAN - 16 : SPAN, :SPAN].astype(F32)[15:16, 0:1]
-    return decode(ref[...], exponent)
+    (line,) = fold(tiles, out, lambda value: encode(value, exponent))
+    row = lax.broadcasted_iota(jnp.int32, (16, SPAN), 0)
+    out[(len(off) + len(pairs)) * SPAN :] = jnp.where(row < 8, line, exponent).astype(BF16)
+
+
+def read_coded(ref, columns):
+    upper, equal = diagonal_masks()
+    off, pairs = tile_order(2, columns)
+    at = (len(off) + len(pairs)) * SPAN
+    tail = ref[at:].astype(F32)
+    exponent = tail[15:16, 0:1]
+    tiles = {place: decode(ref[i * SPAN : (i + 1) * SPAN], exponent) for i, place in enumerate(off)}
+    square = decode(ref[at - SPAN : at], exponent)
+    line = decode(tail[0:1], exponent)
+    tiles[0, 0] = jnp.where(upper, square, 0.0)
+    tiles[1, 1] = jnp.where(equal, line, jnp.where(upper, square.T, 0.0))
+    return tiles
 
 
 def split(value):
@@ -196,12 +201,9 @@
         return carry
 
     lax.fori_loop(0, 3, one_pass, 0)
-    for i, packed in enumerate(fold(total)):
-        out[:, i * BLOCK_W : (i + 1) * BLOCK_W] = packed
-
-
-def tile_of(ref, i, j):
-    return ref[i * SPAN : (i + 1) * SPAN, j * SPAN : (j + 1) * SPAN]
+    lines = fold(Tiles(total, PANELS, PANELS, False), out)
+    row = lax.broadcasted_iota(jnp.int32, (8, SPAN), 0)
+    out[SUM_ROWS - 8 :] = jnp.where(row == 0, lines[0], lines[1])
 
 
 def diagonal_masks():
@@ -210,29 +212,47 @@
     return rows <= columns, rows == columns
 
 
-def fold(ref):
+def tile_order(rows, columns):
+    off = [(i, j) for i in range(rows) for j in range(i + 1, columns)]
+    return off, [(i, i + 1) for i in range(0, rows, 2)]
+
+
+def fold(tiles, out, change=lambda value: value):
     upper, equal = diagonal_masks()
-    for off, (a, b) in ((((0, 1), (0, 2), (0, 3)), (0, 1)), (((1, 2), (1, 3), (2, 3)), (2, 3))):
-        second = tile_of(ref, b, b)
-        square = jnp.where(upper, tile_of(ref, a, a), second)
-        line = jnp.sum(jnp.where(equal, second, 0.0), axis=0, keepdims=True)
-        body = jnp.concatenate([tile_of(ref, *where) for where in off] + [square], axis=1)
-        tail = jnp.concatenate([jnp.zeros((8, 3 * SPAN), F32), jnp.broadcast_to(line, (8, SPAN))], axis=1)
-        yield jnp.concatenate([body, tail], axis=0)
-
-
-def unfold(packs, work):
+    off, pairs = tile_order(tiles.rows, tiles.columns)
+    for i, place in enumerate(off):
+        out[i * SPAN : (i + 1) * SPAN] = change(tiles(*place)).astype(out.dtype)
+    lines = []
+    for i, (a, b) in enumerate(pairs):
+        second = tiles(b, b)
+        at = (len(off) + i) * SPAN
+        lower = second.T if tiles.turn else second
+        out[at : at + SPAN] = change(jnp.where(upper, tiles(a, a), lower)).astype(out.dtype)
+        lines.append(change(jnp.sum(jnp.where(equal, second, 0.0), axis=0, keepdims=True)))
+    return lines
+
+
+class Tiles:
+    def __init__(self, ref, rows, columns, turn):
+        self.ref, self.rows, self.columns, self.turn = ref, rows, columns, turn
+
+    def __call__(self, i, j):
+        return self.ref[i * SPAN : (i + 1) * SPAN, j * SPAN : (j + 1) * SPAN]
+
+
+def unfold(total, work):
     upper, equal = diagonal_masks()
+    off, pairs = tile_order(PANELS, PANELS)
+    for i, (row, column) in enumerate(off):
+        work[row * SPAN : (row + 1) * SPAN, column * SPAN : (column + 1) * SPAN] = total[i * SPAN : (i + 1) * SPAN]
     trace = jnp.zeros((1, 1), F32)
     squares = []
-    for pack, off, (a, b) in zip(
-        packs, (((0, 1), (0, 2), (0, 3)), ((1, 2), (1, 3), (2, 3))), ((0, 1), (2, 3))
-    ):
-        for i, (row, column) in enumerate(off):
-            work[row * SPAN : (row + 1) * SPAN, column * SPAN : (column + 1) * SPAN] = pack[:SPAN, i * SPAN : (i + 1) * SPAN]
-        square = pack[:SPAN, 3 * SPAN :]
+    for i, (a, b) in enumerate(pairs):
+        at = (len(off) + i) * SPAN
+        square = total[at : at + SPAN]
         turned = square.T
-        line = jnp.broadcast_to(pack[SPAN : SPAN + 1, 3 * SPAN :], (SPAN, SPAN))
+        at = (len(off) + len(pairs)) * SPAN + i
+        line = jnp.broadcast_to(total[at : at + 1], (SPAN, SPAN))
         squares.append((a, jnp.where(upper, square, turned)))
         squares.append((b, jnp.where(equal, line, jnp.where(upper, turned, square))))
     for _, square in squares:
@@ -257,7 +277,7 @@
     if start == 0:
         work[...] = jnp.zeros_like(work)
         total = given[0][...] + given[1][...] if received == 2 else given[0][...]
-        unfold((total[:, :BLOCK_W], total[:, BLOCK_W:]), work)
+        unfold(total, work)
     else:
         work[...] = given[0][...]
     previous[...] = jnp.zeros_like(previous)
@@ -326,9 +346,7 @@
             triple(before[:, done:], True), triple(before[:, done:], False), TN, preferred_element_type=F32
         )
         rest[...] = work[done:, done:] - final
-    ready = [upper[k * SPAN : (k + 1) * SPAN, k * SPAN :] for k in range((stop - start) // SPAN)]
-    largest = functools.reduce(jnp.maximum, [jnp.max(jnp.abs(p), axis=(0, 1), keepdims=True) for p in ready])
-    write_coded(ready, out, largest)
+    write_coded(Tiles(upper, (stop - start) // SPAN, panels, True), out)
 
 
 def whiten_kernel(order, *refs, blocks, starts, first, chunks, aliased):
@@ -356,18 +374,14 @@
 
             @pl.when(step == b)
             def _(b=b):
-                upper = read_coded(u_refs[b * count + which])
-                rows = lax.broadcasted_iota(jnp.int32, (SPAN, SPAN), 0)
-                columns = lax.broadcasted_iota(jnp.int32, (SPAN, SPAN), 1)
-                at = 0
-                for k in range(half // SPAN):
-                    panel = upper[:, at : at + width - SPAN * k]
-                    at += width - SPAN * k
-                    pieces = [jnp.zeros((SPAN, SPAN * k), F32)] if k else []
-                    pieces += [jnp.where(rows > columns, 0.0, panel[:, :SPAN]), panel[:, SPAN:]]
-                    high, low = split(jnp.concatenate([p for p in pieces if p.shape[1]], axis=1))
-                    left[k * SPAN : (k + 1) * SPAN, :width] = high
-                    left[k * SPAN : (k + 1) * SPAN, width : 2 * width] = low
+                tiles = read_coded(u_refs[b * count + which], width // SPAN)
+                for row in range(half // SPAN):
+                    rows = slice(row * SPAN, (row + 1) * SPAN)
+                    for column in range(width // SPAN):
+                        value = tiles[row, column] if column >= row else jnp.zeros((SPAN, SPAN), F32)
+                        high, low = split(value)
+                        left[rows, column * SPAN : (column + 1) * SPAN] = high
+                        left[rows, width + column * SPAN : width + (column + 1) * SPAN] = low
 
         for c in range(chunks):
             if count == 1:
@@ -428,7 +442,7 @@
             (x * 2 + c, (x + distance) % chips * 2 + (1 - c if cross else c)) for x in range(chips) for c in range(2)
         ]
 
-    def cut(targets, columns, scalars, name, after=(), limit=VMEM_BYTES):
+    def cut(targets, columns, scalars, name, after=(), limit=OTHER_VMEM):
         specs, arrays = [], []
         for target in targets:
             for array, size, index in columns:
@@ -461,7 +475,7 @@
             in_specs=[pl.BlockSpec((tile, BLOCK_W), lambda b, o: (o, first + b))] + [anywhere] * len(before),
             out_specs=pl.BlockSpec((BLOCK_W, tile), lambda b, o: (first + b, o)),
             input_output_aliases={1: 0} if first else {},
-            compiler_params=params(),
+            compiler_params=params(TURN_VMEM),
             cost_estimate=cost(1.0e9 * count, 2**20),
             name="turn_weight",
         )(out_weight, *before)
@@ -479,7 +493,7 @@
         carriers = pieces[: min(t + 1, per)]
         which = jnp.where(kv == first_kv, 0, 1).astype(jnp.int32)
         meta = jnp.concatenate([jnp.stack([own, turns[t], kv, which]), doc_lengths[0], span_order[0]])
-        folded = jax.ShapeDtypeStruct((SPAN + 8, 2 * BLOCK_W), F32)
+        folded = jax.ShapeDtypeStruct((SUM_ROWS, SPAN), F32)
         peer_kv = blocks * BLOCK_W // HEAD_SIZE
         return pl.pallas_call(
             functools.partial(
@@ -504,7 +518,7 @@
                 + [pl.BlockSpec((tokens, 2 * HEAD_SIZE), lambda i, meta: (0, BLOCK_W // (2 * HEAD_SIZE)))]
                 * (len(carriers) * len(far))
                 + [anywhere] * len(after),
-                out_specs=pl.BlockSpec((SPAN + 8, 2 * BLOCK_W), lambda i, meta: (0, 0)),
+                out_specs=pl.BlockSpec((SUM_ROWS, SPAN), lambda i, meta: (0, 0)),
                 scratch_shapes=[
                     pltpu.VMEM((all_spans, BLOCK_HEADS * SPAN, HEAD_SIZE), BF16),
                     pltpu.VMEM((all_spans, SPAN, HEAD_SIZE), BF16),
@@ -516,7 +530,7 @@
                     pltpu.VMEM((BLOCK_W, BLOCK_W), F32),
                 ],
             ),
-            compiler_params=params(),
+            compiler_params=params(ATTENTION_VMEM),
             cost_estimate=cost(1.4e10, 2**20),
             name="attention_outer_products",
         )(meta, query, peer, *pieces[t], key, value, peer, peer, *[array for carrier in carriers for array in carrier], *after)
@@ -530,16 +544,18 @@
             if t < per:
                 columns += [(array, HEAD_SIZE, lambda target, meta: target * per + meta[2]) for array in (key, value)]
             scalars = jnp.stack([own, turns[t], kv])
-            after = [] if t == 0 else [peer, turned] if t == 1 else [held[t - 2]]
+            after = [] if t == 0 else [peer, turned] if t == 1 else [peer, turned]
             parts = cut(
                 [target_at(*where) for where in far], columns, scalars, "cut_piece", after,
-                VMEM_BYTES if t else 63 * 2**20,
+                OTHER_VMEM if t else FULL_VMEM,
             )
+            if t > 1:
+                *parts, held[t - 2] = lax.optimization_barrier((*parts, held[t - 2]))
             pieces.append([lax.ppermute(part, "seq", moved(*where)) for part, where in zip(parts, far)])
         if t == 0:
             columns = [(query, blocks * BLOCK_W, lambda target, meta: target)]
             columns += [(array, per * HEAD_SIZE, lambda target, meta: target) for array in (key, value)]
-            peer = cut([target_at(0, 1)], columns, own[None], "cut_peer", parts)[0]
+            peer = cut([target_at(0, 1)], columns, own[None], "cut_peer", parts, FULL_VMEM)[0]
             turned = turn(0, 1, peer)
             peer = lax.ppermute(peer, "seq", moved(0, 1))
             turned = turn(1, 1, turned)
@@ -559,20 +575,22 @@
         turned = turn(blocks - 1, 1, turned, grams[-1])
 
     half = BLOCK_W // 2
-    top_width, bottom_width = STARTS[2], PACKED - STARTS[2]
+    top_rows, bottom_rows = [
+        SPAN * (sum(len(part) for part in tile_order(2, columns))) + 16 for columns in (PANELS, PANELS // 2)
+    ]
     scratch = lambda width: [pltpu.VMEM((width, width), F32), pltpu.VMEM((32, width), F32), pltpu.VMEM((half, width), F32)]
 
     def factor_top(*given):
         return pl.pallas_call(
             functools.partial(factor_kernel, start=0, stop=half, received=len(given)),
             out_shape=[
-                jax.ShapeDtypeStruct((SPAN, top_width), BF16),
+                jax.ShapeDtypeStruct((top_rows, SPAN), BF16),
                 jax.ShapeDtypeStruct((half, half), F32),
             ],
             in_specs=[vmem] * len(given),
             out_specs=[vmem] * 2,
             scratch_shapes=scratch(BLOCK_W),
-            compiler_params=params(),
+            compiler_params=params(OTHER_VMEM),
             cost_estimate=cost(1.0e10, 2**20),
             name="factor_top",
         )(*given)
@@ -580,11 +598,11 @@
     def factor_bottom(rest):
         return pl.pallas_call(
             functools.partial(factor_kernel, start=half, stop=BLOCK_W, received=1),
-            out_shape=jax.ShapeDtypeStruct((SPAN, bottom_width), BF16),
+            out_shape=jax.ShapeDtypeStruct((bottom_rows, SPAN), BF16),
             in_specs=[vmem],
             out_specs=vmem,
             scratch_shapes=scratch(half),
-            compiler_params=params(),
+            compiler_params=params(OTHER_VMEM),
             cost_estimate=cost(0.9e10, 2**20),
             name="factor_bottom",
         )(rest)
@@ -638,7 +656,7 @@
                 ],
             ),
             input_output_aliases={1 + len(uppers) + chunks: 0} if more else {},
-            compiler_params=params(),
+            compiler_params=params(WHITEN_VMEM),
             cost_estimate=cost(2.0e9 * len(uppers), 2**20),
             name="whiten_bottom" if starts[0] else "whiten_top",
         )(order, *uppers, *[turned] * chunks, *more)

time: 139 us -> 132 us (0.950)
  the two profiles are of different devices: /device:TPU:14 before, /device:TPU:0 now
where the time goes in v2:
time: 132 us; the launch traced here: 130 us
  Pallas kernels  95 us (72%)
  starting transfers between devices  21.3 us (16%)
  waiting for transfers between devices  11.1 us (8%)
  local copies, waits for them, and re-layouts  1.68 us (1%)
    pallas_call x4, Pallas kernels, grams_of(): pl.pallas_call(functools.partial(attention_kernel, chips=chips, spans=spa...  35.6 us
    pallas_call x3, Pallas kernels, whiten(): pl.pallas_call(functools.partial(whiten_kernel, blocks=count, starts=star...  17.9 us
    pallas_call x4, Pallas kernels, turn(): pl.pallas_call(turn_kernel, out_shape=jax.ShapeDtypeStruct((blocks * BLOC...  16.8 us
    pallas_call x1, Pallas kernels, factor_top(): pl.pallas_call(functools.partial(factor_kernel, start=0, stop=half, recei...  9.33 us
    ppermute x6, starting transfers between devices, shared(): lax.ppermute(array, 'dp', [(z, (z + d) % ring) for z in range(ring)])  9.13 us
    pallas_call x1, Pallas kernels, factor_bottom(): pl.pallas_call(functools.partial(factor_kernel, start=half, stop=BLOCK_W,...  8.22 us
    ppermute x8, starting transfers between devices, shards(): lax.ppermute(part, 'seq', moved(*where))  8.12 us
    pallas_call x5, Pallas kernels, cut(): pl.pallas_call(functools.partial(cut_kernel, targets=len(targets), given=...  7.17 us
  transfers between devices with their start and end apart: 18, of which 4 were waited for; matrix products, arithmetic and copies ran while one was open for 1% of the time, Pallas kernels for 57%

profile of v2, /device:TPU:0, one launch (start us, length us, event | category | flops | bytes accessed | tf_op | source)
XLA Modules:
  0.0 130.4 jit_solution(12514457881606398778)
XLA Ops:
  0.6 2.8 %cut_piece.4 = (bf16[256,768]{1,0:T(8,128)(2,1)}, bf16[256,768]{1,0:T(8,128)(2,1)}) custom-call(s32[3]{0:T(128)} %pad_add_fusion.1.meta, bf16[256,8192]{1,0:T(8,128)(2,1)} %bitcast.21, bf16[256,1024]{1,0:T(8,128)(2,1)} %bitcast.34, bf16[256,1024]{1,0:T(8,128)(2,1)} %bitcast.43, bf16[256,8192]{1,0:T(8,128)(2,1)} %bitcast.22, bf16[256,1024]{1,0:T(8,128)(2,1)} %bitcast.35, ...), custom_call_target="tpu_custom_call" | custom-call | bytes 2097152 | tf_op jit(solution)/shard_map/cut_piece/pallas_call | solution.py:454
  3.4 2.5 %cut_peer.1.refs_0_ = bf16[256,2560]{1,0:T(8,128)(2,1)} custom-call(s32[1]{0:T(128)} %bitcast.4.meta, bf16[256,8192]{1,0:T(8,128)(2,1)} %bitcast.23, bf16[256,1024]{1,0:T(8,128)(2,1)} %bitcast.36, bf16[256,1024]{1,0:T(8,128)(2,1)} %bitcast.45, bf16[256,768]{1,0:T(8,128)(2,1)} %get-tuple-element.19.refs_3_, bf16[256,768]{1,0:T(8,128)(2,1)} %get-tuple-element.20.refs_4_), custom_call_target="tpu_custom_call" | custom-call | bytes 2097152 | tf_op jit(solution)/shard_map/cut_peer/pallas_call | solution.py:454
  6.3 2.5 %collective-permute-start.3 = (bf16[256,768]{1,0:T(8,128)(2,1)}, bf16[256,768]{1,0:T(8,128)(2,1)S(1)}, u32[]{:S(2)}, u32[]{:S(2)}) collective-permute-start(bf16[256,768]{1,0:T(8,128)(2,1)} %get-tuple-element.19.refs_3_), channel_id=1, source_target_pairs={{0,2},{1,3},{2,0},{3,1},{4,6},{5,7},{6,4},{7,5},{8,10},{9,11},{10,... | collective-permute-start | bytes 1179656 | tf_op jit(solution)/shard_map/ppermute | solution.py:554
  9.3 1.3 %copy-done.4 = bf16[256,2560]{1,0:T(8,128)(2,1)S(1)} copy-done((bf16[256,2560]{1,0:T(8,128)(2,1)S(1)}, bf16[256,2560]{1,0:T(8,128)(2,1)}, u32[]{:S(2)}) %copy-start.4) | copy-done | bytes 1310744
  10.6 4.1 %turn_weight.4.refs_0_ = bf16[2048,2048]{1,0:T(8,128)(2,1)} custom-call(bf16[2048,2048]{1,0:T(8,128)(2,1)} %w_ref.7, bf16[256,2560]{1,0:T(8,128)(2,1)S(1)} %copy-done.4), custom_call_target="tpu_custom_call" | custom-call | flops 1000000000 | bytes 1048576 | tf_op jit(solution)/shard_map/turn_weight/pallas_call | solution.py:471
  14.8 4.5 %turn_weight.5.refs_7_.refs_0_ = bf16[2048,2048]{1,0:T(8,128)(2,1)} custom-call(bf16[2048,2048]{1,0:T(8,128)(2,1)} %w_ref.7, bf16[2048,2048]{1,0:T(8,128)(2,1)} %turn_weight.4.refs_0_), custom_call_target="tpu_custom_call", output_to_operand_aliasing={{}: (1, {})} | custom-call | flops 1000000000 | bytes 1048576 | tf_op jit(solution)/shard_map/turn_weight/pallas_call | solution.py:471
  19.5 0.7 cut_piece.5
  20.2 1.8 %collective-permute-start.1 = (bf16[256,768]{1,0:T(8,128)(2,1)S(1)}, bf16[256,768]{1,0:T(8,128)(2,1)S(1)}, u32[]{:S(2)}, u32[]{:S(2)}) collective-permute-start(bf16[256,768]{1,0:T(8,128)(2,1)S(1)} %get-tuple-element.21.refs_1_), channel_id=1, source_target_pairs={{0,2},{1,3},{2,0},{3,1},{4,6},{5,7},{6,4},{7,5},{8,10},{9,11},{10,... | collective-permute-start | bytes 1179656 | tf_op jit(solution)/shard_map/ppermute | solution.py:554
  22.0 4.1 %turn_weight.6.refs_3_.refs_10_.refs_0_ = bf16[2048,2048]{1,0:T(8,128)(2,1)} custom-call(bf16[2048,2048]{1,0:T(8,128)(2,1)} %w_ref.7, bf16[2048,2048]{1,0:T(8,128)(2,1)} %turn_weight.5.refs_7_.refs_0_, bf16[256,768]{1,0:T(8,128)(2,1)S(1)} %get-tuple-element.21.refs_1_), custom_call_target="tpu_custom_call", output_to_operand_aliasing={{}: (1, {})} | custom-call | flops 1000000000 | bytes 1048576 | tf_op jit(solution)/shard_map/turn_weight/pallas_call | solution.py:471
  26.1 1.0 collective-permute-done.4.refs_9_.refs_3_
  27.1 8.9 %attention_outer_products.5 = f32[1032,128]{1,0:T(8,128)S(1)} custom-call(s32[20]{0:T(128)S(1)} %concatenate.14.meta, bf16[256,8192]{1,0:T(8,128)(2,1)S(1)} %bitcast.26, bf16[256,2560]{1,0:T(8,128)(2,1)S(1)} %collective-permute-done.refs_6_.refs_2_.refs_1_.refs_7_, bf16[256,768]{1,0:T(8,128)(2,1)S(1)} %collective-permute-done.3.refs_8_.refs_2_, ...), custom_call_target="tpu_custom_call" | custom-call | flops 14000000000 | bytes 1048576 | tf_op jit(solution)/shard_map/attention_outer_products/pallas_call | solution.py:498
  35.9 1.8 %collective-permute-start.5 = (f32[1032,128]{1,0:T(8,128)S(1)}, f32[1032,128]{1,0:T(8,128)S(1)}, u32[]{:S(2)}, u32[]{:S(2)}) collective-permute-start(f32[1032,128]{1,0:T(8,128)S(1)} %attention_outer_products.5), channel_id=1, source_target_pairs={{0,4},{4,8},{8,12},{12,0},{1,5},{5,9},{9,13},{13,1},{2,6},{6,10},{... | collective-permute-start | bytes 1585160 | tf_op jit(solution)/shard_map/ppermute | solution.py:573
  38.3 1.5 %collective-permute-start.8 = (bf16[256,512]{1,0:T(8,128)(2,1)S(1)}, bf16[256,512]{1,0:T(8,128)(2,1)S(1)}, u32[]{:S(2)}, u32[]{:S(2)}) collective-permute-start(bf16[256,512]{1,0:T(8,128)(2,1)S(1)} %get-tuple-element.29), channel_id=1, source_target_pairs={{0,2},{1,3},{2,0},{3,1},{4,6},{5,7},{6,4},{7,5},{8,10},{9,11},{10,... | collective-permute-start | bytes 786440 | tf_op jit(solution)/shard_map/ppermute | solution.py:554
  40.7 3.3 %collective-permute-done.2.refs_3_.refs_11_ = bf16[256,768]{1,0:T(8,128)(2,1)S(1)} collective-permute-done((bf16[256,768]{1,0:T(8,128)(2,1)S(1)}, bf16[256,768]{1,0:T(8,128)(2,1)S(1)}, u32[]{:S(2)}, u32[]{:S(2)}) %collective-permute-start.2) | collective-permute-done | bytes 393248 | tf_op jit(solution)/shard_map/ppermute | solution.py:554
  43.9 8.9 %attention_outer_products.4 = f32[1032,128]{1,0:T(8,128)S(1)} custom-call(s32[20]{0:T(128)S(1)} %concatenate.13.meta, bf16[256,8192]{1,0:T(8,128)(2,1)S(1)} %bitcast.31, bf16[256,2560]{1,0:T(8,128)(2,1)S(1)} %collective-permute-done.refs_6_.refs_2_.refs_1_.refs_7_, bf16[256,768]{1,0:T(8,128)(2,1)S(1)} %collective-permute-done.1.refs_2_.refs_10_, ...), custom_call_target="tpu_custom_call" | custom-call | flops 14000000000 | bytes 1048576 | tf_op jit(solution)/shard_map/attention_outer_products/pallas_call | solution.py:498
  52.9 1.8 %collective-permute-start.10 = (f32[1032,128]{1,0:T(8,128)S(1)}, f32[1032,128]{1,0:T(8,128)S(1)}, u32[]{:S(2)}, u32[]{:S(2)}) collective-permute-start(f32[1032,128]{1,0:T(8,128)S(1)} %add.51), channel_id=1, source_target_pairs={{0,4},{4,8},{8,12},{12,0},{1,5},{5,9},{9,13},{13,1},{2,6},{6,10},{... | collective-permute-start | bytes 1585160 | tf_op jit(solution)/shard_map/ppermute | solution.py:573
  54.7 1.4 %collective-permute-start.6 = (bf16[256,512]{1,0:T(8,128)(2,1)S(1)}, bf16[256,512]{1,0:T(8,128)(2,1)S(1)}, u32[]{:S(2)}, u32[]{:S(2)}) collective-permute-start(bf16[256,512]{1,0:T(8,128)(2,1)S(1)} %get-tuple-element.25), channel_id=1, source_target_pairs={{0,2},{1,3},{2,0},{3,1},{4,6},{5,7},{6,4},{7,5},{8,10},{9,11},{10,... | collective-permute-start | bytes 786440 | tf_op jit(solution)/shard_map/ppermute | solution.py:554
  56.6 9.0 %attention_outer_products.7 = f32[1032,128]{1,0:T(8,128)S(1)} custom-call(s32[20]{0:T(128)S(1)} %concatenate.15.meta, bf16[256,8192]{1,0:T(8,128)(2,1)S(1)} %bitcast.32, bf16[256,2560]{1,0:T(8,128)(2,1)S(1)} %collective-permute-done.refs_6_.refs_2_.refs_1_.refs_7_, bf16[256,512]{1,0:T(8,128)(2,1)S(1)} %collective-permute-done.8.refs_2_, ...), custom_call_target="tpu_custom_call" | custom-call | flops 14000000000 | bytes 1048576 | tf_op jit(solution)/shard_map/attention_outer_products/pallas_call | solution.py:498
  65.7 3.9 %collective-permute-done.10 = f32[1032,128]{1,0:T(8,128)S(1)} collective-permute-done((f32[1032,128]{1,0:T(8,128)S(1)}, f32[1032,128]{1,0:T(8,128)S(1)}, u32[]{:S(2)}, u32[]{:S(2)}) %collective-permute-start.10) | collective-permute-done | bytes 528416 | tf_op jit(solution)/shard_map/ppermute | solution.py:573
  69.7 8.8 %attention_outer_products.6.refs_0_.refs_1_ = f32[1032,128]{1,0:T(8,128)S(1)} custom-call(s32[20]{0:T(128)S(1)} %concatenate.12.meta, bf16[256,8192]{1,0:T(8,128)(2,1)S(1)} %bitcast.33, bf16[256,2560]{1,0:T(8,128)(2,1)S(1)} %collective-permute-done.refs_6_.refs_2_.refs_1_.refs_7_, bf16[256,512]{1,0:T(8,128)(2,1)S(1)} %collective-permute-done.6.refs_2_, ...), custom_call_target="tpu_custom_call" | custom-call | flops 14000000000 | bytes 1048576 | tf_op jit(solution)/shard_map/attention_outer_products/pallas_call | solution.py:498
  78.6 4.1 %turn_weight.7.refs_2_.refs_3_.refs_4_.refs_5_.refs_6_ = bf16[2048,2048]{1,0:T(8,128)(2,1)} custom-call(bf16[2048,2048]{1,0:T(8,128)(2,1)} %w_ref.7, bf16[2048,2048]{1,0:T(8,128)(2,1)} %turn_weight.6.refs_3_.refs_10_.refs_0_, f32[1032,128]{1,0:T(8,128)S(1)} %attention_outer_products.6.refs_0_.refs_1_), custom_call_target="tpu_custom_call", output_to_operand_aliasing={{}: (1, {})} | custom-call | flops 1000000000 | bytes 1048576 | tf_op jit(solution)/shard_map/turn_weight/pallas_call | solution.py:471
  82.7 2.8 %collective-permute-done.11.refs_1_ = f32[1032,128]{1,0:T(8,128)S(1)} collective-permute-done((f32[1032,128]{1,0:T(8,128)S(1)}, f32[1032,128]{1,0:T(8,128)S(1)}, u32[]{:S(2)}, u32[]{:S(2)}) %collective-permute-start.11) | collective-permute-done | bytes 528416 | tf_op jit(solution)/shard_map/ppermute | solution.py:573
  85.5 9.3 %factor_top.1 = (bf16[784,128]{1,0:T(8,128)(2,1)S(1)}, f32[256,256]{1,0:T(8,128)S(1)}) custom-call(f32[1032,128]{1,0:T(8,128)S(1)} %attention_outer_products.6.refs_0_.refs_1_, f32[1032,128]{1,0:T(8,128)S(1)} %collective-permute-done.11.refs_1_), custom_call_target="tpu_custom_call" | custom-call | flops 10000000000 | bytes 1048576 | tf_op jit(solution)/shard_map/factor_top/pallas_call | solution.py:584
  94.9 1.5 %collective-permute-start.16 = (bf16[784,128]{1,0:T(8,128)(2,1)S(1)}, bf16[784,128]{1,0:T(8,128)(2,1)S(1)}, u32[]{:S(2)}, u32[]{:S(2)}) collective-permute-start(bf16[784,128]{1,0:T(8,128)(2,1)S(1)} %get-tuple-element.32.refs_0_), channel_id=1, source_target_pairs={{0,8},{4,12},{8,0},{12,4},{1,9},{5,13},{9,1},{13,5},{2,10},{6,14},... | collective-permute-start | bytes 602120 | tf_op jit(solution)/shard_map/ppermute | solution.py:615
  96.4 2.3 %collective-permute-start.17 = (bf16[784,128]{1,0:T(8,128)(2,1)S(1)}, bf16[784,128]{1,0:T(8,128)(2,1)S(1)}, u32[]{:S(2)}, u32[]{:S(2)}) collective-permute-start(bf16[784,128]{1,0:T(8,128)(2,1)S(1)} %get-tuple-element.32.refs_0_), channel_id=1, source_target_pairs={{0,12},{4,0},{8,4},{12,8},{1,13},{5,1},{9,5},{13,9},{2,14},{6,2},{... | collective-permute-start | bytes 602120 | tf_op jit(solution)/shard_map/ppermute | solution.py:615
  98.8 8.2 %factor_bottom.1.refs_1_ = bf16[272,128]{1,0:T(8,128)(2,1)S(1)} custom-call(f32[256,256]{1,0:T(8,128)S(1)} %get-tuple-element.31.refs_0_), custom_call_target="tpu_custom_call" | custom-call | flops 8999999488 | bytes 1048576 | tf_op jit(solution)/shard_map/factor_bottom/pallas_call | solution.py:599
  107.0 0.6 collective-permute-start.12
  107.6 1.5 %collective-permute-start.13 = (bf16[272,128]{1,0:T(8,128)(2,1)S(1)}, bf16[272,128]{1,0:T(8,128)(2,1)S(1)}, u32[]{:S(2)}, u32[]{:S(2)}) collective-permute-start(bf16[272,128]{1,0:T(8,128)(2,1)S(1)} %factor_bottom.1.refs_1_), channel_id=1, source_target_pairs={{0,8},{4,12},{8,0},{12,4},{1,9},{5,13},{9,1},{13,5},{2,10},{6,14},... | collective-permute-start | bytes 208904 | tf_op jit(solution)/shard_map/ppermute | solution.py:615
  109.1 3.5 %whiten_top.2.refs_7_ = f32[4,512,2048]{2,1,0:T(8,128)} custom-call(s32[4]{0:T(128)S(1)} %pad_add_fusion.order, bf16[784,128]{1,0:T(8,128)(2,1)S(1)} %get-tuple-element.32.refs_0_, bf16[272,128]{1,0:T(8,128)(2,1)S(1)} %factor_bottom.1.refs_1_, bf16[2048,2048]{1,0:T(8,128)(2,1)S(1)} %copy-done, bf16[2048,2048]{1,0:T(8,128)(2,1)S(1)} %copy-done, ...), custom_call_target="tpu_custom_call" | custom-call | flops 4000000000 | bytes 1048576 | tf_op jit(solution)/shard_map/whiten_top/pallas_call | solution.py:642
  112.7 3.1 %collective-permute-start.14 = (bf16[272,128]{1,0:T(8,128)(2,1)S(1)}, bf16[272,128]{1,0:T(8,128)(2,1)S(1)}, u32[]{:S(2)}, u32[]{:S(2)}) collective-permute-start(bf16[272,128]{1,0:T(8,128)(2,1)S(1)} %factor_bottom.1.refs_1_), channel_id=1, source_target_pairs={{0,12},{4,0},{8,4},{12,8},{1,13},{5,1},{9,5},{13,9},{2,14},{6,2},{... | collective-permute-start | bytes 208904 | tf_op jit(solution)/shard_map/ppermute | solution.py:615
  115.8 8.4 %whiten_top.3.refs_7_ = f32[4,512,2048]{2,1,0:T(8,128)} custom-call(s32[4]{0:T(128)S(1)} %pad_add_fusion.order, bf16[784,128]{1,0:T(8,128)(2,1)S(1)} %collective-permute-done.15.refs_0_, bf16[784,128]{1,0:T(8,128)(2,1)S(1)} %collective-permute-done.16.refs_1_, bf16[784,128]{1,0:T(8,128)(2,1)S(1)} %collective-permute-done.17.refs_2_, ...), custom_call_target="tpu_custom_call", output_to_operand_aliasing={{}: (8, {})} | custom-call | flops 6000000000 | bytes 1048576 | tf_op jit(solution)/shard_map/whiten_top/pallas_call | solution.py:642
  124.2 6.0 %whiten_bottom.1 = f32[4,512,2048]{2,1,0:T(8,128)} custom-call(s32[4]{0:T(128)S(1)} %pad_add_fusion.order, bf16[272,128]{1,0:T(8,128)(2,1)S(1)} %collective-permute-done.12.refs_0_, bf16[272,128]{1,0:T(8,128)(2,1)S(1)} %collective-permute-done.13.refs_1_, bf16[272,128]{1,0:T(8,128)(2,1)S(1)} %collective-permute-done.14.refs_2_, ...), custom_call_target="tpu_custom_call", output_to_operand_aliasing={{}: (8, {})} | custom-call | flops 6000000000 | bytes 1048576 | tf_op jit(solution)/shard_map/whiten_bottom/pallas_call | solution.py:642
  (46 shorter events, 3.9 us)
Async XLA Ops:
  0.6 8.4 %copy-start.5 = (s32[1,8]{1,0:T(1,128)S(1)}, s32[1,8]{1,0:T(1,128)}, u32[]{:S(2)}) copy-start(s32[1,8]{1,0:T(1,128)} %param.9) | copy-start | bytes 100
  0.6 8.4 %copy-start.6 = (s32[1,8]{1,0:T(1,128)S(1)}, s32[1,8]{1,0:T(1,128)}, u32[]{:S(2)}) copy-start(s32[1,8]{1,0:T(1,128)} %param.10) | copy-start | bytes 100
  5.9 13.6 %collective-permute-start = (bf16[256,2560]{1,0:T(8,128)(2,1)}, bf16[256,2560]{1,0:T(8,128)(2,1)S(1)}, u32[]{:S(2)}, u32[]{:S(2)}) collective-permute-start(bf16[256,2560]{1,0:T(8,128)(2,1)} %cut_peer.1.refs_0_), channel_id=1, source_target_pairs={{0,1},{1,0},{2,3},{3,2},{4,5},{5,4},{6,7},{7,6},{8,9},{9,8},{10,11... | collective-permute-start | bytes 3932168 | tf_op jit(solution)/shard_map/ppermute | solution.py:560
  6.3 19.7 %collective-permute-start.3 = (bf16[256,768]{1,0:T(8,128)(2,1)}, bf16[256,768]{1,0:T(8,128)(2,1)S(1)}, u32[]{:S(2)}, u32[]{:S(2)}) collective-permute-start(bf16[256,768]{1,0:T(8,128)(2,1)} %get-tuple-element.19.refs_3_), channel_id=1, source_target_pairs={{0,2},{1,3},{2,0},{3,1},{4,6},{5,7},{6,4},{7,5},{8,10},{9,11},{10,... | collective-permute-start | bytes 1179656 | tf_op jit(solution)/shard_map/ppermute | solution.py:554
  8.8 18.2 %collective-permute-start.4 = (bf16[256,768]{1,0:T(8,128)(2,1)}, bf16[256,768]{1,0:T(8,128)(2,1)S(1)}, u32[]{:S(2)}, u32[]{:S(2)}) collective-permute-start(bf16[256,768]{1,0:T(8,128)(2,1)} %get-tuple-element.20.refs_4_), channel_id=1, source_target_pairs={{0,3},{1,2},{2,1},{3,0},{4,7},{5,6},{6,5},{7,4},{8,11},{9,10},{10,... | collective-permute-start | bytes 1179656 | tf_op jit(solution)/shard_map/ppermute | solution.py:554
  9.3 1.3 %copy-start.4 = (bf16[256,2560]{1,0:T(8,128)(2,1)S(1)}, bf16[256,2560]{1,0:T(8,128)(2,1)}, u32[]{:S(2)}) copy-start(bf16[256,2560]{1,0:T(8,128)(2,1)} %cut_peer.1.refs_0_) | copy-start | bytes 3932164
  14.8 4.7 %copy-start.1 = (bf16[1,256,8192]{2,1,0:T(8,128)(2,1)S(1)}, bf16[1,256,8192]{2,1,0:T(8,128)(2,1)}, u32[]{:S(2)}) copy-start(bf16[1,256,8192]{2,1,0:T(8,128)(2,1)} %param.6) | copy-start | bytes 12582916
  14.8 4.7 %copy-start.2 = (bf16[1,256,1024]{2,1,0:T(8,128)(2,1)S(1)}, bf16[1,256,1024]{2,1,0:T(8,128)(2,1)}, u32[]{:S(2)}) copy-start(bf16[1,256,1024]{2,1,0:T(8,128)(2,1)} %param.7) | copy-start | bytes 1572868
  14.8 4.7 %copy-start.3 = (bf16[1,256,1024]{2,1,0:T(8,128)(2,1)S(1)}, bf16[1,256,1024]{2,1,0:T(8,128)(2,1)}, u32[]{:S(2)}) copy-start(bf16[1,256,1024]{2,1,0:T(8,128)(2,1)} %param.8) | copy-start | bytes 1572868
  20.2 20.5 %collective-permute-start.1 = (bf16[256,768]{1,0:T(8,128)(2,1)S(1)}, bf16[256,768]{1,0:T(8,128)(2,1)S(1)}, u32[]{:S(2)}, u32[]{:S(2)}) collective-permute-start(bf16[256,768]{1,0:T(8,128)(2,1)S(1)} %get-tuple-element.21.refs_1_), channel_id=1, source_target_pairs={{0,2},{1,3},{2,0},{3,1},{4,6},{5,7},{6,4},{7,5},{8,10},{9,11},{10,... | collective-permute-start | bytes 1179656 | tf_op jit(solution)/shard_map/ppermute | solution.py:554
  22.0 21.9 %collective-permute-start.2 = (bf16[256,768]{1,0:T(8,128)(2,1)S(1)}, bf16[256,768]{1,0:T(8,128)(2,1)S(1)}, u32[]{:S(2)}, u32[]{:S(2)}) collective-permute-start(bf16[256,768]{1,0:T(8,128)(2,1)S(1)} %get-tuple-element.24), channel_id=1, source_target_pairs={{0,3},{1,2},{2,1},{3,0},{4,7},{5,6},{6,5},{7,4},{8,11},{9,10},{10,... | collective-permute-start | bytes 1179656 | tf_op jit(solution)/shard_map/ppermute | solution.py:554
  35.9 16.9 %collective-permute-start.5 = (f32[1032,128]{1,0:T(8,128)S(1)}, f32[1032,128]{1,0:T(8,128)S(1)}, u32[]{:S(2)}, u32[]{:S(2)}) collective-permute-start(f32[1032,128]{1,0:T(8,128)S(1)} %attention_outer_products.5), channel_id=1, source_target_pairs={{0,4},{4,8},{8,12},{12,0},{1,5},{5,9},{9,13},{13,1},{2,6},{6,10},{... | collective-permute-start | bytes 1585160 | tf_op jit(solution)/shard_map/ppermute | solution.py:573
  38.3 18.3 %collective-permute-start.8 = (bf16[256,512]{1,0:T(8,128)(2,1)S(1)}, bf16[256,512]{1,0:T(8,128)(2,1)S(1)}, u32[]{:S(2)}, u32[]{:S(2)}) collective-permute-start(bf16[256,512]{1,0:T(8,128)(2,1)S(1)} %get-tuple-element.29), channel_id=1, source_target_pairs={{0,2},{1,3},{2,0},{3,1},{4,6},{5,7},{6,4},{7,5},{8,10},{9,11},{10,... | collective-permute-start | bytes 786440 | tf_op jit(solution)/shard_map/ppermute | solution.py:554
  39.8 16.8 %collective-permute-start.9 = (bf16[256,512]{1,0:T(8,128)(2,1)S(1)}, bf16[256,512]{1,0:T(8,128)(2,1)S(1)}, u32[]{:S(2)}, u32[]{:S(2)}) collective-permute-start(bf16[256,512]{1,0:T(8,128)(2,1)S(1)} %get-tuple-element.30), channel_id=1, source_target_pairs={{0,3},{1,2},{2,1},{3,0},{4,7},{5,6},{6,5},{7,4},{8,11},{9,10},{10,... | collective-permute-start | bytes 786440 | tf_op jit(solution)/shard_map/ppermute | solution.py:554
  52.9 16.7 %collective-permute-start.10 = (f32[1032,128]{1,0:T(8,128)S(1)}, f32[1032,128]{1,0:T(8,128)S(1)}, u32[]{:S(2)}, u32[]{:S(2)}) collective-permute-start(f32[1032,128]{1,0:T(8,128)S(1)} %add.51), channel_id=1, source_target_pairs={{0,4},{4,8},{8,12},{12,0},{1,5},{5,9},{9,13},{13,1},{2,6},{6,10},{... | collective-permute-start | bytes 1585160 | tf_op jit(solution)/shard_map/ppermute | solution.py:573
  54.7 15.0 %collective-permute-start.6 = (bf16[256,512]{1,0:T(8,128)(2,1)S(1)}, bf16[256,512]{1,0:T(8,128)(2,1)S(1)}, u32[]{:S(2)}, u32[]{:S(2)}) collective-permute-start(bf16[256,512]{1,0:T(8,128)(2,1)S(1)} %get-tuple-element.25), channel_id=1, source_target_pairs={{0,2},{1,3},{2,0},{3,1},{4,6},{5,7},{6,4},{7,5},{8,10},{9,11},{10,... | collective-permute-start | bytes 786440 | tf_op jit(solution)/shard_map/ppermute | solution.py:554
  56.1 13.6 %collective-permute-start.7 = (bf16[256,512]{1,0:T(8,128)(2,1)S(1)}, bf16[256,512]{1,0:T(8,128)(2,1)S(1)}, u32[]{:S(2)}, u32[]{:S(2)}) collective-permute-start(bf16[256,512]{1,0:T(8,128)(2,1)S(1)} %get-tuple-element.26), channel_id=1, source_target_pairs={{0,3},{1,2},{2,1},{3,0},{4,7},{5,6},{6,5},{7,4},{8,11},{9,10},{10,... | collective-permute-start | bytes 786440 | tf_op jit(solution)/shard_map/ppermute | solution.py:554
  69.7 15.9 %collective-permute-start.11 = (f32[1032,128]{1,0:T(8,128)S(1)}, f32[1032,128]{1,0:T(8,128)S(1)}, u32[]{:S(2)}, u32[]{:S(2)}) collective-permute-start(f32[1032,128]{1,0:T(8,128)S(1)} %add.52), channel_id=1, source_target_pairs={{0,4},{4,8},{8,12},{12,0},{1,5},{5,9},{9,13},{13,1},{2,6},{6,10},{... | collective-permute-start | bytes 1585160 | tf_op jit(solution)/shard_map/ppermute | solution.py:573
  94.9 17.8 %collective-permute-start.15 = (bf16[784,128]{1,0:T(8,128)(2,1)S(1)}, bf16[784,128]{1,0:T(8,128)(2,1)S(1)}, u32[]{:S(2)}, u32[]{:S(2)}) collective-permute-start(bf16[784,128]{1,0:T(8,128)(2,1)S(1)} %get-tuple-element.32.refs_0_), channel_id=1, source_target_pairs={{0,4},{4,8},{8,12},{12,0},{1,5},{5,9},{9,13},{13,1},{2,6},{6,10},{... | collective-permute-start | bytes 602120 | tf_op jit(solution)/shard_map/ppermute | solution.py:615
  94.9 20.9 %collective-permute-start.16 = (bf16[784,128]{1,0:T(8,128)(2,1)S(1)}, bf16[784,128]{1,0:T(8,128)(2,1)S(1)}, u32[]{:S(2)}, u32[]{:S(2)}) collective-permute-start(bf16[784,128]{1,0:T(8,128)(2,1)S(1)} %get-tuple-element.32.refs_0_), channel_id=1, source_target_pairs={{0,8},{4,12},{8,0},{12,4},{1,9},{5,13},{9,1},{13,5},{2,10},{6,14},... | collective-permute-start | bytes 602120 | tf_op jit(solution)/shard_map/ppermute | solution.py:615
  96.4 19.4 %collective-permute-start.17 = (bf16[784,128]{1,0:T(8,128)(2,1)S(1)}, bf16[784,128]{1,0:T(8,128)(2,1)S(1)}, u32[]{:S(2)}, u32[]{:S(2)}) collective-permute-start(bf16[784,128]{1,0:T(8,128)(2,1)S(1)} %get-tuple-element.32.refs_0_), channel_id=1, source_target_pairs={{0,12},{4,0},{8,4},{12,8},{1,13},{5,1},{9,5},{13,9},{2,14},{6,2},{... | collective-permute-start | bytes 602120 | tf_op jit(solution)/shard_map/ppermute | solution.py:615
  98.8 10.4 %copy-start = (bf16[2048,2048]{1,0:T(8,128)(2,1)S(1)}, bf16[2048,2048]{1,0:T(8,128)(2,1)}, u32[]{:S(2)}) copy-start(bf16[2048,2048]{1,0:T(8,128)(2,1)} %turn_weight.7.refs_2_.refs_3_.refs_4_.refs_5_.refs_6_) | copy-start | bytes 25165828
  107.0 17.2 %collective-permute-start.12 = (bf16[272,128]{1,0:T(8,128)(2,1)S(1)}, bf16[272,128]{1,0:T(8,128)(2,1)S(1)}, u32[]{:S(2)}, u32[]{:S(2)}) collective-permute-start(bf16[272,128]{1,0:T(8,128)(2,1)S(1)} %factor_bottom.1.refs_1_), channel_id=1, source_target_pairs={{0,4},{4,8},{8,12},{12,0},{1,5},{5,9},{9,13},{13,1},{2,6},{6,10},{... | collective-permute-start | bytes 208904 | tf_op jit(solution)/shard_map/ppermute | solution.py:615
  107.6 16.6 %collective-permute-start.13 = (bf16[272,128]{1,0:T(8,128)(2,1)S(1)}, bf16[272,128]{1,0:T(8,128)(2,1)S(1)}, u32[]{:S(2)}, u32[]{:S(2)}) collective-permute-start(bf16[272,128]{1,0:T(8,128)(2,1)S(1)} %factor_bottom.1.refs_1_), channel_id=1, source_target_pairs={{0,8},{4,12},{8,0},{12,4},{1,9},{5,13},{9,1},{13,5},{2,10},{6,14},... | collective-permute-start | bytes 208904 | tf_op jit(solution)/shard_map/ppermute | solution.py:615
  112.7 11.5 %collective-permute-start.14 = (bf16[272,128]{1,0:T(8,128)(2,1)S(1)}, bf16[272,128]{1,0:T(8,128)(2,1)S(1)}, u32[]{:S(2)}, u32[]{:S(2)}) collective-permute-start(bf16[272,128]{1,0:T(8,128)(2,1)S(1)} %factor_bottom.1.refs_1_), channel_id=1, source_target_pairs={{0,12},{4,0},{8,4},{12,8},{1,13},{5,1},{9,5},{13,9},{2,14},{6,2},{... | collective-permute-start | bytes 208904 | tf_op jit(solution)/shard_map/ppermute | solution.py:615

commit v3 on v2

--- a/solution.py
+++ b/solution.py
@@ -49,7 +49,8 @@
 
 def decode(code, exponent):
     code = code.astype(F32)
-    root = jnp.exp2(jnp.log(jnp.maximum(jnp.abs(code), 1e-37)) * (0.125 / math.log(2.0)) + (exponent - 15.0))
+    quarter = lax.rsqrt(lax.rsqrt(jnp.maximum(jnp.abs(code), 1e-37)))
+    root = quarter * lax.rsqrt(quarter) * jnp.exp2(exponent - 15.0)
     return jnp.where(code < 0.0, -root, root)
 
 
@@ -141,7 +142,7 @@
 
     factor = HEAD_SIZE ** (-0.5) / math.log(2.0)
 
-    def one_span(q, carry):
+    def place_of(q):
         source = q // spans
         distance, cross = source // 2, lax.rem(source, 2)
         device = lax.rem(chip - distance + chips, chips) * 2 + lax.rem(core + cross, 2)
@@ -155,41 +156,46 @@
             begin = jnp.where(at <= first_row, at, begin)
             query_begin = jnp.where(query_pos >= at, at, query_begin)
             at = at + meta[lengths + d]
-        count = position - begin // SPAN + 1
-        lanes = pl.ds(pl.multiple_of(q * SPAN, SPAN), SPAN)
+        return position, query_pos, query_begin, position - begin // SPAN + 1
+
+    def one_pair(p, carry):
+        pair = [(which, 2 * p + which, place_of(2 * p + which)) for which in range(2)]
+        count = jnp.maximum(pair[0][2][3], pair[1][2][3])
 
         for n in range(1, most + 1):
 
             @pl.when(count == n)
             def _(n=n):
-                held = [slots[position - n + 1 + i] for i in range(n)]
-                for i in range(n):
-                    key_pos = lax.broadcasted_iota(jnp.int32, (SPAN, SPAN), 0) + (position - n + 1 + i) * SPAN
-                    seen = (key_pos <= query_pos) & (key_pos >= query_begin)
-                    limits[i * SPAN : (i + 1) * SPAN] = jnp.where(seen, 3e38, -1e30)
-                key_part = jnp.concatenate([keys[slot] for slot in held], axis=0)
-                value_part = jnp.concatenate([values[slot] for slot in held], axis=1)
-                scores = lax.dot_general(key_part, queries[q], NT, preferred_element_type=F32)
-                limit = limits[: n * SPAN]
-                scores = jnp.minimum(scores, jnp.concatenate([limit] * BLOCK_HEADS, axis=1))
-                largest = jnp.max(scores, axis=0, keepdims=True)
-                lifted = jnp.exp2((scores - largest) * factor)
-                summed = jnp.sum(lifted, axis=0, keepdims=True)
-                weights = (lifted * (1.0 / summed)).astype(BF16)
-                mixed = jnp.dot(value_part, weights, preferred_element_type=F32)
-                for h in range(BLOCK_HEADS):
-                    one_head = mixed[:, h * SPAN : (h + 1) * SPAN]
-                    columns = slice(h * HEAD_SIZE, (h + 1) * HEAD_SIZE)
-                    high, low = split(one_head)
-                    left[0, columns, lanes] = high
-                    left[1, columns, lanes] = low
-                    high, low = split(one_head.T)
-                    right[0, lanes, columns] = high
-                    right[1, lanes, columns] = low
+                for which, q, (position, query_pos, query_begin, _) in pair:
+                    lanes = pl.ds(pl.multiple_of(q * SPAN, SPAN), SPAN)
+                    held = [slots[jnp.maximum(position - n + 1 + i, 0)] for i in range(n)]
+                    for i in range(n):
+                        key_pos = lax.broadcasted_iota(jnp.int32, (SPAN, SPAN), 0) + (position - n + 1 + i) * SPAN
+                        seen = (key_pos <= query_pos) & (key_pos >= query_begin)
+                        limits[which, i * SPAN : (i + 1) * SPAN] = jnp.where(seen, 3e38, -1e30)
+                    key_part = jnp.concatenate([keys[slot] for slot in held], axis=0)
+                    value_part = jnp.concatenate([values[slot] for slot in held], axis=1)
+                    scores = lax.dot_general(key_part, queries[q], NT, preferred_element_type=F32)
+                    limit = limits[which, : n * SPAN]
+                    scores = jnp.minimum(scores, jnp.concatenate([limit] * BLOCK_HEADS, axis=1))
+                    largest = jnp.max(scores, axis=0, keepdims=True)
+                    lifted = jnp.exp2((scores - largest) * factor)
+                    summed = jnp.sum(lifted, axis=0, keepdims=True)
+                    weights = (lifted * (1.0 / summed)).astype(BF16)
+                    mixed = jnp.dot(value_part, weights, preferred_element_type=F32)
+                    for h in range(BLOCK_HEADS):
+                        one_head = mixed[:, h * SPAN : (h + 1) * SPAN]
+                        columns = slice(h * HEAD_SIZE, (h + 1) * HEAD_SIZE)
+                        high, low = split(one_head)
+                        left[0, columns, lanes] = high
+                        left[1, columns, lanes] = low
+                        high, low = split(one_head.T)
+                        right[0, lanes, columns] = high
+                        right[1, lanes, columns] = low
 
         return carry
 
-    lax.fori_loop(0, all_spans, one_span, 0)
+    lax.fori_loop(0, all_spans // 2, one_pair, 0)
 
     half = BLOCK_W // 2
     total[...] = jnp.zeros_like(total)
@@ -303,27 +309,35 @@
             square = jnp.where(tile_index == k, current[:, k * SPAN : (k + 1) * SPAN], square)
         square = pltpu.roll(square, turn, 1)
         line = lax.broadcasted_iota(jnp.int32, (8, SPAN), 0)
-        held = [
-            {q: jnp.broadcast_to(square[8 * q : 8 * q + 8, j : j + 1], (8, SPAN)) for q in range(j // 8, groups)}
-            for j in range(step)
-        ]
+        square = [square[8 * q : 8 * q + 8] for q in range(groups)]
         body = [[current[8 * q : 8 * q + 8, k * SPAN : (k + 1) * SPAN] for k in range(panels)] for q in range(groups)]
         scales = [jnp.zeros((8, SPAN), F32) for _ in range(groups)]
 
         def spread(value, i):
             return jnp.broadcast_to(value[i % 8 : i % 8 + 1], (8, SPAN))
 
+        def column(j):
+            return {q: jnp.broadcast_to(square[q][:, j : j + 1], (8, SPAN)) for q in range(j // 8, groups)}
+
+        ahead = 4
+        held = {j: column(j) for j in range(ahead)}
         for i in range(step):
             at = i // 8
-            root = lax.rsqrt(spread(held[i][at], i))
+            pivots = held.pop(i)
+            root = lax.rsqrt(spread(pivots[at], i))
             inverse = root * root
             scales[at] = jnp.where(line == i % 8, root, scales[at])
-            ratio = {q: held[i][q] * inverse for q in range(at, groups)}
+            ratio = {q: pivots[q] * inverse for q in range(at, groups)}
             ratio[at] = jnp.where(line > i % 8, ratio[at], 0.0)
-            for j in range(i + 1, step):
-                entry = spread(held[i][j // 8], j)
+            for j in held:
+                entry = spread(pivots[j // 8], j)
                 for q in range(j // 8, groups):
                     held[j][q] = held[j][q] - ratio[q] * entry
+            pivot_row = spread(square[at], i)
+            for q in range(at, groups):
+                square[q] = square[q] - ratio[q] * pivot_row
+            if i + ahead < step:
+                held[i + ahead] = column(i + ahead)
             for k in range(panels):
                 pivot_row = spread(body[at][k], i)
                 for q in range(at, groups):
@@ -352,12 +366,11 @@
 def whiten_kernel(order, *refs, blocks, starts, first, chunks, aliased):
     count = len(starts)
     u_refs, refs = refs[: blocks * count], refs[blocks * count :]
-    w_refs, refs = refs[:chunks], refs[chunks + aliased :]
+    w_ref, refs = refs[0], refs[1 + aliased :]
     out, left, ready, sems = refs
     half = BLOCK_W // 2
     chunk = ready.shape[2] // chunks
     step = pl.program_id(0)
-    lowest = starts[0]
 
     def copy(number, which, c):
         slot = lax.rem(number * count + which, 2)
@@ -383,6 +396,8 @@
                         left[rows, column * SPAN : (column + 1) * SPAN] = high
                         left[rows, width + column * SPAN : width + (column + 1) * SPAN] = low
 
+        above = 0 if blocks == 1 else order[first + step] * BLOCK_W
+        depths = pl.ds(pl.multiple_of(above + start, SPAN), width)
         for c in range(chunks):
             if count == 1:
 
@@ -396,7 +411,7 @@
                 def _(c=c):
                     copy(step - 1, which, c).wait()
 
-            weight = w_refs[c][start - lowest :]
+            weight = w_ref[depths, c * chunk : (c + 1) * chunk]
             product = jnp.dot(
                 left[:, : 2 * width], jnp.concatenate([weight, weight], axis=0), preferred_element_type=F32
             )
@@ -524,7 +539,7 @@
                     pltpu.VMEM((all_spans, SPAN, HEAD_SIZE), BF16),
                     pltpu.VMEM((all_spans, HEAD_SIZE, SPAN), BF16),
                     pltpu.SMEM((all_spans,), jnp.int32),
-                    pltpu.VMEM((most * SPAN, SPAN), F32),
+                    pltpu.VMEM((2, most * SPAN, SPAN), F32),
                     pltpu.VMEM((2, BLOCK_W, all_spans * SPAN), BF16),
                     pltpu.VMEM((2, all_spans * SPAN, BLOCK_W), BF16),
                     pltpu.VMEM((BLOCK_W, BLOCK_W), F32),
@@ -630,15 +645,11 @@
     def whiten(uppers, first, starts, result):
         more = [] if result is None else [result]
         depth = BLOCK_W - starts[0]
+        weights = vmem if len(uppers) > len(starts) else pl.BlockSpec(
+            (BLOCK_W, features), lambda b, order: (order[first + b], 0)
+        )
         chunks = features // tile
         count = len(uppers) // len(starts)
-        weights = [
-            pl.BlockSpec(
-                (depth, tile),
-                lambda b, order, c=c: (order[first + b] * (BLOCK_W // depth) + starts[0] // depth, c),
-            )
-            for c in range(chunks)
-        ]
         return pl.pallas_call(
             functools.partial(
                 whiten_kernel, blocks=count, starts=starts, first=first, chunks=chunks, aliased=len(more)
@@ -647,7 +658,7 @@
             grid_spec=pltpu.PrefetchScalarGridSpec(
                 num_scalar_prefetch=1,
                 grid=(count,),
-                in_specs=[vmem] * len(uppers) + weights + [anywhere] * len(more),
+                in_specs=[vmem] * len(uppers) + [weights] + [anywhere] * len(more),
                 out_specs=anywhere,
                 scratch_shapes=[
                     pltpu.VMEM((half, 2 * depth), BF16),
@@ -655,11 +666,11 @@
                     pltpu.SemaphoreType.DMA((2, chunks)),
                 ],
             ),
-            input_output_aliases={1 + len(uppers) + chunks: 0} if more else {},
+            input_output_aliases={2 + len(uppers): 0} if more else {},
             compiler_params=params(WHITEN_VMEM),
             cost_estimate=cost(2.0e9 * len(uppers), 2**20),
             name="whiten_bottom" if starts[0] else "whiten_top",
-        )(order, *uppers, *[turned] * chunks, *more)
+        )(order, *uppers, turned, *more)
 
     result = whiten([tops[0], bottoms[0]], 0, (0, half), None)
     result = whiten(tops[1:], 1, (0,), result)

time: 132 us -> 131 us (level)
  Pallas kernels: 95 us -> 93.3 us
  waiting for transfers between devices: 11.1 us -> 12.7 us
    pallas_call x4, Pallas kernels: 35.6 us -> 34.1 us  [grams_of(): pl.pallas_call(functools.partial(attention_kernel, chips=chips, spans=spa...]
  transfers between devices with their start and end apart: 18 -> 18, of which waited for: 4 -> 4; matrix products, arithmetic and copies ran while one was open for 1% -> 1% of each run, Pallas kernels for 57% -> 56%
where the time goes in v3:
time: 131 us; the launch traced here: 129 us
  Pallas kernels  93.3 us (71%)
  starting transfers between devices  20.2 us (15%)
  waiting for transfers between devices  12.7 us (10%)
  local copies, waits for them, and re-layouts  1.68 us (1%)
    pallas_call x4, Pallas kernels, grams_of(): pl.pallas_call(functools.partial(attention_kernel, chips=chips, spans=spa...  34.1 us
    pallas_call x3, Pallas kernels, whiten(): pl.pallas_call(functools.partial(whiten_kernel, blocks=count, starts=star...  17 us
    pallas_call x4, Pallas kernels, turn(): pl.pallas_call(turn_kernel, out_shape=jax.ShapeDtypeStruct((blocks * BLOC...  16.8 us
    pallas_call x1, Pallas kernels, factor_top(): pl.pallas_call(functools.partial(factor_kernel, start=0, stop=half, recei...  9.59 us
    ppermute x6, starting transfers between devices, shared(): lax.ppermute(array, 'dp', [(z, (z + d) % ring) for z in range(ring)])  9.22 us
    pallas_call x1, Pallas kernels, factor_bottom(): pl.pallas_call(functools.partial(factor_kernel, start=half, stop=BLOCK_W,...  8.69 us
    ppermute x8, starting transfers between devices, shards(): lax.ppermute(part, 'seq', moved(*where))  8.12 us
    ppermute x3, waiting for transfers between devices, shards(): lax.ppermute(held[done], 'dp', [(z, (z + 1) % ring) for z in range(ring)])  7.26 us
  transfers between devices with their start and end apart: 18, of which 4 were waited for; matrix products, arithmetic and copies ran while one was open for 1% of the time, Pallas kernels for 56%

profile of v3, /device:TPU:0, one launch (start us, length us, event | category | flops | bytes accessed | tf_op | source)
XLA Modules:
  0.0 129.2 jit_solution(17714500964635950358)
XLA Ops:
  0.6 2.8 %cut_piece.4 = (bf16[256,768]{1,0:T(8,128)(2,1)}, bf16[256,768]{1,0:T(8,128)(2,1)}) custom-call(s32[3]{0:T(128)} %pad_add_fusion.1.meta, bf16[256,8192]{1,0:T(8,128)(2,1)} %bitcast.21, bf16[256,1024]{1,0:T(8,128)(2,1)} %bitcast.34, bf16[256,1024]{1,0:T(8,128)(2,1)} %bitcast.43, bf16[256,8192]{1,0:T(8,128)(2,1)} %bitcast.22, bf16[256,1024]{1,0:T(8,128)(2,1)} %bitcast.35, ...), custom_call_target="tpu_custom_call" | custom-call | bytes 2097152 | tf_op jit(solution)/shard_map/cut_piece/pallas_call | solution.py:469
  3.4 2.5 %cut_peer.1.refs_0_ = bf16[256,2560]{1,0:T(8,128)(2,1)} custom-call(s32[1]{0:T(128)} %bitcast.4.meta, bf16[256,8192]{1,0:T(8,128)(2,1)} %bitcast.23, bf16[256,1024]{1,0:T(8,128)(2,1)} %bitcast.36, bf16[256,1024]{1,0:T(8,128)(2,1)} %bitcast.45, bf16[256,768]{1,0:T(8,128)(2,1)} %get-tuple-element.19.refs_3_, bf16[256,768]{1,0:T(8,128)(2,1)} %get-tuple-element.20.refs_4_), custom_call_target="tpu_custom_call" | custom-call | bytes 2097152 | tf_op jit(solution)/shard_map/cut_peer/pallas_call | solution.py:469
  6.3 2.5 %collective-permute-start.3 = (bf16[256,768]{1,0:T(8,128)(2,1)}, bf16[256,768]{1,0:T(8,128)(2,1)S(1)}, u32[]{:S(2)}, u32[]{:S(2)}) collective-permute-start(bf16[256,768]{1,0:T(8,128)(2,1)} %get-tuple-element.19.refs_3_), channel_id=1, source_target_pairs={{0,2},{1,3},{2,0},{3,1},{4,6},{5,7},{6,4},{7,5},{8,10},{9,11},{10,... | collective-permute-start | bytes 1179656 | tf_op jit(solution)/shard_map/ppermute | solution.py:569
  9.3 1.3 %copy-done.4 = bf16[256,2560]{1,0:T(8,128)(2,1)S(1)} copy-done((bf16[256,2560]{1,0:T(8,128)(2,1)S(1)}, bf16[256,2560]{1,0:T(8,128)(2,1)}, u32[]{:S(2)}) %copy-start.4) | copy-done | bytes 1310744
  10.6 4.1 %turn_weight.4.refs_0_ = bf16[2048,2048]{1,0:T(8,128)(2,1)} custom-call(bf16[2048,2048]{1,0:T(8,128)(2,1)} %w_ref.7, bf16[256,2560]{1,0:T(8,128)(2,1)S(1)} %copy-done.4), custom_call_target="tpu_custom_call" | custom-call | flops 1000000000 | bytes 1048576 | tf_op jit(solution)/shard_map/turn_weight/pallas_call | solution.py:486
  14.8 4.5 %turn_weight.5.refs_7_.refs_0_ = bf16[2048,2048]{1,0:T(8,128)(2,1)} custom-call(bf16[2048,2048]{1,0:T(8,128)(2,1)} %w_ref.7, bf16[2048,2048]{1,0:T(8,128)(2,1)} %turn_weight.4.refs_0_), custom_call_target="tpu_custom_call", output_to_operand_aliasing={{}: (1, {})} | custom-call | flops 1000000000 | bytes 1048576 | tf_op jit(solution)/shard_map/turn_weight/pallas_call | solution.py:486
  19.5 0.7 cut_piece.5
  20.2 1.8 %collective-permute-start.1 = (bf16[256,768]{1,0:T(8,128)(2,1)S(1)}, bf16[256,768]{1,0:T(8,128)(2,1)S(1)}, u32[]{:S(2)}, u32[]{:S(2)}) collective-permute-start(bf16[256,768]{1,0:T(8,128)(2,1)S(1)} %get-tuple-element.21.refs_1_), channel_id=1, source_target_pairs={{0,2},{1,3},{2,0},{3,1},{4,6},{5,7},{6,4},{7,5},{8,10},{9,11},{10,... | collective-permute-start | bytes 1179656 | tf_op jit(solution)/shard_map/ppermute | solution.py:569
  22.0 4.1 %turn_weight.6.refs_3_.refs_10_.refs_0_ = bf16[2048,2048]{1,0:T(8,128)(2,1)} custom-call(bf16[2048,2048]{1,0:T(8,128)(2,1)} %w_ref.7, bf16[2048,2048]{1,0:T(8,128)(2,1)} %turn_weight.5.refs_7_.refs_0_, bf16[256,768]{1,0:T(8,128)(2,1)S(1)} %get-tuple-element.21.refs_1_), custom_call_target="tpu_custom_call", output_to_operand_aliasing={{}: (1, {})} | custom-call | flops 1000000000 | bytes 1048576 | tf_op jit(solution)/shard_map/turn_weight/pallas_call | solution.py:486
  26.1 1.0 collective-permute-done.4.refs_9_.refs_3_
  27.1 8.4 %attention_outer_products.5 = f32[1032,128]{1,0:T(8,128)S(1)} custom-call(s32[20]{0:T(128)S(1)} %concatenate.14.meta, bf16[256,8192]{1,0:T(8,128)(2,1)S(1)} %bitcast.26, bf16[256,2560]{1,0:T(8,128)(2,1)S(1)} %collective-permute-done.refs_6_.refs_2_.refs_1_.refs_7_, bf16[256,768]{1,0:T(8,128)(2,1)S(1)} %collective-permute-done.3.refs_8_.refs_2_, ...), custom_call_target="tpu_custom_call" | custom-call | flops 14000000000 | bytes 1048576 | tf_op jit(solution)/shard_map/attention_outer_products/pallas_call | solution.py:513
  35.4 1.2 collective-permute-start.5
  37.2 1.5 %collective-permute-start.8 = (bf16[256,512]{1,0:T(8,128)(2,1)S(1)}, bf16[256,512]{1,0:T(8,128)(2,1)S(1)}, u32[]{:S(2)}, u32[]{:S(2)}) collective-permute-start(bf16[256,512]{1,0:T(8,128)(2,1)S(1)} %get-tuple-element.29), channel_id=1, source_target_pairs={{0,2},{1,3},{2,0},{3,1},{4,6},{5,7},{6,4},{7,5},{8,10},{9,11},{10,... | collective-permute-start | bytes 786440 | tf_op jit(solution)/shard_map/ppermute | solution.py:569
  39.5 4.4 %collective-permute-done.2.refs_3_.refs_11_ = bf16[256,768]{1,0:T(8,128)(2,1)S(1)} collective-permute-done((bf16[256,768]{1,0:T(8,128)(2,1)S(1)}, bf16[256,768]{1,0:T(8,128)(2,1)S(1)}, u32[]{:S(2)}, u32[]{:S(2)}) %collective-permute-start.2) | collective-permute-done | bytes 393248 | tf_op jit(solution)/shard_map/ppermute | solution.py:569
  43.9 8.6 %attention_outer_products.4 = f32[1032,128]{1,0:T(8,128)S(1)} custom-call(s32[20]{0:T(128)S(1)} %concatenate.13.meta, bf16[256,8192]{1,0:T(8,128)(2,1)S(1)} %bitcast.31, bf16[256,2560]{1,0:T(8,128)(2,1)S(1)} %collective-permute-done.refs_6_.refs_2_.refs_1_.refs_7_, bf16[256,768]{1,0:T(8,128)(2,1)S(1)} %collective-permute-done.1.refs_2_.refs_10_, ...), custom_call_target="tpu_custom_call" | custom-call | flops 14000000000 | bytes 1048576 | tf_op jit(solution)/shard_map/attention_outer_products/pallas_call | solution.py:513
  52.6 1.2 collective-permute-start.10
  53.7 1.4 %collective-permute-start.6 = (bf16[256,512]{1,0:T(8,128)(2,1)S(1)}, bf16[256,512]{1,0:T(8,128)(2,1)S(1)}, u32[]{:S(2)}, u32[]{:S(2)}) collective-permute-start(bf16[256,512]{1,0:T(8,128)(2,1)S(1)} %get-tuple-element.25), channel_id=1, source_target_pairs={{0,2},{1,3},{2,0},{3,1},{4,6},{5,7},{6,4},{7,5},{8,10},{9,11},{10,... | collective-permute-start | bytes 786440 | tf_op jit(solution)/shard_map/ppermute | solution.py:569
  55.7 8.5 %attention_outer_products.7 = f32[1032,128]{1,0:T(8,128)S(1)} custom-call(s32[20]{0:T(128)S(1)} %concatenate.15.meta, bf16[256,8192]{1,0:T(8,128)(2,1)S(1)} %bitcast.32, bf16[256,2560]{1,0:T(8,128)(2,1)S(1)} %collective-permute-done.refs_6_.refs_2_.refs_1_.refs_7_, bf16[256,512]{1,0:T(8,128)(2,1)S(1)} %collective-permute-done.8.refs_2_, ...), custom_call_target="tpu_custom_call" | custom-call | flops 14000000000 | bytes 1048576 | tf_op jit(solution)/shard_map/attention_outer_products/pallas_call | solution.py:513
  64.2 4.6 %collective-permute-done.10 = f32[1032,128]{1,0:T(8,128)S(1)} collective-permute-done((f32[1032,128]{1,0:T(8,128)S(1)}, f32[1032,128]{1,0:T(8,128)S(1)}, u32[]{:S(2)}, u32[]{:S(2)}) %collective-permute-start.10) | collective-permute-done | bytes 528416 | tf_op jit(solution)/shard_map/ppermute | solution.py:588
  69.0 8.6 %attention_outer_products.6.refs_0_.refs_1_ = f32[1032,128]{1,0:T(8,128)S(1)} custom-call(s32[20]{0:T(128)S(1)} %concatenate.12.meta, bf16[256,8192]{1,0:T(8,128)(2,1)S(1)} %bitcast.33, bf16[256,2560]{1,0:T(8,128)(2,1)S(1)} %collective-permute-done.refs_6_.refs_2_.refs_1_.refs_7_, bf16[256,512]{1,0:T(8,128)(2,1)S(1)} %collective-permute-done.6.refs_2_, ...), custom_call_target="tpu_custom_call" | custom-call | flops 14000000000 | bytes 1048576 | tf_op jit(solution)/shard_map/attention_outer_products/pallas_call | solution.py:513
  77.5 4.1 %turn_weight.7.refs_2_.refs_3_ = bf16[2048,2048]{1,0:T(8,128)(2,1)} custom-call(bf16[2048,2048]{1,0:T(8,128)(2,1)} %w_ref.7, bf16[2048,2048]{1,0:T(8,128)(2,1)} %turn_weight.6.refs_3_.refs_10_.refs_0_, f32[1032,128]{1,0:T(8,128)S(1)} %attention_outer_products.6.refs_0_.refs_1_), custom_call_target="tpu_custom_call", output_to_operand_aliasing={{}: (1, {})} | custom-call | flops 1000000000 | bytes 1048576 | tf_op jit(solution)/shard_map/turn_weight/pallas_call | solution.py:486
  81.6 2.7 %collective-permute-done.11.refs_1_ = f32[1032,128]{1,0:T(8,128)S(1)} collective-permute-done((f32[1032,128]{1,0:T(8,128)S(1)}, f32[1032,128]{1,0:T(8,128)S(1)}, u32[]{:S(2)}, u32[]{:S(2)}) %collective-permute-start.11) | collective-permute-done | bytes 528416 | tf_op jit(solution)/shard_map/ppermute | solution.py:588
  84.3 9.6 %factor_top.1 = (bf16[784,128]{1,0:T(8,128)(2,1)S(1)}, f32[256,256]{1,0:T(8,128)S(1)}) custom-call(f32[1032,128]{1,0:T(8,128)S(1)} %attention_outer_products.6.refs_0_.refs_1_, f32[1032,128]{1,0:T(8,128)S(1)} %collective-permute-done.11.refs_1_), custom_call_target="tpu_custom_call" | custom-call | flops 10000000000 | bytes 1048576 | tf_op jit(solution)/shard_map/factor_top/pallas_call | solution.py:599
  94.0 1.1 collective-permute-start.16
  95.1 2.7 %collective-permute-start.17 = (bf16[784,128]{1,0:T(8,128)(2,1)S(1)}, bf16[784,128]{1,0:T(8,128)(2,1)S(1)}, u32[]{:S(2)}, u32[]{:S(2)}) collective-permute-start(bf16[784,128]{1,0:T(8,128)(2,1)S(1)} %get-tuple-element.32.refs_0_), channel_id=1, source_target_pairs={{0,12},{4,0},{8,4},{12,8},{1,13},{5,1},{9,5},{13,9},{2,14},{6,2},{... | collective-permute-start | bytes 602120 | tf_op jit(solution)/shard_map/ppermute | solution.py:630
  97.8 8.7 %factor_bottom.1.refs_1_ = bf16[272,128]{1,0:T(8,128)(2,1)S(1)} custom-call(f32[256,256]{1,0:T(8,128)S(1)} %get-tuple-element.31.refs_0_), custom_call_target="tpu_custom_call" | custom-call | flops 8999999488 | bytes 1048576 | tf_op jit(solution)/shard_map/factor_bottom/pallas_call | solution.py:614
  106.5 0.6 collective-permute-start.12
  107.1 1.5 %collective-permute-start.13 = (bf16[272,128]{1,0:T(8,128)(2,1)S(1)}, bf16[272,128]{1,0:T(8,128)(2,1)S(1)}, u32[]{:S(2)}, u32[]{:S(2)}) collective-permute-start(bf16[272,128]{1,0:T(8,128)(2,1)S(1)} %factor_bottom.1.refs_1_), channel_id=1, source_target_pairs={{0,8},{4,12},{8,0},{12,4},{1,9},{5,13},{9,1},{13,5},{2,10},{6,14},... | collective-permute-start | bytes 208904 | tf_op jit(solution)/shard_map/ppermute | solution.py:630
  108.7 3.6 %whiten_top.2.refs_4_ = f32[4,512,2048]{2,1,0:T(8,128)} custom-call(s32[4]{0:T(128)S(1)} %pad_add_fusion.order, bf16[784,128]{1,0:T(8,128)(2,1)S(1)} %get-tuple-element.32.refs_0_, bf16[272,128]{1,0:T(8,128)(2,1)S(1)} %factor_bottom.1.refs_1_, bf16[2048,2048]{1,0:T(8,128)(2,1)S(1)} %copy-done), custom_call_target="tpu_custom_call" | custom-call | flops 4000000000 | bytes 1048576 | tf_op jit(solution)/shard_map/whiten_top/pallas_call | solution.py:653
  112.3 3.2 %collective-permute-start.14 = (bf16[272,128]{1,0:T(8,128)(2,1)S(1)}, bf16[272,128]{1,0:T(8,128)(2,1)S(1)}, u32[]{:S(2)}, u32[]{:S(2)}) collective-permute-start(bf16[272,128]{1,0:T(8,128)(2,1)S(1)} %factor_bottom.1.refs_1_), channel_id=1, source_target_pairs={{0,12},{4,0},{8,4},{12,8},{1,13},{5,1},{9,5},{13,9},{2,14},{6,2},{... | collective-permute-start | bytes 208904 | tf_op jit(solution)/shard_map/ppermute | solution.py:630
  115.5 7.8 %whiten_top.3.refs_4_ = f32[4,512,2048]{2,1,0:T(8,128)} custom-call(s32[4]{0:T(128)S(1)} %pad_add_fusion.order, bf16[784,128]{1,0:T(8,128)(2,1)S(1)} %collective-permute-done.15.refs_0_, bf16[784,128]{1,0:T(8,128)(2,1)S(1)} %collective-permute-done.16.refs_1_, bf16[784,128]{1,0:T(8,128)(2,1)S(1)} %collective-permute-done.17.refs_2_, ...), custom_call_target="tpu_custom_call", output_to_operand_aliasing={{}: (5, {})} | custom-call | flops 6000000000 | bytes 1048576 | tf_op jit(solution)/shard_map/whiten_top/pallas_call | solution.py:653
  123.3 5.7 %whiten_bottom.1 = f32[4,512,2048]{2,1,0:T(8,128)} custom-call(s32[4]{0:T(128)S(1)} %pad_add_fusion.order, bf16[272,128]{1,0:T(8,128)(2,1)S(1)} %collective-permute-done.12.refs_0_, bf16[272,128]{1,0:T(8,128)(2,1)S(1)} %collective-permute-done.13.refs_1_, bf16[272,128]{1,0:T(8,128)(2,1)S(1)} %collective-permute-done.14.refs_2_, ...), custom_call_target="tpu_custom_call", output_to_operand_aliasing={{}: (5, {})} | custom-call | flops 6000000000 | bytes 1048576 | tf_op jit(solution)/shard_map/whiten_bottom/pallas_call | solution.py:653
  (46 shorter events, 4.0 us)
Async XLA Ops:
  0.6 8.4 %copy-start.5 = (s32[1,8]{1,0:T(1,128)S(1)}, s32[1,8]{1,0:T(1,128)}, u32[]{:S(2)}) copy-start(s32[1,8]{1,0:T(1,128)} %param.9) | copy-start | bytes 100
  0.6 8.4 %copy-start.6 = (s32[1,8]{1,0:T(1,128)S(1)}, s32[1,8]{1,0:T(1,128)}, u32[]{:S(2)}) copy-start(s32[1,8]{1,0:T(1,128)} %param.10) | copy-start | bytes 100
  5.9 13.6 %collective-permute-start = (bf16[256,2560]{1,0:T(8,128)(2,1)}, bf16[256,2560]{1,0:T(8,128)(2,1)S(1)}, u32[]{:S(2)}, u32[]{:S(2)}) collective-permute-start(bf16[256,2560]{1,0:T(8,128)(2,1)} %cut_peer.1.refs_0_), channel_id=1, source_target_pairs={{0,1},{1,0},{2,3},{3,2},{4,5},{5,4},{6,7},{7,6},{8,9},{9,8},{10,11... | collective-permute-start | bytes 3932168 | tf_op jit(solution)/shard_map/ppermute | solution.py:575
  6.3 19.7 %collective-permute-start.3 = (bf16[256,768]{1,0:T(8,128)(2,1)}, bf16[256,768]{1,0:T(8,128)(2,1)S(1)}, u32[]{:S(2)}, u32[]{:S(2)}) collective-permute-start(bf16[256,768]{1,0:T(8,128)(2,1)} %get-tuple-element.19.refs_3_), channel_id=1, source_target_pairs={{0,2},{1,3},{2,0},{3,1},{4,6},{5,7},{6,4},{7,5},{8,10},{9,11},{10,... | collective-permute-start | bytes 1179656 | tf_op jit(solution)/shard_map/ppermute | solution.py:569
  8.8 18.2 %collective-permute-start.4 = (bf16[256,768]{1,0:T(8,128)(2,1)}, bf16[256,768]{1,0:T(8,128)(2,1)S(1)}, u32[]{:S(2)}, u32[]{:S(2)}) collective-permute-start(bf16[256,768]{1,0:T(8,128)(2,1)} %get-tuple-element.20.refs_4_), channel_id=1, source_target_pairs={{0,3},{1,2},{2,1},{3,0},{4,7},{5,6},{6,5},{7,4},{8,11},{9,10},{10,... | collective-permute-start | bytes 1179656 | tf_op jit(solution)/shard_map/ppermute | solution.py:569
  9.3 1.3 %copy-start.4 = (bf16[256,2560]{1,0:T(8,128)(2,1)S(1)}, bf16[256,2560]{1,0:T(8,128)(2,1)}, u32[]{:S(2)}) copy-start(bf16[256,2560]{1,0:T(8,128)(2,1)} %cut_peer.1.refs_0_) | copy-start | bytes 3932164
  14.8 4.7 %copy-start.1 = (bf16[1,256,8192]{2,1,0:T(8,128)(2,1)S(1)}, bf16[1,256,8192]{2,1,0:T(8,128)(2,1)}, u32[]{:S(2)}) copy-start(bf16[1,256,8192]{2,1,0:T(8,128)(2,1)} %param.6) | copy-start | bytes 12582916
  14.8 4.7 %copy-start.2 = (bf16[1,256,1024]{2,1,0:T(8,128)(2,1)S(1)}, bf16[1,256,1024]{2,1,0:T(8,128)(2,1)}, u32[]{:S(2)}) copy-start(bf16[1,256,1024]{2,1,0:T(8,128)(2,1)} %param.7) | copy-start | bytes 1572868
  14.8 4.7 %copy-start.3 = (bf16[1,256,1024]{2,1,0:T(8,128)(2,1)S(1)}, bf16[1,256,1024]{2,1,0:T(8,128)(2,1)}, u32[]{:S(2)}) copy-start(bf16[1,256,1024]{2,1,0:T(8,128)(2,1)} %param.8) | copy-start | bytes 1572868
  20.2 19.3 %collective-permute-start.1 = (bf16[256,768]{1,0:T(8,128)(2,1)S(1)}, bf16[256,768]{1,0:T(8,128)(2,1)S(1)}, u32[]{:S(2)}, u32[]{:S(2)}) collective-permute-start(bf16[256,768]{1,0:T(8,128)(2,1)S(1)} %get-tuple-element.21.refs_1_), channel_id=1, source_target_pairs={{0,2},{1,3},{2,0},{3,1},{4,6},{5,7},{6,4},{7,5},{8,10},{9,11},{10,... | collective-permute-start | bytes 1179656 | tf_op jit(solution)/shard_map/ppermute | solution.py:569
  22.0 21.9 %collective-permute-start.2 = (bf16[256,768]{1,0:T(8,128)(2,1)S(1)}, bf16[256,768]{1,0:T(8,128)(2,1)S(1)}, u32[]{:S(2)}, u32[]{:S(2)}) collective-permute-start(bf16[256,768]{1,0:T(8,128)(2,1)S(1)} %get-tuple-element.24), channel_id=1, source_target_pairs={{0,3},{1,2},{2,1},{3,0},{4,7},{5,6},{6,5},{7,4},{8,11},{9,10},{10,... | collective-permute-start | bytes 1179656 | tf_op jit(solution)/shard_map/ppermute | solution.py:569
  35.4 17.1 %collective-permute-start.5 = (f32[1032,128]{1,0:T(8,128)S(1)}, f32[1032,128]{1,0:T(8,128)S(1)}, u32[]{:S(2)}, u32[]{:S(2)}) collective-permute-start(f32[1032,128]{1,0:T(8,128)S(1)} %attention_outer_products.5), channel_id=1, source_target_pairs={{0,4},{4,8},{8,12},{12,0},{1,5},{5,9},{9,13},{13,1},{2,6},{6,10},{... | collective-permute-start | bytes 1585160 | tf_op jit(solution)/shard_map/ppermute | solution.py:588
  37.2 18.5 %collective-permute-start.8 = (bf16[256,512]{1,0:T(8,128)(2,1)S(1)}, bf16[256,512]{1,0:T(8,128)(2,1)S(1)}, u32[]{:S(2)}, u32[]{:S(2)}) collective-permute-start(bf16[256,512]{1,0:T(8,128)(2,1)S(1)} %get-tuple-element.29), channel_id=1, source_target_pairs={{0,2},{1,3},{2,0},{3,1},{4,6},{5,7},{6,4},{7,5},{8,10},{9,11},{10,... | collective-permute-start | bytes 786440 | tf_op jit(solution)/shard_map/ppermute | solution.py:569
  38.7 17.0 %collective-permute-start.9 = (bf16[256,512]{1,0:T(8,128)(2,1)S(1)}, bf16[256,512]{1,0:T(8,128)(2,1)S(1)}, u32[]{:S(2)}, u32[]{:S(2)}) collective-permute-start(bf16[256,512]{1,0:T(8,128)(2,1)S(1)} %get-tuple-element.30), channel_id=1, source_target_pairs={{0,3},{1,2},{2,1},{3,0},{4,7},{5,6},{6,5},{7,4},{8,11},{9,10},{10,... | collective-permute-start | bytes 786440 | tf_op jit(solution)/shard_map/ppermute | solution.py:569
  52.6 16.3 %collective-permute-start.10 = (f32[1032,128]{1,0:T(8,128)S(1)}, f32[1032,128]{1,0:T(8,128)S(1)}, u32[]{:S(2)}, u32[]{:S(2)}) collective-permute-start(f32[1032,128]{1,0:T(8,128)S(1)} %add.51), channel_id=1, source_target_pairs={{0,4},{4,8},{8,12},{12,0},{1,5},{5,9},{9,13},{13,1},{2,6},{6,10},{... | collective-permute-start | bytes 1585160 | tf_op jit(solution)/shard_map/ppermute | solution.py:588
  53.7 15.2 %collective-permute-start.6 = (bf16[256,512]{1,0:T(8,128)(2,1)S(1)}, bf16[256,512]{1,0:T(8,128)(2,1)S(1)}, u32[]{:S(2)}, u32[]{:S(2)}) collective-permute-start(bf16[256,512]{1,0:T(8,128)(2,1)S(1)} %get-tuple-element.25), channel_id=1, source_target_pairs={{0,2},{1,3},{2,0},{3,1},{4,6},{5,7},{6,4},{7,5},{8,10},{9,11},{10,... | collective-permute-start | bytes 786440 | tf_op jit(solution)/shard_map/ppermute | solution.py:569
  55.2 13.8 %collective-permute-start.7 = (bf16[256,512]{1,0:T(8,128)(2,1)S(1)}, bf16[256,512]{1,0:T(8,128)(2,1)S(1)}, u32[]{:S(2)}, u32[]{:S(2)}) collective-permute-start(bf16[256,512]{1,0:T(8,128)(2,1)S(1)} %get-tuple-element.26), channel_id=1, source_target_pairs={{0,3},{1,2},{2,1},{3,0},{4,7},{5,6},{6,5},{7,4},{8,11},{9,10},{10,... | collective-permute-start | bytes 786440 | tf_op jit(solution)/shard_map/ppermute | solution.py:569
  68.9 15.5 %collective-permute-start.11 = (f32[1032,128]{1,0:T(8,128)S(1)}, f32[1032,128]{1,0:T(8,128)S(1)}, u32[]{:S(2)}, u32[]{:S(2)}) collective-permute-start(f32[1032,128]{1,0:T(8,128)S(1)} %add.52), channel_id=1, source_target_pairs={{0,4},{4,8},{8,12},{12,0},{1,5},{5,9},{9,13},{13,1},{2,6},{6,10},{... | collective-permute-start | bytes 1585160 | tf_op jit(solution)/shard_map/ppermute | solution.py:588
  93.9 18.3 %collective-permute-start.15 = (bf16[784,128]{1,0:T(8,128)(2,1)S(1)}, bf16[784,128]{1,0:T(8,128)(2,1)S(1)}, u32[]{:S(2)}, u32[]{:S(2)}) collective-permute-start(bf16[784,128]{1,0:T(8,128)(2,1)S(1)} %get-tuple-element.32.refs_0_), channel_id=1, source_target_pairs={{0,4},{4,8},{8,12},{12,0},{1,5},{5,9},{9,13},{13,1},{2,6},{6,10},{... | collective-permute-start | bytes 602120 | tf_op jit(solution)/shard_map/ppermute | solution.py:630
  94.0 21.4 %collective-permute-start.16 = (bf16[784,128]{1,0:T(8,128)(2,1)S(1)}, bf16[784,128]{1,0:T(8,128)(2,1)S(1)}, u32[]{:S(2)}, u32[]{:S(2)}) collective-permute-start(bf16[784,128]{1,0:T(8,128)(2,1)S(1)} %get-tuple-element.32.refs_0_), channel_id=1, source_target_pairs={{0,8},{4,12},{8,0},{12,4},{1,9},{5,13},{9,1},{13,5},{2,10},{6,14},... | collective-permute-start | bytes 602120 | tf_op jit(solution)/shard_map/ppermute | solution.py:630
  95.1 20.3 %collective-permute-start.17 = (bf16[784,128]{1,0:T(8,128)(2,1)S(1)}, bf16[784,128]{1,0:T(8,128)(2,1)S(1)}, u32[]{:S(2)}, u32[]{:S(2)}) collective-permute-start(bf16[784,128]{1,0:T(8,128)(2,1)S(1)} %get-tuple-element.32.refs_0_), channel_id=1, source_target_pairs={{0,12},{4,0},{8,4},{12,8},{1,13},{5,1},{9,5},{13,9},{2,14},{6,2},{... | collective-permute-start | bytes 602120 | tf_op jit(solution)/shard_map/ppermute | solution.py:630
  97.8 10.9 %copy-start = (bf16[2048,2048]{1,0:T(8,128)(2,1)S(1)}, bf16[2048,2048]{1,0:T(8,128)(2,1)}, u32[]{:S(2)}) copy-start(bf16[2048,2048]{1,0:T(8,128)(2,1)} %turn_weight.7.refs_2_.refs_3_) | copy-start | bytes 25165828
  106.5 16.8 %collective-permute-start.12 = (bf16[272,128]{1,0:T(8,128)(2,1)S(1)}, bf16[272,128]{1,0:T(8,128)(2,1)S(1)}, u32[]{:S(2)}, u32[]{:S(2)}) collective-permute-start(bf16[272,128]{1,0:T(8,128)(2,1)S(1)} %factor_bottom.1.refs_1_), channel_id=1, source_target_pairs={{0,4},{4,8},{8,12},{12,0},{1,5},{5,9},{9,13},{13,1},{2,6},{6,10},{... | collective-permute-start | bytes 208904 | tf_op jit(solution)/shard_map/ppermute | solution.py:630
  107.1 16.2 %collective-permute-start.13 = (bf16[272,128]{1,0:T(8,128)(2,1)S(1)}, bf16[272,128]{1,0:T(8,128)(2,1)S(1)}, u32[]{:S(2)}, u32[]{:S(2)}) collective-permute-start(bf16[272,128]{1,0:T(8,128)(2,1)S(1)} %factor_bottom.1.refs_1_), channel_id=1, source_target_pairs={{0,8},{4,12},{8,0},{12,4},{1,9},{5,13},{9,1},{13,5},{2,10},{6,14},... | collective-permute-start | bytes 208904 | tf_op jit(solution)/shard_map/ppermute | solution.py:630
  112.3 11.1 %collective-permute-start.14 = (bf16[272,128]{1,0:T(8,128)(2,1)S(1)}, bf16[272,128]{1,0:T(8,128)(2,1)S(1)}, u32[]{:S(2)}, u32[]{:S(2)}) collective-permute-start(bf16[272,128]{1,0:T(8,128)(2,1)S(1)} %factor_bottom.1.refs_1_), channel_id=1, source_target_pairs={{0,12},{4,0},{8,4},{12,8},{1,13},{5,1},{9,5},{13,9},{2,14},{6,2},{... | collective-permute-start | bytes 208904 | tf_op jit(solution)/shard_map/ppermute | solution.py:630

commit v4 on v3

--- a/solution.py
+++ b/solution.py
@@ -18,7 +18,7 @@
 BLOCK_HEADS = BLOCK_W // HEAD_SIZE
 KV_BLOCKS = GROUP // BLOCK_HEADS
 PANELS = BLOCK_W // SPAN
-SUM_ROWS = SPAN * (PANELS * (PANELS - 1) // 2 + PANELS // 2) + 8
+SUM_ROWS = SPAN * PANELS + 8
 VMEM_BYTES = 50 * 2**20
 FULL_VMEM = 63 * 2**20
 TURN_VMEM = 50 * 2**20
@@ -105,7 +105,7 @@
     near = sources + 4
     query_refs, near_refs = refs[:sources], refs[sources:near]
     far_refs = refs[near : near + sets * (sources - 2)]
-    out, queries, keys, values, slots, limits, left, right, total = refs[near + sets * (sources - 2) + waited :]
+    top, bottom, queries, keys, values, slots, limits, left, right, total = refs[near + sets * (sources - 2) + waited :]
     own = meta[0]
     chip, core = own // 2, lax.rem(own, 2)
     lengths = 4
@@ -207,9 +207,10 @@
         return carry
 
     lax.fori_loop(0, 3, one_pass, 0)
-    lines = fold(Tiles(total, PANELS, PANELS, False), out)
-    row = lax.broadcasted_iota(jnp.int32, (8, SPAN), 0)
-    out[SUM_ROWS - 8 :] = jnp.where(row == 0, lines[0], lines[1])
+    for out, where in zip((top, bottom), sum_tiles()):
+        off, pair = where
+        (line,) = fold(Tiles(total, PANELS, PANELS, False), out, where=(off, [pair]))
+        out[SUM_ROWS - 8 :] = jnp.broadcast_to(line, (8, SPAN))
 
 
 def diagonal_masks():
@@ -223,9 +224,15 @@
     return off, [(i, i + 1) for i in range(0, rows, 2)]
 
 
-def fold(tiles, out, change=lambda value: value):
+def sum_tiles():
+    off, pairs = tile_order(PANELS, PANELS)
+    half = len(off) // 2
+    return [(off[:half], pairs[0]), (off[half:], pairs[1])]
+
+
+def fold(tiles, out, change=lambda value: value, where=None):
     upper, equal = diagonal_masks()
-    off, pairs = tile_order(tiles.rows, tiles.columns)
+    off, pairs = tile_order(tiles.rows, tiles.columns) if where is None else where
     for i, place in enumerate(off):
         out[i * SPAN : (i + 1) * SPAN] = change(tiles(*place)).astype(out.dtype)
     lines = []
@@ -246,19 +253,17 @@
         return self.ref[i * SPAN : (i + 1) * SPAN, j * SPAN : (j + 1) * SPAN]
 
 
-def unfold(total, work):
+def unfold(halves, work):
     upper, equal = diagonal_masks()
-    off, pairs = tile_order(PANELS, PANELS)
-    for i, (row, column) in enumerate(off):
-        work[row * SPAN : (row + 1) * SPAN, column * SPAN : (column + 1) * SPAN] = total[i * SPAN : (i + 1) * SPAN]
     trace = jnp.zeros((1, 1), F32)
     squares = []
-    for i, (a, b) in enumerate(pairs):
-        at = (len(off) + i) * SPAN
+    for total, (off, (a, b)) in zip(halves, sum_tiles()):
+        for i, (row, column) in enumerate(off):
+            work[row * SPAN : (row + 1) * SPAN, column * SPAN : (column + 1) * SPAN] = total[i * SPAN : (i + 1) * SPAN]
+        at = len(off) * SPAN
         square = total[at : at + SPAN]
         turned = square.T
-        at = (len(off) + len(pairs)) * SPAN + i
-        line = jnp.broadcast_to(total[at : at + 1], (SPAN, SPAN))
+        line = jnp.broadcast_to(total[at + SPAN : at + SPAN + 1], (SPAN, SPAN))
         squares.append((a, jnp.where(upper, square, turned)))
         squares.append((b, jnp.where(equal, line, jnp.where(upper, turned, square))))
     for _, square in squares:
@@ -282,8 +287,10 @@
     work, previous, upper = refs
     if start == 0:
         work[...] = jnp.zeros_like(work)
-        total = given[0][...] + given[1][...] if received == 2 else given[0][...]
-        unfold(total, work)
+        halves = [ref[...] for ref in given[:2]]
+        if received == 4:
+            halves = [mine + ref[...] for mine, ref in zip(halves, given[2:])]
+        unfold(halves, work)
     else:
         work[...] = given[0][...]
     previous[...] = jnp.zeros_like(previous)
@@ -321,18 +328,22 @@
 
         ahead = 4
         held = {j: column(j) for j in range(ahead)}
+        pivot = spread(held[0][0], 0)
         for i in range(step):
             at = i // 8
             pivots = held.pop(i)
-            root = lax.rsqrt(spread(pivots[at], i))
+            root = lax.rsqrt(pivot)
             inverse = root * root
+            if i + 1 < step:
+                entry = spread(pivots[(i + 1) // 8], i + 1)
+                pivot = spread(held[i + 1][(i + 1) // 8], i + 1) - (entry * entry) * inverse
+            for j in held:
+                entry = spread(pivots[j // 8], j)
+                for q in range(j // 8, groups):
+                    held[j][q] = held[j][q] - (pivots[q] * entry) * inverse
             scales[at] = jnp.where(line == i % 8, root, scales[at])
             ratio = {q: pivots[q] * inverse for q in range(at, groups)}
             ratio[at] = jnp.where(line > i % 8, ratio[at], 0.0)
-            for j in held:
-                entry = spread(pivots[j // 8], j)
-                for q in range(j // 8, groups):
-                    held[j][q] = held[j][q] - ratio[q] * entry
             pivot_row = spread(square[at], i)
             for q in range(at, groups):
                 square[q] = square[q] - ratio[q] * pivot_row
@@ -366,7 +377,8 @@
 def whiten_kernel(order, *refs, blocks, starts, first, chunks, aliased):
     count = len(starts)
     u_refs, refs = refs[: blocks * count], refs[blocks * count :]
-    w_ref, refs = refs[0], refs[1 + aliased :]
+    w_refs, refs = refs[:chunks], refs[chunks + aliased :]
+    lowest = starts[0]
     out, left, ready, sems = refs
     half = BLOCK_W // 2
     chunk = ready.shape[2] // chunks
@@ -396,8 +408,6 @@
                         left[rows, column * SPAN : (column + 1) * SPAN] = high
                         left[rows, width + column * SPAN : width + (column + 1) * SPAN] = low
 
-        above = 0 if blocks == 1 else order[first + step] * BLOCK_W
-        depths = pl.ds(pl.multiple_of(above + start, SPAN), width)
         for c in range(chunks):
             if count == 1:
 
@@ -411,7 +421,7 @@
                 def _(c=c):
                     copy(step - 1, which, c).wait()
 
-            weight = w_ref[depths, c * chunk : (c + 1) * chunk]
+            weight = w_refs[c][start - lowest :]
             product = jnp.dot(
                 left[:, : 2 * width], jnp.concatenate([weight, weight], axis=0), preferred_element_type=F32
             )
@@ -516,7 +526,7 @@
                 chips=chips, spans=spans, all_spans=all_spans, documents=documents, most=most, sets=len(carriers),
                 waited=len(after),
             ),
-            out_shape=folded,
+            out_shape=[folded] * 2,
             grid_spec=pltpu.PrefetchScalarGridSpec(
                 num_scalar_prefetch=1,
                 grid=(1,),
@@ -533,7 +543,7 @@
                 + [pl.BlockSpec((tokens, 2 * HEAD_SIZE), lambda i, meta: (0, BLOCK_W // (2 * HEAD_SIZE)))]
                 * (len(carriers) * len(far))
                 + [anywhere] * len(after),
-                out_specs=pl.BlockSpec((SUM_ROWS, SPAN), lambda i, meta: (0, 0)),
+                out_specs=[pl.BlockSpec((SUM_ROWS, SPAN), lambda i, meta: (0, 0))] * 2,
                 scratch_shapes=[
                     pltpu.VMEM((all_spans, BLOCK_HEADS * SPAN, HEAD_SIZE), BF16),
                     pltpu.VMEM((all_spans, SPAN, HEAD_SIZE), BF16),
@@ -583,11 +593,11 @@
         if done == 0 or not in_ring:
             held.append(grams[done])
         else:
-            held.append(grams[done] + carried if done < ring - 1 else None)
+            held.append([mine + theirs for mine, theirs in zip(grams[done], carried)] if done < ring - 1 else None)
         if in_ring and done < ring - 1:
-            carried = lax.ppermute(held[done], "dp", [(z, (z + 1) % ring) for z in range(ring)])
+            carried = [lax.ppermute(part, "dp", [(z, (z + 1) % ring) for z in range(ring)]) for part in held[done]]
     if blocks > 2:
-        turned = turn(blocks - 1, 1, turned, grams[-1])
+        turned = turn(blocks - 1, 1, turned, *grams[-1])
 
     half = BLOCK_W // 2
     top_rows, bottom_rows = [
@@ -623,7 +633,7 @@
         )(rest)
 
     if in_ring:
-        top, rest = factor_top(grams[ring - 1], carried)
+        top, rest = factor_top(*grams[ring - 1], *carried)
 
         def shared(array):
             return [array] + [
@@ -635,7 +645,7 @@
         bottoms = shared(bottom)
         order = jnp.stack([lax.rem(place - d + ring, ring) for d in range(ring)])
     else:
-        halves = [factor_top(lax.psum(grams[t], "dp")) for t in range(blocks)]
+        halves = [factor_top(*[lax.psum(part, "dp") for part in grams[t]]) for t in range(blocks)]
         tops = [top for top, _ in halves]
         bottoms = [factor_bottom(rest) for _, rest in halves]
         bottom = bottoms[0]
@@ -645,10 +655,14 @@
     def whiten(uppers, first, starts, result):
         more = [] if result is None else [result]
         depth = BLOCK_W - starts[0]
-        weights = vmem if len(uppers) > len(starts) else pl.BlockSpec(
-            (BLOCK_W, features), lambda b, order: (order[first + b], 0)
-        )
         chunks = features // tile
+        weights = [
+            pl.BlockSpec(
+                (depth, tile),
+                lambda b, order, c=c: (order[first + b] * (BLOCK_W // depth) + starts[0] // depth, c),
+            )
+            for c in range(chunks)
+        ]
         count = len(uppers) // len(starts)
         return pl.pallas_call(
             functools.partial(
@@ -658,7 +672,7 @@
             grid_spec=pltpu.PrefetchScalarGridSpec(
                 num_scalar_prefetch=1,
                 grid=(count,),
-                in_specs=[vmem] * len(uppers) + [weights] + [anywhere] * len(more),
+                in_specs=[vmem] * len(uppers) + weights + [anywhere] * len(more),
                 out_specs=anywhere,
                 scratch_shapes=[
                     pltpu.VMEM((half, 2 * depth), BF16),
@@ -666,11 +680,11 @@
                     pltpu.SemaphoreType.DMA((2, chunks)),
                 ],
             ),
-            input_output_aliases={2 + len(uppers): 0} if more else {},
+            input_output_aliases={1 + len(uppers) + chunks: 0} if more else {},
             compiler_params=params(WHITEN_VMEM),
             cost_estimate=cost(2.0e9 * len(uppers), 2**20),
             name="whiten_bottom" if starts[0] else "whiten_top",
-        )(order, *uppers, turned, *more)
+        )(order, *uppers, *[turned] * chunks, *more)
 
     result = whiten([tops[0], bottoms[0]], 0, (0, half), None)
     result = whiten(tops[1:], 1, (0,), result)

time: 131 us -> 130 us (level)
  waiting for transfers between devices: 12.7 us -> 6.02 us
  starting transfers between devices: 20.2 us -> 26.4 us
    ppermute x3 -> x6, starting transfers between devices: 2.41 us -> 8.79 us  [shards(): lax.ppermute(part, 'dp', [(z, (z + 1) % ring) for z in range(ring)])]
    ppermute x3 -> x6, waiting for transfers between devices: 7.26 us -> 2.21 us  [shards(): lax.ppermute(part, 'dp', [(z, (z + 1) % ring) for z in range(ring)])]
    pallas_call x4, Pallas kernels: 34.1 us -> 31.9 us  [grams_of(): pl.pallas_call(functools.partial(attention_kernel, chips=chips, spans=spa...]
    ppermute x8, waiting for transfers between devices: 5.39 us -> 3.79 us  [shards(): lax.ppermute(part, 'seq', moved(*where))]
  transfers between devices with their start and end apart: 18 -> 21, of which waited for: 4 -> 5; matrix products, arithmetic and copies ran while one was open for 1% -> 1% of each run, Pallas kernels for 56% -> 56%
where the time goes in v4:
time: 130 us; the launch traced here: 128 us
  Pallas kernels  92.5 us (71%)
  starting transfers between devices  26.4 us (20%)
  waiting for transfers between devices  6.02 us (5%)
  local copies, waits for them, and re-layouts  1.68 us (1%)
    pallas_call x4, Pallas kernels, grams_of(): pl.pallas_call(functools.partial(attention_kernel, chips=chips, spans=spa...  31.9 us
    pallas_call x3, Pallas kernels, whiten(): pl.pallas_call(functools.partial(whiten_kernel, blocks=count, starts=star...  18 us
    pallas_call x4, Pallas kernels, turn(): pl.pallas_call(turn_kernel, out_shape=jax.ShapeDtypeStruct((blocks * BLOC...  16.8 us
    pallas_call x1, Pallas kernels, factor_top(): pl.pallas_call(functools.partial(factor_kernel, start=0, stop=half, recei...  9.8 us
    ppermute x6, starting transfers between devices, shared(): lax.ppermute(array, 'dp', [(z, (z + d) % ring) for z in range(ring)])  9.22 us
    pallas_call x1, Pallas kernels, factor_bottom(): pl.pallas_call(functools.partial(factor_kernel, start=half, stop=BLOCK_W,...  8.92 us
    ppermute x6, starting transfers between devices, shards(): lax.ppermute(part, 'dp', [(z, (z + 1) % ring) for z in range(ring)])  8.79 us
    ppermute x8, starting transfers between devices, shards(): lax.ppermute(part, 'seq', moved(*where))  7.91 us
  transfers between devices with their start and end apart: 21, of which 5 were waited for; matrix products, arithmetic and copies ran while one was open for 1% of the time, Pallas kernels for 56%

profile of v4, /device:TPU:0, one launch (start us, length us, event | category | flops | bytes accessed | tf_op | source)
XLA Modules:
  0.0 127.9 jit_solution(3086497602440493235)
XLA Ops:
  0.6 2.8 %cut_piece.4 = (bf16[256,768]{1,0:T(8,128)(2,1)}, bf16[256,768]{1,0:T(8,128)(2,1)}) custom-call(s32[3]{0:T(128)} %pad_add_fusion.1.meta, bf16[256,8192]{1,0:T(8,128)(2,1)} %bitcast.21, bf16[256,1024]{1,0:T(8,128)(2,1)} %bitcast.34, bf16[256,1024]{1,0:T(8,128)(2,1)} %bitcast.43, bf16[256,8192]{1,0:T(8,128)(2,1)} %bitcast.22, bf16[256,1024]{1,0:T(8,128)(2,1)} %bitcast.35, ...), custom_call_target="tpu_custom_call" | custom-call | bytes 2097152 | tf_op jit(solution)/shard_map/cut_piece/pallas_call | solution.py:479
  3.4 2.5 %cut_peer.1.refs_0_ = bf16[256,2560]{1,0:T(8,128)(2,1)} custom-call(s32[1]{0:T(128)} %bitcast.4.meta, bf16[256,8192]{1,0:T(8,128)(2,1)} %bitcast.23, bf16[256,1024]{1,0:T(8,128)(2,1)} %bitcast.36, bf16[256,1024]{1,0:T(8,128)(2,1)} %bitcast.45, bf16[256,768]{1,0:T(8,128)(2,1)} %get-tuple-element.27.refs_3_, bf16[256,768]{1,0:T(8,128)(2,1)} %get-tuple-element.28.refs_4_), custom_call_target="tpu_custom_call" | custom-call | bytes 2097152 | tf_op jit(solution)/shard_map/cut_peer/pallas_call | solution.py:479
  6.3 2.5 %collective-permute-start.3 = (bf16[256,768]{1,0:T(8,128)(2,1)}, bf16[256,768]{1,0:T(8,128)(2,1)S(1)}, u32[]{:S(2)}, u32[]{:S(2)}) collective-permute-start(bf16[256,768]{1,0:T(8,128)(2,1)} %get-tuple-element.27.refs_3_), channel_id=1, source_target_pairs={{0,2},{1,3},{2,0},{3,1},{4,6},{5,7},{6,4},{7,5},{8,10},{9,11},{10,... | collective-permute-start | bytes 1179656 | tf_op jit(solution)/shard_map/ppermute | solution.py:579
  9.3 1.3 %copy-done.4 = bf16[256,2560]{1,0:T(8,128)(2,1)S(1)} copy-done((bf16[256,2560]{1,0:T(8,128)(2,1)S(1)}, bf16[256,2560]{1,0:T(8,128)(2,1)}, u32[]{:S(2)}) %copy-start.4) | copy-done | bytes 1310744
  10.6 4.1 %turn_weight.4.refs_0_ = bf16[2048,2048]{1,0:T(8,128)(2,1)} custom-call(bf16[2048,2048]{1,0:T(8,128)(2,1)} %w_ref.7, bf16[256,2560]{1,0:T(8,128)(2,1)S(1)} %copy-done.4), custom_call_target="tpu_custom_call" | custom-call | flops 1000000000 | bytes 1048576 | tf_op jit(solution)/shard_map/turn_weight/pallas_call | solution.py:496
  14.8 4.5 %turn_weight.5.refs_7_.refs_0_ = bf16[2048,2048]{1,0:T(8,128)(2,1)} custom-call(bf16[2048,2048]{1,0:T(8,128)(2,1)} %w_ref.7, bf16[2048,2048]{1,0:T(8,128)(2,1)} %turn_weight.4.refs_0_), custom_call_target="tpu_custom_call", output_to_operand_aliasing={{}: (1, {})} | custom-call | flops 1000000000 | bytes 1048576 | tf_op jit(solution)/shard_map/turn_weight/pallas_call | solution.py:496
  20.2 1.8 %collective-permute-start.1 = (bf16[256,768]{1,0:T(8,128)(2,1)S(1)}, bf16[256,768]{1,0:T(8,128)(2,1)S(1)}, u32[]{:S(2)}, u32[]{:S(2)}) collective-permute-start(bf16[256,768]{1,0:T(8,128)(2,1)S(1)} %get-tuple-element.29.refs_1_), channel_id=1, source_target_pairs={{0,2},{1,3},{2,0},{3,1},{4,6},{5,7},{6,4},{7,5},{8,10},{9,11},{10,... | collective-permute-start | bytes 1179656 | tf_op jit(solution)/shard_map/ppermute | solution.py:579
  22.0 4.1 %turn_weight.6.refs_3_.refs_10_.refs_0_ = bf16[2048,2048]{1,0:T(8,128)(2,1)} custom-call(bf16[2048,2048]{1,0:T(8,128)(2,1)} %w_ref.7, bf16[2048,2048]{1,0:T(8,128)(2,1)} %turn_weight.5.refs_7_.refs_0_, bf16[256,768]{1,0:T(8,128)(2,1)S(1)} %get-tuple-element.29.refs_1_), custom_call_target="tpu_custom_call", output_to_operand_aliasing={{}: (1, {})} | custom-call | flops 1000000000 | bytes 1048576 | tf_op jit(solution)/shard_map/turn_weight/pallas_call | solution.py:496
  26.0 1.0 collective-permute-done.4.refs_9_.refs_3_
  27.0 7.8 %attention_outer_products.5 = (f32[520,128]{1,0:T(8,128)S(1)}, f32[520,128]{1,0:T(8,128)S(1)}) custom-call(s32[20]{0:T(128)S(1)} %concatenate.14.meta, bf16[256,8192]{1,0:T(8,128)(2,1)S(1)} %bitcast.26, bf16[256,2560]{1,0:T(8,128)(2,1)S(1)} %collective-permute-done.refs_6_.refs_2_.refs_1_.refs_7_, ...), custom_call_target="tpu_custom_call" | custom-call | flops 14000000000 | bytes 1048576 | tf_op jit(solution)/shard_map/attention_outer_products/pallas_call | solution.py:523
  34.9 1.9 %collective-permute-start.6 = (f32[520,128]{1,0:T(8,128)S(1)}, f32[520,128]{1,0:T(8,128)S(1)}, u32[]{:S(2)}, u32[]{:S(2)}) collective-permute-start(f32[520,128]{1,0:T(8,128)S(1)} %get-tuple-element.36), channel_id=1, source_target_pairs={{0,4},{4,8},{8,12},{12,0},{1,5},{5,9},{9,13},{13,1},{2,6},{6,10},{... | collective-permute-start | bytes 798728 | tf_op jit(solution)/shard_map/ppermute | solution.py:598
  36.8 1.7 %collective-permute-start.5 = (f32[520,128]{1,0:T(8,128)S(1)}, f32[520,128]{1,0:T(8,128)S(1)}, u32[]{:S(2)}, u32[]{:S(2)}) collective-permute-start(f32[520,128]{1,0:T(8,128)S(1)} %get-tuple-element.34), channel_id=1, source_target_pairs={{0,4},{4,8},{8,12},{12,0},{1,5},{5,9},{9,13},{13,1},{2,6},{6,10},{... | collective-permute-start | bytes 798728 | tf_op jit(solution)/shard_map/ppermute | solution.py:598
  39.1 1.2 collective-permute-start.10
  41.5 2.4 %collective-permute-done.2.refs_3_.refs_11_ = bf16[256,768]{1,0:T(8,128)(2,1)S(1)} collective-permute-done((bf16[256,768]{1,0:T(8,128)(2,1)S(1)}, bf16[256,768]{1,0:T(8,128)(2,1)S(1)}, u32[]{:S(2)}, u32[]{:S(2)}) %collective-permute-start.2) | collective-permute-done | bytes 393248 | tf_op jit(solution)/shard_map/ppermute | solution.py:579
  43.9 8.0 %attention_outer_products.4 = (f32[520,128]{1,0:T(8,128)S(1)}, f32[520,128]{1,0:T(8,128)S(1)}) custom-call(s32[20]{0:T(128)S(1)} %concatenate.13.meta, bf16[256,8192]{1,0:T(8,128)(2,1)S(1)} %bitcast.31, bf16[256,2560]{1,0:T(8,128)(2,1)S(1)} %collective-permute-done.refs_6_.refs_2_.refs_1_.refs_7_, ...), custom_call_target="tpu_custom_call" | custom-call | flops 14000000000 | bytes 1048576 | tf_op jit(solution)/shard_map/attention_outer_products/pallas_call | solution.py:523
  52.0 1.9 %collective-permute-start.13 = (f32[520,128]{1,0:T(8,128)S(1)}, f32[520,128]{1,0:T(8,128)S(1)}, u32[]{:S(2)}, u32[]{:S(2)}) collective-permute-start(f32[520,128]{1,0:T(8,128)S(1)} %add.58), channel_id=1, source_target_pairs={{0,4},{4,8},{8,12},{12,0},{1,5},{5,9},{9,13},{13,1},{2,6},{6,10},{... | collective-permute-start | bytes 798728 | tf_op jit(solution)/shard_map/ppermute | solution.py:598
  53.9 1.8 %collective-permute-start.11 = (f32[520,128]{1,0:T(8,128)S(1)}, f32[520,128]{1,0:T(8,128)S(1)}, u32[]{:S(2)}, u32[]{:S(2)}) collective-permute-start(f32[520,128]{1,0:T(8,128)S(1)} %add.57), channel_id=1, source_target_pairs={{0,4},{4,8},{8,12},{12,0},{1,5},{5,9},{9,13},{13,1},{2,6},{6,10},{... | collective-permute-start | bytes 798728 | tf_op jit(solution)/shard_map/ppermute | solution.py:598
  55.7 1.5 %collective-permute-start.7 = (bf16[256,512]{1,0:T(8,128)(2,1)S(1)}, bf16[256,512]{1,0:T(8,128)(2,1)S(1)}, u32[]{:S(2)}, u32[]{:S(2)}) collective-permute-start(bf16[256,512]{1,0:T(8,128)(2,1)S(1)} %get-tuple-element.37), channel_id=1, source_target_pairs={{0,2},{1,3},{2,0},{3,1},{4,6},{5,7},{6,4},{7,5},{8,10},{9,11},{10,... | collective-permute-start | bytes 786440 | tf_op jit(solution)/shard_map/ppermute | solution.py:579
  57.3 8.0 %attention_outer_products.7 = (f32[520,128]{1,0:T(8,128)S(1)}, f32[520,128]{1,0:T(8,128)S(1)}) custom-call(s32[20]{0:T(128)S(1)} %concatenate.15.meta, bf16[256,8192]{1,0:T(8,128)(2,1)S(1)} %bitcast.32, bf16[256,2560]{1,0:T(8,128)(2,1)S(1)} %collective-permute-done.refs_6_.refs_2_.refs_1_.refs_7_, bf16[256,512]{1,0:T(8,128)(2,1)S(1)} %collective-permute-done.9.refs_2_, ...), custom_call_target="tpu_custom_call" | custom-call | flops 14000000000 | bytes 1048576 | tf_op jit(solution)/shard_map/attention_outer_products/pallas_call | solution.py:523
  65.4 1.5 %collective-permute-start.14 = (f32[520,128]{1,0:T(8,128)S(1)}, f32[520,128]{1,0:T(8,128)S(1)}, u32[]{:S(2)}, u32[]{:S(2)}) collective-permute-start(f32[520,128]{1,0:T(8,128)S(1)} %add.60), channel_id=1, source_target_pairs={{0,4},{4,8},{8,12},{12,0},{1,5},{5,9},{9,13},{13,1},{2,6},{6,10},{... | collective-permute-start | bytes 798728 | tf_op jit(solution)/shard_map/ppermute | solution.py:598
  66.9 1.9 %collective-permute-done.11 = f32[520,128]{1,0:T(8,128)S(1)} collective-permute-done((f32[520,128]{1,0:T(8,128)S(1)}, f32[520,128]{1,0:T(8,128)S(1)}, u32[]{:S(2)}, u32[]{:S(2)}) %collective-permute-start.11) | collective-permute-done | bytes 266272 | tf_op jit(solution)/shard_map/ppermute | solution.py:598
  69.2 8.0 %attention_outer_products.6 = (f32[520,128]{1,0:T(8,128)S(1)}, f32[520,128]{1,0:T(8,128)S(1)}) custom-call(s32[20]{0:T(128)S(1)} %concatenate.12.meta, bf16[256,8192]{1,0:T(8,128)(2,1)S(1)} %bitcast.33, bf16[256,2560]{1,0:T(8,128)(2,1)S(1)} %collective-permute-done.refs_6_.refs_2_.refs_1_.refs_7_, bf16[256,512]{1,0:T(8,128)(2,1)S(1)} %collective-permute-done.7.refs_2_, ...), custom_call_target="tpu_custom_call" | custom-call | flops 14000000000 | bytes 1048576 | tf_op jit(solution)/shard_map/attention_outer_products/pallas_call | solution.py:523
  77.3 4.1 %turn_weight.7.refs_2_.refs_3_.refs_4_.refs_5_.refs_6_ = bf16[2048,2048]{1,0:T(8,128)(2,1)} custom-call(bf16[2048,2048]{1,0:T(8,128)(2,1)} %w_ref.7, bf16[2048,2048]{1,0:T(8,128)(2,1)} %turn_weight.6.refs_3_.refs_10_.refs_0_, f32[520,128]{1,0:T(8,128)S(1)} %get-tuple-element.39.refs_0_.refs_1_, ...), custom_call_target="tpu_custom_call", output_to_operand_aliasing={{}: (1, {})} | custom-call | flops 1000000000 | bytes 1048576 | tf_op jit(solution)/shard_map/turn_weight/pallas_call | solution.py:496
  81.7 9.8 %factor_top.1 = (bf16[784,128]{1,0:T(8,128)(2,1)S(1)}, f32[256,256]{1,0:T(8,128)S(1)}) custom-call(f32[520,128]{1,0:T(8,128)S(1)} %get-tuple-element.39.refs_0_.refs_1_, f32[520,128]{1,0:T(8,128)S(1)} %get-tuple-element.40.refs_1_.refs_2_, f32[520,128]{1,0:T(8,128)S(1)} %collective-permute-done.12.refs_2_, f32[520,128]{1,0:T(8,128)S(1)} %collective-permute-done.14.refs_3_), custom_call_target="tpu_custom_call" | custom-call | flops 10000000000 | bytes 1048576 | tf_op jit(solution)/shard_map/factor_top/pallas_call | solution.py:609
  91.5 1.3 %collective-permute-start.18 = (bf16[784,128]{1,0:T(8,128)(2,1)S(1)}, bf16[784,128]{1,0:T(8,128)(2,1)S(1)}, u32[]{:S(2)}, u32[]{:S(2)}) collective-permute-start(bf16[784,128]{1,0:T(8,128)(2,1)S(1)} %get-tuple-element.48.refs_0_), channel_id=1, source_target_pairs={{0,4},{4,8},{8,12},{12,0},{1,5},{5,9},{9,13},{13,1},{2,6},{6,10},{... | collective-permute-start | bytes 602120 | tf_op jit(solution)/shard_map/ppermute | solution.py:640
  92.9 2.4 %collective-permute-start.19 = (bf16[784,128]{1,0:T(8,128)(2,1)S(1)}, bf16[784,128]{1,0:T(8,128)(2,1)S(1)}, u32[]{:S(2)}, u32[]{:S(2)}) collective-permute-start(bf16[784,128]{1,0:T(8,128)(2,1)S(1)} %get-tuple-element.48.refs_0_), channel_id=1, source_target_pairs={{0,8},{4,12},{8,0},{12,4},{1,9},{5,13},{9,1},{13,5},{2,10},{6,14},... | collective-permute-start | bytes 602120 | tf_op jit(solution)/shard_map/ppermute | solution.py:640
  95.3 1.2 collective-permute-start.20
  96.5 8.9 %factor_bottom.1.refs_1_ = bf16[272,128]{1,0:T(8,128)(2,1)S(1)} custom-call(f32[256,256]{1,0:T(8,128)S(1)} %get-tuple-element.47.refs_0_), custom_call_target="tpu_custom_call" | custom-call | flops 8999999488 | bytes 1048576 | tf_op jit(solution)/shard_map/factor_bottom/pallas_call | solution.py:624
  106.8 3.6 %whiten_top.2.refs_7_ = f32[4,512,2048]{2,1,0:T(8,128)} custom-call(s32[4]{0:T(128)S(1)} %pad_add_fusion.order, bf16[784,128]{1,0:T(8,128)(2,1)S(1)} %get-tuple-element.48.refs_0_, bf16[272,128]{1,0:T(8,128)(2,1)S(1)} %factor_bottom.1.refs_1_, bf16[2048,2048]{1,0:T(8,128)(2,1)S(1)} %copy-done, bf16[2048,2048]{1,0:T(8,128)(2,1)S(1)} %copy-done, ...), custom_call_target="tpu_custom_call" | custom-call | flops 4000000000 | bytes 1048576 | tf_op jit(solution)/shard_map/whiten_top/pallas_call | solution.py:667
  110.4 2.9 %collective-permute-start.17 = (bf16[272,128]{1,0:T(8,128)(2,1)S(1)}, bf16[272,128]{1,0:T(8,128)(2,1)S(1)}, u32[]{:S(2)}, u32[]{:S(2)}) collective-permute-start(bf16[272,128]{1,0:T(8,128)(2,1)S(1)} %factor_bottom.1.refs_1_), channel_id=1, source_target_pairs={{0,12},{4,0},{8,4},{12,8},{1,13},{5,1},{9,5},{13,9},{2,14},{6,2},{... | collective-permute-start | bytes 208904 | tf_op jit(solution)/shard_map/ppermute | solution.py:640
  113.3 8.4 %whiten_top.3.refs_7_ = f32[4,512,2048]{2,1,0:T(8,128)} custom-call(s32[4]{0:T(128)S(1)} %pad_add_fusion.order, bf16[784,128]{1,0:T(8,128)(2,1)S(1)} %collective-permute-done.18.refs_0_, bf16[784,128]{1,0:T(8,128)(2,1)S(1)} %collective-permute-done.19.refs_1_, bf16[784,128]{1,0:T(8,128)(2,1)S(1)} %collective-permute-done.20.refs_2_, ...), custom_call_target="tpu_custom_call", output_to_operand_aliasing={{}: (8, {})} | custom-call | flops 6000000000 | bytes 1048576 | tf_op jit(solution)/shard_map/whiten_top/pallas_call | solution.py:667
  121.7 6.0 %whiten_bottom.1 = f32[4,512,2048]{2,1,0:T(8,128)} custom-call(s32[4]{0:T(128)S(1)} %pad_add_fusion.order, bf16[272,128]{1,0:T(8,128)(2,1)S(1)} %collective-permute-done.15.refs_0_, bf16[272,128]{1,0:T(8,128)(2,1)S(1)} %collective-permute-done.16.refs_1_, bf16[272,128]{1,0:T(8,128)(2,1)S(1)} %collective-permute-done.17.refs_2_, ...), custom_call_target="tpu_custom_call", output_to_operand_aliasing={{}: (8, {})} | custom-call | flops 6000000000 | bytes 1048576 | tf_op jit(solution)/shard_map/whiten_bottom/pallas_call | solution.py:667
  (54 shorter events, 6.7 us)
Async XLA Ops:
  0.6 8.4 %copy-start.5 = (s32[1,8]{1,0:T(1,128)S(1)}, s32[1,8]{1,0:T(1,128)}, u32[]{:S(2)}) copy-start(s32[1,8]{1,0:T(1,128)} %param.9) | copy-start | bytes 100
  0.6 8.4 %copy-start.6 = (s32[1,8]{1,0:T(1,128)S(1)}, s32[1,8]{1,0:T(1,128)}, u32[]{:S(2)}) copy-start(s32[1,8]{1,0:T(1,128)} %param.10) | copy-start | bytes 100
  5.9 13.6 %collective-permute-start = (bf16[256,2560]{1,0:T(8,128)(2,1)}, bf16[256,2560]{1,0:T(8,128)(2,1)S(1)}, u32[]{:S(2)}, u32[]{:S(2)}) collective-permute-start(bf16[256,2560]{1,0:T(8,128)(2,1)} %cut_peer.1.refs_0_), channel_id=1, source_target_pairs={{0,1},{1,0},{2,3},{3,2},{4,5},{5,4},{6,7},{7,6},{8,9},{9,8},{10,11... | collective-permute-start | bytes 3932168 | tf_op jit(solution)/shard_map/ppermute | solution.py:585
  6.3 19.7 %collective-permute-start.3 = (bf16[256,768]{1,0:T(8,128)(2,1)}, bf16[256,768]{1,0:T(8,128)(2,1)S(1)}, u32[]{:S(2)}, u32[]{:S(2)}) collective-permute-start(bf16[256,768]{1,0:T(8,128)(2,1)} %get-tuple-element.27.refs_3_), channel_id=1, source_target_pairs={{0,2},{1,3},{2,0},{3,1},{4,6},{5,7},{6,4},{7,5},{8,10},{9,11},{10,... | collective-permute-start | bytes 1179656 | tf_op jit(solution)/shard_map/ppermute | solution.py:579
  8.8 18.2 %collective-permute-start.4 = (bf16[256,768]{1,0:T(8,128)(2,1)}, bf16[256,768]{1,0:T(8,128)(2,1)S(1)}, u32[]{:S(2)}, u32[]{:S(2)}) collective-permute-start(bf16[256,768]{1,0:T(8,128)(2,1)} %get-tuple-element.28.refs_4_), channel_id=1, source_target_pairs={{0,3},{1,2},{2,1},{3,0},{4,7},{5,6},{6,5},{7,4},{8,11},{9,10},{10,... | collective-permute-start | bytes 1179656 | tf_op jit(solution)/shard_map/ppermute | solution.py:579
  9.3 1.3 %copy-start.4 = (bf16[256,2560]{1,0:T(8,128)(2,1)S(1)}, bf16[256,2560]{1,0:T(8,128)(2,1)}, u32[]{:S(2)}) copy-start(bf16[256,2560]{1,0:T(8,128)(2,1)} %cut_peer.1.refs_0_) | copy-start | bytes 3932164
  14.8 4.7 %copy-start.1 = (bf16[1,256,8192]{2,1,0:T(8,128)(2,1)S(1)}, bf16[1,256,8192]{2,1,0:T(8,128)(2,1)}, u32[]{:S(2)}) copy-start(bf16[1,256,8192]{2,1,0:T(8,128)(2,1)} %param.6) | copy-start | bytes 12582916
  14.8 4.7 %copy-start.2 = (bf16[1,256,1024]{2,1,0:T(8,128)(2,1)S(1)}, bf16[1,256,1024]{2,1,0:T(8,128)(2,1)}, u32[]{:S(2)}) copy-start(bf16[1,256,1024]{2,1,0:T(8,128)(2,1)} %param.7) | copy-start | bytes 1572868
  14.8 4.7 %copy-start.3 = (bf16[1,256,1024]{2,1,0:T(8,128)(2,1)S(1)}, bf16[1,256,1024]{2,1,0:T(8,128)(2,1)}, u32[]{:S(2)}) copy-start(bf16[1,256,1024]{2,1,0:T(8,128)(2,1)} %param.8) | copy-start | bytes 1572868
  20.2 20.7 %collective-permute-start.1 = (bf16[256,768]{1,0:T(8,128)(2,1)S(1)}, bf16[256,768]{1,0:T(8,128)(2,1)S(1)}, u32[]{:S(2)}, u32[]{:S(2)}) collective-permute-start(bf16[256,768]{1,0:T(8,128)(2,1)S(1)} %get-tuple-element.29.refs_1_), channel_id=1, source_target_pairs={{0,2},{1,3},{2,0},{3,1},{4,6},{5,7},{6,4},{7,5},{8,10},{9,11},{10,... | collective-permute-start | bytes 1179656 | tf_op jit(solution)/shard_map/ppermute | solution.py:579
  22.0 21.9 %collective-permute-start.2 = (bf16[256,768]{1,0:T(8,128)(2,1)S(1)}, bf16[256,768]{1,0:T(8,128)(2,1)S(1)}, u32[]{:S(2)}, u32[]{:S(2)}) collective-permute-start(bf16[256,768]{1,0:T(8,128)(2,1)S(1)} %get-tuple-element.32), channel_id=1, source_target_pairs={{0,3},{1,2},{2,1},{3,0},{4,7},{5,6},{6,5},{7,4},{8,11},{9,10},{10,... | collective-permute-start | bytes 1179656 | tf_op jit(solution)/shard_map/ppermute | solution.py:579
  34.9 17.1 %collective-permute-start.6 = (f32[520,128]{1,0:T(8,128)S(1)}, f32[520,128]{1,0:T(8,128)S(1)}, u32[]{:S(2)}, u32[]{:S(2)}) collective-permute-start(f32[520,128]{1,0:T(8,128)S(1)} %get-tuple-element.36), channel_id=1, source_target_pairs={{0,4},{4,8},{8,12},{12,0},{1,5},{5,9},{9,13},{13,1},{2,6},{6,10},{... | collective-permute-start | bytes 798728 | tf_op jit(solution)/shard_map/ppermute | solution.py:598
  36.8 17.1 %collective-permute-start.5 = (f32[520,128]{1,0:T(8,128)S(1)}, f32[520,128]{1,0:T(8,128)S(1)}, u32[]{:S(2)}, u32[]{:S(2)}) collective-permute-start(f32[520,128]{1,0:T(8,128)S(1)} %get-tuple-element.34), channel_id=1, source_target_pairs={{0,4},{4,8},{8,12},{12,0},{1,5},{5,9},{9,13},{13,1},{2,6},{6,10},{... | collective-permute-start | bytes 798728 | tf_op jit(solution)/shard_map/ppermute | solution.py:598
  39.1 18.1 %collective-permute-start.10 = (bf16[256,512]{1,0:T(8,128)(2,1)S(1)}, bf16[256,512]{1,0:T(8,128)(2,1)S(1)}, u32[]{:S(2)}, u32[]{:S(2)}) collective-permute-start(bf16[256,512]{1,0:T(8,128)(2,1)S(1)} %get-tuple-element.44), channel_id=1, source_target_pairs={{0,3},{1,2},{2,1},{3,0},{4,7},{5,6},{6,5},{7,4},{8,11},{9,10},{10,... | collective-permute-start | bytes 786440 | tf_op jit(solution)/shard_map/ppermute | solution.py:579
  40.9 16.5 %collective-permute-start.9 = (bf16[256,512]{1,0:T(8,128)(2,1)S(1)}, bf16[256,512]{1,0:T(8,128)(2,1)S(1)}, u32[]{:S(2)}, u32[]{:S(2)}) collective-permute-start(bf16[256,512]{1,0:T(8,128)(2,1)S(1)} %get-tuple-element.43), channel_id=1, source_target_pairs={{0,2},{1,3},{2,0},{3,1},{4,6},{5,7},{6,4},{7,5},{8,10},{9,11},{10,... | collective-permute-start | bytes 786440 | tf_op jit(solution)/shard_map/ppermute | solution.py:579
  52.0 13.4 %collective-permute-start.13 = (f32[520,128]{1,0:T(8,128)S(1)}, f32[520,128]{1,0:T(8,128)S(1)}, u32[]{:S(2)}, u32[]{:S(2)}) collective-permute-start(f32[520,128]{1,0:T(8,128)S(1)} %add.58), channel_id=1, source_target_pairs={{0,4},{4,8},{8,12},{12,0},{1,5},{5,9},{9,13},{13,1},{2,6},{6,10},{... | collective-permute-start | bytes 798728 | tf_op jit(solution)/shard_map/ppermute | solution.py:598
  53.9 14.9 %collective-permute-start.11 = (f32[520,128]{1,0:T(8,128)S(1)}, f32[520,128]{1,0:T(8,128)S(1)}, u32[]{:S(2)}, u32[]{:S(2)}) collective-permute-start(f32[520,128]{1,0:T(8,128)S(1)} %add.57), channel_id=1, source_target_pairs={{0,4},{4,8},{8,12},{12,0},{1,5},{5,9},{9,13},{13,1},{2,6},{6,10},{... | collective-permute-start | bytes 798728 | tf_op jit(solution)/shard_map/ppermute | solution.py:598
  55.7 13.2 %collective-permute-start.7 = (bf16[256,512]{1,0:T(8,128)(2,1)S(1)}, bf16[256,512]{1,0:T(8,128)(2,1)S(1)}, u32[]{:S(2)}, u32[]{:S(2)}) collective-permute-start(bf16[256,512]{1,0:T(8,128)(2,1)S(1)} %get-tuple-element.37), channel_id=1, source_target_pairs={{0,2},{1,3},{2,0},{3,1},{4,6},{5,7},{6,4},{7,5},{8,10},{9,11},{10,... | collective-permute-start | bytes 786440 | tf_op jit(solution)/shard_map/ppermute | solution.py:579
  57.1 12.1 %collective-permute-start.8 = (bf16[256,512]{1,0:T(8,128)(2,1)S(1)}, bf16[256,512]{1,0:T(8,128)(2,1)S(1)}, u32[]{:S(2)}, u32[]{:S(2)}) collective-permute-start(bf16[256,512]{1,0:T(8,128)(2,1)S(1)} %get-tuple-element.38), channel_id=1, source_target_pairs={{0,3},{1,2},{2,1},{3,0},{4,7},{5,6},{6,5},{7,4},{8,11},{9,10},{10,... | collective-permute-start | bytes 786440 | tf_op jit(solution)/shard_map/ppermute | solution.py:579
  65.4 16.0 %collective-permute-start.14 = (f32[520,128]{1,0:T(8,128)S(1)}, f32[520,128]{1,0:T(8,128)S(1)}, u32[]{:S(2)}, u32[]{:S(2)}) collective-permute-start(f32[520,128]{1,0:T(8,128)S(1)} %add.60), channel_id=1, source_target_pairs={{0,4},{4,8},{8,12},{12,0},{1,5},{5,9},{9,13},{13,1},{2,6},{6,10},{... | collective-permute-start | bytes 798728 | tf_op jit(solution)/shard_map/ppermute | solution.py:598
  68.8 12.9 %collective-permute-start.12 = (f32[520,128]{1,0:T(8,128)S(1)}, f32[520,128]{1,0:T(8,128)S(1)}, u32[]{:S(2)}, u32[]{:S(2)}) collective-permute-start(f32[520,128]{1,0:T(8,128)S(1)} %add.59), channel_id=1, source_target_pairs={{0,4},{4,8},{8,12},{12,0},{1,5},{5,9},{9,13},{13,1},{2,6},{6,10},{... | collective-permute-start | bytes 798728 | tf_op jit(solution)/shard_map/ppermute | solution.py:598
  91.5 18.8 %collective-permute-start.18 = (bf16[784,128]{1,0:T(8,128)(2,1)S(1)}, bf16[784,128]{1,0:T(8,128)(2,1)S(1)}, u32[]{:S(2)}, u32[]{:S(2)}) collective-permute-start(bf16[784,128]{1,0:T(8,128)(2,1)S(1)} %get-tuple-element.48.refs_0_), channel_id=1, source_target_pairs={{0,4},{4,8},{8,12},{12,0},{1,5},{5,9},{9,13},{13,1},{2,6},{6,10},{... | collective-permute-start | bytes 602120 | tf_op jit(solution)/shard_map/ppermute | solution.py:640
  92.9 20.4 %collective-permute-start.19 = (bf16[784,128]{1,0:T(8,128)(2,1)S(1)}, bf16[784,128]{1,0:T(8,128)(2,1)S(1)}, u32[]{:S(2)}, u32[]{:S(2)}) collective-permute-start(bf16[784,128]{1,0:T(8,128)(2,1)S(1)} %get-tuple-element.48.refs_0_), channel_id=1, source_target_pairs={{0,8},{4,12},{8,0},{12,4},{1,9},{5,13},{9,1},{13,5},{2,10},{6,14},... | collective-permute-start | bytes 602120 | tf_op jit(solution)/shard_map/ppermute | solution.py:640
  95.3 18.0 %collective-permute-start.20 = (bf16[784,128]{1,0:T(8,128)(2,1)S(1)}, bf16[784,128]{1,0:T(8,128)(2,1)S(1)}, u32[]{:S(2)}, u32[]{:S(2)}) collective-permute-start(bf16[784,128]{1,0:T(8,128)(2,1)S(1)} %get-tuple-element.48.refs_0_), channel_id=1, source_target_pairs={{0,12},{4,0},{8,4},{12,8},{1,13},{5,1},{9,5},{13,9},{2,14},{6,2},{... | collective-permute-start | bytes 602120 | tf_op jit(solution)/shard_map/ppermute | solution.py:640
  96.5 10.3 %copy-start = (bf16[2048,2048]{1,0:T(8,128)(2,1)S(1)}, bf16[2048,2048]{1,0:T(8,128)(2,1)}, u32[]{:S(2)}) copy-start(bf16[2048,2048]{1,0:T(8,128)(2,1)} %turn_weight.7.refs_2_.refs_3_.refs_4_.refs_5_.refs_6_) | copy-start | bytes 25165828
  105.4 16.2 %collective-permute-start.15 = (bf16[272,128]{1,0:T(8,128)(2,1)S(1)}, bf16[272,128]{1,0:T(8,128)(2,1)S(1)}, u32[]{:S(2)}, u32[]{:S(2)}) collective-permute-start(bf16[272,128]{1,0:T(8,128)(2,1)S(1)} %factor_bottom.1.refs_1_), channel_id=1, source_target_pairs={{0,4},{4,8},{8,12},{12,0},{1,5},{5,9},{9,13},{13,1},{2,6},{6,10},{... | collective-permute-start | bytes 208904 | tf_op jit(solution)/shard_map/ppermute | solution.py:640
  106.3 15.4 %collective-permute-start.16 = (bf16[272,128]{1,0:T(8,128)(2,1)S(1)}, bf16[272,128]{1,0:T(8,128)(2,1)S(1)}, u32[]{:S(2)}, u32[]{:S(2)}) collective-permute-start(bf16[272,128]{1,0:T(8,128)(2,1)S(1)} %factor_bottom.1.refs_1_), channel_id=1, source_target_pairs={{0,8},{4,12},{8,0},{12,4},{1,9},{5,13},{9,1},{13,5},{2,10},{6,14},... | collective-permute-start | bytes 208904 | tf_op jit(solution)/shard_map/ppermute | solution.py:640
  110.4 11.3 %collective-permute-start.17 = (bf16[272,128]{1,0:T(8,128)(2,1)S(1)}, bf16[272,128]{1,0:T(8,128)(2,1)S(1)}, u32[]{:S(2)}, u32[]{:S(2)}) collective-permute-start(bf16[272,128]{1,0:T(8,128)(2,1)S(1)} %factor_bottom.1.refs_1_), channel_id=1, source_target_pairs={{0,12},{4,0},{8,4},{12,8},{1,13},{5,1},{9,5},{13,9},{2,14},{6,2},{... | collective-permute-start | bytes 208904 | tf_op jit(solution)/shard_map/ppermute | solution.py:640

commit v5 on v4

--- a/solution.py
+++ b/solution.py
@@ -21,7 +21,6 @@
 SUM_ROWS = SPAN * PANELS + 8
 VMEM_BYTES = 50 * 2**20
 FULL_VMEM = 63 * 2**20
-TURN_VMEM = 50 * 2**20
 ATTENTION_VMEM = 44 * 2**20
 WHITEN_VMEM = 44 * 2**20
 OTHER_VMEM = 44 * 2**20
@@ -96,16 +95,12 @@
             at += ref.shape[1]
 
 
-def turn_kernel(w_ref, *refs):
-    refs[-1][...] = w_ref[...].T
-
-
-def attention_kernel(meta, *refs, chips, spans, all_spans, documents, most, sets, waited):
+def attention_kernel(meta, *refs, chips, spans, all_spans, documents, most, sets):
     sources = 2 * chips
     near = sources + 4
     query_refs, near_refs = refs[:sources], refs[sources:near]
     far_refs = refs[near : near + sets * (sources - 2)]
-    top, bottom, queries, keys, values, slots, limits, left, right, total = refs[near + sets * (sources - 2) + waited :]
+    top, bottom, queries, keys, values, slots, limits, left, total = refs[near + sets * (sources - 2) :]
     own = meta[0]
     chip, core = own // 2, lax.rem(own, 2)
     lengths = 4
@@ -189,9 +184,6 @@
                         high, low = split(one_head)
                         left[0, columns, lanes] = high
                         left[1, columns, lanes] = low
-                        high, low = split(one_head.T)
-                        right[0, lanes, columns] = high
-                        right[1, lanes, columns] = low
 
         return carry
 
@@ -202,8 +194,8 @@
 
     def one_pass(i, carry):
         a, b = lax.rem(i, 2), i // 2
-        total[:half] += jnp.dot(left[a, :half], right[b], preferred_element_type=F32)
-        total[half:, half:] += jnp.dot(left[a, half:], right[b, :, half:], preferred_element_type=F32)
+        total[:half] += lax.dot_general(left[a, :half], left[b], NT, preferred_element_type=F32)
+        total[half:, half:] += lax.dot_general(left[a, half:], left[b, half:], NT, preferred_element_type=F32)
         return carry
 
     lax.fori_loop(0, 3, one_pass, 0)
@@ -316,39 +308,27 @@
             square = jnp.where(tile_index == k, current[:, k * SPAN : (k + 1) * SPAN], square)
         square = pltpu.roll(square, turn, 1)
         line = lax.broadcasted_iota(jnp.int32, (8, SPAN), 0)
-        square = [square[8 * q : 8 * q + 8] for q in range(groups)]
+        held = [
+            {q: jnp.broadcast_to(square[8 * q : 8 * q + 8, j : j + 1], (8, SPAN)) for q in range(j // 8, groups)}
+            for j in range(step)
+        ]
         body = [[current[8 * q : 8 * q + 8, k * SPAN : (k + 1) * SPAN] for k in range(panels)] for q in range(groups)]
         scales = [jnp.zeros((8, SPAN), F32) for _ in range(groups)]
 
         def spread(value, i):
             return jnp.broadcast_to(value[i % 8 : i % 8 + 1], (8, SPAN))
 
-        def column(j):
-            return {q: jnp.broadcast_to(square[q][:, j : j + 1], (8, SPAN)) for q in range(j // 8, groups)}
-
-        ahead = 4
-        held = {j: column(j) for j in range(ahead)}
-        pivot = spread(held[0][0], 0)
         for i in range(step):
             at = i // 8
-            pivots = held.pop(i)
-            root = lax.rsqrt(pivot)
+            root = lax.rsqrt(spread(held[i][at], i))
             inverse = root * root
-            if i + 1 < step:
-                entry = spread(pivots[(i + 1) // 8], i + 1)
-                pivot = spread(held[i + 1][(i + 1) // 8], i + 1) - (entry * entry) * inverse
-            for j in held:
-                entry = spread(pivots[j // 8], j)
+            scales[at] = jnp.where(line == i % 8, root, scales[at])
+            ratio = {q: held[i][q] * inverse for q in range(at, groups)}
+            ratio[at] = jnp.where(line > i % 8, ratio[at], 0.0)
+            for j in range(i + 1, step):
+                entry = spread(held[i][j // 8], j)
                 for q in range(j // 8, groups):
-                    held[j][q] = held[j][q] - (pivots[q] * entry) * inverse
-            scales[at] = jnp.where(line == i % 8, root, scales[at])
-            ratio = {q: pivots[q] * inverse for q in range(at, groups)}
-            ratio[at] = jnp.where(line > i % 8, ratio[at], 0.0)
-            pivot_row = spread(square[at], i)
-            for q in range(at, groups):
-                square[q] = square[q] - ratio[q] * pivot_row
-            if i + ahead < step:
-                held[i + ahead] = column(i + ahead)
+                    held[j][q] = held[j][q] - ratio[q] * entry
             for k in range(panels):
                 pivot_row = spread(body[at][k], i)
                 for q in range(at, groups):
@@ -405,8 +385,9 @@
                     for column in range(width // SPAN):
                         value = tiles[row, column] if column >= row else jnp.zeros((SPAN, SPAN), F32)
                         high, low = split(value)
-                        left[rows, column * SPAN : (column + 1) * SPAN] = high
-                        left[rows, width + column * SPAN : width + (column + 1) * SPAN] = low
+                        columns = slice(column * SPAN, (column + 1) * SPAN)
+                        left[rows, columns] = high
+                        left[half + row * SPAN : half + (row + 1) * SPAN, columns] = low
 
         for c in range(chunks):
             if count == 1:
@@ -421,11 +402,9 @@
                 def _(c=c):
                     copy(step - 1, which, c).wait()
 
-            weight = w_refs[c][start - lowest :]
-            product = jnp.dot(
-                left[:, : 2 * width], jnp.concatenate([weight, weight], axis=0), preferred_element_type=F32
-            )
-            ready[lax.rem(step * count + which, 2), :, c * chunk : (c + 1) * chunk] = product
+            weight = w_refs[c][:, start - lowest :]
+            product = lax.dot_general(left[:, :width], weight, NT, preferred_element_type=F32)
+            ready[lax.rem(step * count + which, 2), :, c * chunk : (c + 1) * chunk] = product[:half] + product[half:]
             copy(step, which, c).start()
 
     @pl.when(step == blocks - 1)
@@ -492,19 +471,6 @@
 
     tile = 512
 
-    def turn(first, count, *before):
-        return pl.pallas_call(
-            turn_kernel,
-            out_shape=jax.ShapeDtypeStruct((blocks * BLOCK_W, features), BF16),
-            grid=(count, features // tile),
-            in_specs=[pl.BlockSpec((tile, BLOCK_W), lambda b, o: (o, first + b))] + [anywhere] * len(before),
-            out_specs=pl.BlockSpec((BLOCK_W, tile), lambda b, o: (first + b, o)),
-            input_output_aliases={1: 0} if first else {},
-            compiler_params=params(TURN_VMEM),
-            cost_estimate=cost(1.0e9 * count, 2**20),
-            name="turn_weight",
-        )(out_weight, *before)
-
     def target_at(distance, cross):
         return lambda meta: lax.rem(meta[0] // 2 + distance, chips) * 2 + lax.rem(lax.rem(meta[0], 2) + cross, 2)
 
@@ -513,7 +479,7 @@
 
     most = all_spans // 2 + 1
 
-    def grams_of(t, peer, after):
+    def grams_of(t, peer):
         kv = turns[t] // KV_BLOCKS
         carriers = pieces[: min(t + 1, per)]
         which = jnp.where(kv == first_kv, 0, 1).astype(jnp.int32)
@@ -524,7 +490,6 @@
             functools.partial(
                 attention_kernel,
                 chips=chips, spans=spans, all_spans=all_spans, documents=documents, most=most, sets=len(carriers),
-                waited=len(after),
             ),
             out_shape=[folded] * 2,
             grid_spec=pltpu.PrefetchScalarGridSpec(
@@ -541,8 +506,7 @@
                     pl.BlockSpec((tokens, HEAD_SIZE), lambda i, meta: (0, peer_kv + per + meta[2])),
                 ]
                 + [pl.BlockSpec((tokens, 2 * HEAD_SIZE), lambda i, meta: (0, BLOCK_W // (2 * HEAD_SIZE)))]
-                * (len(carriers) * len(far))
-                + [anywhere] * len(after),
+                * (len(carriers) * len(far)),
                 out_specs=[pl.BlockSpec((SUM_ROWS, SPAN), lambda i, meta: (0, 0))] * 2,
                 scratch_shapes=[
                     pltpu.VMEM((all_spans, BLOCK_HEADS * SPAN, HEAD_SIZE), BF16),
@@ -551,14 +515,13 @@
                     pltpu.SMEM((all_spans,), jnp.int32),
                     pltpu.VMEM((2, most * SPAN, SPAN), F32),
                     pltpu.VMEM((2, BLOCK_W, all_spans * SPAN), BF16),
-                    pltpu.VMEM((2, all_spans * SPAN, BLOCK_W), BF16),
                     pltpu.VMEM((BLOCK_W, BLOCK_W), F32),
                 ],
             ),
             compiler_params=params(ATTENTION_VMEM),
             cost_estimate=cost(1.4e10, 2**20),
             name="attention_outer_products",
-        )(meta, query, peer, *pieces[t], key, value, peer, peer, *[array for carrier in carriers for array in carrier], *after)
+        )(meta, query, peer, *pieces[t], key, value, peer, peer, *[array for carrier in carriers for array in carrier])
 
     grams = []
     held = []
@@ -569,7 +532,7 @@
             if t < per:
                 columns += [(array, HEAD_SIZE, lambda target, meta: target * per + meta[2]) for array in (key, value)]
             scalars = jnp.stack([own, turns[t], kv])
-            after = [] if t == 0 else [peer, turned] if t == 1 else [peer, turned]
+            after = [] if t == 0 else [peer]
             parts = cut(
                 [target_at(*where) for where in far], columns, scalars, "cut_piece", after,
                 OTHER_VMEM if t else FULL_VMEM,
@@ -581,23 +544,16 @@
             columns = [(query, blocks * BLOCK_W, lambda target, meta: target)]
             columns += [(array, per * HEAD_SIZE, lambda target, meta: target) for array in (key, value)]
             peer = cut([target_at(0, 1)], columns, own[None], "cut_peer", parts, FULL_VMEM)[0]
-            turned = turn(0, 1, peer)
             peer = lax.ppermute(peer, "seq", moved(0, 1))
-            turned = turn(1, 1, turned)
             continue
-        if t == 1:
-            for b in range(2, blocks - 1):
-                turned = turn(b, 1, turned, parts[0])
         done = t - 1
-        grams.append(grams_of(done, peer, [turned] if t == 1 else []))
+        grams.append(grams_of(done, peer))
         if done == 0 or not in_ring:
             held.append(grams[done])
         else:
             held.append([mine + theirs for mine, theirs in zip(grams[done], carried)] if done < ring - 1 else None)
         if in_ring and done < ring - 1:
             carried = [lax.ppermute(part, "dp", [(z, (z + 1) % ring) for z in range(ring)]) for part in held[done]]
-    if blocks > 2:
-        turned = turn(blocks - 1, 1, turned, *grams[-1])
 
     half = BLOCK_W // 2
     top_rows, bottom_rows = [
@@ -658,8 +614,8 @@
         chunks = features // tile
         weights = [
             pl.BlockSpec(
-                (depth, tile),
-                lambda b, order, c=c: (order[first + b] * (BLOCK_W // depth) + starts[0] // depth, c),
+                (tile, depth),
+                lambda b, order, c=c: (c, order[first + b] * (BLOCK_W // depth) + starts[0] // depth),
             )
             for c in range(chunks)
         ]
@@ -675,7 +631,7 @@
                 in_specs=[vmem] * len(uppers) + weights + [anywhere] * len(more),
                 out_specs=anywhere,
                 scratch_shapes=[
-                    pltpu.VMEM((half, 2 * depth), BF16),
+                    pltpu.VMEM((2 * half, depth), BF16),
                     pltpu.VMEM((2, half, features), F32),
                     pltpu.SemaphoreType.DMA((2, chunks)),
                 ],
@@ -684,7 +640,7 @@
             compiler_params=params(WHITEN_VMEM),
             cost_estimate=cost(2.0e9 * len(uppers), 2**20),
             name="whiten_bottom" if starts[0] else "whiten_top",
-        )(order, *uppers, *[turned] * chunks, *more)
+        )(order, *uppers, *[out_weight] * chunks, *more)
 
     result = whiten([tops[0], bottoms[0]], 0, (0, half), None)
     result = whiten(tops[1:], 1, (0,), result)

time: 130 us -> 129 us (level)
  Pallas kernels: 92.5 us -> 76.3 us
  waiting for transfers between devices: 6.02 us -> 20.3 us
  local copies, waits for them, and re-layouts: 1.68 us -> 3.58 us
    pallas_call x4 -> x0, Pallas kernels: 16.8 us -> none  [turn(): pl.pallas_call(turn_kernel, out_shape=jax.ShapeDtypeStruct((blocks * BLOC...]
    ppermute x8, waiting for transfers between devices: 3.79 us -> 13.5 us  [shards(): lax.ppermute(part, 'seq', moved(*where))]
    ppermute x6, waiting for transfers between devices: 2.21 us -> 6.79 us  [shards(): lax.ppermute(part, 'dp', [(z, (z + 1) % ring) for z in range(ring)])]
    unnamed x14 -> x16, local copies, waits for them, and re-layouts: 1.35 us -> 3.25 us
  transfers between devices with their start and end apart: 21 -> 21, of which waited for: 5 -> 5; matrix products, arithmetic and copies ran while one was open for 1% -> 1% of each run, Pallas kernels for 56% -> 43%
where the time goes in v5:
time: 129 us; the launch traced here: 128 us
  Pallas kernels  76.3 us (59%)
  starting transfers between devices  26 us (20%)
  waiting for transfers between devices  20.3 us (16%)
  local copies, waits for them, and re-layouts  3.58 us (3%)
    pallas_call x4, Pallas kernels, grams_of(): pl.pallas_call(functools.partial(attention_kernel, chips=chips, spans=spa...  32.9 us
    pallas_call x3, Pallas kernels, whiten(): pl.pallas_call(functools.partial(whiten_kernel, blocks=count, starts=star...  18.7 us
    ppermute x8, waiting for transfers between devices, shards(): lax.ppermute(part, 'seq', moved(*where))  13.5 us
    pallas_call x1, Pallas kernels, factor_top(): pl.pallas_call(functools.partial(factor_kernel, start=0, stop=half, recei...  9.33 us
    ppermute x6, starting transfers between devices, shared(): lax.ppermute(array, 'dp', [(z, (z + d) % ring) for z in range(ring)])  9.19 us
    ppermute x8, starting transfers between devices, shards(): lax.ppermute(part, 'seq', moved(*where))  8.69 us
    pallas_call x1, Pallas kernels, factor_bottom(): pl.pallas_call(functools.partial(factor_kernel, start=half, stop=BLOCK_W,...  8.22 us
    ppermute x6, starting transfers between devices, shards(): lax.ppermute(part, 'dp', [(z, (z + 1) % ring) for z in range(ring)])  7.66 us
  transfers between devices with their start and end apart: 21, of which 5 were waited for; matrix products, arithmetic and copies ran while one was open for 1% of the time, Pallas kernels for 43%

profile of v5, /device:TPU:0, one launch (start us, length us, event | category | flops | bytes accessed | tf_op | source)
XLA Modules:
  0.0 127.6 jit_solution(17421061777483024029)
XLA Ops:
  0.6 2.8 %cut_piece.4 = (bf16[256,768]{1,0:T(8,128)(2,1)}, bf16[256,768]{1,0:T(8,128)(2,1)}) custom-call(s32[3]{0:T(128)} %pad_add_fusion.1.meta, bf16[256,8192]{1,0:T(8,128)(2,1)} %bitcast.23, bf16[256,1024]{1,0:T(8,128)(2,1)} %bitcast.36, bf16[256,1024]{1,0:T(8,128)(2,1)} %bitcast.45, bf16[256,8192]{1,0:T(8,128)(2,1)} %bitcast.24, bf16[256,1024]{1,0:T(8,128)(2,1)} %bitcast.37, ...), custom_call_target="tpu_custom_call" | custom-call | bytes 2097152 | tf_op jit(solution)/shard_map/cut_piece/pallas_call | solution.py:458
  3.4 2.4 %cut_peer.1 = bf16[256,2560]{1,0:T(8,128)(2,1)} custom-call(s32[1]{0:T(128)} %bitcast.4.meta, bf16[256,8192]{1,0:T(8,128)(2,1)} %bitcast.25, bf16[256,1024]{1,0:T(8,128)(2,1)} %bitcast.38, bf16[256,1024]{1,0:T(8,128)(2,1)} %bitcast.47, bf16[256,768]{1,0:T(8,128)(2,1)} %get-tuple-element.27.refs_3_, bf16[256,768]{1,0:T(8,128)(2,1)} %get-tuple-element.28.refs_4_), custom_call_target="tpu_custom_call" | custom-call | bytes 2097152 | tf_op jit(solution)/shard_map/cut_peer/pallas_call | solution.py:458
  6.3 2.5 %collective-permute-start.3 = (bf16[256,768]{1,0:T(8,128)(2,1)}, bf16[256,768]{1,0:T(8,128)(2,1)S(1)}, u32[]{:S(2)}, u32[]{:S(2)}) collective-permute-start(bf16[256,768]{1,0:T(8,128)(2,1)} %get-tuple-element.27.refs_3_), channel_id=1, source_target_pairs={{0,2},{1,3},{2,0},{3,1},{4,6},{5,7},{6,4},{7,5},{8,10},{9,11},{10,... | collective-permute-start | bytes 1179656 | tf_op jit(solution)/shard_map/ppermute | solution.py:542
  9.5 2.2 %copy-done = bf16[1,256,8192]{2,1,0:T(8,128)(2,1)S(1)} copy-done((bf16[1,256,8192]{2,1,0:T(8,128)(2,1)S(1)}, bf16[1,256,8192]{2,1,0:T(8,128)(2,1)}, u32[]{:S(2)}) %copy-start) | copy-done | bytes 4194328
  11.7 1.0 copy-done.2
  12.8 0.7 cut_piece.6
  13.5 2.6 %collective-permute-start.1 = (bf16[256,768]{1,0:T(8,128)(2,1)S(1)}, bf16[256,768]{1,0:T(8,128)(2,1)S(1)}, u32[]{:S(2)}, u32[]{:S(2)}) collective-permute-start(bf16[256,768]{1,0:T(8,128)(2,1)S(1)} %get-tuple-element.31), channel_id=1, source_target_pairs={{0,2},{1,3},{2,0},{3,1},{4,6},{5,7},{6,4},{7,5},{8,10},{9,11},{10,... | collective-permute-start | bytes 1179656 | tf_op jit(solution)/shard_map/ppermute | solution.py:542
  16.1 2.9 %collective-permute-done.3.refs_8_.refs_2_ = bf16[256,768]{1,0:T(8,128)(2,1)S(1)} collective-permute-done((bf16[256,768]{1,0:T(8,128)(2,1)}, bf16[256,768]{1,0:T(8,128)(2,1)S(1)}, u32[]{:S(2)}, u32[]{:S(2)}) %collective-permute-start.3) | collective-permute-done | bytes 393248 | tf_op jit(solution)/shard_map/ppermute | solution.py:542
  19.0 8.1 %collective-permute-done.4.refs_9_.refs_3_ = bf16[256,768]{1,0:T(8,128)(2,1)S(1)} collective-permute-done((bf16[256,768]{1,0:T(8,128)(2,1)}, bf16[256,768]{1,0:T(8,128)(2,1)S(1)}, u32[]{:S(2)}, u32[]{:S(2)}) %collective-permute-start.4) | collective-permute-done | bytes 393248 | tf_op jit(solution)/shard_map/ppermute | solution.py:542
  27.0 8.1 %attention_outer_products.5 = (f32[520,128]{1,0:T(8,128)S(1)}, f32[520,128]{1,0:T(8,128)S(1)}) custom-call(s32[20]{0:T(128)S(1)} %concatenate.14.meta, bf16[256,8192]{1,0:T(8,128)(2,1)S(1)} %bitcast.28, bf16[256,2560]{1,0:T(8,128)(2,1)S(1)} %collective-permute-done.refs_2_.refs_6_.refs_1_.refs_7_, ...), custom_call_target="tpu_custom_call" | custom-call | flops 14000000000 | bytes 1048576 | tf_op jit(solution)/shard_map/attention_outer_products/pallas_call | solution.py:489
  35.2 1.1 collective-permute-start.6
  36.3 2.1 %collective-permute-start.5 = (f32[520,128]{1,0:T(8,128)S(1)}, f32[520,128]{1,0:T(8,128)S(1)}, u32[]{:S(2)}, u32[]{:S(2)}) collective-permute-start(f32[520,128]{1,0:T(8,128)S(1)} %get-tuple-element.34), channel_id=1, source_target_pairs={{0,4},{4,8},{8,12},{12,0},{1,5},{5,9},{9,13},{13,1},{2,6},{6,10},{... | collective-permute-start | bytes 798728 | tf_op jit(solution)/shard_map/ppermute | solution.py:556
  39.0 1.2 collective-permute-start.10
  41.4 2.5 %collective-permute-done.2.refs_3_.refs_11_ = bf16[256,768]{1,0:T(8,128)(2,1)S(1)} collective-permute-done((bf16[256,768]{1,0:T(8,128)(2,1)S(1)}, bf16[256,768]{1,0:T(8,128)(2,1)S(1)}, u32[]{:S(2)}, u32[]{:S(2)}) %collective-permute-start.2) | collective-permute-done | bytes 393248 | tf_op jit(solution)/shard_map/ppermute | solution.py:542
  43.9 8.3 %attention_outer_products.4 = (f32[520,128]{1,0:T(8,128)S(1)}, f32[520,128]{1,0:T(8,128)S(1)}) custom-call(s32[20]{0:T(128)S(1)} %concatenate.13.meta, bf16[256,8192]{1,0:T(8,128)(2,1)S(1)} %bitcast.33, bf16[256,2560]{1,0:T(8,128)(2,1)S(1)} %collective-permute-done.refs_2_.refs_6_.refs_1_.refs_7_, ...), custom_call_target="tpu_custom_call" | custom-call | flops 14000000000 | bytes 1048576 | tf_op jit(solution)/shard_map/attention_outer_products/pallas_call | solution.py:489
  52.2 1.1 collective-permute-start.13
  53.4 2.2 %collective-permute-start.11 = (f32[520,128]{1,0:T(8,128)S(1)}, f32[520,128]{1,0:T(8,128)S(1)}, u32[]{:S(2)}, u32[]{:S(2)}) collective-permute-start(f32[520,128]{1,0:T(8,128)S(1)} %add.57), channel_id=1, source_target_pairs={{0,4},{4,8},{8,12},{12,0},{1,5},{5,9},{9,13},{13,1},{2,6},{6,10},{... | collective-permute-start | bytes 798728 | tf_op jit(solution)/shard_map/ppermute | solution.py:556
  55.6 1.5 %collective-permute-start.7 = (bf16[256,512]{1,0:T(8,128)(2,1)S(1)}, bf16[256,512]{1,0:T(8,128)(2,1)S(1)}, u32[]{:S(2)}, u32[]{:S(2)}) collective-permute-start(bf16[256,512]{1,0:T(8,128)(2,1)S(1)} %get-tuple-element.37), channel_id=1, source_target_pairs={{0,2},{1,3},{2,0},{3,1},{4,6},{5,7},{6,4},{7,5},{8,10},{9,11},{10,... | collective-permute-start | bytes 786440 | tf_op jit(solution)/shard_map/ppermute | solution.py:542
  57.3 8.1 %attention_outer_products.7 = (f32[520,128]{1,0:T(8,128)S(1)}, f32[520,128]{1,0:T(8,128)S(1)}) custom-call(s32[20]{0:T(128)S(1)} %concatenate.15.meta, bf16[256,8192]{1,0:T(8,128)(2,1)S(1)} %bitcast.34, bf16[256,2560]{1,0:T(8,128)(2,1)S(1)} %collective-permute-done.refs_2_.refs_6_.refs_1_.refs_7_, bf16[256,512]{1,0:T(8,128)(2,1)S(1)} %collective-permute-done.9.refs_2_, ...), custom_call_target="tpu_custom_call" | custom-call | flops 14000000000 | bytes 1048576 | tf_op jit(solution)/shard_map/attention_outer_products/pallas_call | solution.py:489
  65.5 1.0 collective-permute-start.14
  66.5 2.5 %collective-permute-done.11 = f32[520,128]{1,0:T(8,128)S(1)} collective-permute-done((f32[520,128]{1,0:T(8,128)S(1)}, f32[520,128]{1,0:T(8,128)S(1)}, u32[]{:S(2)}, u32[]{:S(2)}) %collective-permute-start.11) | collective-permute-done | bytes 266272 | tf_op jit(solution)/shard_map/ppermute | solution.py:556
  69.2 8.3 %attention_outer_products.6 = (f32[520,128]{1,0:T(8,128)S(1)}, f32[520,128]{1,0:T(8,128)S(1)}) custom-call(s32[20]{0:T(128)S(1)} %concatenate.12.meta, bf16[256,8192]{1,0:T(8,128)(2,1)S(1)} %bitcast.35, bf16[256,2560]{1,0:T(8,128)(2,1)S(1)} %collective-permute-done.refs_2_.refs_6_.refs_1_.refs_7_, bf16[256,512]{1,0:T(8,128)(2,1)S(1)} %collective-permute-done.7.refs_2_, ...), custom_call_target="tpu_custom_call" | custom-call | flops 14000000000 | bytes 1048576 | tf_op jit(solution)/shard_map/attention_outer_products/pallas_call | solution.py:489
  77.5 4.3 %collective-permute-done.12.refs_2_ = f32[520,128]{1,0:T(8,128)S(1)} collective-permute-done((f32[520,128]{1,0:T(8,128)S(1)}, f32[520,128]{1,0:T(8,128)S(1)}, u32[]{:S(2)}, u32[]{:S(2)}) %collective-permute-start.12) | collective-permute-done | bytes 266272 | tf_op jit(solution)/shard_map/ppermute | solution.py:556
  81.8 9.3 %factor_top.1 = (bf16[784,128]{1,0:T(8,128)(2,1)S(1)}, f32[256,256]{1,0:T(8,128)S(1)}) custom-call(f32[520,128]{1,0:T(8,128)S(1)} %get-tuple-element.39.refs_0_, f32[520,128]{1,0:T(8,128)S(1)} %get-tuple-element.40.refs_1_, f32[520,128]{1,0:T(8,128)S(1)} %collective-permute-done.12.refs_2_, f32[520,128]{1,0:T(8,128)S(1)} %collective-permute-done.14.refs_3_), custom_call_target="tpu_custom_call" | custom-call | flops 10000000000 | bytes 1048576 | tf_op jit(solution)/shard_map/factor_top/pallas_call | solution.py:565
  91.2 1.0 collective-permute-start.19
  92.2 2.8 %collective-permute-start.20 = (bf16[784,128]{1,0:T(8,128)(2,1)S(1)}, bf16[784,128]{1,0:T(8,128)(2,1)S(1)}, u32[]{:S(2)}, u32[]{:S(2)}) collective-permute-start(bf16[784,128]{1,0:T(8,128)(2,1)S(1)} %get-tuple-element.48.refs_0_), channel_id=1, source_target_pairs={{0,12},{4,0},{8,4},{12,8},{1,13},{5,1},{9,5},{13,9},{2,14},{6,2},{... | collective-permute-start | bytes 602120 | tf_op jit(solution)/shard_map/ppermute | solution.py:596
  95.0 8.2 %factor_bottom.1.refs_1_ = bf16[272,128]{1,0:T(8,128)(2,1)S(1)} custom-call(f32[256,256]{1,0:T(8,128)S(1)} %get-tuple-element.47.refs_0_), custom_call_target="tpu_custom_call" | custom-call | flops 8999999488 | bytes 1048576 | tf_op jit(solution)/shard_map/factor_bottom/pallas_call | solution.py:580
  103.9 1.5 %collective-permute-start.16 = (bf16[272,128]{1,0:T(8,128)(2,1)S(1)}, bf16[272,128]{1,0:T(8,128)(2,1)S(1)}, u32[]{:S(2)}, u32[]{:S(2)}) collective-permute-start(bf16[272,128]{1,0:T(8,128)(2,1)S(1)} %factor_bottom.1.refs_1_), channel_id=1, source_target_pairs={{0,8},{4,12},{8,0},{12,4},{1,9},{5,13},{9,1},{13,5},{2,10},{6,14},... | collective-permute-start | bytes 208904 | tf_op jit(solution)/shard_map/ppermute | solution.py:596
  105.4 3.5 %whiten_top.2.refs_7_ = f32[4,512,2048]{2,1,0:T(8,128)} custom-call(s32[4]{0:T(128)S(1)} %pad_add_fusion.order, bf16[784,128]{1,0:T(8,128)(2,1)S(1)} %get-tuple-element.48.refs_0_, bf16[272,128]{1,0:T(8,128)(2,1)S(1)} %factor_bottom.1.refs_1_, bf16[2048,2048]{1,0:T(8,128)(2,1)S(1)} %bitcast.22, bf16[2048,2048]{1,0:T(8,128)(2,1)S(1)} %bitcast.22, ...), custom_call_target="tpu_custom_call" | custom-call | flops 4000000000 | bytes 1048576 | tf_op jit(solution)/shard_map/whiten_top/pallas_call | solution.py:623
  108.9 3.2 %collective-permute-start.17 = (bf16[272,128]{1,0:T(8,128)(2,1)S(1)}, bf16[272,128]{1,0:T(8,128)(2,1)S(1)}, u32[]{:S(2)}, u32[]{:S(2)}) collective-permute-start(bf16[272,128]{1,0:T(8,128)(2,1)S(1)} %factor_bottom.1.refs_1_), channel_id=1, source_target_pairs={{0,12},{4,0},{8,4},{12,8},{1,13},{5,1},{9,5},{13,9},{2,14},{6,2},{... | collective-permute-start | bytes 208904 | tf_op jit(solution)/shard_map/ppermute | solution.py:596
  112.1 8.7 %whiten_top.3.refs_7_ = f32[4,512,2048]{2,1,0:T(8,128)} custom-call(s32[4]{0:T(128)S(1)} %pad_add_fusion.order, bf16[784,128]{1,0:T(8,128)(2,1)S(1)} %collective-permute-done.18.refs_0_, bf16[784,128]{1,0:T(8,128)(2,1)S(1)} %collective-permute-done.19.refs_1_, bf16[784,128]{1,0:T(8,128)(2,1)S(1)} %collective-permute-done.20.refs_2_, ...), custom_call_target="tpu_custom_call", output_to_operand_aliasing={{}: (8, {})} | custom-call | flops 6000000000 | bytes 1048576 | tf_op jit(solution)/shard_map/whiten_top/pallas_call | solution.py:623
  120.8 6.5 %whiten_bottom.1 = f32[4,512,2048]{2,1,0:T(8,128)} custom-call(s32[4]{0:T(128)S(1)} %pad_add_fusion.order, bf16[272,128]{1,0:T(8,128)(2,1)S(1)} %collective-permute-done.15.refs_0_, bf16[272,128]{1,0:T(8,128)(2,1)S(1)} %collective-permute-done.16.refs_1_, bf16[272,128]{1,0:T(8,128)(2,1)S(1)} %collective-permute-done.17.refs_2_, ...), custom_call_target="tpu_custom_call", output_to_operand_aliasing={{}: (8, {})} | custom-call | flops 6000000000 | bytes 1048576 | tf_op jit(solution)/shard_map/whiten_bottom/pallas_call | solution.py:623
  (53 shorter events, 4.7 us)
Async XLA Ops:
  0.6 8.4 %copy-start.4 = (s32[1,8]{1,0:T(1,128)S(1)}, s32[1,8]{1,0:T(1,128)}, u32[]{:S(2)}) copy-start(s32[1,8]{1,0:T(1,128)} %param.9) | copy-start | bytes 100
  0.6 8.4 %copy-start.5 = (s32[1,8]{1,0:T(1,128)S(1)}, s32[1,8]{1,0:T(1,128)}, u32[]{:S(2)}) copy-start(s32[1,8]{1,0:T(1,128)} %param.10) | copy-start | bytes 100
  0.6 8.9 %copy-start.1 = (bf16[1,256,1024]{2,1,0:T(8,128)(2,1)S(1)}, bf16[1,256,1024]{2,1,0:T(8,128)(2,1)}, u32[]{:S(2)}) copy-start(bf16[1,256,1024]{2,1,0:T(8,128)(2,1)} %param.7) | copy-start | bytes 1572868
  5.9 3.7 %collective-permute-start = (bf16[256,2560]{1,0:T(8,128)(2,1)}, bf16[256,2560]{1,0:T(8,128)(2,1)S(1)}, u32[]{:S(2)}, u32[]{:S(2)}) collective-permute-start(bf16[256,2560]{1,0:T(8,128)(2,1)} %cut_peer.1), channel_id=1, source_target_pairs={{0,1},{1,0},{2,3},{3,2},{4,5},{5,4},{6,7},{7,6},{8,9},{9,8},{10,11... | collective-permute-start | bytes 3932168 | tf_op jit(solution)/shard_map/ppermute | solution.py:547
  6.3 12.7 %collective-permute-start.3 = (bf16[256,768]{1,0:T(8,128)(2,1)}, bf16[256,768]{1,0:T(8,128)(2,1)S(1)}, u32[]{:S(2)}, u32[]{:S(2)}) collective-permute-start(bf16[256,768]{1,0:T(8,128)(2,1)} %get-tuple-element.27.refs_3_), channel_id=1, source_target_pairs={{0,2},{1,3},{2,0},{3,1},{4,6},{5,7},{6,4},{7,5},{8,10},{9,11},{10,... | collective-permute-start | bytes 1179656 | tf_op jit(solution)/shard_map/ppermute | solution.py:542
  8.8 18.2 %collective-permute-start.4 = (bf16[256,768]{1,0:T(8,128)(2,1)}, bf16[256,768]{1,0:T(8,128)(2,1)S(1)}, u32[]{:S(2)}, u32[]{:S(2)}) collective-permute-start(bf16[256,768]{1,0:T(8,128)(2,1)} %get-tuple-element.28.refs_4_), channel_id=1, source_target_pairs={{0,3},{1,2},{2,1},{3,0},{4,7},{5,6},{6,5},{7,4},{8,11},{9,10},{10,... | collective-permute-start | bytes 1179656 | tf_op jit(solution)/shard_map/ppermute | solution.py:542
  9.5 2.2 %copy-start = (bf16[1,256,8192]{2,1,0:T(8,128)(2,1)S(1)}, bf16[1,256,8192]{2,1,0:T(8,128)(2,1)}, u32[]{:S(2)}) copy-start(bf16[1,256,8192]{2,1,0:T(8,128)(2,1)} %param.6) | copy-start | bytes 12582916
  11.7 1.0 copy-start.2
  13.5 27.4 %collective-permute-start.1 = (bf16[256,768]{1,0:T(8,128)(2,1)S(1)}, bf16[256,768]{1,0:T(8,128)(2,1)S(1)}, u32[]{:S(2)}, u32[]{:S(2)}) collective-permute-start(bf16[256,768]{1,0:T(8,128)(2,1)S(1)} %get-tuple-element.31), channel_id=1, source_target_pairs={{0,2},{1,3},{2,0},{3,1},{4,6},{5,7},{6,4},{7,5},{8,10},{9,11},{10,... | collective-permute-start | bytes 1179656 | tf_op jit(solution)/shard_map/ppermute | solution.py:542
  16.0 27.8 %collective-permute-start.2 = (bf16[256,768]{1,0:T(8,128)(2,1)S(1)}, bf16[256,768]{1,0:T(8,128)(2,1)S(1)}, u32[]{:S(2)}, u32[]{:S(2)}) collective-permute-start(bf16[256,768]{1,0:T(8,128)(2,1)S(1)} %get-tuple-element.32), channel_id=1, source_target_pairs={{0,3},{1,2},{2,1},{3,0},{4,7},{5,6},{6,5},{7,4},{8,11},{9,10},{10,... | collective-permute-start | bytes 1179656 | tf_op jit(solution)/shard_map/ppermute | solution.py:542
  35.2 17.0 %collective-permute-start.6 = (f32[520,128]{1,0:T(8,128)S(1)}, f32[520,128]{1,0:T(8,128)S(1)}, u32[]{:S(2)}, u32[]{:S(2)}) collective-permute-start(f32[520,128]{1,0:T(8,128)S(1)} %get-tuple-element.36), channel_id=1, source_target_pairs={{0,4},{4,8},{8,12},{12,0},{1,5},{5,9},{9,13},{13,1},{2,6},{6,10},{... | collective-permute-start | bytes 798728 | tf_op jit(solution)/shard_map/ppermute | solution.py:556
  36.3 7.6 %copy-start.3 = (bf16[1,256,1024]{2,1,0:T(8,128)(2,1)S(1)}, bf16[1,256,1024]{2,1,0:T(8,128)(2,1)}, u32[]{:S(2)}) copy-start(bf16[1,256,1024]{2,1,0:T(8,128)(2,1)} %param.8) | copy-start | bytes 1572868
  36.3 17.1 %collective-permute-start.5 = (f32[520,128]{1,0:T(8,128)S(1)}, f32[520,128]{1,0:T(8,128)S(1)}, u32[]{:S(2)}, u32[]{:S(2)}) collective-permute-start(f32[520,128]{1,0:T(8,128)S(1)} %get-tuple-element.34), channel_id=1, source_target_pairs={{0,4},{4,8},{8,12},{12,0},{1,5},{5,9},{9,13},{13,1},{2,6},{6,10},{... | collective-permute-start | bytes 798728 | tf_op jit(solution)/shard_map/ppermute | solution.py:556
  39.0 18.1 %collective-permute-start.10 = (bf16[256,512]{1,0:T(8,128)(2,1)S(1)}, bf16[256,512]{1,0:T(8,128)(2,1)S(1)}, u32[]{:S(2)}, u32[]{:S(2)}) collective-permute-start(bf16[256,512]{1,0:T(8,128)(2,1)S(1)} %get-tuple-element.44), channel_id=1, source_target_pairs={{0,3},{1,2},{2,1},{3,0},{4,7},{5,6},{6,5},{7,4},{8,11},{9,10},{10,... | collective-permute-start | bytes 786440 | tf_op jit(solution)/shard_map/ppermute | solution.py:542
  40.8 16.5 %collective-permute-start.9 = (bf16[256,512]{1,0:T(8,128)(2,1)S(1)}, bf16[256,512]{1,0:T(8,128)(2,1)S(1)}, u32[]{:S(2)}, u32[]{:S(2)}) collective-permute-start(bf16[256,512]{1,0:T(8,128)(2,1)S(1)} %get-tuple-element.43), channel_id=1, source_target_pairs={{0,2},{1,3},{2,0},{3,1},{4,6},{5,7},{6,4},{7,5},{8,10},{9,11},{10,... | collective-permute-start | bytes 786440 | tf_op jit(solution)/shard_map/ppermute | solution.py:542
  52.2 13.2 %collective-permute-start.13 = (f32[520,128]{1,0:T(8,128)S(1)}, f32[520,128]{1,0:T(8,128)S(1)}, u32[]{:S(2)}, u32[]{:S(2)}) collective-permute-start(f32[520,128]{1,0:T(8,128)S(1)} %add.58), channel_id=1, source_target_pairs={{0,4},{4,8},{8,12},{12,0},{1,5},{5,9},{9,13},{13,1},{2,6},{6,10},{... | collective-permute-start | bytes 798728 | tf_op jit(solution)/shard_map/ppermute | solution.py:556
  53.4 15.6 %collective-permute-start.11 = (f32[520,128]{1,0:T(8,128)S(1)}, f32[520,128]{1,0:T(8,128)S(1)}, u32[]{:S(2)}, u32[]{:S(2)}) collective-permute-start(f32[520,128]{1,0:T(8,128)S(1)} %add.57), channel_id=1, source_target_pairs={{0,4},{4,8},{8,12},{12,0},{1,5},{5,9},{9,13},{13,1},{2,6},{6,10},{... | collective-permute-start | bytes 798728 | tf_op jit(solution)/shard_map/ppermute | solution.py:556
  55.6 13.5 %collective-permute-start.7 = (bf16[256,512]{1,0:T(8,128)(2,1)S(1)}, bf16[256,512]{1,0:T(8,128)(2,1)S(1)}, u32[]{:S(2)}, u32[]{:S(2)}) collective-permute-start(bf16[256,512]{1,0:T(8,128)(2,1)S(1)} %get-tuple-element.37), channel_id=1, source_target_pairs={{0,2},{1,3},{2,0},{3,1},{4,6},{5,7},{6,4},{7,5},{8,10},{9,11},{10,... | collective-permute-start | bytes 786440 | tf_op jit(solution)/shard_map/ppermute | solution.py:542
  57.1 12.1 %collective-permute-start.8 = (bf16[256,512]{1,0:T(8,128)(2,1)S(1)}, bf16[256,512]{1,0:T(8,128)(2,1)S(1)}, u32[]{:S(2)}, u32[]{:S(2)}) collective-permute-start(bf16[256,512]{1,0:T(8,128)(2,1)S(1)} %get-tuple-element.38), channel_id=1, source_target_pairs={{0,3},{1,2},{2,1},{3,0},{4,7},{5,6},{6,5},{7,4},{8,11},{9,10},{10,... | collective-permute-start | bytes 786440 | tf_op jit(solution)/shard_map/ppermute | solution.py:542
  65.5 12.0 %collective-permute-start.14 = (f32[520,128]{1,0:T(8,128)S(1)}, f32[520,128]{1,0:T(8,128)S(1)}, u32[]{:S(2)}, u32[]{:S(2)}) collective-permute-start(f32[520,128]{1,0:T(8,128)S(1)} %add.60), channel_id=1, source_target_pairs={{0,4},{4,8},{8,12},{12,0},{1,5},{5,9},{9,13},{13,1},{2,6},{6,10},{... | collective-permute-start | bytes 798728 | tf_op jit(solution)/shard_map/ppermute | solution.py:556
  69.1 12.7 %collective-permute-start.12 = (f32[520,128]{1,0:T(8,128)S(1)}, f32[520,128]{1,0:T(8,128)S(1)}, u32[]{:S(2)}, u32[]{:S(2)}) collective-permute-start(f32[520,128]{1,0:T(8,128)S(1)} %add.59), channel_id=1, source_target_pairs={{0,4},{4,8},{8,12},{12,0},{1,5},{5,9},{9,13},{13,1},{2,6},{6,10},{... | collective-permute-start | bytes 798728 | tf_op jit(solution)/shard_map/ppermute | solution.py:556
  69.2 36.2 %slice-start = ((s8[8388608]{0:T(1024)(128)(4,1)}), s8[4194304]{0:T(1024)(128)(4,1)S(1)}, s32[]{:S(2)}) async-start(s8[8388608]{0:T(1024)(128)(4,1)} %bitcast.21), calls=%async_computation | async-start | bytes 8388608
  81.8 23.6 %slice-start.1 = ((s8[8388608]{0:T(1024)(128)(4,1)}), s8[4194304]{0:T(1024)(128)(4,1)S(1)}, s32[]{:S(2)}) async-start(s8[8388608]{0:T(1024)(128)(4,1)} %bitcast.21), calls=%async_computation.1 | async-start | bytes 8388608
  91.1 17.8 %collective-permute-start.18 = (bf16[784,128]{1,0:T(8,128)(2,1)S(1)}, bf16[784,128]{1,0:T(8,128)(2,1)S(1)}, u32[]{:S(2)}, u32[]{:S(2)}) collective-permute-start(bf16[784,128]{1,0:T(8,128)(2,1)S(1)} %get-tuple-element.48.refs_0_), channel_id=1, source_target_pairs={{0,4},{4,8},{8,12},{12,0},{1,5},{5,9},{9,13},{13,1},{2,6},{6,10},{... | collective-permute-start | bytes 602120 | tf_op jit(solution)/shard_map/ppermute | solution.py:596
  91.2 20.9 %collective-permute-start.19 = (bf16[784,128]{1,0:T(8,128)(2,1)S(1)}, bf16[784,128]{1,0:T(8,128)(2,1)S(1)}, u32[]{:S(2)}, u32[]{:S(2)}) collective-permute-start(bf16[784,128]{1,0:T(8,128)(2,1)S(1)} %get-tuple-element.48.refs_0_), channel_id=1, source_target_pairs={{0,8},{4,12},{8,0},{12,4},{1,9},{5,13},{9,1},{13,5},{2,10},{6,14},... | collective-permute-start | bytes 602120 | tf_op jit(solution)/shard_map/ppermute | solution.py:596
  92.2 19.9 %collective-permute-start.20 = (bf16[784,128]{1,0:T(8,128)(2,1)S(1)}, bf16[784,128]{1,0:T(8,128)(2,1)S(1)}, u32[]{:S(2)}, u32[]{:S(2)}) collective-permute-start(bf16[784,128]{1,0:T(8,128)(2,1)S(1)} %get-tuple-element.48.refs_0_), channel_id=1, source_target_pairs={{0,12},{4,0},{8,4},{12,8},{1,13},{5,1},{9,5},{13,9},{2,14},{6,2},{... | collective-permute-start | bytes 602120 | tf_op jit(solution)/shard_map/ppermute | solution.py:596
  103.2 17.6 %collective-permute-start.15 = (bf16[272,128]{1,0:T(8,128)(2,1)S(1)}, bf16[272,128]{1,0:T(8,128)(2,1)S(1)}, u32[]{:S(2)}, u32[]{:S(2)}) collective-permute-start(bf16[272,128]{1,0:T(8,128)(2,1)S(1)} %factor_bottom.1.refs_1_), channel_id=1, source_target_pairs={{0,4},{4,8},{8,12},{12,0},{1,5},{5,9},{9,13},{13,1},{2,6},{6,10},{... | collective-permute-start | bytes 208904 | tf_op jit(solution)/shard_map/ppermute | solution.py:596
  103.9 16.9 %collective-permute-start.16 = (bf16[272,128]{1,0:T(8,128)(2,1)S(1)}, bf16[272,128]{1,0:T(8,128)(2,1)S(1)}, u32[]{:S(2)}, u32[]{:S(2)}) collective-permute-start(bf16[272,128]{1,0:T(8,128)(2,1)S(1)} %factor_bottom.1.refs_1_), channel_id=1, source_target_pairs={{0,8},{4,12},{8,0},{12,4},{1,9},{5,13},{9,1},{13,5},{2,10},{6,14},... | collective-permute-start | bytes 208904 | tf_op jit(solution)/shard_map/ppermute | solution.py:596
  108.9 11.9 %collective-permute-start.17 = (bf16[272,128]{1,0:T(8,128)(2,1)S(1)}, bf16[272,128]{1,0:T(8,128)(2,1)S(1)}, u32[]{:S(2)}, u32[]{:S(2)}) collective-permute-start(bf16[272,128]{1,0:T(8,128)(2,1)S(1)} %factor_bottom.1.refs_1_), channel_id=1, source_target_pairs={{0,12},{4,0},{8,4},{12,8},{1,13},{5,1},{9,5},{13,9},{2,14},{6,2},{... | collective-permute-start | bytes 208904 | tf_op jit(solution)/shard_map/ppermute | solution.py:596

commit v6 on v5

--- a/solution.py
+++ b/solution.py
@@ -354,9 +354,9 @@
     write_coded(Tiles(upper, (stop - start) // SPAN, panels, True), out)
 
 
-def whiten_kernel(order, *refs, blocks, starts, first, chunks, aliased):
+def whiten_kernel(order, *refs, blocks, given, starts, first, chunks, aliased):
     count = len(starts)
-    u_refs, refs = refs[: blocks * count], refs[blocks * count :]
+    u_refs, refs = refs[:given], refs[given:]
     w_refs, refs = refs[:chunks], refs[chunks + aliased :]
     lowest = starts[0]
     out, left, ready, sems = refs
@@ -375,9 +375,9 @@
 
     for which, start in enumerate(starts):
         width = BLOCK_W - start
-        for b in range(blocks):
-
-            @pl.when(step == b)
+        for b in range(given // count):
+
+            @pl.when((step == b) | (given < blocks * count))
             def _(b=b):
                 tiles = read_coded(u_refs[b * count + which], width // SPAN)
                 for row in range(half // SPAN):
@@ -479,13 +479,12 @@
 
     most = all_spans // 2 + 1
 
-    def grams_of(t, peer):
+    def grams_of(t):
         kv = turns[t] // KV_BLOCKS
         carriers = pieces[: min(t + 1, per)]
         which = jnp.where(kv == first_kv, 0, 1).astype(jnp.int32)
         meta = jnp.concatenate([jnp.stack([own, turns[t], kv, which]), doc_lengths[0], span_order[0]])
         folded = jax.ShapeDtypeStruct((SUM_ROWS, SPAN), F32)
-        peer_kv = blocks * BLOCK_W // HEAD_SIZE
         return pl.pallas_call(
             functools.partial(
                 attention_kernel,
@@ -497,14 +496,10 @@
                 grid=(1,),
                 in_specs=[
                     pl.BlockSpec((tokens, BLOCK_W), lambda i, meta: (0, meta[0] * blocks + meta[1])),
-                    pl.BlockSpec((tokens, BLOCK_W), lambda i, meta: (0, meta[1])),
+                    pl.BlockSpec((tokens, BLOCK_W), lambda i, meta: (0, meta[0] * blocks + meta[1])),
                 ]
                 + [pl.BlockSpec((tokens, BLOCK_W), lambda i, meta: (0, 0))] * len(far)
-                + [pl.BlockSpec((tokens, HEAD_SIZE), lambda i, meta: (0, meta[0] * per + meta[2]))] * 2
-                + [
-                    pl.BlockSpec((tokens, HEAD_SIZE), lambda i, meta: (0, peer_kv + meta[2])),
-                    pl.BlockSpec((tokens, HEAD_SIZE), lambda i, meta: (0, peer_kv + per + meta[2])),
-                ]
+                + [pl.BlockSpec((tokens, HEAD_SIZE), lambda i, meta: (0, meta[0] * per + meta[2]))] * 4
                 + [pl.BlockSpec((tokens, 2 * HEAD_SIZE), lambda i, meta: (0, BLOCK_W // (2 * HEAD_SIZE)))]
                 * (len(carriers) * len(far)),
                 out_specs=[pl.BlockSpec((SUM_ROWS, SPAN), lambda i, meta: (0, 0))] * 2,
@@ -521,10 +516,11 @@
             compiler_params=params(ATTENTION_VMEM),
             cost_estimate=cost(1.4e10, 2**20),
             name="attention_outer_products",
-        )(meta, query, peer, *pieces[t], key, value, peer, peer, *[array for carrier in carriers for array in carrier])
+        )(meta, query, peer[0], *pieces[t], key, value, *peer[1:], *[a for carrier in carriers for a in carrier])
 
     grams = []
     held = []
+    peer = [lax.ppermute(array, "seq", moved(0, 1)) for array in (query, key, value)]
     for t in range(blocks + 1):
         if t < blocks:
             kv = first_kv if t == 0 else per - 1 - first_kv
@@ -532,7 +528,7 @@
             if t < per:
                 columns += [(array, HEAD_SIZE, lambda target, meta: target * per + meta[2]) for array in (key, value)]
             scalars = jnp.stack([own, turns[t], kv])
-            after = [] if t == 0 else [peer]
+            after = [] if t == 0 else peer[1:2]
             parts = cut(
                 [target_at(*where) for where in far], columns, scalars, "cut_piece", after,
                 OTHER_VMEM if t else FULL_VMEM,
@@ -541,13 +537,9 @@
                 *parts, held[t - 2] = lax.optimization_barrier((*parts, held[t - 2]))
             pieces.append([lax.ppermute(part, "seq", moved(*where)) for part, where in zip(parts, far)])
         if t == 0:
-            columns = [(query, blocks * BLOCK_W, lambda target, meta: target)]
-            columns += [(array, per * HEAD_SIZE, lambda target, meta: target) for array in (key, value)]
-            peer = cut([target_at(0, 1)], columns, own[None], "cut_peer", parts, FULL_VMEM)[0]
-            peer = lax.ppermute(peer, "seq", moved(0, 1))
             continue
         done = t - 1
-        grams.append(grams_of(done, peer))
+        grams.append(grams_of(done))
         if done == 0 or not in_ring:
             held.append(grams[done])
         else:
@@ -598,20 +590,23 @@
 
         tops = shared(top)
         bottom = factor_bottom(rest)
-        bottoms = shared(bottom)
+        bottoms = lax.all_gather(bottom, "dp", axis=0, tiled=True)
         order = jnp.stack([lax.rem(place - d + ring, ring) for d in range(ring)])
     else:
         halves = [factor_top(*[lax.psum(part, "dp") for part in grams[t]]) for t in range(blocks)]
         tops = [top for top, _ in halves]
-        bottoms = [factor_bottom(rest) for _, rest in halves]
-        bottom = bottoms[0]
+        bottoms = jnp.concatenate([factor_bottom(rest) for _, rest in halves], axis=0)
+        bottom = bottoms[:bottom_rows]
         order = jnp.arange(blocks, dtype=jnp.int32)
 
 
-    def whiten(uppers, first, starts, result):
+    def whiten(uppers, first, starts, result, gathered=0):
         more = [] if result is None else [result]
         depth = BLOCK_W - starts[0]
         chunks = features // tile
+        triangles = [vmem] * len(uppers)
+        if gathered:
+            triangles = [pl.BlockSpec((bottom_rows, SPAN), lambda b, order: (order[first + b], 0))]
         weights = [
             pl.BlockSpec(
                 (tile, depth),
@@ -619,16 +614,16 @@
             )
             for c in range(chunks)
         ]
-        count = len(uppers) // len(starts)
+        count = gathered or len(uppers) // len(starts)
         return pl.pallas_call(
             functools.partial(
-                whiten_kernel, blocks=count, starts=starts, first=first, chunks=chunks, aliased=len(more)
+                whiten_kernel, blocks=count, given=len(uppers), starts=starts, first=first, chunks=chunks, aliased=len(more)
             ),
             out_shape=jax.ShapeDtypeStruct((blocks, BLOCK_W, features), F32),
             grid_spec=pltpu.PrefetchScalarGridSpec(
                 num_scalar_prefetch=1,
                 grid=(count,),
-                in_specs=[vmem] * len(uppers) + weights + [anywhere] * len(more),
+                in_specs=triangles + weights + [anywhere] * len(more),
                 out_specs=anywhere,
                 scratch_shapes=[
                     pltpu.VMEM((2 * half, depth), BF16),
@@ -642,9 +637,11 @@
             name="whiten_bottom" if starts[0] else "whiten_top",
         )(order, *uppers, *[out_weight] * chunks, *more)
 
-    result = whiten([tops[0], bottoms[0]], 0, (0, half), None)
-    result = whiten(tops[1:], 1, (0,), result)
-    return whiten(bottoms[1:], 1, (half,), result)
+    result = whiten([tops[0], bottom], 0, (0, half), None)
+    result = whiten(tops[1:2], 1, (0,), result)
+    if blocks > 2:
+        result = whiten(tops[2:], 2, (0,), result)
+    return whiten([bottoms], 1, (half,), result, blocks - 1)
 
 
 def solution(mesh):

time: 129 us -> 136 us (1.054)
  blocking collectives: 0 us -> 14.1 us
  waiting for transfers between devices: 20.3 us -> 14.1 us
  starting transfers between devices: 26 us -> 21.6 us
  local copies, waits for them, and re-layouts: 3.58 us -> 7.3 us
    all_gather x0 -> x1, blocking collectives: none -> 14.1 us  [shards(): bottoms = lax.all_gather(bottom, 'dp', axis=0, tiled=True)]
    ppermute x6 -> x3, starting transfers between devices: 9.19 us -> 3.88 us  [shared(): lax.ppermute(array, 'dp', [(z, (z + d) % ring) for z in range(ring)])]
    ppermute x8, waiting for transfers between devices: 13.5 us -> 10.1 us  [shards(): lax.ppermute(part, 'seq', moved(*where))]
    pallas_call x4, Pallas kernels: 32.9 us -> 35.8 us  [grams_of(): pl.pallas_call(functools.partial(attention_kernel, chips=chips, spans=spa...]
    ppermute x6, waiting for transfers between devices: 6.79 us -> 3.95 us  [shards(): lax.ppermute(part, 'dp', [(z, (z + 1) % ring) for z in range(ring)])]
    concatenate x4, local copies, waits for them, and re-layouts: 0.33 us -> 3 us  [grams_of(): jnp.concatenate([jnp.stack([own, turns[t], kv, which]), doc_lengths[0], s...]
    pallas_call x5 -> x4, Pallas kernels: 7.14 us -> 4.68 us  [cut(): pl.pallas_call(functools.partial(cut_kernel, targets=len(targets), given=...]
    pallas_call x3 -> x4, Pallas kernels: 18.7 us -> 19.1 us  [whiten(): pl.pallas_call(functools.partial(whiten_kernel, blocks=count, given=len(u...]
  transfers between devices with their start and end apart: 21 -> 20, of which waited for: 5 -> 5; matrix products, arithmetic and copies ran while one was open for 1% -> 3% of each run, Pallas kernels for 43% -> 41%
where the time goes in v6:
time: 136 us
  Pallas kernels  77.1 us (57%)
  starting transfers between devices  21.6 us (16%)
  waiting for transfers between devices  14.1 us (10%)
  blocking collectives  14.1 us (10%)
  local copies, waits for them, and re-layouts  7.3 us (5%)
    pallas_call x4, Pallas kernels, grams_of(): pl.pallas_call(functools.partial(attention_kernel, chips=chips, spans=spa...  35.8 us
    pallas_call x4, Pallas kernels, whiten(): pl.pallas_call(functools.partial(whiten_kernel, blocks=count, given=len(u...  19.1 us
    all_gather x1, blocking collectives, shards(): bottoms = lax.all_gather(bottom, 'dp', axis=0, tiled=True)  14.1 us
    ppermute x8, waiting for transfers between devices, shards(): lax.ppermute(part, 'seq', moved(*where))  10.1 us
    pallas_call x1, Pallas kernels, factor_top(): pl.pallas_call(functools.partial(factor_kernel, start=0, stop=half, recei...  9.32 us
    ppermute x8, starting transfers between devices, shards(): lax.ppermute(part, 'seq', moved(*where))  8.62 us
    pallas_call x1, Pallas kernels, factor_bottom(): pl.pallas_call(functools.partial(factor_kernel, start=half, stop=BLOCK_W,...  8.22 us
    ppermute x6, starting transfers between devices, shards(): lax.ppermute(part, 'dp', [(z, (z + 1) % ring) for z in range(ring)])  8.1 us
  transfers between devices with their start and end apart: 20, of which 5 were waited for; matrix products, arithmetic and copies ran while one was open for 3% of the time, Pallas kernels for 41%

profile of v6, /device:TPU:0, one launch (start us, length us, event | category | flops | bytes accessed | tf_op | source)
XLA Modules:
  0.0 135.6 jit_solution(311735151548044935)
XLA Ops:
  1.6 2.8 %cut_piece.6 = (bf16[256,768]{1,0:T(8,128)(2,1)}, bf16[256,768]{1,0:T(8,128)(2,1)}) custom-call(s32[3]{0:T(128)} %pad_add_fusion.1.meta, bf16[256,8192]{1,0:T(8,128)(2,1)} %bitcast.24, bf16[256,1024]{1,0:T(8,128)(2,1)} %bitcast.37, bf16[256,1024]{1,0:T(8,128)(2,1)} %bitcast.46, bf16[256,8192]{1,0:T(8,128)(2,1)} %bitcast.25, bf16[256,1024]{1,0:T(8,128)(2,1)} %bitcast.38, ...), custom_call_target="tpu_custom_call" | custom-call | bytes 2097152 | tf_op jit(solution)/shard_map/cut_piece/pallas_call | solution.py:458
  4.4 2.5 %collective-permute-start.5 = (bf16[256,768]{1,0:T(8,128)(2,1)}, bf16[256,768]{1,0:T(8,128)(2,1)S(1)}, u32[]{:S(2)}, u32[]{:S(2)}) collective-permute-start(bf16[256,768]{1,0:T(8,128)(2,1)} %get-tuple-element.31), channel_id=1, source_target_pairs={{0,2},{1,3},{2,0},{3,1},{4,6},{5,7},{6,4},{7,5},{8,10},{9,11},{10,... | collective-permute-start | bytes 1179656 | tf_op jit(solution)/shard_map/ppermute | solution.py:538
  7.8 0.8 concatenate.15.meta
  8.5 0.8 concatenate.13.meta
  10.3 2.2 %copy-done = bf16[1,256,8192]{2,1,0:T(8,128)(2,1)S(1)} copy-done((bf16[1,256,8192]{2,1,0:T(8,128)(2,1)S(1)}, bf16[1,256,8192]{2,1,0:T(8,128)(2,1)}, u32[]{:S(2)}) %copy-start) | copy-done | bytes 4194328
  12.5 1.0 copy-done.2
  13.5 1.0 copy-done.4
  15.2 1.8 %collective-permute-start.2 = (bf16[256,768]{1,0:T(8,128)(2,1)S(1)}, bf16[256,768]{1,0:T(8,128)(2,1)S(1)}, u32[]{:S(2)}, u32[]{:S(2)}) collective-permute-start(bf16[256,768]{1,0:T(8,128)(2,1)S(1)} %get-tuple-element.29), channel_id=1, source_target_pairs={{0,2},{1,3},{2,0},{3,1},{4,6},{5,7},{6,4},{7,5},{8,10},{9,11},{10,... | collective-permute-start | bytes 1179656 | tf_op jit(solution)/shard_map/ppermute | solution.py:538
  18.2 0.8 collective-permute-start.3
  19.0 6.1 %collective-permute-done.6.refs_9_.refs_3_ = bf16[256,768]{1,0:T(8,128)(2,1)S(1)} collective-permute-done((bf16[256,768]{1,0:T(8,128)(2,1)}, bf16[256,768]{1,0:T(8,128)(2,1)S(1)}, u32[]{:S(2)}, u32[]{:S(2)}) %collective-permute-start.6) | collective-permute-done | bytes 393248 | tf_op jit(solution)/shard_map/ppermute | solution.py:538
  25.1 8.8 %attention_outer_products.5 = (f32[520,128]{1,0:T(8,128)S(1)}, f32[520,128]{1,0:T(8,128)S(1)}) custom-call(s32[20]{0:T(128)S(1)} %concatenate.14.meta, bf16[256,8192]{1,0:T(8,128)(2,1)S(1)} %bitcast.32, bf16[256,8192]{1,0:T(8,128)(2,1)} %collective-permute-done.refs_1_, bf16[256,768]{1,0:T(8,128)(2,1)S(1)} %collective-permute-done.5.refs_8_.refs_2_, ...), custom_call_target="tpu_custom_call" | custom-call | flops 14000000000 | bytes 1048576 | tf_op jit(solution)/shard_map/attention_outer_products/pallas_call | solution.py:488
  34.0 1.7 %collective-permute-start.8 = (f32[520,128]{1,0:T(8,128)S(1)}, f32[520,128]{1,0:T(8,128)S(1)}, u32[]{:S(2)}, u32[]{:S(2)}) collective-permute-start(f32[520,128]{1,0:T(8,128)S(1)} %get-tuple-element.36), channel_id=1, source_target_pairs={{0,4},{4,8},{8,12},{12,0},{1,5},{5,9},{9,13},{13,1},{2,6},{6,10},{... | collective-permute-start | bytes 798728 | tf_op jit(solution)/shard_map/ppermute | solution.py:548
  35.7 1.2 collective-permute-start.7
  36.9 1.5 %collective-permute-start.11 = (bf16[256,512]{1,0:T(8,128)(2,1)S(1)}, bf16[256,512]{1,0:T(8,128)(2,1)S(1)}, u32[]{:S(2)}, u32[]{:S(2)}) collective-permute-start(bf16[256,512]{1,0:T(8,128)(2,1)S(1)} %get-tuple-element.43), channel_id=1, source_target_pairs={{0,2},{1,3},{2,0},{3,1},{4,6},{5,7},{6,4},{7,5},{8,10},{9,11},{10,... | collective-permute-start | bytes 786440 | tf_op jit(solution)/shard_map/ppermute | solution.py:538
  38.4 3.6 %collective-permute-done.3.refs_3_.refs_11_ = bf16[256,768]{1,0:T(8,128)(2,1)S(1)} collective-permute-done((bf16[256,768]{1,0:T(8,128)(2,1)S(1)}, bf16[256,768]{1,0:T(8,128)(2,1)S(1)}, u32[]{:S(2)}, u32[]{:S(2)}) %collective-permute-start.3) | collective-permute-done | bytes 393248 | tf_op jit(solution)/shard_map/ppermute | solution.py:538
  42.0 9.0 %attention_outer_products.4 = (f32[520,128]{1,0:T(8,128)S(1)}, f32[520,128]{1,0:T(8,128)S(1)}) custom-call(s32[20]{0:T(128)S(1)} %concatenate.13.meta, bf16[256,8192]{1,0:T(8,128)(2,1)S(1)} %bitcast.33, bf16[256,8192]{1,0:T(8,128)(2,1)} %collective-permute-done.refs_1_, bf16[256,768]{1,0:T(8,128)(2,1)S(1)} %collective-permute-done.2.refs_2_.refs_10_, ...), custom_call_target="tpu_custom_call" | custom-call | flops 14000000000 | bytes 1048576 | tf_op jit(solution)/shard_map/attention_outer_products/pallas_call | solution.py:488
  51.1 1.7 %collective-permute-start.15 = (f32[520,128]{1,0:T(8,128)S(1)}, f32[520,128]{1,0:T(8,128)S(1)}, u32[]{:S(2)}, u32[]{:S(2)}) collective-permute-start(f32[520,128]{1,0:T(8,128)S(1)} %add.58), channel_id=1, source_target_pairs={{0,4},{4,8},{8,12},{12,0},{1,5},{5,9},{9,13},{13,1},{2,6},{6,10},{... | collective-permute-start | bytes 798728 | tf_op jit(solution)/shard_map/ppermute | solution.py:548
  52.8 1.3 collective-permute-start.13
  54.0 1.4 %collective-permute-start.10 = (bf16[256,512]{1,0:T(8,128)(2,1)S(1)}, bf16[256,512]{1,0:T(8,128)(2,1)S(1)}, u32[]{:S(2)}, u32[]{:S(2)}) collective-permute-start(bf16[256,512]{1,0:T(8,128)(2,1)S(1)} %get-tuple-element.38), channel_id=1, source_target_pairs={{0,3},{1,2},{2,1},{3,0},{4,7},{5,6},{6,5},{7,4},{8,11},{9,10},{10,... | collective-permute-start | bytes 786440 | tf_op jit(solution)/shard_map/ppermute | solution.py:538
  56.0 8.9 %attention_outer_products.7 = (f32[520,128]{1,0:T(8,128)S(1)}, f32[520,128]{1,0:T(8,128)S(1)}) custom-call(s32[20]{0:T(128)S(1)} %concatenate.15.meta, bf16[256,8192]{1,0:T(8,128)(2,1)S(1)} %bitcast.34, bf16[256,8192]{1,0:T(8,128)(2,1)} %collective-permute-done.refs_1_, bf16[256,512]{1,0:T(8,128)(2,1)S(1)} %collective-permute-done.11.refs_2_, ...), custom_call_target="tpu_custom_call" | custom-call | flops 14000000000 | bytes 1048576 | tf_op jit(solution)/shard_map/attention_outer_products/pallas_call | solution.py:488
  64.9 2.2 %collective-permute-start.16 = (f32[520,128]{1,0:T(8,128)S(1)}, f32[520,128]{1,0:T(8,128)S(1)}, u32[]{:S(2)}, u32[]{:S(2)}) collective-permute-start(f32[520,128]{1,0:T(8,128)S(1)} %add.60), channel_id=1, source_target_pairs={{0,4},{4,8},{8,12},{12,0},{1,5},{5,9},{9,13},{13,1},{2,6},{6,10},{... | collective-permute-start | bytes 798728 | tf_op jit(solution)/shard_map/ppermute | solution.py:548
  68.3 9.1 %attention_outer_products.6 = (f32[520,128]{1,0:T(8,128)S(1)}, f32[520,128]{1,0:T(8,128)S(1)}) custom-call(s32[20]{0:T(128)S(1)} %concatenate.12.meta, bf16[256,8192]{1,0:T(8,128)(2,1)S(1)} %bitcast.35, bf16[256,8192]{1,0:T(8,128)(2,1)} %collective-permute-done.refs_1_, bf16[256,512]{1,0:T(8,128)(2,1)S(1)} %collective-permute-done.9.refs_2_, ...), custom_call_target="tpu_custom_call" | custom-call | flops 14000000000 | bytes 1048576 | tf_op jit(solution)/shard_map/attention_outer_products/pallas_call | solution.py:488
  77.3 3.3 %collective-permute-done.14.refs_2_ = f32[520,128]{1,0:T(8,128)S(1)} collective-permute-done((f32[520,128]{1,0:T(8,128)S(1)}, f32[520,128]{1,0:T(8,128)S(1)}, u32[]{:S(2)}, u32[]{:S(2)}) %collective-permute-start.14) | collective-permute-done | bytes 266272 | tf_op jit(solution)/shard_map/ppermute | solution.py:548
  80.7 9.3 %factor_top.1 = (bf16[784,128]{1,0:T(8,128)(2,1)S(1)}, f32[256,256]{1,0:T(8,128)S(1)}) custom-call(f32[520,128]{1,0:T(8,128)S(1)} %get-tuple-element.39.refs_0_, f32[520,128]{1,0:T(8,128)S(1)} %get-tuple-element.40.refs_1_, f32[520,128]{1,0:T(8,128)S(1)} %collective-permute-done.14.refs_2_, f32[520,128]{1,0:T(8,128)S(1)} %collective-permute-done.16.refs_3_), custom_call_target="tpu_custom_call" | custom-call | flops 10000000000 | bytes 1048576 | tf_op jit(solution)/shard_map/factor_top/pallas_call | solution.py:557
  90.4 1.2 collective-permute-start.17
  91.7 2.2 %collective-permute-start.18 = (bf16[784,128]{1,0:T(8,128)(2,1)S(1)}, bf16[784,128]{1,0:T(8,128)(2,1)S(1)}, u32[]{:S(2)}, u32[]{:S(2)}) collective-permute-start(bf16[784,128]{1,0:T(8,128)(2,1)S(1)} %get-tuple-element.48.refs_0_), channel_id=1, source_target_pairs={{0,12},{4,0},{8,4},{12,8},{1,13},{5,1},{9,5},{13,9},{2,14},{6,2},{... | collective-permute-start | bytes 602120 | tf_op jit(solution)/shard_map/ppermute | solution.py:588
  93.9 8.2 %factor_bottom.1.refs_1_ = bf16[272,128]{1,0:T(8,128)(2,1)S(1)} custom-call(f32[256,256]{1,0:T(8,128)S(1)} %get-tuple-element.47.refs_0_), custom_call_target="tpu_custom_call" | custom-call | flops 8999999488 | bytes 1048576 | tf_op jit(solution)/shard_map/factor_bottom/pallas_call | solution.py:572
  102.1 3.5 %whiten_top.3.refs_5_ = f32[4,512,2048]{2,1,0:T(8,128)} custom-call(s32[4]{0:T(128)S(1)} %pad_add_fusion.order, bf16[784,128]{1,0:T(8,128)(2,1)S(1)} %get-tuple-element.48.refs_0_, bf16[272,128]{1,0:T(8,128)(2,1)S(1)} %factor_bottom.1.refs_1_, bf16[2048,2048]{1,0:T(8,128)(2,1)S(1)} %bitcast.22, bf16[2048,2048]{1,0:T(8,128)(2,1)S(1)} %bitcast.22, ...), custom_call_target="tpu_custom_call" | custom-call | flops 4000000000 | bytes 1048576 | tf_op jit(solution)/shard_map/whiten_top/pallas_call | solution.py:618
  105.6 14.1 %all_gather.3.refs_0_ = bf16[1088,128]{1,0:T(8,128)(2,1)S(1)} all-gather(bf16[272,128]{1,0:T(8,128)(2,1)S(1)} %factor_bottom.1.refs_1_), channel_id=1, replica_groups=mesh['groups'=2,'dp'=4,'seq'=4] {'dp'}, dimensions={0}, use_global_device_ids=true | all-gather | bytes 348160 | tf_op jit(solution)/shard_map/all_gather | solution.py:593
  119.7 2.8 %whiten_top.4.refs_6_ = f32[4,512,2048]{2,1,0:T(8,128)} custom-call(s32[4]{0:T(128)S(1)} %pad_add_fusion.order, bf16[784,128]{1,0:T(8,128)(2,1)S(1)} %collective-permute-done.19.refs_0_, bf16[2048,2048]{1,0:T(8,128)(2,1)S(1)} %bitcast.22, bf16[2048,2048]{1,0:T(8,128)(2,1)S(1)} %bitcast.22, ...), custom_call_target="tpu_custom_call", output_to_operand_aliasing={{}: (6, {})} | custom-call | flops 2000000000 | bytes 1048576 | tf_op jit(solution)/shard_map/whiten_top/pallas_call | solution.py:618
  122.6 6.3 %whiten_top.5.refs_5_ = f32[4,512,2048]{2,1,0:T(8,128)} custom-call(s32[4]{0:T(128)S(1)} %pad_add_fusion.order, bf16[784,128]{1,0:T(8,128)(2,1)S(1)} %collective-permute-done.17.refs_0_, bf16[784,128]{1,0:T(8,128)(2,1)S(1)} %collective-permute-done.18.refs_1_, bf16[2048,2048]{1,0:T(8,128)(2,1)S(1)} %bitcast.22, ...), custom_call_target="tpu_custom_call", output_to_operand_aliasing={{}: (7, {})} | custom-call | flops 4000000000 | bytes 1048576 | tf_op jit(solution)/shard_map/whiten_top/pallas_call | solution.py:618
  128.8 6.5 %whiten_bottom.1 = f32[4,512,2048]{2,1,0:T(8,128)} custom-call(s32[4]{0:T(128)S(1)} %pad_add_fusion.order, bf16[1088,128]{1,0:T(8,128)(2,1)S(1)} %all_gather.3.refs_0_, bf16[2048,2048]{1,0:T(8,128)(2,1)S(1)} %bitcast.22, bf16[2048,2048]{1,0:T(8,128)(2,1)S(1)} %bitcast.22, bf16[2048,2048]{1,0:T(8,128)(2,1)S(1)} %bitcast.22, ...), custom_call_target="tpu_custom_call", output_to_operand_aliasing={{}: (6, {})} | custom-call | flops 2000000000 | bytes 1048576 | tf_op jit(solution)/shard_map/whiten_bottom/pallas_call | solution.py:618
  (52 shorter events, 7.6 us)
Async XLA Ops:
  0.0 25.1 %collective-permute-start = (bf16[256,8192]{1,0:T(8,128)(2,1)}, bf16[256,8192]{1,0:T(8,128)(2,1)}, u32[]{:S(2)}, u32[]{:S(2)}) collective-permute-start(bf16[256,8192]{1,0:T(8,128)(2,1)} %bitcast.23), channel_id=1, source_target_pairs={{0,1},{1,0},{2,3},{3,2},{4,5},{5,4},{6,7},{7,6},{8,9},{9,8},{10,11... | collective-permute-start | bytes 12582920 | tf_op jit(solution)/shard_map/ppermute | solution.py:523
  0.5 9.8 %collective-permute-start.1 = (bf16[256,1024]{1,0:T(8,128)(2,1)}, bf16[256,1024]{1,0:T(8,128)(2,1)}, u32[]{:S(2)}, u32[]{:S(2)}) collective-permute-start(bf16[256,1024]{1,0:T(8,128)(2,1)} %bitcast.36), channel_id=1, source_target_pairs={{0,1},{1,0},{2,3},{3,2},{4,5},{5,4},{6,7},{7,6},{8,9},{9,8},{10,11... | collective-permute-start | bytes 1572872 | tf_op jit(solution)/shard_map/ppermute | solution.py:523
  0.5 24.6 %collective-permute-start.4 = (bf16[256,1024]{1,0:T(8,128)(2,1)}, bf16[256,1024]{1,0:T(8,128)(2,1)}, u32[]{:S(2)}, u32[]{:S(2)}) collective-permute-start(bf16[256,1024]{1,0:T(8,128)(2,1)} %bitcast.45), channel_id=1, source_target_pairs={{0,1},{1,0},{2,3},{3,2},{4,5},{5,4},{6,7},{7,6},{8,9},{9,8},{10,11... | collective-permute-start | bytes 1572872 | tf_op jit(solution)/shard_map/ppermute | solution.py:523
  1.6 23.5 %copy-start.3 = (bf16[1,256,1024]{2,1,0:T(8,128)(2,1)S(1)}, bf16[1,256,1024]{2,1,0:T(8,128)(2,1)}, u32[]{:S(2)}) copy-start(bf16[1,256,1024]{2,1,0:T(8,128)(2,1)} %param.7) | copy-start | bytes 1572868
  4.4 13.8 %collective-permute-start.5 = (bf16[256,768]{1,0:T(8,128)(2,1)}, bf16[256,768]{1,0:T(8,128)(2,1)S(1)}, u32[]{:S(2)}, u32[]{:S(2)}) collective-permute-start(bf16[256,768]{1,0:T(8,128)(2,1)} %get-tuple-element.31), channel_id=1, source_target_pairs={{0,2},{1,3},{2,0},{3,1},{4,6},{5,7},{6,4},{7,5},{8,10},{9,11},{10,... | collective-permute-start | bytes 1179656 | tf_op jit(solution)/shard_map/ppermute | solution.py:538
  6.9 18.2 %collective-permute-start.6 = (bf16[256,768]{1,0:T(8,128)(2,1)}, bf16[256,768]{1,0:T(8,128)(2,1)S(1)}, u32[]{:S(2)}, u32[]{:S(2)}) collective-permute-start(bf16[256,768]{1,0:T(8,128)(2,1)} %get-tuple-element.32), channel_id=1, source_target_pairs={{0,3},{1,2},{2,1},{3,0},{4,7},{5,6},{6,5},{7,4},{8,11},{9,10},{10,... | collective-permute-start | bytes 1179656 | tf_op jit(solution)/shard_map/ppermute | solution.py:538
  10.3 2.2 %copy-start = (bf16[1,256,8192]{2,1,0:T(8,128)(2,1)S(1)}, bf16[1,256,8192]{2,1,0:T(8,128)(2,1)}, u32[]{:S(2)}) copy-start(bf16[1,256,8192]{2,1,0:T(8,128)(2,1)} %param.6) | copy-start | bytes 12582916
  12.5 1.0 copy-start.2
  13.5 1.0 copy-start.4
  14.5 3.1 %copy-start.1 = (bf16[1,256,8192]{2,1,0:T(8,128)(2,1)S(1)}, bf16[1,256,8192]{2,1,0:T(8,128)(2,1)}, u32[]{:S(2)}) copy-start(bf16[1,256,8192]{2,1,0:T(8,128)(2,1)} %param.6) | copy-start | bytes 12582916
  14.5 10.6 %copy-start.5 = (bf16[1,256,1024]{2,1,0:T(8,128)(2,1)S(1)}, bf16[1,256,1024]{2,1,0:T(8,128)(2,1)}, u32[]{:S(2)}) copy-start(bf16[1,256,1024]{2,1,0:T(8,128)(2,1)} %param.8) | copy-start | bytes 1572868
  15.2 23.1 %collective-permute-start.2 = (bf16[256,768]{1,0:T(8,128)(2,1)S(1)}, bf16[256,768]{1,0:T(8,128)(2,1)S(1)}, u32[]{:S(2)}, u32[]{:S(2)}) collective-permute-start(bf16[256,768]{1,0:T(8,128)(2,1)S(1)} %get-tuple-element.29), channel_id=1, source_target_pairs={{0,2},{1,3},{2,0},{3,1},{4,6},{5,7},{6,4},{7,5},{8,10},{9,11},{10,... | collective-permute-start | bytes 1179656 | tf_op jit(solution)/shard_map/ppermute | solution.py:538
  18.2 23.7 %collective-permute-start.3 = (bf16[256,768]{1,0:T(8,128)(2,1)S(1)}, bf16[256,768]{1,0:T(8,128)(2,1)S(1)}, u32[]{:S(2)}, u32[]{:S(2)}) collective-permute-start(bf16[256,768]{1,0:T(8,128)(2,1)S(1)} %get-tuple-element.30), channel_id=1, source_target_pairs={{0,3},{1,2},{2,1},{3,0},{4,7},{5,6},{6,5},{7,4},{8,11},{9,10},{10,... | collective-permute-start | bytes 1179656 | tf_op jit(solution)/shard_map/ppermute | solution.py:538
  34.0 17.0 %collective-permute-start.8 = (f32[520,128]{1,0:T(8,128)S(1)}, f32[520,128]{1,0:T(8,128)S(1)}, u32[]{:S(2)}, u32[]{:S(2)}) collective-permute-start(f32[520,128]{1,0:T(8,128)S(1)} %get-tuple-element.36), channel_id=1, source_target_pairs={{0,4},{4,8},{8,12},{12,0},{1,5},{5,9},{9,13},{13,1},{2,6},{6,10},{... | collective-permute-start | bytes 798728 | tf_op jit(solution)/shard_map/ppermute | solution.py:548
  35.7 17.1 %collective-permute-start.7 = (f32[520,128]{1,0:T(8,128)S(1)}, f32[520,128]{1,0:T(8,128)S(1)}, u32[]{:S(2)}, u32[]{:S(2)}) collective-permute-start(f32[520,128]{1,0:T(8,128)S(1)} %get-tuple-element.34), channel_id=1, source_target_pairs={{0,4},{4,8},{8,12},{12,0},{1,5},{5,9},{9,13},{13,1},{2,6},{6,10},{... | collective-permute-start | bytes 798728 | tf_op jit(solution)/shard_map/ppermute | solution.py:548
  36.9 18.6 %collective-permute-start.11 = (bf16[256,512]{1,0:T(8,128)(2,1)S(1)}, bf16[256,512]{1,0:T(8,128)(2,1)S(1)}, u32[]{:S(2)}, u32[]{:S(2)}) collective-permute-start(bf16[256,512]{1,0:T(8,128)(2,1)S(1)} %get-tuple-element.43), channel_id=1, source_target_pairs={{0,2},{1,3},{2,0},{3,1},{4,6},{5,7},{6,4},{7,5},{8,10},{9,11},{10,... | collective-permute-start | bytes 786440 | tf_op jit(solution)/shard_map/ppermute | solution.py:538
  38.4 17.6 %collective-permute-start.12 = (bf16[256,512]{1,0:T(8,128)(2,1)S(1)}, bf16[256,512]{1,0:T(8,128)(2,1)S(1)}, u32[]{:S(2)}, u32[]{:S(2)}) collective-permute-start(bf16[256,512]{1,0:T(8,128)(2,1)S(1)} %get-tuple-element.44), channel_id=1, source_target_pairs={{0,3},{1,2},{2,1},{3,0},{4,7},{5,6},{6,5},{7,4},{8,11},{9,10},{10,... | collective-permute-start | bytes 786440 | tf_op jit(solution)/shard_map/ppermute | solution.py:538
  51.1 13.8 %collective-permute-start.15 = (f32[520,128]{1,0:T(8,128)S(1)}, f32[520,128]{1,0:T(8,128)S(1)}, u32[]{:S(2)}, u32[]{:S(2)}) collective-permute-start(f32[520,128]{1,0:T(8,128)S(1)} %add.58), channel_id=1, source_target_pairs={{0,4},{4,8},{8,12},{12,0},{1,5},{5,9},{9,13},{13,1},{2,6},{6,10},{... | collective-permute-start | bytes 798728 | tf_op jit(solution)/shard_map/ppermute | solution.py:548
  52.8 15.0 %collective-permute-start.13 = (f32[520,128]{1,0:T(8,128)S(1)}, f32[520,128]{1,0:T(8,128)S(1)}, u32[]{:S(2)}, u32[]{:S(2)}) collective-permute-start(f32[520,128]{1,0:T(8,128)S(1)} %add.57), channel_id=1, source_target_pairs={{0,4},{4,8},{8,12},{12,0},{1,5},{5,9},{9,13},{13,1},{2,6},{6,10},{... | collective-permute-start | bytes 798728 | tf_op jit(solution)/shard_map/ppermute | solution.py:548
  54.0 13.8 %collective-permute-start.10 = (bf16[256,512]{1,0:T(8,128)(2,1)S(1)}, bf16[256,512]{1,0:T(8,128)(2,1)S(1)}, u32[]{:S(2)}, u32[]{:S(2)}) collective-permute-start(bf16[256,512]{1,0:T(8,128)(2,1)S(1)} %get-tuple-element.38), channel_id=1, source_target_pairs={{0,3},{1,2},{2,1},{3,0},{4,7},{5,6},{6,5},{7,4},{8,11},{9,10},{10,... | collective-permute-start | bytes 786440 | tf_op jit(solution)/shard_map/ppermute | solution.py:538
  55.5 12.8 %collective-permute-start.9 = (bf16[256,512]{1,0:T(8,128)(2,1)S(1)}, bf16[256,512]{1,0:T(8,128)(2,1)S(1)}, u32[]{:S(2)}, u32[]{:S(2)}) collective-permute-start(bf16[256,512]{1,0:T(8,128)(2,1)S(1)} %get-tuple-element.37), channel_id=1, source_target_pairs={{0,2},{1,3},{2,0},{3,1},{4,6},{5,7},{6,4},{7,5},{8,10},{9,11},{10,... | collective-permute-start | bytes 786440 | tf_op jit(solution)/shard_map/ppermute | solution.py:538
  64.9 12.4 %collective-permute-start.16 = (f32[520,128]{1,0:T(8,128)S(1)}, f32[520,128]{1,0:T(8,128)S(1)}, u32[]{:S(2)}, u32[]{:S(2)}) collective-permute-start(f32[520,128]{1,0:T(8,128)S(1)} %add.60), channel_id=1, source_target_pairs={{0,4},{4,8},{8,12},{12,0},{1,5},{5,9},{9,13},{13,1},{2,6},{6,10},{... | collective-permute-start | bytes 798728 | tf_op jit(solution)/shard_map/ppermute | solution.py:548
  67.8 12.9 %collective-permute-start.14 = (f32[520,128]{1,0:T(8,128)S(1)}, f32[520,128]{1,0:T(8,128)S(1)}, u32[]{:S(2)}, u32[]{:S(2)}) collective-permute-start(f32[520,128]{1,0:T(8,128)S(1)} %add.59), channel_id=1, source_target_pairs={{0,4},{4,8},{8,12},{12,0},{1,5},{5,9},{9,13},{13,1},{2,6},{6,10},{... | collective-permute-start | bytes 798728 | tf_op jit(solution)/shard_map/ppermute | solution.py:548
  90.0 12.1 %slice-start = ((s8[8388608]{0:T(1024)(128)(4,1)}), s8[4194304]{0:T(1024)(128)(4,1)S(1)}, s32[]{:S(2)}) async-start(s8[8388608]{0:T(1024)(128)(4,1)} %bitcast.21), calls=%async_computation | async-start | bytes 8388608
  90.0 29.7 %collective-permute-start.19 = (bf16[784,128]{1,0:T(8,128)(2,1)S(1)}, bf16[784,128]{1,0:T(8,128)(2,1)S(1)}, u32[]{:S(2)}, u32[]{:S(2)}) collective-permute-start(bf16[784,128]{1,0:T(8,128)(2,1)S(1)} %get-tuple-element.48.refs_0_), channel_id=1, source_target_pairs={{0,4},{4,8},{8,12},{12,0},{1,5},{5,9},{9,13},{13,1},{2,6},{6,10},{... | collective-permute-start | bytes 602120 | tf_op jit(solution)/shard_map/ppermute | solution.py:588
  90.4 32.1 %collective-permute-start.17 = (bf16[784,128]{1,0:T(8,128)(2,1)S(1)}, bf16[784,128]{1,0:T(8,128)(2,1)S(1)}, u32[]{:S(2)}, u32[]{:S(2)}) collective-permute-start(bf16[784,128]{1,0:T(8,128)(2,1)S(1)} %get-tuple-element.48.refs_0_), channel_id=1, source_target_pairs={{0,8},{4,12},{8,0},{12,4},{1,9},{5,13},{9,1},{13,5},{2,10},{6,14},... | collective-permute-start | bytes 602120 | tf_op jit(solution)/shard_map/ppermute | solution.py:588
  91.7 30.9 %collective-permute-start.18 = (bf16[784,128]{1,0:T(8,128)(2,1)S(1)}, bf16[784,128]{1,0:T(8,128)(2,1)S(1)}, u32[]{:S(2)}, u32[]{:S(2)}) collective-permute-start(bf16[784,128]{1,0:T(8,128)(2,1)S(1)} %get-tuple-element.48.refs_0_), channel_id=1, source_target_pairs={{0,12},{4,0},{8,4},{12,8},{1,13},{5,1},{9,5},{13,9},{2,14},{6,2},{... | collective-permute-start | bytes 602120 | tf_op jit(solution)/shard_map/ppermute | solution.py:588
  93.9 8.2 %slice-start.1 = ((s8[8388608]{0:T(1024)(128)(4,1)}), s8[4194304]{0:T(1024)(128)(4,1)S(1)}, s32[]{:S(2)}) async-start(s8[8388608]{0:T(1024)(128)(4,1)} %bitcast.21), calls=%async_computation.1 | async-start | bytes 8388608

commit v7 on v5

--- a/solution.py
+++ b/solution.py
@@ -479,7 +479,7 @@
 
     most = all_spans // 2 + 1
 
-    def grams_of(t, peer):
+    def grams_of(t):
         kv = turns[t] // KV_BLOCKS
         carriers = pieces[: min(t + 1, per)]
         which = jnp.where(kv == first_kv, 0, 1).astype(jnp.int32)
@@ -521,10 +521,14 @@
             compiler_params=params(ATTENTION_VMEM),
             cost_estimate=cost(1.4e10, 2**20),
             name="attention_outer_products",
-        )(meta, query, peer, *pieces[t], key, value, peer, peer, *[array for carrier in carriers for array in carrier])
+        )(meta, query, peer, *pieces[t], key, value, peer, peer, *[a for carrier in carriers for a in carrier])
 
     grams = []
     held = []
+    swapped = [lax.ppermute(array, "seq", moved(0, 1)) for array in (query, key, value)]
+    widths = (blocks * BLOCK_W, per * HEAD_SIZE, per * HEAD_SIZE)
+    columns = [(array, width, lambda target, meta: target) for array, width in zip(swapped, widths)]
+    peer = cut([lambda meta: meta[0]], columns, own[None], "cut_peer")[0]
     for t in range(blocks + 1):
         if t < blocks:
             kv = first_kv if t == 0 else per - 1 - first_kv
@@ -532,7 +536,7 @@
             if t < per:
                 columns += [(array, HEAD_SIZE, lambda target, meta: target * per + meta[2]) for array in (key, value)]
             scalars = jnp.stack([own, turns[t], kv])
-            after = [] if t == 0 else [peer]
+            after = [] if t == 0 else swapped[1:2]
             parts = cut(
                 [target_at(*where) for where in far], columns, scalars, "cut_piece", after,
                 OTHER_VMEM if t else FULL_VMEM,
@@ -541,13 +545,9 @@
                 *parts, held[t - 2] = lax.optimization_barrier((*parts, held[t - 2]))
             pieces.append([lax.ppermute(part, "seq", moved(*where)) for part, where in zip(parts, far)])
         if t == 0:
-            columns = [(query, blocks * BLOCK_W, lambda target, meta: target)]
-            columns += [(array, per * HEAD_SIZE, lambda target, meta: target) for array in (key, value)]
-            peer = cut([target_at(0, 1)], columns, own[None], "cut_peer", parts, FULL_VMEM)[0]
-            peer = lax.ppermute(peer, "seq", moved(0, 1))
             continue
         done = t - 1
-        grams.append(grams_of(done, peer))
+        grams.append(grams_of(done))
         if done == 0 or not in_ring:
             held.append(grams[done])
         else:
@@ -604,7 +604,6 @@
         halves = [factor_top(*[lax.psum(part, "dp") for part in grams[t]]) for t in range(blocks)]
         tops = [top for top, _ in halves]
         bottoms = [factor_bottom(rest) for _, rest in halves]
-        bottom = bottoms[0]
         order = jnp.arange(blocks, dtype=jnp.int32)
 
 
@@ -643,7 +642,9 @@
         )(order, *uppers, *[out_weight] * chunks, *more)
 
     result = whiten([tops[0], bottoms[0]], 0, (0, half), None)
-    result = whiten(tops[1:], 1, (0,), result)
+    result = whiten(tops[1:2], 1, (0,), result)
+    if blocks > 2:
+        result = whiten(tops[2:], 2, (0,), result)
     return whiten(bottoms[1:], 1, (half,), result)
 
 

time: 129 us -> 126 us (0.977)
  waiting for transfers between devices: 20.3 us -> 14 us
  local copies, waits for them, and re-layouts: 3.58 us -> 7.3 us
  Pallas kernels: 76.3 us -> 74.5 us
  starting transfers between devices: 26 us -> 27.7 us
    ppermute x8, waiting for transfers between devices: 13.5 us -> 9.45 us  [shards(): lax.ppermute(part, 'seq', moved(*where))]
    concatenate x4, local copies, waits for them, and re-layouts: 0.33 us -> 3 us  [grams_of(): jnp.concatenate([jnp.stack([own, turns[t], kv, which]), doc_lengths[0], s...]
    ppermute x6, waiting for transfers between devices: 6.79 us -> 4.51 us  [shards(): lax.ppermute(part, 'dp', [(z, (z + 1) % ring) for z in range(ring)])]
    pallas_call x3 -> x4, Pallas kernels: 18.7 us -> 19.1 us  [whiten(): pl.pallas_call(functools.partial(whiten_kernel, blocks=count, starts=star...]
  transfers between devices with their start and end apart: 21 -> 23, of which waited for: 5 -> 5; matrix products, arithmetic and copies ran while one was open for 1% -> 3% of each run, Pallas kernels for 43% -> 47%
where the time goes in v7:
time: 126 us; the launch traced here: 125 us
  Pallas kernels  74.5 us (59%)
  starting transfers between devices  27.7 us (22%)
  waiting for transfers between devices  14 us (11%)
  local copies, waits for them, and re-layouts  7.3 us (6%)
    pallas_call x4, Pallas kernels, grams_of(): pl.pallas_call(functools.partial(attention_kernel, chips=chips, spans=spa...  32 us
    pallas_call x4, Pallas kernels, whiten(): pl.pallas_call(functools.partial(whiten_kernel, blocks=count, starts=star...  19.1 us
    ppermute x8, waiting for transfers between devices, shards(): lax.ppermute(part, 'seq', moved(*where))  9.45 us
    pallas_call x1, Pallas kernels, factor_top(): pl.pallas_call(functools.partial(factor_kernel, start=0, stop=half, recei...  9.33 us
    ppermute x6, starting transfers between devices, shared(): lax.ppermute(array, 'dp', [(z, (z + d) % ring) for z in range(ring)])  9.19 us
    ppermute x6, starting transfers between devices, shards(): lax.ppermute(part, 'dp', [(z, (z + 1) % ring) for z in range(ring)])  8.93 us
    ppermute x8, starting transfers between devices, shards(): lax.ppermute(part, 'seq', moved(*where))  8.6 us
    pallas_call x1, Pallas kernels, factor_bottom(): pl.pallas_call(functools.partial(factor_kernel, start=half, stop=BLOCK_W,...  8.22 us
  transfers between devices with their start and end apart: 23, of which 5 were waited for; matrix products, arithmetic and copies ran while one was open for 3% of the time, Pallas kernels for 47%

profile of v7, /device:TPU:0, one launch (start us, length us, event | category | flops | bytes accessed | tf_op | source)
XLA Modules:
  0.0 124.9 jit_solution(17113005285432676229)
XLA Ops:
  1.6 2.7 %cut_piece.6 = (bf16[256,768]{1,0:T(8,128)(2,1)}, bf16[256,768]{1,0:T(8,128)(2,1)}) custom-call(s32[3]{0:T(128)} %pad_add_fusion.1.meta, bf16[256,8192]{1,0:T(8,128)(2,1)} %bitcast.24, bf16[256,1024]{1,0:T(8,128)(2,1)} %bitcast.37, bf16[256,1024]{1,0:T(8,128)(2,1)} %bitcast.46, bf16[256,8192]{1,0:T(8,128)(2,1)} %bitcast.25, bf16[256,1024]{1,0:T(8,128)(2,1)} %bitcast.38, ...), custom_call_target="tpu_custom_call" | custom-call | bytes 2097152 | tf_op jit(solution)/shard_map/cut_piece/pallas_call | solution.py:458
  4.3 2.5 %collective-permute-start.5 = (bf16[256,768]{1,0:T(8,128)(2,1)}, bf16[256,768]{1,0:T(8,128)(2,1)S(1)}, u32[]{:S(2)}, u32[]{:S(2)}) collective-permute-start(bf16[256,768]{1,0:T(8,128)(2,1)} %get-tuple-element.31), channel_id=1, source_target_pairs={{0,2},{1,3},{2,0},{3,1},{4,6},{5,7},{6,4},{7,5},{8,10},{9,11},{10,... | collective-permute-start | bytes 1179656 | tf_op jit(solution)/shard_map/ppermute | solution.py:546
  10.2 2.2 %copy-done = bf16[1,256,8192]{2,1,0:T(8,128)(2,1)S(1)} copy-done((bf16[1,256,8192]{2,1,0:T(8,128)(2,1)S(1)}, bf16[1,256,8192]{2,1,0:T(8,128)(2,1)}, u32[]{:S(2)}) %copy-start) | copy-done | bytes 4194328
  12.4 1.0 copy-done.2
  13.4 1.0 copy-done.4
  15.2 1.8 %collective-permute-start.3 = (bf16[256,768]{1,0:T(8,128)(2,1)S(1)}, bf16[256,768]{1,0:T(8,128)(2,1)S(1)}, u32[]{:S(2)}, u32[]{:S(2)}) collective-permute-start(bf16[256,768]{1,0:T(8,128)(2,1)S(1)} %get-tuple-element.29), channel_id=1, source_target_pairs={{0,2},{1,3},{2,0},{3,1},{4,6},{5,7},{6,4},{7,5},{8,10},{9,11},{10,... | collective-permute-start | bytes 1179656 | tf_op jit(solution)/shard_map/ppermute | solution.py:546
  18.9 1.3 %cut_peer.1.refs_1_.refs_6_.refs_7_ = bf16[256,2560]{1,0:T(8,128)(2,1)S(1)} custom-call(s32[1]{0:T(128)} %bitcast.4.meta, bf16[256,8192]{1,0:T(8,128)(2,1)} %collective-permute-done.refs_0_, bf16[256,1024]{1,0:T(8,128)(2,1)S(1)} %collective-permute-done.1.refs_1_.refs_2_.refs_6_, bf16[256,1024]{1,0:T(8,128)(2,1)} %collective-permute-done.2.refs_2_), custom_call_target="tpu_custom_call" | custom-call | bytes 2097152 | tf_op jit(solution)/shard_map/cut_peer/pallas_call | solution.py:458
  20.3 4.8 %collective-permute-done.6.refs_9_.refs_3_ = bf16[256,768]{1,0:T(8,128)(2,1)S(1)} collective-permute-done((bf16[256,768]{1,0:T(8,128)(2,1)}, bf16[256,768]{1,0:T(8,128)(2,1)S(1)}, u32[]{:S(2)}, u32[]{:S(2)}) %collective-permute-start.6) | collective-permute-done | bytes 393248 | tf_op jit(solution)/shard_map/ppermute | solution.py:546
  25.1 7.9 %attention_outer_products.5 = (f32[520,128]{1,0:T(8,128)S(1)}, f32[520,128]{1,0:T(8,128)S(1)}) custom-call(s32[20]{0:T(128)S(1)} %concatenate.14.meta, bf16[256,8192]{1,0:T(8,128)(2,1)S(1)} %bitcast.32, bf16[256,2560]{1,0:T(8,128)(2,1)S(1)} %cut_peer.1.refs_1_.refs_6_.refs_7_, bf16[256,768]{1,0:T(8,128)(2,1)S(1)} %collective-permute-done.5.refs_8_.refs_2_, ...), custom_call_target="tpu_custom_call" | custom-call | flops 14000000000 | bytes 1048576 | tf_op jit(solution)/shard_map/attention_outer_products/pallas_call | solution.py:489
  33.0 2.1 %collective-permute-start.8 = (f32[520,128]{1,0:T(8,128)S(1)}, f32[520,128]{1,0:T(8,128)S(1)}, u32[]{:S(2)}, u32[]{:S(2)}) collective-permute-start(f32[520,128]{1,0:T(8,128)S(1)} %get-tuple-element.36), channel_id=1, source_target_pairs={{0,4},{4,8},{8,12},{12,0},{1,5},{5,9},{9,13},{13,1},{2,6},{6,10},{... | collective-permute-start | bytes 798728 | tf_op jit(solution)/shard_map/ppermute | solution.py:556
  35.9 1.5 %collective-permute-start.11 = (bf16[256,512]{1,0:T(8,128)(2,1)S(1)}, bf16[256,512]{1,0:T(8,128)(2,1)S(1)}, u32[]{:S(2)}, u32[]{:S(2)}) collective-permute-start(bf16[256,512]{1,0:T(8,128)(2,1)S(1)} %get-tuple-element.43), channel_id=1, source_target_pairs={{0,2},{1,3},{2,0},{3,1},{4,6},{5,7},{6,4},{7,5},{8,10},{9,11},{10,... | collective-permute-start | bytes 786440 | tf_op jit(solution)/shard_map/ppermute | solution.py:546
  37.4 4.5 %collective-permute-done.4.refs_3_.refs_11_ = bf16[256,768]{1,0:T(8,128)(2,1)S(1)} collective-permute-done((bf16[256,768]{1,0:T(8,128)(2,1)S(1)}, bf16[256,768]{1,0:T(8,128)(2,1)S(1)}, u32[]{:S(2)}, u32[]{:S(2)}) %collective-permute-start.4) | collective-permute-done | bytes 393248 | tf_op jit(solution)/shard_map/ppermute | solution.py:546
  41.9 8.1 %attention_outer_products.4 = (f32[520,128]{1,0:T(8,128)S(1)}, f32[520,128]{1,0:T(8,128)S(1)}) custom-call(s32[20]{0:T(128)S(1)} %concatenate.13.meta, bf16[256,8192]{1,0:T(8,128)(2,1)S(1)} %bitcast.33, bf16[256,2560]{1,0:T(8,128)(2,1)S(1)} %cut_peer.1.refs_1_.refs_6_.refs_7_, bf16[256,768]{1,0:T(8,128)(2,1)S(1)} %collective-permute-done.3.refs_2_.refs_10_, ...), custom_call_target="tpu_custom_call" | custom-call | flops 14000000000 | bytes 1048576 | tf_op jit(solution)/shard_map/attention_outer_products/pallas_call | solution.py:489
  50.1 2.1 %collective-permute-start.15 = (f32[520,128]{1,0:T(8,128)S(1)}, f32[520,128]{1,0:T(8,128)S(1)}, u32[]{:S(2)}, u32[]{:S(2)}) collective-permute-start(f32[520,128]{1,0:T(8,128)S(1)} %add.58), channel_id=1, source_target_pairs={{0,4},{4,8},{8,12},{12,0},{1,5},{5,9},{9,13},{13,1},{2,6},{6,10},{... | collective-permute-start | bytes 798728 | tf_op jit(solution)/shard_map/ppermute | solution.py:556
  52.2 0.9 collective-permute-start.13
  53.1 1.4 %collective-permute-start.10 = (bf16[256,512]{1,0:T(8,128)(2,1)S(1)}, bf16[256,512]{1,0:T(8,128)(2,1)S(1)}, u32[]{:S(2)}, u32[]{:S(2)}) collective-permute-start(bf16[256,512]{1,0:T(8,128)(2,1)S(1)} %get-tuple-element.38), channel_id=1, source_target_pairs={{0,3},{1,2},{2,1},{3,0},{4,7},{5,6},{6,5},{7,4},{8,11},{9,10},{10,... | collective-permute-start | bytes 786440 | tf_op jit(solution)/shard_map/ppermute | solution.py:546
  55.0 7.9 %attention_outer_products.7 = (f32[520,128]{1,0:T(8,128)S(1)}, f32[520,128]{1,0:T(8,128)S(1)}) custom-call(s32[20]{0:T(128)S(1)} %concatenate.15.meta, bf16[256,8192]{1,0:T(8,128)(2,1)S(1)} %bitcast.34, bf16[256,2560]{1,0:T(8,128)(2,1)S(1)} %cut_peer.1.refs_1_.refs_6_.refs_7_, bf16[256,512]{1,0:T(8,128)(2,1)S(1)} %collective-permute-done.11.refs_2_, ...), custom_call_target="tpu_custom_call" | custom-call | flops 14000000000 | bytes 1048576 | tf_op jit(solution)/shard_map/attention_outer_products/pallas_call | solution.py:489
  63.0 2.8 %collective-permute-start.16 = (f32[520,128]{1,0:T(8,128)S(1)}, f32[520,128]{1,0:T(8,128)S(1)}, u32[]{:S(2)}, u32[]{:S(2)}) collective-permute-start(f32[520,128]{1,0:T(8,128)S(1)} %add.60), channel_id=1, source_target_pairs={{0,4},{4,8},{8,12},{12,0},{1,5},{5,9},{9,13},{13,1},{2,6},{6,10},{... | collective-permute-start | bytes 798728 | tf_op jit(solution)/shard_map/ppermute | solution.py:556
  65.8 1.2 collective-permute-done.13
  67.3 8.1 %attention_outer_products.6 = (f32[520,128]{1,0:T(8,128)S(1)}, f32[520,128]{1,0:T(8,128)S(1)}) custom-call(s32[20]{0:T(128)S(1)} %concatenate.12.meta, bf16[256,8192]{1,0:T(8,128)(2,1)S(1)} %bitcast.35, bf16[256,2560]{1,0:T(8,128)(2,1)S(1)} %cut_peer.1.refs_1_.refs_6_.refs_7_, bf16[256,512]{1,0:T(8,128)(2,1)S(1)} %collective-permute-done.9.refs_2_, ...), custom_call_target="tpu_custom_call" | custom-call | flops 14000000000 | bytes 1048576 | tf_op jit(solution)/shard_map/attention_outer_products/pallas_call | solution.py:489
  75.4 3.3 %collective-permute-done.14.refs_2_ = f32[520,128]{1,0:T(8,128)S(1)} collective-permute-done((f32[520,128]{1,0:T(8,128)S(1)}, f32[520,128]{1,0:T(8,128)S(1)}, u32[]{:S(2)}, u32[]{:S(2)}) %collective-permute-start.14) | collective-permute-done | bytes 266272 | tf_op jit(solution)/shard_map/ppermute | solution.py:556
  78.8 9.3 %factor_top.1 = (bf16[784,128]{1,0:T(8,128)(2,1)S(1)}, f32[256,256]{1,0:T(8,128)S(1)}) custom-call(f32[520,128]{1,0:T(8,128)S(1)} %get-tuple-element.39.refs_0_, f32[520,128]{1,0:T(8,128)S(1)} %get-tuple-element.40.refs_1_, f32[520,128]{1,0:T(8,128)S(1)} %collective-permute-done.14.refs_2_, f32[520,128]{1,0:T(8,128)S(1)} %collective-permute-done.16.refs_3_), custom_call_target="tpu_custom_call" | custom-call | flops 10000000000 | bytes 1048576 | tf_op jit(solution)/shard_map/factor_top/pallas_call | solution.py:565
  88.1 1.0 collective-permute-start.22
  89.1 1.3 %collective-permute-start.20 = (bf16[784,128]{1,0:T(8,128)(2,1)S(1)}, bf16[784,128]{1,0:T(8,128)(2,1)S(1)}, u32[]{:S(2)}, u32[]{:S(2)}) collective-permute-start(bf16[784,128]{1,0:T(8,128)(2,1)S(1)} %get-tuple-element.48.refs_0_), channel_id=1, source_target_pairs={{0,8},{4,12},{8,0},{12,4},{1,9},{5,13},{9,1},{13,5},{2,10},{6,14},... | collective-permute-start | bytes 602120 | tf_op jit(solution)/shard_map/ppermute | solution.py:596
  90.5 1.5 %collective-permute-start.21 = (bf16[784,128]{1,0:T(8,128)(2,1)S(1)}, bf16[784,128]{1,0:T(8,128)(2,1)S(1)}, u32[]{:S(2)}, u32[]{:S(2)}) collective-permute-start(bf16[784,128]{1,0:T(8,128)(2,1)S(1)} %get-tuple-element.48.refs_0_), channel_id=1, source_target_pairs={{0,12},{4,0},{8,4},{12,8},{1,13},{5,1},{9,5},{13,9},{2,14},{6,2},{... | collective-permute-start | bytes 602120 | tf_op jit(solution)/shard_map/ppermute | solution.py:596
  92.0 8.2 %factor_bottom.1.refs_1_ = bf16[272,128]{1,0:T(8,128)(2,1)S(1)} custom-call(f32[256,256]{1,0:T(8,128)S(1)} %get-tuple-element.47.refs_0_), custom_call_target="tpu_custom_call" | custom-call | flops 8999999488 | bytes 1048576 | tf_op jit(solution)/shard_map/factor_bottom/pallas_call | solution.py:580
  100.8 1.5 %collective-permute-start.18 = (bf16[272,128]{1,0:T(8,128)(2,1)S(1)}, bf16[272,128]{1,0:T(8,128)(2,1)S(1)}, u32[]{:S(2)}, u32[]{:S(2)}) collective-permute-start(bf16[272,128]{1,0:T(8,128)(2,1)S(1)} %factor_bottom.1.refs_1_), channel_id=1, source_target_pairs={{0,8},{4,12},{8,0},{12,4},{1,9},{5,13},{9,1},{13,5},{2,10},{6,14},... | collective-permute-start | bytes 208904 | tf_op jit(solution)/shard_map/ppermute | solution.py:596
  102.4 3.5 %whiten_top.3.refs_5_ = f32[4,512,2048]{2,1,0:T(8,128)} custom-call(s32[4]{0:T(128)S(1)} %pad_add_fusion.order, bf16[784,128]{1,0:T(8,128)(2,1)S(1)} %get-tuple-element.48.refs_0_, bf16[272,128]{1,0:T(8,128)(2,1)S(1)} %factor_bottom.1.refs_1_, bf16[2048,2048]{1,0:T(8,128)(2,1)S(1)} %bitcast.22, bf16[2048,2048]{1,0:T(8,128)(2,1)S(1)} %bitcast.22, ...), custom_call_target="tpu_custom_call" | custom-call | flops 4000000000 | bytes 1048576 | tf_op jit(solution)/shard_map/whiten_top/pallas_call | solution.py:622
  105.9 3.2 %collective-permute-start.19 = (bf16[272,128]{1,0:T(8,128)(2,1)S(1)}, bf16[272,128]{1,0:T(8,128)(2,1)S(1)}, u32[]{:S(2)}, u32[]{:S(2)}) collective-permute-start(bf16[272,128]{1,0:T(8,128)(2,1)S(1)} %factor_bottom.1.refs_1_), channel_id=1, source_target_pairs={{0,12},{4,0},{8,4},{12,8},{1,13},{5,1},{9,5},{13,9},{2,14},{6,2},{... | collective-permute-start | bytes 208904 | tf_op jit(solution)/shard_map/ppermute | solution.py:596
  109.0 2.8 %whiten_top.4.refs_6_ = f32[4,512,2048]{2,1,0:T(8,128)} custom-call(s32[4]{0:T(128)S(1)} %pad_add_fusion.order, bf16[784,128]{1,0:T(8,128)(2,1)S(1)} %collective-permute-done.22.refs_0_, bf16[2048,2048]{1,0:T(8,128)(2,1)S(1)} %bitcast.22, bf16[2048,2048]{1,0:T(8,128)(2,1)S(1)} %bitcast.22, ...), custom_call_target="tpu_custom_call", output_to_operand_aliasing={{}: (6, {})} | custom-call | flops 2000000000 | bytes 1048576 | tf_op jit(solution)/shard_map/whiten_top/pallas_call | solution.py:622
  111.9 6.3 %whiten_top.5.refs_7_ = f32[4,512,2048]{2,1,0:T(8,128)} custom-call(s32[4]{0:T(128)S(1)} %pad_add_fusion.order, bf16[784,128]{1,0:T(8,128)(2,1)S(1)} %collective-permute-done.20.refs_0_, bf16[784,128]{1,0:T(8,128)(2,1)S(1)} %collective-permute-done.21.refs_1_, bf16[2048,2048]{1,0:T(8,128)(2,1)S(1)} %bitcast.22, ...), custom_call_target="tpu_custom_call", output_to_operand_aliasing={{}: (7, {})} | custom-call | flops 4000000000 | bytes 1048576 | tf_op jit(solution)/shard_map/whiten_top/pallas_call | solution.py:622
  118.2 6.5 %whiten_bottom.1 = f32[4,512,2048]{2,1,0:T(8,128)} custom-call(s32[4]{0:T(128)S(1)} %pad_add_fusion.order, bf16[272,128]{1,0:T(8,128)(2,1)S(1)} %collective-permute-done.17.refs_0_, bf16[272,128]{1,0:T(8,128)(2,1)S(1)} %collective-permute-done.18.refs_1_, bf16[272,128]{1,0:T(8,128)(2,1)S(1)} %collective-permute-done.19.refs_2_, ...), custom_call_target="tpu_custom_call", output_to_operand_aliasing={{}: (8, {})} | custom-call | flops 6000000000 | bytes 1048576 | tf_op jit(solution)/shard_map/whiten_bottom/pallas_call | solution.py:622
  (58 shorter events, 10.1 us)
Async XLA Ops:
  0.0 18.9 %collective-permute-start = (bf16[256,8192]{1,0:T(8,128)(2,1)}, bf16[256,8192]{1,0:T(8,128)(2,1)}, u32[]{:S(2)}, u32[]{:S(2)}) collective-permute-start(bf16[256,8192]{1,0:T(8,128)(2,1)} %bitcast.23), channel_id=1, source_target_pairs={{0,1},{1,0},{2,3},{3,2},{4,5},{5,4},{6,7},{7,6},{8,9},{9,8},{10,11... | collective-permute-start | bytes 12582920 | tf_op jit(solution)/shard_map/ppermute | solution.py:528
  0.5 9.7 %collective-permute-start.1 = (bf16[256,1024]{1,0:T(8,128)(2,1)}, bf16[256,1024]{1,0:T(8,128)(2,1)S(1)}, u32[]{:S(2)}, u32[]{:S(2)}) collective-permute-start(bf16[256,1024]{1,0:T(8,128)(2,1)} %bitcast.36), channel_id=1, source_target_pairs={{0,1},{1,0},{2,3},{3,2},{4,5},{5,4},{6,7},{7,6},{8,9},{9,8},{10,11... | collective-permute-start | bytes 1572872 | tf_op jit(solution)/shard_map/ppermute | solution.py:528
  0.5 17.7 %collective-permute-start.2 = (bf16[256,1024]{1,0:T(8,128)(2,1)}, bf16[256,1024]{1,0:T(8,128)(2,1)}, u32[]{:S(2)}, u32[]{:S(2)}) collective-permute-start(bf16[256,1024]{1,0:T(8,128)(2,1)} %bitcast.45), channel_id=1, source_target_pairs={{0,1},{1,0},{2,3},{3,2},{4,5},{5,4},{6,7},{7,6},{8,9},{9,8},{10,11... | collective-permute-start | bytes 1572872 | tf_op jit(solution)/shard_map/ppermute | solution.py:528
  4.3 15.9 %collective-permute-start.5 = (bf16[256,768]{1,0:T(8,128)(2,1)}, bf16[256,768]{1,0:T(8,128)(2,1)S(1)}, u32[]{:S(2)}, u32[]{:S(2)}) collective-permute-start(bf16[256,768]{1,0:T(8,128)(2,1)} %get-tuple-element.31), channel_id=1, source_target_pairs={{0,2},{1,3},{2,0},{3,1},{4,6},{5,7},{6,4},{7,5},{8,10},{9,11},{10,... | collective-permute-start | bytes 1179656 | tf_op jit(solution)/shard_map/ppermute | solution.py:546
  6.8 18.2 %collective-permute-start.6 = (bf16[256,768]{1,0:T(8,128)(2,1)}, bf16[256,768]{1,0:T(8,128)(2,1)S(1)}, u32[]{:S(2)}, u32[]{:S(2)}) collective-permute-start(bf16[256,768]{1,0:T(8,128)(2,1)} %get-tuple-element.32), channel_id=1, source_target_pairs={{0,3},{1,2},{2,1},{3,0},{4,7},{5,6},{6,5},{7,4},{8,11},{9,10},{10,... | collective-permute-start | bytes 1179656 | tf_op jit(solution)/shard_map/ppermute | solution.py:546
  10.2 2.2 %copy-start = (bf16[1,256,8192]{2,1,0:T(8,128)(2,1)S(1)}, bf16[1,256,8192]{2,1,0:T(8,128)(2,1)}, u32[]{:S(2)}) copy-start(bf16[1,256,8192]{2,1,0:T(8,128)(2,1)} %param.6) | copy-start | bytes 12582916
  12.4 1.0 copy-start.2
  13.4 1.0 copy-start.4
  14.5 3.1 %copy-start.1 = (bf16[1,256,8192]{2,1,0:T(8,128)(2,1)S(1)}, bf16[1,256,8192]{2,1,0:T(8,128)(2,1)}, u32[]{:S(2)}) copy-start(bf16[1,256,8192]{2,1,0:T(8,128)(2,1)} %param.6) | copy-start | bytes 12582916
  14.5 10.6 %copy-start.3 = (bf16[1,256,1024]{2,1,0:T(8,128)(2,1)S(1)}, bf16[1,256,1024]{2,1,0:T(8,128)(2,1)}, u32[]{:S(2)}) copy-start(bf16[1,256,1024]{2,1,0:T(8,128)(2,1)} %param.7) | copy-start | bytes 1572868
  14.5 10.6 %copy-start.5 = (bf16[1,256,1024]{2,1,0:T(8,128)(2,1)S(1)}, bf16[1,256,1024]{2,1,0:T(8,128)(2,1)}, u32[]{:S(2)}) copy-start(bf16[1,256,1024]{2,1,0:T(8,128)(2,1)} %param.8) | copy-start | bytes 1572868
  15.2 22.2 %collective-permute-start.3 = (bf16[256,768]{1,0:T(8,128)(2,1)S(1)}, bf16[256,768]{1,0:T(8,128)(2,1)S(1)}, u32[]{:S(2)}, u32[]{:S(2)}) collective-permute-start(bf16[256,768]{1,0:T(8,128)(2,1)S(1)} %get-tuple-element.29), channel_id=1, source_target_pairs={{0,2},{1,3},{2,0},{3,1},{4,6},{5,7},{6,4},{7,5},{8,10},{9,11},{10,... | collective-permute-start | bytes 1179656 | tf_op jit(solution)/shard_map/ppermute | solution.py:546
  18.2 23.7 %collective-permute-start.4 = (bf16[256,768]{1,0:T(8,128)(2,1)S(1)}, bf16[256,768]{1,0:T(8,128)(2,1)S(1)}, u32[]{:S(2)}, u32[]{:S(2)}) collective-permute-start(bf16[256,768]{1,0:T(8,128)(2,1)S(1)} %get-tuple-element.30), channel_id=1, source_target_pairs={{0,3},{1,2},{2,1},{3,0},{4,7},{5,6},{6,5},{7,4},{8,11},{9,10},{10,... | collective-permute-start | bytes 1179656 | tf_op jit(solution)/shard_map/ppermute | solution.py:546
  33.0 17.0 %collective-permute-start.8 = (f32[520,128]{1,0:T(8,128)S(1)}, f32[520,128]{1,0:T(8,128)S(1)}, u32[]{:S(2)}, u32[]{:S(2)}) collective-permute-start(f32[520,128]{1,0:T(8,128)S(1)} %get-tuple-element.36), channel_id=1, source_target_pairs={{0,4},{4,8},{8,12},{12,0},{1,5},{5,9},{9,13},{13,1},{2,6},{6,10},{... | collective-permute-start | bytes 798728 | tf_op jit(solution)/shard_map/ppermute | solution.py:556
  35.1 17.1 %collective-permute-start.7 = (f32[520,128]{1,0:T(8,128)S(1)}, f32[520,128]{1,0:T(8,128)S(1)}, u32[]{:S(2)}, u32[]{:S(2)}) collective-permute-start(f32[520,128]{1,0:T(8,128)S(1)} %get-tuple-element.34), channel_id=1, source_target_pairs={{0,4},{4,8},{8,12},{12,0},{1,5},{5,9},{9,13},{13,1},{2,6},{6,10},{... | collective-permute-start | bytes 798728 | tf_op jit(solution)/shard_map/ppermute | solution.py:556
  35.9 18.6 %collective-permute-start.11 = (bf16[256,512]{1,0:T(8,128)(2,1)S(1)}, bf16[256,512]{1,0:T(8,128)(2,1)S(1)}, u32[]{:S(2)}, u32[]{:S(2)}) collective-permute-start(bf16[256,512]{1,0:T(8,128)(2,1)S(1)} %get-tuple-element.43), channel_id=1, source_target_pairs={{0,2},{1,3},{2,0},{3,1},{4,6},{5,7},{6,4},{7,5},{8,10},{9,11},{10,... | collective-permute-start | bytes 786440 | tf_op jit(solution)/shard_map/ppermute | solution.py:546
  37.4 17.7 %collective-permute-start.12 = (bf16[256,512]{1,0:T(8,128)(2,1)S(1)}, bf16[256,512]{1,0:T(8,128)(2,1)S(1)}, u32[]{:S(2)}, u32[]{:S(2)}) collective-permute-start(bf16[256,512]{1,0:T(8,128)(2,1)S(1)} %get-tuple-element.44), channel_id=1, source_target_pairs={{0,3},{1,2},{2,1},{3,0},{4,7},{5,6},{6,5},{7,4},{8,11},{9,10},{10,... | collective-permute-start | bytes 786440 | tf_op jit(solution)/shard_map/ppermute | solution.py:546
  50.1 12.9 %collective-permute-start.15 = (f32[520,128]{1,0:T(8,128)S(1)}, f32[520,128]{1,0:T(8,128)S(1)}, u32[]{:S(2)}, u32[]{:S(2)}) collective-permute-start(f32[520,128]{1,0:T(8,128)S(1)} %add.58), channel_id=1, source_target_pairs={{0,4},{4,8},{8,12},{12,0},{1,5},{5,9},{9,13},{13,1},{2,6},{6,10},{... | collective-permute-start | bytes 798728 | tf_op jit(solution)/shard_map/ppermute | solution.py:556
  52.2 14.7 %collective-permute-start.13 = (f32[520,128]{1,0:T(8,128)S(1)}, f32[520,128]{1,0:T(8,128)S(1)}, u32[]{:S(2)}, u32[]{:S(2)}) collective-permute-start(f32[520,128]{1,0:T(8,128)S(1)} %add.57), channel_id=1, source_target_pairs={{0,4},{4,8},{8,12},{12,0},{1,5},{5,9},{9,13},{13,1},{2,6},{6,10},{... | collective-permute-start | bytes 798728 | tf_op jit(solution)/shard_map/ppermute | solution.py:556
  53.1 14.1 %collective-permute-start.10 = (bf16[256,512]{1,0:T(8,128)(2,1)S(1)}, bf16[256,512]{1,0:T(8,128)(2,1)S(1)}, u32[]{:S(2)}, u32[]{:S(2)}) collective-permute-start(bf16[256,512]{1,0:T(8,128)(2,1)S(1)} %get-tuple-element.38), channel_id=1, source_target_pairs={{0,3},{1,2},{2,1},{3,0},{4,7},{5,6},{6,5},{7,4},{8,11},{9,10},{10,... | collective-permute-start | bytes 786440 | tf_op jit(solution)/shard_map/ppermute | solution.py:546
  54.5 12.8 %collective-permute-start.9 = (bf16[256,512]{1,0:T(8,128)(2,1)S(1)}, bf16[256,512]{1,0:T(8,128)(2,1)S(1)}, u32[]{:S(2)}, u32[]{:S(2)}) collective-permute-start(bf16[256,512]{1,0:T(8,128)(2,1)S(1)} %get-tuple-element.37), channel_id=1, source_target_pairs={{0,2},{1,3},{2,0},{3,1},{4,6},{5,7},{6,4},{7,5},{8,10},{9,11},{10,... | collective-permute-start | bytes 786440 | tf_op jit(solution)/shard_map/ppermute | solution.py:546
  63.0 12.4 %collective-permute-start.16 = (f32[520,128]{1,0:T(8,128)S(1)}, f32[520,128]{1,0:T(8,128)S(1)}, u32[]{:S(2)}, u32[]{:S(2)}) collective-permute-start(f32[520,128]{1,0:T(8,128)S(1)} %add.60), channel_id=1, source_target_pairs={{0,4},{4,8},{8,12},{12,0},{1,5},{5,9},{9,13},{13,1},{2,6},{6,10},{... | collective-permute-start | bytes 798728 | tf_op jit(solution)/shard_map/ppermute | solution.py:556
  67.0 11.8 %collective-permute-start.14 = (f32[520,128]{1,0:T(8,128)S(1)}, f32[520,128]{1,0:T(8,128)S(1)}, u32[]{:S(2)}, u32[]{:S(2)}) collective-permute-start(f32[520,128]{1,0:T(8,128)S(1)} %add.59), channel_id=1, source_target_pairs={{0,4},{4,8},{8,12},{12,0},{1,5},{5,9},{9,13},{13,1},{2,6},{6,10},{... | collective-permute-start | bytes 798728 | tf_op jit(solution)/shard_map/ppermute | solution.py:556
  88.1 14.3 %slice-start = ((s8[8388608]{0:T(1024)(128)(4,1)}), s8[4194304]{0:T(1024)(128)(4,1)S(1)}, s32[]{:S(2)}) async-start(s8[8388608]{0:T(1024)(128)(4,1)} %bitcast.21), calls=%async_computation | async-start | bytes 8388608
  88.1 17.8 %collective-permute-start.22 = (bf16[784,128]{1,0:T(8,128)(2,1)S(1)}, bf16[784,128]{1,0:T(8,128)(2,1)S(1)}, u32[]{:S(2)}, u32[]{:S(2)}) collective-permute-start(bf16[784,128]{1,0:T(8,128)(2,1)S(1)} %get-tuple-element.48.refs_0_), channel_id=1, source_target_pairs={{0,4},{4,8},{8,12},{12,0},{1,5},{5,9},{9,13},{13,1},{2,6},{6,10},{... | collective-permute-start | bytes 602120 | tf_op jit(solution)/shard_map/ppermute | solution.py:596
  89.1 22.7 %collective-permute-start.20 = (bf16[784,128]{1,0:T(8,128)(2,1)S(1)}, bf16[784,128]{1,0:T(8,128)(2,1)S(1)}, u32[]{:S(2)}, u32[]{:S(2)}) collective-permute-start(bf16[784,128]{1,0:T(8,128)(2,1)S(1)} %get-tuple-element.48.refs_0_), channel_id=1, source_target_pairs={{0,8},{4,12},{8,0},{12,4},{1,9},{5,13},{9,1},{13,5},{2,10},{6,14},... | collective-permute-start | bytes 602120 | tf_op jit(solution)/shard_map/ppermute | solution.py:596
  90.5 21.4 %collective-permute-start.21 = (bf16[784,128]{1,0:T(8,128)(2,1)S(1)}, bf16[784,128]{1,0:T(8,128)(2,1)S(1)}, u32[]{:S(2)}, u32[]{:S(2)}) collective-permute-start(bf16[784,128]{1,0:T(8,128)(2,1)S(1)} %get-tuple-element.48.refs_0_), channel_id=1, source_target_pairs={{0,12},{4,0},{8,4},{12,8},{1,13},{5,1},{9,5},{13,9},{2,14},{6,2},{... | collective-permute-start | bytes 602120 | tf_op jit(solution)/shard_map/ppermute | solution.py:596
  92.0 10.4 %slice-start.1 = ((s8[8388608]{0:T(1024)(128)(4,1)}), s8[4194304]{0:T(1024)(128)(4,1)S(1)}, s32[]{:S(2)}) async-start(s8[8388608]{0:T(1024)(128)(4,1)} %bitcast.21), calls=%async_computation.1 | async-start | bytes 8388608
  100.2 17.9 %collective-permute-start.17 = (bf16[272,128]{1,0:T(8,128)(2,1)S(1)}, bf16[272,128]{1,0:T(8,128)(2,1)S(1)}, u32[]{:S(2)}, u32[]{:S(2)}) collective-permute-start(bf16[272,128]{1,0:T(8,128)(2,1)S(1)} %factor_bottom.1.refs_1_), channel_id=1, source_target_pairs={{0,4},{4,8},{8,12},{12,0},{1,5},{5,9},{9,13},{13,1},{2,6},{6,10},{... | collective-permute-start | bytes 208904 | tf_op jit(solution)/shard_map/ppermute | solution.py:596
  100.8 17.3 %collective-permute-start.18 = (bf16[272,128]{1,0:T(8,128)(2,1)S(1)}, bf16[272,128]{1,0:T(8,128)(2,1)S(1)}, u32[]{:S(2)}, u32[]{:S(2)}) collective-permute-start(bf16[272,128]{1,0:T(8,128)(2,1)S(1)} %factor_bottom.1.refs_1_), channel_id=1, source_target_pairs={{0,8},{4,12},{8,0},{12,4},{1,9},{5,13},{9,1},{13,5},{2,10},{6,14},... | collective-permute-start | bytes 208904 | tf_op jit(solution)/shard_map/ppermute | solution.py:596
  105.9 12.3 %collective-permute-start.19 = (bf16[272,128]{1,0:T(8,128)(2,1)S(1)}, bf16[272,128]{1,0:T(8,128)(2,1)S(1)}, u32[]{:S(2)}, u32[]{:S(2)}) collective-permute-start(bf16[272,128]{1,0:T(8,128)(2,1)S(1)} %factor_bottom.1.refs_1_), channel_id=1, source_target_pairs={{0,12},{4,0},{8,4},{12,8},{1,13},{5,1},{9,5},{13,9},{2,14},{6,2},{... | collective-permute-start | bytes 208904 | tf_op jit(solution)/shard_map/ppermute | solution.py:596

commit v8 on v7

--- a/solution.py
+++ b/solution.py
@@ -643,9 +643,11 @@
 
     result = whiten([tops[0], bottoms[0]], 0, (0, half), None)
     result = whiten(tops[1:2], 1, (0,), result)
+    result = whiten(bottoms[1:2], 1, (half,), result)
     if blocks > 2:
-        result = whiten(tops[2:], 2, (0,), result)
-    return whiten(bottoms[1:], 1, (half,), result)
+        rest = [half_block for pair in zip(tops[2:], bottoms[2:]) for half_block in pair]
+        result = whiten(rest, 2, (0, half), result)
+    return result
 
 
 def solution(mesh):

time: 126 us -> 124 us (0.984); the launches traced: 125 us -> 124 us
  waiting for transfers between devices: 14 us -> 15.5 us
    ppermute x6, waiting for transfers between devices: 4.51 us -> 5.84 us  [shards(): lax.ppermute(part, 'dp', [(z, (z + 1) % ring) for z in range(ring)])]
  transfers between devices with their start and end apart: 23 -> 23, of which waited for: 5 -> 5; matrix products, arithmetic and copies ran while one was open for 3% -> 3% of each run, Pallas kernels for 47% -> 44%
where the time goes in v8:
time: 124 us
  Pallas kernels  73.3 us (59%)
  starting transfers between devices  26.7 us (22%)
  waiting for transfers between devices  15.5 us (12%)
  local copies, waits for them, and re-layouts  7.3 us (6%)
    pallas_call x4, Pallas kernels, grams_of(): pl.pallas_call(functools.partial(attention_kernel, chips=chips, spans=spa...  32 us
    pallas_call x4, Pallas kernels, whiten(): pl.pallas_call(functools.partial(whiten_kernel, blocks=count, starts=star...  17.9 us
    ppermute x8, waiting for transfers between devices, shards(): lax.ppermute(part, 'seq', moved(*where))  9.63 us
    pallas_call x1, Pallas kernels, factor_top(): pl.pallas_call(functools.partial(factor_kernel, start=0, stop=half, recei...  9.33 us
    ppermute x6, starting transfers between devices, shared(): lax.ppermute(array, 'dp', [(z, (z + d) % ring) for z in range(ring)])  9.19 us
    ppermute x8, starting transfers between devices, shards(): lax.ppermute(part, 'seq', moved(*where))  8.64 us
    pallas_call x1, Pallas kernels, factor_bottom(): pl.pallas_call(functools.partial(factor_kernel, start=half, stop=BLOCK_W,...  8.22 us
    ppermute x6, starting transfers between devices, shards(): lax.ppermute(part, 'dp', [(z, (z + 1) % ring) for z in range(ring)])  7.88 us
  transfers between devices with their start and end apart: 23, of which 5 were waited for; matrix products, arithmetic and copies ran while one was open for 3% of the time, Pallas kernels for 44%

profile of v8, /device:TPU:0, one launch (start us, length us, event | category | flops | bytes accessed | tf_op | source)
XLA Modules:
  0.0 124.2 jit_solution(3123114026410404828)
XLA Ops:
  1.6 2.7 %cut_piece.6 = (bf16[256,768]{1,0:T(8,128)(2,1)}, bf16[256,768]{1,0:T(8,128)(2,1)}) custom-call(s32[3]{0:T(128)} %pad_add_fusion.1.meta, bf16[256,8192]{1,0:T(8,128)(2,1)} %bitcast.24, bf16[256,1024]{1,0:T(8,128)(2,1)} %bitcast.37, bf16[256,1024]{1,0:T(8,128)(2,1)} %bitcast.46, bf16[256,8192]{1,0:T(8,128)(2,1)} %bitcast.25, bf16[256,1024]{1,0:T(8,128)(2,1)} %bitcast.38, ...), custom_call_target="tpu_custom_call" | custom-call | bytes 2097152 | tf_op jit(solution)/shard_map/cut_piece/pallas_call | solution.py:458
  4.3 2.5 %collective-permute-start.5 = (bf16[256,768]{1,0:T(8,128)(2,1)}, bf16[256,768]{1,0:T(8,128)(2,1)S(1)}, u32[]{:S(2)}, u32[]{:S(2)}) collective-permute-start(bf16[256,768]{1,0:T(8,128)(2,1)} %get-tuple-element.31), channel_id=1, source_target_pairs={{0,2},{1,3},{2,0},{3,1},{4,6},{5,7},{6,4},{7,5},{8,10},{9,11},{10,... | collective-permute-start | bytes 1179656 | tf_op jit(solution)/shard_map/ppermute | solution.py:546
  10.2 2.2 %copy-done = bf16[1,256,8192]{2,1,0:T(8,128)(2,1)S(1)} copy-done((bf16[1,256,8192]{2,1,0:T(8,128)(2,1)S(1)}, bf16[1,256,8192]{2,1,0:T(8,128)(2,1)}, u32[]{:S(2)}) %copy-start) | copy-done | bytes 4194328
  12.4 1.0 copy-done.2
  13.4 1.0 copy-done.4
  15.2 1.8 %collective-permute-start.3 = (bf16[256,768]{1,0:T(8,128)(2,1)S(1)}, bf16[256,768]{1,0:T(8,128)(2,1)S(1)}, u32[]{:S(2)}, u32[]{:S(2)}) collective-permute-start(bf16[256,768]{1,0:T(8,128)(2,1)S(1)} %get-tuple-element.29), channel_id=1, source_target_pairs={{0,2},{1,3},{2,0},{3,1},{4,6},{5,7},{6,4},{7,5},{8,10},{9,11},{10,... | collective-permute-start | bytes 1179656 | tf_op jit(solution)/shard_map/ppermute | solution.py:546
  18.9 1.3 %cut_peer.1.refs_1_.refs_6_.refs_7_ = bf16[256,2560]{1,0:T(8,128)(2,1)S(1)} custom-call(s32[1]{0:T(128)} %bitcast.4.meta, bf16[256,8192]{1,0:T(8,128)(2,1)} %collective-permute-done.refs_0_, bf16[256,1024]{1,0:T(8,128)(2,1)S(1)} %collective-permute-done.1.refs_1_.refs_2_.refs_6_, bf16[256,1024]{1,0:T(8,128)(2,1)} %collective-permute-done.2.refs_2_), custom_call_target="tpu_custom_call" | custom-call | bytes 2097152 | tf_op jit(solution)/shard_map/cut_peer/pallas_call | solution.py:458
  20.3 4.8 %collective-permute-done.6.refs_9_.refs_3_ = bf16[256,768]{1,0:T(8,128)(2,1)S(1)} collective-permute-done((bf16[256,768]{1,0:T(8,128)(2,1)}, bf16[256,768]{1,0:T(8,128)(2,1)S(1)}, u32[]{:S(2)}, u32[]{:S(2)}) %collective-permute-start.6) | collective-permute-done | bytes 393248 | tf_op jit(solution)/shard_map/ppermute | solution.py:546
  25.1 7.9 %attention_outer_products.5 = (f32[520,128]{1,0:T(8,128)S(1)}, f32[520,128]{1,0:T(8,128)S(1)}) custom-call(s32[20]{0:T(128)S(1)} %concatenate.14.meta, bf16[256,8192]{1,0:T(8,128)(2,1)S(1)} %bitcast.32, bf16[256,2560]{1,0:T(8,128)(2,1)S(1)} %cut_peer.1.refs_1_.refs_6_.refs_7_, bf16[256,768]{1,0:T(8,128)(2,1)S(1)} %collective-permute-done.5.refs_8_.refs_2_, ...), custom_call_target="tpu_custom_call" | custom-call | flops 14000000000 | bytes 1048576 | tf_op jit(solution)/shard_map/attention_outer_products/pallas_call | solution.py:489
  33.0 1.1 collective-permute-start.8
  34.1 2.4 %collective-permute-start.7 = (f32[520,128]{1,0:T(8,128)S(1)}, f32[520,128]{1,0:T(8,128)S(1)}, u32[]{:S(2)}, u32[]{:S(2)}) collective-permute-start(f32[520,128]{1,0:T(8,128)S(1)} %get-tuple-element.34), channel_id=1, source_target_pairs={{0,4},{4,8},{8,12},{12,0},{1,5},{5,9},{9,13},{13,1},{2,6},{6,10},{... | collective-permute-start | bytes 798728 | tf_op jit(solution)/shard_map/ppermute | solution.py:556
  36.4 1.5 %collective-permute-start.11 = (bf16[256,512]{1,0:T(8,128)(2,1)S(1)}, bf16[256,512]{1,0:T(8,128)(2,1)S(1)}, u32[]{:S(2)}, u32[]{:S(2)}) collective-permute-start(bf16[256,512]{1,0:T(8,128)(2,1)S(1)} %get-tuple-element.43), channel_id=1, source_target_pairs={{0,2},{1,3},{2,0},{3,1},{4,6},{5,7},{6,4},{7,5},{8,10},{9,11},{10,... | collective-permute-start | bytes 786440 | tf_op jit(solution)/shard_map/ppermute | solution.py:546
  37.9 4.0 %collective-permute-done.4.refs_3_.refs_11_ = bf16[256,768]{1,0:T(8,128)(2,1)S(1)} collective-permute-done((bf16[256,768]{1,0:T(8,128)(2,1)S(1)}, bf16[256,768]{1,0:T(8,128)(2,1)S(1)}, u32[]{:S(2)}, u32[]{:S(2)}) %collective-permute-start.4) | collective-permute-done | bytes 393248 | tf_op jit(solution)/shard_map/ppermute | solution.py:546
  41.9 8.1 %attention_outer_products.4 = (f32[520,128]{1,0:T(8,128)S(1)}, f32[520,128]{1,0:T(8,128)S(1)}) custom-call(s32[20]{0:T(128)S(1)} %concatenate.13.meta, bf16[256,8192]{1,0:T(8,128)(2,1)S(1)} %bitcast.33, bf16[256,2560]{1,0:T(8,128)(2,1)S(1)} %cut_peer.1.refs_1_.refs_6_.refs_7_, bf16[256,768]{1,0:T(8,128)(2,1)S(1)} %collective-permute-done.3.refs_2_.refs_10_, ...), custom_call_target="tpu_custom_call" | custom-call | flops 14000000000 | bytes 1048576 | tf_op jit(solution)/shard_map/attention_outer_products/pallas_call | solution.py:489
  50.1 1.1 collective-permute-start.15
  51.2 2.4 %collective-permute-start.13 = (f32[520,128]{1,0:T(8,128)S(1)}, f32[520,128]{1,0:T(8,128)S(1)}, u32[]{:S(2)}, u32[]{:S(2)}) collective-permute-start(f32[520,128]{1,0:T(8,128)S(1)} %add.57), channel_id=1, source_target_pairs={{0,4},{4,8},{8,12},{12,0},{1,5},{5,9},{9,13},{13,1},{2,6},{6,10},{... | collective-permute-start | bytes 798728 | tf_op jit(solution)/shard_map/ppermute | solution.py:556
  53.6 1.4 %collective-permute-start.10 = (bf16[256,512]{1,0:T(8,128)(2,1)S(1)}, bf16[256,512]{1,0:T(8,128)(2,1)S(1)}, u32[]{:S(2)}, u32[]{:S(2)}) collective-permute-start(bf16[256,512]{1,0:T(8,128)(2,1)S(1)} %get-tuple-element.38), channel_id=1, source_target_pairs={{0,3},{1,2},{2,1},{3,0},{4,7},{5,6},{6,5},{7,4},{8,11},{9,10},{10,... | collective-permute-start | bytes 786440 | tf_op jit(solution)/shard_map/ppermute | solution.py:546
  55.6 7.9 %attention_outer_products.7 = (f32[520,128]{1,0:T(8,128)S(1)}, f32[520,128]{1,0:T(8,128)S(1)}) custom-call(s32[20]{0:T(128)S(1)} %concatenate.15.meta, bf16[256,8192]{1,0:T(8,128)(2,1)S(1)} %bitcast.34, bf16[256,2560]{1,0:T(8,128)(2,1)S(1)} %cut_peer.1.refs_1_.refs_6_.refs_7_, bf16[256,512]{1,0:T(8,128)(2,1)S(1)} %collective-permute-done.11.refs_2_, ...), custom_call_target="tpu_custom_call" | custom-call | flops 14000000000 | bytes 1048576 | tf_op jit(solution)/shard_map/attention_outer_products/pallas_call | solution.py:489
  64.4 2.5 %collective-permute-done.13 = f32[520,128]{1,0:T(8,128)S(1)} collective-permute-done((f32[520,128]{1,0:T(8,128)S(1)}, f32[520,128]{1,0:T(8,128)S(1)}, u32[]{:S(2)}, u32[]{:S(2)}) %collective-permute-start.13) | collective-permute-done | bytes 266272 | tf_op jit(solution)/shard_map/ppermute | solution.py:556
  67.0 0.9 collective-permute-done.9.refs_2_
  67.8 8.1 %attention_outer_products.6 = (f32[520,128]{1,0:T(8,128)S(1)}, f32[520,128]{1,0:T(8,128)S(1)}) custom-call(s32[20]{0:T(128)S(1)} %concatenate.12.meta, bf16[256,8192]{1,0:T(8,128)(2,1)S(1)} %bitcast.35, bf16[256,2560]{1,0:T(8,128)(2,1)S(1)} %cut_peer.1.refs_1_.refs_6_.refs_7_, bf16[256,512]{1,0:T(8,128)(2,1)S(1)} %collective-permute-done.9.refs_2_, ...), custom_call_target="tpu_custom_call" | custom-call | flops 14000000000 | bytes 1048576 | tf_op jit(solution)/shard_map/attention_outer_products/pallas_call | solution.py:489
  76.0 3.3 %collective-permute-done.14.refs_2_ = f32[520,128]{1,0:T(8,128)S(1)} collective-permute-done((f32[520,128]{1,0:T(8,128)S(1)}, f32[520,128]{1,0:T(8,128)S(1)}, u32[]{:S(2)}, u32[]{:S(2)}) %collective-permute-start.14) | collective-permute-done | bytes 266272 | tf_op jit(solution)/shard_map/ppermute | solution.py:556
  79.3 9.3 %factor_top.1 = (bf16[784,128]{1,0:T(8,128)(2,1)S(1)}, f32[256,256]{1,0:T(8,128)S(1)}) custom-call(f32[520,128]{1,0:T(8,128)S(1)} %get-tuple-element.39.refs_0_, f32[520,128]{1,0:T(8,128)S(1)} %get-tuple-element.40.refs_1_, f32[520,128]{1,0:T(8,128)S(1)} %collective-permute-done.14.refs_2_, f32[520,128]{1,0:T(8,128)S(1)} %collective-permute-done.16.refs_3_), custom_call_target="tpu_custom_call" | custom-call | flops 10000000000 | bytes 1048576 | tf_op jit(solution)/shard_map/factor_top/pallas_call | solution.py:565
  88.7 1.3 %collective-permute-start.17 = (bf16[784,128]{1,0:T(8,128)(2,1)S(1)}, bf16[784,128]{1,0:T(8,128)(2,1)S(1)}, u32[]{:S(2)}, u32[]{:S(2)}) collective-permute-start(bf16[784,128]{1,0:T(8,128)(2,1)S(1)} %get-tuple-element.47.refs_0_), channel_id=1, source_target_pairs={{0,8},{4,12},{8,0},{12,4},{1,9},{5,13},{9,1},{13,5},{2,10},{6,14},... | collective-permute-start | bytes 602120 | tf_op jit(solution)/shard_map/ppermute | solution.py:596
  90.0 2.5 %collective-permute-start.19 = (bf16[784,128]{1,0:T(8,128)(2,1)S(1)}, bf16[784,128]{1,0:T(8,128)(2,1)S(1)}, u32[]{:S(2)}, u32[]{:S(2)}) collective-permute-start(bf16[784,128]{1,0:T(8,128)(2,1)S(1)} %get-tuple-element.47.refs_0_), channel_id=1, source_target_pairs={{0,12},{4,0},{8,4},{12,8},{1,13},{5,1},{9,5},{13,9},{2,14},{6,2},{... | collective-permute-start | bytes 602120 | tf_op jit(solution)/shard_map/ppermute | solution.py:596
  92.5 8.2 %factor_bottom.1.refs_1_ = bf16[272,128]{1,0:T(8,128)(2,1)S(1)} custom-call(f32[256,256]{1,0:T(8,128)S(1)} %get-tuple-element.48.refs_0_), custom_call_target="tpu_custom_call" | custom-call | flops 8999999488 | bytes 1048576 | tf_op jit(solution)/shard_map/factor_bottom/pallas_call | solution.py:580
  101.4 1.5 %collective-permute-start.18 = (bf16[272,128]{1,0:T(8,128)(2,1)S(1)}, bf16[272,128]{1,0:T(8,128)(2,1)S(1)}, u32[]{:S(2)}, u32[]{:S(2)}) collective-permute-start(bf16[272,128]{1,0:T(8,128)(2,1)S(1)} %factor_bottom.1.refs_1_), channel_id=1, source_target_pairs={{0,8},{4,12},{8,0},{12,4},{1,9},{5,13},{9,1},{13,5},{2,10},{6,14},... | collective-permute-start | bytes 208904 | tf_op jit(solution)/shard_map/ppermute | solution.py:596
  102.9 3.5 %whiten_top.3.refs_5_ = f32[4,512,2048]{2,1,0:T(8,128)} custom-call(s32[4]{0:T(128)S(1)} %pad_add_fusion.order, bf16[784,128]{1,0:T(8,128)(2,1)S(1)} %get-tuple-element.47.refs_0_, bf16[272,128]{1,0:T(8,128)(2,1)S(1)} %factor_bottom.1.refs_1_, bf16[2048,2048]{1,0:T(8,128)(2,1)S(1)} %bitcast.22, bf16[2048,2048]{1,0:T(8,128)(2,1)S(1)} %bitcast.22, ...), custom_call_target="tpu_custom_call" | custom-call | flops 4000000000 | bytes 1048576 | tf_op jit(solution)/shard_map/whiten_top/pallas_call | solution.py:622
  106.4 3.2 %collective-permute-start.20 = (bf16[272,128]{1,0:T(8,128)(2,1)S(1)}, bf16[272,128]{1,0:T(8,128)(2,1)S(1)}, u32[]{:S(2)}, u32[]{:S(2)}) collective-permute-start(bf16[272,128]{1,0:T(8,128)(2,1)S(1)} %factor_bottom.1.refs_1_), channel_id=1, source_target_pairs={{0,12},{4,0},{8,4},{12,8},{1,13},{5,1},{9,5},{13,9},{2,14},{6,2},{... | collective-permute-start | bytes 208904 | tf_op jit(solution)/shard_map/ppermute | solution.py:596
  109.6 2.8 %whiten_top.4.refs_5_ = f32[4,512,2048]{2,1,0:T(8,128)} custom-call(s32[4]{0:T(128)S(1)} %pad_add_fusion.order, bf16[784,128]{1,0:T(8,128)(2,1)S(1)} %collective-permute-done.22.refs_0_, bf16[2048,2048]{1,0:T(8,128)(2,1)S(1)} %bitcast.22, bf16[2048,2048]{1,0:T(8,128)(2,1)S(1)} %bitcast.22, ...), custom_call_target="tpu_custom_call", output_to_operand_aliasing={{}: (6, {})} | custom-call | flops 2000000000 | bytes 1048576 | tf_op jit(solution)/shard_map/whiten_top/pallas_call | solution.py:622
  112.4 2.3 %whiten_bottom.1.refs_8_ = f32[4,512,2048]{2,1,0:T(8,128)} custom-call(s32[4]{0:T(128)S(1)} %pad_add_fusion.order, bf16[272,128]{1,0:T(8,128)(2,1)S(1)} %collective-permute-done.21.refs_0_, bf16[2048,2048]{1,0:T(8,128)(2,1)S(1)} %bitcast.22, bf16[2048,2048]{1,0:T(8,128)(2,1)S(1)} %bitcast.22, ...), custom_call_target="tpu_custom_call", output_to_operand_aliasing={{}: (6, {})} | custom-call | flops 2000000000 | bytes 1048576 | tf_op jit(solution)/shard_map/whiten_bottom/pallas_call | solution.py:622
  114.8 9.3 %whiten_top.5 = f32[4,512,2048]{2,1,0:T(8,128)} custom-call(s32[4]{0:T(128)S(1)} %pad_add_fusion.order, bf16[784,128]{1,0:T(8,128)(2,1)S(1)} %collective-permute-done.17.refs_0_, bf16[272,128]{1,0:T(8,128)(2,1)S(1)} %collective-permute-done.18.refs_1_, bf16[784,128]{1,0:T(8,128)(2,1)S(1)} %collective-permute-done.19.refs_2_, ...), custom_call_target="tpu_custom_call", output_to_operand_aliasing={{}: (9, {})} | custom-call | flops 8000000000 | bytes 1048576 | tf_op jit(solution)/shard_map/whiten_top/pallas_call | solution.py:622
  (58 shorter events, 10.0 us)
Async XLA Ops:
  0.0 18.9 %collective-permute-start = (bf16[256,8192]{1,0:T(8,128)(2,1)}, bf16[256,8192]{1,0:T(8,128)(2,1)}, u32[]{:S(2)}, u32[]{:S(2)}) collective-permute-start(bf16[256,8192]{1,0:T(8,128)(2,1)} %bitcast.23), channel_id=1, source_target_pairs={{0,1},{1,0},{2,3},{3,2},{4,5},{5,4},{6,7},{7,6},{8,9},{9,8},{10,11... | collective-permute-start | bytes 12582920 | tf_op jit(solution)/shard_map/ppermute | solution.py:528
  0.5 9.7 %collective-permute-start.1 = (bf16[256,1024]{1,0:T(8,128)(2,1)}, bf16[256,1024]{1,0:T(8,128)(2,1)S(1)}, u32[]{:S(2)}, u32[]{:S(2)}) collective-permute-start(bf16[256,1024]{1,0:T(8,128)(2,1)} %bitcast.36), channel_id=1, source_target_pairs={{0,1},{1,0},{2,3},{3,2},{4,5},{5,4},{6,7},{7,6},{8,9},{9,8},{10,11... | collective-permute-start | bytes 1572872 | tf_op jit(solution)/shard_map/ppermute | solution.py:528
  0.5 17.7 %collective-permute-start.2 = (bf16[256,1024]{1,0:T(8,128)(2,1)}, bf16[256,1024]{1,0:T(8,128)(2,1)}, u32[]{:S(2)}, u32[]{:S(2)}) collective-permute-start(bf16[256,1024]{1,0:T(8,128)(2,1)} %bitcast.45), channel_id=1, source_target_pairs={{0,1},{1,0},{2,3},{3,2},{4,5},{5,4},{6,7},{7,6},{8,9},{9,8},{10,11... | collective-permute-start | bytes 1572872 | tf_op jit(solution)/shard_map/ppermute | solution.py:528
  4.3 15.9 %collective-permute-start.5 = (bf16[256,768]{1,0:T(8,128)(2,1)}, bf16[256,768]{1,0:T(8,128)(2,1)S(1)}, u32[]{:S(2)}, u32[]{:S(2)}) collective-permute-start(bf16[256,768]{1,0:T(8,128)(2,1)} %get-tuple-element.31), channel_id=1, source_target_pairs={{0,2},{1,3},{2,0},{3,1},{4,6},{5,7},{6,4},{7,5},{8,10},{9,11},{10,... | collective-permute-start | bytes 1179656 | tf_op jit(solution)/shard_map/ppermute | solution.py:546
  6.8 18.2 %collective-permute-start.6 = (bf16[256,768]{1,0:T(8,128)(2,1)}, bf16[256,768]{1,0:T(8,128)(2,1)S(1)}, u32[]{:S(2)}, u32[]{:S(2)}) collective-permute-start(bf16[256,768]{1,0:T(8,128)(2,1)} %get-tuple-element.32), channel_id=1, source_target_pairs={{0,3},{1,2},{2,1},{3,0},{4,7},{5,6},{6,5},{7,4},{8,11},{9,10},{10,... | collective-permute-start | bytes 1179656 | tf_op jit(solution)/shard_map/ppermute | solution.py:546
  10.2 2.2 %copy-start = (bf16[1,256,8192]{2,1,0:T(8,128)(2,1)S(1)}, bf16[1,256,8192]{2,1,0:T(8,128)(2,1)}, u32[]{:S(2)}) copy-start(bf16[1,256,8192]{2,1,0:T(8,128)(2,1)} %param.6) | copy-start | bytes 12582916
  12.4 1.0 copy-start.2
  13.4 1.0 copy-start.4
  14.5 3.1 %copy-start.1 = (bf16[1,256,8192]{2,1,0:T(8,128)(2,1)S(1)}, bf16[1,256,8192]{2,1,0:T(8,128)(2,1)}, u32[]{:S(2)}) copy-start(bf16[1,256,8192]{2,1,0:T(8,128)(2,1)} %param.6) | copy-start | bytes 12582916
  14.5 10.6 %copy-start.3 = (bf16[1,256,1024]{2,1,0:T(8,128)(2,1)S(1)}, bf16[1,256,1024]{2,1,0:T(8,128)(2,1)}, u32[]{:S(2)}) copy-start(bf16[1,256,1024]{2,1,0:T(8,128)(2,1)} %param.7) | copy-start | bytes 1572868
  14.5 10.6 %copy-start.5 = (bf16[1,256,1024]{2,1,0:T(8,128)(2,1)S(1)}, bf16[1,256,1024]{2,1,0:T(8,128)(2,1)}, u32[]{:S(2)}) copy-start(bf16[1,256,1024]{2,1,0:T(8,128)(2,1)} %param.8) | copy-start | bytes 1572868
  15.2 22.7 %collective-permute-start.3 = (bf16[256,768]{1,0:T(8,128)(2,1)S(1)}, bf16[256,768]{1,0:T(8,128)(2,1)S(1)}, u32[]{:S(2)}, u32[]{:S(2)}) collective-permute-start(bf16[256,768]{1,0:T(8,128)(2,1)S(1)} %get-tuple-element.29), channel_id=1, source_target_pairs={{0,2},{1,3},{2,0},{3,1},{4,6},{5,7},{6,4},{7,5},{8,10},{9,11},{10,... | collective-permute-start | bytes 1179656 | tf_op jit(solution)/shard_map/ppermute | solution.py:546
  18.2 23.7 %collective-permute-start.4 = (bf16[256,768]{1,0:T(8,128)(2,1)S(1)}, bf16[256,768]{1,0:T(8,128)(2,1)S(1)}, u32[]{:S(2)}, u32[]{:S(2)}) collective-permute-start(bf16[256,768]{1,0:T(8,128)(2,1)S(1)} %get-tuple-element.30), channel_id=1, source_target_pairs={{0,3},{1,2},{2,1},{3,0},{4,7},{5,6},{6,5},{7,4},{8,11},{9,10},{10,... | collective-permute-start | bytes 1179656 | tf_op jit(solution)/shard_map/ppermute | solution.py:546
  33.0 17.0 %collective-permute-start.8 = (f32[520,128]{1,0:T(8,128)S(1)}, f32[520,128]{1,0:T(8,128)S(1)}, u32[]{:S(2)}, u32[]{:S(2)}) collective-permute-start(f32[520,128]{1,0:T(8,128)S(1)} %get-tuple-element.36), channel_id=1, source_target_pairs={{0,4},{4,8},{8,12},{12,0},{1,5},{5,9},{9,13},{13,1},{2,6},{6,10},{... | collective-permute-start | bytes 798728 | tf_op jit(solution)/shard_map/ppermute | solution.py:556
  34.1 17.1 %collective-permute-start.7 = (f32[520,128]{1,0:T(8,128)S(1)}, f32[520,128]{1,0:T(8,128)S(1)}, u32[]{:S(2)}, u32[]{:S(2)}) collective-permute-start(f32[520,128]{1,0:T(8,128)S(1)} %get-tuple-element.34), channel_id=1, source_target_pairs={{0,4},{4,8},{8,12},{12,0},{1,5},{5,9},{9,13},{13,1},{2,6},{6,10},{... | collective-permute-start | bytes 798728 | tf_op jit(solution)/shard_map/ppermute | solution.py:556
  36.4 18.6 %collective-permute-start.11 = (bf16[256,512]{1,0:T(8,128)(2,1)S(1)}, bf16[256,512]{1,0:T(8,128)(2,1)S(1)}, u32[]{:S(2)}, u32[]{:S(2)}) collective-permute-start(bf16[256,512]{1,0:T(8,128)(2,1)S(1)} %get-tuple-element.43), channel_id=1, source_target_pairs={{0,2},{1,3},{2,0},{3,1},{4,6},{5,7},{6,4},{7,5},{8,10},{9,11},{10,... | collective-permute-start | bytes 786440 | tf_op jit(solution)/shard_map/ppermute | solution.py:546
  37.9 17.7 %collective-permute-start.12 = (bf16[256,512]{1,0:T(8,128)(2,1)S(1)}, bf16[256,512]{1,0:T(8,128)(2,1)S(1)}, u32[]{:S(2)}, u32[]{:S(2)}) collective-permute-start(bf16[256,512]{1,0:T(8,128)(2,1)S(1)} %get-tuple-element.44), channel_id=1, source_target_pairs={{0,3},{1,2},{2,1},{3,0},{4,7},{5,6},{6,5},{7,4},{8,11},{9,10},{10,... | collective-permute-start | bytes 786440 | tf_op jit(solution)/shard_map/ppermute | solution.py:546
  50.1 13.4 %collective-permute-start.15 = (f32[520,128]{1,0:T(8,128)S(1)}, f32[520,128]{1,0:T(8,128)S(1)}, u32[]{:S(2)}, u32[]{:S(2)}) collective-permute-start(f32[520,128]{1,0:T(8,128)S(1)} %add.58), channel_id=1, source_target_pairs={{0,4},{4,8},{8,12},{12,0},{1,5},{5,9},{9,13},{13,1},{2,6},{6,10},{... | collective-permute-start | bytes 798728 | tf_op jit(solution)/shard_map/ppermute | solution.py:556
  51.2 15.6 %collective-permute-start.13 = (f32[520,128]{1,0:T(8,128)S(1)}, f32[520,128]{1,0:T(8,128)S(1)}, u32[]{:S(2)}, u32[]{:S(2)}) collective-permute-start(f32[520,128]{1,0:T(8,128)S(1)} %add.57), channel_id=1, source_target_pairs={{0,4},{4,8},{8,12},{12,0},{1,5},{5,9},{9,13},{13,1},{2,6},{6,10},{... | collective-permute-start | bytes 798728 | tf_op jit(solution)/shard_map/ppermute | solution.py:556
  53.6 13.3 %collective-permute-start.10 = (bf16[256,512]{1,0:T(8,128)(2,1)S(1)}, bf16[256,512]{1,0:T(8,128)(2,1)S(1)}, u32[]{:S(2)}, u32[]{:S(2)}) collective-permute-start(bf16[256,512]{1,0:T(8,128)(2,1)S(1)} %get-tuple-element.38), channel_id=1, source_target_pairs={{0,3},{1,2},{2,1},{3,0},{4,7},{5,6},{6,5},{7,4},{8,11},{9,10},{10,... | collective-permute-start | bytes 786440 | tf_op jit(solution)/shard_map/ppermute | solution.py:546
  55.1 12.8 %collective-permute-start.9 = (bf16[256,512]{1,0:T(8,128)(2,1)S(1)}, bf16[256,512]{1,0:T(8,128)(2,1)S(1)}, u32[]{:S(2)}, u32[]{:S(2)}) collective-permute-start(bf16[256,512]{1,0:T(8,128)(2,1)S(1)} %get-tuple-element.37), channel_id=1, source_target_pairs={{0,2},{1,3},{2,0},{3,1},{4,6},{5,7},{6,4},{7,5},{8,10},{9,11},{10,... | collective-permute-start | bytes 786440 | tf_op jit(solution)/shard_map/ppermute | solution.py:546
  63.5 12.4 %collective-permute-start.16 = (f32[520,128]{1,0:T(8,128)S(1)}, f32[520,128]{1,0:T(8,128)S(1)}, u32[]{:S(2)}, u32[]{:S(2)}) collective-permute-start(f32[520,128]{1,0:T(8,128)S(1)} %add.60), channel_id=1, source_target_pairs={{0,4},{4,8},{8,12},{12,0},{1,5},{5,9},{9,13},{13,1},{2,6},{6,10},{... | collective-permute-start | bytes 798728 | tf_op jit(solution)/shard_map/ppermute | solution.py:556
  66.9 12.4 %collective-permute-start.14 = (f32[520,128]{1,0:T(8,128)S(1)}, f32[520,128]{1,0:T(8,128)S(1)}, u32[]{:S(2)}, u32[]{:S(2)}) collective-permute-start(f32[520,128]{1,0:T(8,128)S(1)} %add.59), channel_id=1, source_target_pairs={{0,4},{4,8},{8,12},{12,0},{1,5},{5,9},{9,13},{13,1},{2,6},{6,10},{... | collective-permute-start | bytes 798728 | tf_op jit(solution)/shard_map/ppermute | solution.py:556
  88.6 14.3 %slice-start = ((s8[8388608]{0:T(1024)(128)(4,1)}), s8[4194304]{0:T(1024)(128)(4,1)S(1)}, s32[]{:S(2)}) async-start(s8[8388608]{0:T(1024)(128)(4,1)} %bitcast.21), calls=%async_computation | async-start | bytes 8388608
  88.6 17.8 %collective-permute-start.22 = (bf16[784,128]{1,0:T(8,128)(2,1)S(1)}, bf16[784,128]{1,0:T(8,128)(2,1)S(1)}, u32[]{:S(2)}, u32[]{:S(2)}) collective-permute-start(bf16[784,128]{1,0:T(8,128)(2,1)S(1)} %get-tuple-element.47.refs_0_), channel_id=1, source_target_pairs={{0,4},{4,8},{8,12},{12,0},{1,5},{5,9},{9,13},{13,1},{2,6},{6,10},{... | collective-permute-start | bytes 602120 | tf_op jit(solution)/shard_map/ppermute | solution.py:596
  88.7 26.0 %collective-permute-start.17 = (bf16[784,128]{1,0:T(8,128)(2,1)S(1)}, bf16[784,128]{1,0:T(8,128)(2,1)S(1)}, u32[]{:S(2)}, u32[]{:S(2)}) collective-permute-start(bf16[784,128]{1,0:T(8,128)(2,1)S(1)} %get-tuple-element.47.refs_0_), channel_id=1, source_target_pairs={{0,8},{4,12},{8,0},{12,4},{1,9},{5,13},{9,1},{13,5},{2,10},{6,14},... | collective-permute-start | bytes 602120 | tf_op jit(solution)/shard_map/ppermute | solution.py:596
  90.0 24.7 %collective-permute-start.19 = (bf16[784,128]{1,0:T(8,128)(2,1)S(1)}, bf16[784,128]{1,0:T(8,128)(2,1)S(1)}, u32[]{:S(2)}, u32[]{:S(2)}) collective-permute-start(bf16[784,128]{1,0:T(8,128)(2,1)S(1)} %get-tuple-element.47.refs_0_), channel_id=1, source_target_pairs={{0,12},{4,0},{8,4},{12,8},{1,13},{5,1},{9,5},{13,9},{2,14},{6,2},{... | collective-permute-start | bytes 602120 | tf_op jit(solution)/shard_map/ppermute | solution.py:596
  92.5 10.4 %slice-start.1 = ((s8[8388608]{0:T(1024)(128)(4,1)}), s8[4194304]{0:T(1024)(128)(4,1)S(1)}, s32[]{:S(2)}) async-start(s8[8388608]{0:T(1024)(128)(4,1)} %bitcast.21), calls=%async_computation.1 | async-start | bytes 8388608
  100.8 11.6 %collective-permute-start.21 = (bf16[272,128]{1,0:T(8,128)(2,1)S(1)}, bf16[272,128]{1,0:T(8,128)(2,1)S(1)}, u32[]{:S(2)}, u32[]{:S(2)}) collective-permute-start(bf16[272,128]{1,0:T(8,128)(2,1)S(1)} %factor_bottom.1.refs_1_), channel_id=1, source_target_pairs={{0,4},{4,8},{8,12},{12,0},{1,5},{5,9},{9,13},{13,1},{2,6},{6,10},{... | collective-permute-start | bytes 208904 | tf_op jit(solution)/shard_map/ppermute | solution.py:596
  101.4 13.4 %collective-permute-start.18 = (bf16[272,128]{1,0:T(8,128)(2,1)S(1)}, bf16[272,128]{1,0:T(8,128)(2,1)S(1)}, u32[]{:S(2)}, u32[]{:S(2)}) collective-permute-start(bf16[272,128]{1,0:T(8,128)(2,1)S(1)} %factor_bottom.1.refs_1_), channel_id=1, source_target_pairs={{0,8},{4,12},{8,0},{12,4},{1,9},{5,13},{9,1},{13,5},{2,10},{6,14},... | collective-permute-start | bytes 208904 | tf_op jit(solution)/shard_map/ppermute | solution.py:596
  106.4 8.3 %collective-permute-start.20 = (bf16[272,128]{1,0:T(8,128)(2,1)S(1)}, bf16[272,128]{1,0:T(8,128)(2,1)S(1)}, u32[]{:S(2)}, u32[]{:S(2)}) collective-permute-start(bf16[272,128]{1,0:T(8,128)(2,1)S(1)} %factor_bottom.1.refs_1_), channel_id=1, source_target_pairs={{0,12},{4,0},{8,4},{12,8},{1,13},{5,1},{9,5},{13,9},{2,14},{6,2},{... | collective-permute-start | bytes 208904 | tf_op jit(solution)/shard_map/ppermute | solution.py:596

commit v9 on v8

--- a/solution.py
+++ b/solution.py
@@ -591,15 +591,21 @@
     if in_ring:
         top, rest = factor_top(*grams[ring - 1], *carried)
 
+        paired = ring & (ring - 1) == 0
+        distances = [1] + list(range(ring - 1, 1, -1)) if paired else list(range(1, ring))
+
+        def partner(z, d):
+            return z ^ d if paired else (z + d) % ring
+
         def shared(array):
             return [array] + [
-                lax.ppermute(array, "dp", [(z, (z + d) % ring) for z in range(ring)]) for d in range(1, ring)
+                lax.ppermute(array, "dp", [(z, partner(z, d)) for z in range(ring)]) for d in distances
             ]
 
         tops = shared(top)
         bottom = factor_bottom(rest)
         bottoms = shared(bottom)
-        order = jnp.stack([lax.rem(place - d + ring, ring) for d in range(ring)])
+        order = jnp.stack([place] + [place ^ d if paired else lax.rem(place - d + ring, ring) for d in distances])
     else:
         halves = [factor_top(*[lax.psum(part, "dp") for part in grams[t]]) for t in range(blocks)]
         tops = [top for top, _ in halves]

time: 124 us -> 125 us (level); the launches traced: 124 us -> 124 us
  Pallas kernels: 73.3 us -> 71.4 us
    ppermute x6, starting transfers between devices: 7.88 us -> 10.6 us  [shards(): lax.ppermute(part, 'dp', [(z, (z + 1) % ring) for z in range(ring)])]
    pallas_call x4, Pallas kernels: 32 us -> 29.8 us  [grams_of(): pl.pallas_call(functools.partial(attention_kernel, chips=chips, spans=spa...]
    ppermute x6, starting transfers between devices: 9.19 us -> 7.17 us  [shared(): lax.ppermute(array, 'dp', [(z, partner(z, d)) for z in range(ring)])]
    ppermute x6, waiting for transfers between devices: 0.02 us -> 2 us  [shared(): lax.ppermute(array, 'dp', [(z, partner(z, d)) for z in range(ring)])]
  transfers between devices with their start and end apart: 23 -> 23, of which waited for: 5 -> 6; matrix products, arithmetic and copies ran while one was open for 3% -> 3% of each run, Pallas kernels for 44% -> 42%
where the time goes in v9:
time: 125 us; the launch traced here: 124 us
  Pallas kernels  71.4 us (57%)
  starting transfers between devices  27.4 us (22%)
  waiting for transfers between devices  16.4 us (13%)
  local copies, waits for them, and re-layouts  7.3 us (6%)
    pallas_call x4, Pallas kernels, grams_of(): pl.pallas_call(functools.partial(attention_kernel, chips=chips, spans=spa...  29.8 us
    pallas_call x4, Pallas kernels, whiten(): pl.pallas_call(functools.partial(whiten_kernel, blocks=count, starts=star...  18.1 us
    ppermute x6, starting transfers between devices, shards(): lax.ppermute(part, 'dp', [(z, (z + 1) % ring) for z in range(ring)])  10.6 us
    ppermute x8, waiting for transfers between devices, shards(): lax.ppermute(part, 'seq', moved(*where))  9.64 us
    pallas_call x1, Pallas kernels, factor_top(): pl.pallas_call(functools.partial(factor_kernel, start=0, stop=half, recei...  9.33 us
    ppermute x8, starting transfers between devices, shards(): lax.ppermute(part, 'seq', moved(*where))  8.66 us
    pallas_call x1, Pallas kernels, factor_bottom(): pl.pallas_call(functools.partial(factor_kernel, start=half, stop=BLOCK_W,...  8.22 us
    ppermute x6, starting transfers between devices, shared(): lax.ppermute(array, 'dp', [(z, partner(z, d)) for z in range(ring)])  7.17 us
  transfers between devices with their start and end apart: 23, of which 6 were waited for; matrix products, arithmetic and copies ran while one was open for 3% of the time, Pallas kernels for 42%

profile of v9, /device:TPU:0, one launch (start us, length us, event | category | flops | bytes accessed | tf_op | source)
XLA Modules:
  0.0 123.8 jit_solution(17081758110885187101)
XLA Ops:
  1.6 2.7 %cut_piece.6 = (bf16[256,768]{1,0:T(8,128)(2,1)}, bf16[256,768]{1,0:T(8,128)(2,1)}) custom-call(s32[3]{0:T(128)} %pad_add_fusion.1.meta, bf16[256,8192]{1,0:T(8,128)(2,1)} %bitcast.25, bf16[256,1024]{1,0:T(8,128)(2,1)} %bitcast.38, bf16[256,1024]{1,0:T(8,128)(2,1)} %bitcast.47, bf16[256,8192]{1,0:T(8,128)(2,1)} %bitcast.26, bf16[256,1024]{1,0:T(8,128)(2,1)} %bitcast.39, ...), custom_call_target="tpu_custom_call" | custom-call | bytes 2097152 | tf_op jit(solution)/shard_map/cut_piece/pallas_call | solution.py:458
  4.3 2.5 %collective-permute-start.5 = (bf16[256,768]{1,0:T(8,128)(2,1)}, bf16[256,768]{1,0:T(8,128)(2,1)S(1)}, u32[]{:S(2)}, u32[]{:S(2)}) collective-permute-start(bf16[256,768]{1,0:T(8,128)(2,1)} %get-tuple-element.31), channel_id=1, source_target_pairs={{0,2},{1,3},{2,0},{3,1},{4,6},{5,7},{6,4},{7,5},{8,10},{9,11},{10,... | collective-permute-start | bytes 1179656 | tf_op jit(solution)/shard_map/ppermute | solution.py:546
  10.2 2.2 %copy-done = bf16[1,256,8192]{2,1,0:T(8,128)(2,1)S(1)} copy-done((bf16[1,256,8192]{2,1,0:T(8,128)(2,1)S(1)}, bf16[1,256,8192]{2,1,0:T(8,128)(2,1)}, u32[]{:S(2)}) %copy-start) | copy-done | bytes 4194328
  12.4 1.0 copy-done.2
  15.1 1.8 %collective-permute-start.3 = (bf16[256,768]{1,0:T(8,128)(2,1)S(1)}, bf16[256,768]{1,0:T(8,128)(2,1)S(1)}, u32[]{:S(2)}, u32[]{:S(2)}) collective-permute-start(bf16[256,768]{1,0:T(8,128)(2,1)S(1)} %get-tuple-element.29), channel_id=1, source_target_pairs={{0,2},{1,3},{2,0},{3,1},{4,6},{5,7},{6,4},{7,5},{8,10},{9,11},{10,... | collective-permute-start | bytes 1179656 | tf_op jit(solution)/shard_map/ppermute | solution.py:546
  18.9 1.3 %cut_peer.1.refs_1_.refs_6_.refs_7_ = bf16[256,2560]{1,0:T(8,128)(2,1)S(1)} custom-call(s32[1]{0:T(128)} %bitcast.4.meta, bf16[256,8192]{1,0:T(8,128)(2,1)} %collective-permute-done.refs_0_, bf16[256,1024]{1,0:T(8,128)(2,1)S(1)} %collective-permute-done.1.refs_1_.refs_2_.refs_6_, bf16[256,1024]{1,0:T(8,128)(2,1)} %collective-permute-done.2.refs_2_), custom_call_target="tpu_custom_call" | custom-call | bytes 2097152 | tf_op jit(solution)/shard_map/cut_peer/pallas_call | solution.py:458
  20.2 4.8 %collective-permute-done.6.refs_9_.refs_3_ = bf16[256,768]{1,0:T(8,128)(2,1)S(1)} collective-permute-done((bf16[256,768]{1,0:T(8,128)(2,1)}, bf16[256,768]{1,0:T(8,128)(2,1)S(1)}, u32[]{:S(2)}, u32[]{:S(2)}) %collective-permute-start.6) | collective-permute-done | bytes 393248 | tf_op jit(solution)/shard_map/ppermute | solution.py:546
  25.0 7.4 %attention_outer_products.5 = (f32[520,128]{1,0:T(8,128)S(1)}, f32[520,128]{1,0:T(8,128)S(1)}) custom-call(s32[20]{0:T(128)S(1)} %concatenate.14.meta, bf16[256,8192]{1,0:T(8,128)(2,1)S(1)} %bitcast.33, bf16[256,2560]{1,0:T(8,128)(2,1)S(1)} %cut_peer.1.refs_1_.refs_6_.refs_7_, bf16[256,768]{1,0:T(8,128)(2,1)S(1)} %collective-permute-done.5.refs_8_.refs_2_, ...), custom_call_target="tpu_custom_call" | custom-call | flops 14000000000 | bytes 1048576 | tf_op jit(solution)/shard_map/attention_outer_products/pallas_call | solution.py:489
  32.4 2.5 %collective-permute-start.8 = (f32[520,128]{1,0:T(8,128)S(1)}, f32[520,128]{1,0:T(8,128)S(1)}, u32[]{:S(2)}, u32[]{:S(2)}) collective-permute-start(f32[520,128]{1,0:T(8,128)S(1)} %get-tuple-element.36), channel_id=1, source_target_pairs={{0,4},{4,8},{8,12},{12,0},{1,5},{5,9},{9,13},{13,1},{2,6},{6,10},{... | collective-permute-start | bytes 798728 | tf_op jit(solution)/shard_map/ppermute | solution.py:556
  34.9 1.5 %collective-permute-start.7 = (f32[520,128]{1,0:T(8,128)S(1)}, f32[520,128]{1,0:T(8,128)S(1)}, u32[]{:S(2)}, u32[]{:S(2)}) collective-permute-start(f32[520,128]{1,0:T(8,128)S(1)} %get-tuple-element.34), channel_id=1, source_target_pairs={{0,4},{4,8},{8,12},{12,0},{1,5},{5,9},{9,13},{13,1},{2,6},{6,10},{... | collective-permute-start | bytes 798728 | tf_op jit(solution)/shard_map/ppermute | solution.py:556
  36.4 1.5 %collective-permute-start.11 = (bf16[256,512]{1,0:T(8,128)(2,1)S(1)}, bf16[256,512]{1,0:T(8,128)(2,1)S(1)}, u32[]{:S(2)}, u32[]{:S(2)}) collective-permute-start(bf16[256,512]{1,0:T(8,128)(2,1)S(1)} %get-tuple-element.43), channel_id=1, source_target_pairs={{0,2},{1,3},{2,0},{3,1},{4,6},{5,7},{6,4},{7,5},{8,10},{9,11},{10,... | collective-permute-start | bytes 786440 | tf_op jit(solution)/shard_map/ppermute | solution.py:546
  37.9 4.0 %collective-permute-done.4.refs_3_.refs_11_ = bf16[256,768]{1,0:T(8,128)(2,1)S(1)} collective-permute-done((bf16[256,768]{1,0:T(8,128)(2,1)S(1)}, bf16[256,768]{1,0:T(8,128)(2,1)S(1)}, u32[]{:S(2)}, u32[]{:S(2)}) %collective-permute-start.4) | collective-permute-done | bytes 393248 | tf_op jit(solution)/shard_map/ppermute | solution.py:546
  41.9 7.6 %attention_outer_products.4 = (f32[520,128]{1,0:T(8,128)S(1)}, f32[520,128]{1,0:T(8,128)S(1)}) custom-call(s32[20]{0:T(128)S(1)} %concatenate.13.meta, bf16[256,8192]{1,0:T(8,128)(2,1)S(1)} %bitcast.34, bf16[256,2560]{1,0:T(8,128)(2,1)S(1)} %cut_peer.1.refs_1_.refs_6_.refs_7_, bf16[256,768]{1,0:T(8,128)(2,1)S(1)} %collective-permute-done.3.refs_2_.refs_10_, ...), custom_call_target="tpu_custom_call" | custom-call | flops 14000000000 | bytes 1048576 | tf_op jit(solution)/shard_map/attention_outer_products/pallas_call | solution.py:489
  49.5 2.5 %collective-permute-start.15 = (f32[520,128]{1,0:T(8,128)S(1)}, f32[520,128]{1,0:T(8,128)S(1)}, u32[]{:S(2)}, u32[]{:S(2)}) collective-permute-start(f32[520,128]{1,0:T(8,128)S(1)} %add.33), channel_id=1, source_target_pairs={{0,4},{4,8},{8,12},{12,0},{1,5},{5,9},{9,13},{13,1},{2,6},{6,10},{... | collective-permute-start | bytes 798728 | tf_op jit(solution)/shard_map/ppermute | solution.py:556
  52.0 1.6 %collective-permute-start.13 = (f32[520,128]{1,0:T(8,128)S(1)}, f32[520,128]{1,0:T(8,128)S(1)}, u32[]{:S(2)}, u32[]{:S(2)}) collective-permute-start(f32[520,128]{1,0:T(8,128)S(1)} %add.32), channel_id=1, source_target_pairs={{0,4},{4,8},{8,12},{12,0},{1,5},{5,9},{9,13},{13,1},{2,6},{6,10},{... | collective-permute-start | bytes 798728 | tf_op jit(solution)/shard_map/ppermute | solution.py:556
  53.6 1.4 %collective-permute-start.10 = (bf16[256,512]{1,0:T(8,128)(2,1)S(1)}, bf16[256,512]{1,0:T(8,128)(2,1)S(1)}, u32[]{:S(2)}, u32[]{:S(2)}) collective-permute-start(bf16[256,512]{1,0:T(8,128)(2,1)S(1)} %get-tuple-element.38), channel_id=1, source_target_pairs={{0,3},{1,2},{2,1},{3,0},{4,7},{5,6},{6,5},{7,4},{8,11},{9,10},{10,... | collective-permute-start | bytes 786440 | tf_op jit(solution)/shard_map/ppermute | solution.py:546
  55.6 7.4 %attention_outer_products.7 = (f32[520,128]{1,0:T(8,128)S(1)}, f32[520,128]{1,0:T(8,128)S(1)}) custom-call(s32[20]{0:T(128)S(1)} %concatenate.15.meta, bf16[256,8192]{1,0:T(8,128)(2,1)S(1)} %bitcast.35, bf16[256,2560]{1,0:T(8,128)(2,1)S(1)} %cut_peer.1.refs_1_.refs_6_.refs_7_, bf16[256,512]{1,0:T(8,128)(2,1)S(1)} %collective-permute-done.11.refs_2_, ...), custom_call_target="tpu_custom_call" | custom-call | flops 14000000000 | bytes 1048576 | tf_op jit(solution)/shard_map/attention_outer_products/pallas_call | solution.py:489
  63.0 2.4 %collective-permute-start.16 = (f32[520,128]{1,0:T(8,128)S(1)}, f32[520,128]{1,0:T(8,128)S(1)}, u32[]{:S(2)}, u32[]{:S(2)}) collective-permute-start(f32[520,128]{1,0:T(8,128)S(1)} %add.35), channel_id=1, source_target_pairs={{0,4},{4,8},{8,12},{12,0},{1,5},{5,9},{9,13},{13,1},{2,6},{6,10},{... | collective-permute-start | bytes 798728 | tf_op jit(solution)/shard_map/ppermute | solution.py:556
  65.3 1.4 %collective-permute-done.13 = f32[520,128]{1,0:T(8,128)S(1)} collective-permute-done((f32[520,128]{1,0:T(8,128)S(1)}, f32[520,128]{1,0:T(8,128)S(1)}, u32[]{:S(2)}, u32[]{:S(2)}) %collective-permute-start.13) | collective-permute-done | bytes 266272 | tf_op jit(solution)/shard_map/ppermute | solution.py:556
  67.8 7.6 %attention_outer_products.6 = (f32[520,128]{1,0:T(8,128)S(1)}, f32[520,128]{1,0:T(8,128)S(1)}) custom-call(s32[20]{0:T(128)S(1)} %concatenate.12.meta, bf16[256,8192]{1,0:T(8,128)(2,1)S(1)} %bitcast.36, bf16[256,2560]{1,0:T(8,128)(2,1)S(1)} %cut_peer.1.refs_1_.refs_6_.refs_7_, bf16[256,512]{1,0:T(8,128)(2,1)S(1)} %collective-permute-done.9.refs_2_, ...), custom_call_target="tpu_custom_call" | custom-call | flops 14000000000 | bytes 1048576 | tf_op jit(solution)/shard_map/attention_outer_products/pallas_call | solution.py:489
  75.4 3.3 %collective-permute-done.14.refs_2_ = f32[520,128]{1,0:T(8,128)S(1)} collective-permute-done((f32[520,128]{1,0:T(8,128)S(1)}, f32[520,128]{1,0:T(8,128)S(1)}, u32[]{:S(2)}, u32[]{:S(2)}) %collective-permute-start.14) | collective-permute-done | bytes 266272 | tf_op jit(solution)/shard_map/ppermute | solution.py:556
  78.7 9.3 %factor_top.1 = (bf16[784,128]{1,0:T(8,128)(2,1)S(1)}, f32[256,256]{1,0:T(8,128)S(1)}) custom-call(f32[520,128]{1,0:T(8,128)S(1)} %get-tuple-element.39.refs_0_, f32[520,128]{1,0:T(8,128)S(1)} %get-tuple-element.40.refs_1_, f32[520,128]{1,0:T(8,128)S(1)} %collective-permute-done.14.refs_2_, f32[520,128]{1,0:T(8,128)S(1)} %collective-permute-done.16.refs_3_), custom_call_target="tpu_custom_call" | custom-call | flops 10000000000 | bytes 1048576 | tf_op jit(solution)/shard_map/factor_top/pallas_call | solution.py:565
  88.6 1.5 %collective-permute-start.17 = (bf16[784,128]{1,0:T(8,128)(2,1)S(1)}, bf16[784,128]{1,0:T(8,128)(2,1)S(1)}, u32[]{:S(2)}, u32[]{:S(2)}) collective-permute-start(bf16[784,128]{1,0:T(8,128)(2,1)S(1)} %get-tuple-element.47.refs_0_), channel_id=1, source_target_pairs={{0,12},{4,8},{8,4},{12,0},{1,13},{5,9},{9,5},{13,1},{2,14},{6,10},... | collective-permute-start | bytes 602120 | tf_op jit(solution)/shard_map/ppermute | solution.py:602
  90.1 1.5 %collective-permute-start.19 = (bf16[784,128]{1,0:T(8,128)(2,1)S(1)}, bf16[784,128]{1,0:T(8,128)(2,1)S(1)}, u32[]{:S(2)}, u32[]{:S(2)}) collective-permute-start(bf16[784,128]{1,0:T(8,128)(2,1)S(1)} %get-tuple-element.47.refs_0_), channel_id=1, source_target_pairs={{0,8},{4,12},{8,0},{12,4},{1,9},{5,13},{9,1},{13,5},{2,10},{6,14},... | collective-permute-start | bytes 602120 | tf_op jit(solution)/shard_map/ppermute | solution.py:602
  91.6 8.2 %factor_bottom.1.refs_1_ = bf16[272,128]{1,0:T(8,128)(2,1)S(1)} custom-call(f32[256,256]{1,0:T(8,128)S(1)} %get-tuple-element.48.refs_0_), custom_call_target="tpu_custom_call" | custom-call | flops 8999999488 | bytes 1048576 | tf_op jit(solution)/shard_map/factor_bottom/pallas_call | solution.py:580
  99.8 1.5 %collective-permute-start.21 = (bf16[272,128]{1,0:T(8,128)(2,1)S(1)}, bf16[272,128]{1,0:T(8,128)(2,1)S(1)}, u32[]{:S(2)}, u32[]{:S(2)}) collective-permute-start(bf16[272,128]{1,0:T(8,128)(2,1)S(1)} %factor_bottom.1.refs_1_), channel_id=1, source_target_pairs={{0,4},{4,0},{8,12},{12,8},{1,5},{5,1},{9,13},{13,9},{2,6},{6,2},{1... | collective-permute-start | bytes 208904 | tf_op jit(solution)/shard_map/ppermute | solution.py:602
  101.3 1.5 %collective-permute-start.18 = (bf16[272,128]{1,0:T(8,128)(2,1)S(1)}, bf16[272,128]{1,0:T(8,128)(2,1)S(1)}, u32[]{:S(2)}, u32[]{:S(2)}) collective-permute-start(bf16[272,128]{1,0:T(8,128)(2,1)S(1)} %factor_bottom.1.refs_1_), channel_id=1, source_target_pairs={{0,12},{4,8},{8,4},{12,0},{1,13},{5,9},{9,5},{13,1},{2,14},{6,10},... | collective-permute-start | bytes 208904 | tf_op jit(solution)/shard_map/ppermute | solution.py:602
  102.8 3.5 %whiten_top.3.refs_5_ = f32[4,512,2048]{2,1,0:T(8,128)} custom-call(s32[4]{0:T(128)S(1)} %pad_add_fusion.order, bf16[784,128]{1,0:T(8,128)(2,1)S(1)} %get-tuple-element.47.refs_0_, bf16[272,128]{1,0:T(8,128)(2,1)S(1)} %factor_bottom.1.refs_1_, bf16[2048,2048]{1,0:T(8,128)(2,1)S(1)} %bitcast.23, bf16[2048,2048]{1,0:T(8,128)(2,1)S(1)} %bitcast.23, ...), custom_call_target="tpu_custom_call" | custom-call | flops 4000000000 | bytes 1048576 | tf_op jit(solution)/shard_map/whiten_top/pallas_call | solution.py:628
  107.0 2.8 %whiten_top.4.refs_5_ = f32[4,512,2048]{2,1,0:T(8,128)} custom-call(s32[4]{0:T(128)S(1)} %pad_add_fusion.order, bf16[784,128]{1,0:T(8,128)(2,1)S(1)} %collective-permute-done.22.refs_0_, bf16[2048,2048]{1,0:T(8,128)(2,1)S(1)} %bitcast.23, bf16[2048,2048]{1,0:T(8,128)(2,1)S(1)} %bitcast.23, ...), custom_call_target="tpu_custom_call", output_to_operand_aliasing={{}: (6, {})} | custom-call | flops 2000000000 | bytes 1048576 | tf_op jit(solution)/shard_map/whiten_top/pallas_call | solution.py:628
  109.8 2.3 %whiten_bottom.1.refs_8_ = f32[4,512,2048]{2,1,0:T(8,128)} custom-call(s32[4]{0:T(128)S(1)} %pad_add_fusion.order, bf16[272,128]{1,0:T(8,128)(2,1)S(1)} %collective-permute-done.21.refs_0_, bf16[2048,2048]{1,0:T(8,128)(2,1)S(1)} %bitcast.23, bf16[2048,2048]{1,0:T(8,128)(2,1)S(1)} %bitcast.23, ...), custom_call_target="tpu_custom_call", output_to_operand_aliasing={{}: (6, {})} | custom-call | flops 2000000000 | bytes 1048576 | tf_op jit(solution)/shard_map/whiten_bottom/pallas_call | solution.py:628
  112.1 2.0 %collective-permute-done.20.refs_3_ = bf16[272,128]{1,0:T(8,128)(2,1)S(1)} collective-permute-done((bf16[272,128]{1,0:T(8,128)(2,1)S(1)}, bf16[272,128]{1,0:T(8,128)(2,1)S(1)}, u32[]{:S(2)}, u32[]{:S(2)}) %collective-permute-start.20) | collective-permute-done | bytes 69664 | tf_op jit(solution)/shard_map/ppermute | solution.py:602
  114.1 9.5 %whiten_top.5 = f32[4,512,2048]{2,1,0:T(8,128)} custom-call(s32[4]{0:T(128)S(1)} %pad_add_fusion.order, bf16[784,128]{1,0:T(8,128)(2,1)S(1)} %collective-permute-done.17.refs_0_, bf16[272,128]{1,0:T(8,128)(2,1)S(1)} %collective-permute-done.18.refs_1_, bf16[784,128]{1,0:T(8,128)(2,1)S(1)} %collective-permute-done.19.refs_2_, ...), custom_call_target="tpu_custom_call", output_to_operand_aliasing={{}: (9, {})} | custom-call | flops 8000000000 | bytes 1048576 | tf_op jit(solution)/shard_map/whiten_top/pallas_call | solution.py:628
  (58 shorter events, 11.7 us)
Async XLA Ops:
  0.0 18.9 %collective-permute-start = (bf16[256,8192]{1,0:T(8,128)(2,1)}, bf16[256,8192]{1,0:T(8,128)(2,1)}, u32[]{:S(2)}, u32[]{:S(2)}) collective-permute-start(bf16[256,8192]{1,0:T(8,128)(2,1)} %bitcast.24), channel_id=1, source_target_pairs={{0,1},{1,0},{2,3},{3,2},{4,5},{5,4},{6,7},{7,6},{8,9},{9,8},{10,11... | collective-permute-start | bytes 12582920 | tf_op jit(solution)/shard_map/ppermute | solution.py:528
  0.5 9.7 %collective-permute-start.1 = (bf16[256,1024]{1,0:T(8,128)(2,1)}, bf16[256,1024]{1,0:T(8,128)(2,1)S(1)}, u32[]{:S(2)}, u32[]{:S(2)}) collective-permute-start(bf16[256,1024]{1,0:T(8,128)(2,1)} %bitcast.37), channel_id=1, source_target_pairs={{0,1},{1,0},{2,3},{3,2},{4,5},{5,4},{6,7},{7,6},{8,9},{9,8},{10,11... | collective-permute-start | bytes 1572872 | tf_op jit(solution)/shard_map/ppermute | solution.py:528
  0.5 17.6 %collective-permute-start.2 = (bf16[256,1024]{1,0:T(8,128)(2,1)}, bf16[256,1024]{1,0:T(8,128)(2,1)}, u32[]{:S(2)}, u32[]{:S(2)}) collective-permute-start(bf16[256,1024]{1,0:T(8,128)(2,1)} %bitcast.46), channel_id=1, source_target_pairs={{0,1},{1,0},{2,3},{3,2},{4,5},{5,4},{6,7},{7,6},{8,9},{9,8},{10,11... | collective-permute-start | bytes 1572872 | tf_op jit(solution)/shard_map/ppermute | solution.py:528
  4.3 15.9 %collective-permute-start.5 = (bf16[256,768]{1,0:T(8,128)(2,1)}, bf16[256,768]{1,0:T(8,128)(2,1)S(1)}, u32[]{:S(2)}, u32[]{:S(2)}) collective-permute-start(bf16[256,768]{1,0:T(8,128)(2,1)} %get-tuple-element.31), channel_id=1, source_target_pairs={{0,2},{1,3},{2,0},{3,1},{4,6},{5,7},{6,4},{7,5},{8,10},{9,11},{10,... | collective-permute-start | bytes 1179656 | tf_op jit(solution)/shard_map/ppermute | solution.py:546
  6.8 18.2 %collective-permute-start.6 = (bf16[256,768]{1,0:T(8,128)(2,1)}, bf16[256,768]{1,0:T(8,128)(2,1)S(1)}, u32[]{:S(2)}, u32[]{:S(2)}) collective-permute-start(bf16[256,768]{1,0:T(8,128)(2,1)} %get-tuple-element.32), channel_id=1, source_target_pairs={{0,3},{1,2},{2,1},{3,0},{4,7},{5,6},{6,5},{7,4},{8,11},{9,10},{10,... | collective-permute-start | bytes 1179656 | tf_op jit(solution)/shard_map/ppermute | solution.py:546
  10.2 2.2 %copy-start = (bf16[1,256,8192]{2,1,0:T(8,128)(2,1)S(1)}, bf16[1,256,8192]{2,1,0:T(8,128)(2,1)}, u32[]{:S(2)}) copy-start(bf16[1,256,8192]{2,1,0:T(8,128)(2,1)} %param.6) | copy-start | bytes 12582916
  12.4 1.0 copy-start.2
  13.4 1.0 copy-start.4
  14.4 3.1 %copy-start.1 = (bf16[1,256,8192]{2,1,0:T(8,128)(2,1)S(1)}, bf16[1,256,8192]{2,1,0:T(8,128)(2,1)}, u32[]{:S(2)}) copy-start(bf16[1,256,8192]{2,1,0:T(8,128)(2,1)} %param.6) | copy-start | bytes 12582916
  14.4 10.6 %copy-start.3 = (bf16[1,256,1024]{2,1,0:T(8,128)(2,1)S(1)}, bf16[1,256,1024]{2,1,0:T(8,128)(2,1)}, u32[]{:S(2)}) copy-start(bf16[1,256,1024]{2,1,0:T(8,128)(2,1)} %param.7) | copy-start | bytes 1572868
  14.4 10.6 %copy-start.5 = (bf16[1,256,1024]{2,1,0:T(8,128)(2,1)S(1)}, bf16[1,256,1024]{2,1,0:T(8,128)(2,1)}, u32[]{:S(2)}) copy-start(bf16[1,256,1024]{2,1,0:T(8,128)(2,1)} %param.8) | copy-start | bytes 1572868
  15.1 22.7 %collective-permute-start.3 = (bf16[256,768]{1,0:T(8,128)(2,1)S(1)}, bf16[256,768]{1,0:T(8,128)(2,1)S(1)}, u32[]{:S(2)}, u32[]{:S(2)}) collective-permute-start(bf16[256,768]{1,0:T(8,128)(2,1)S(1)} %get-tuple-element.29), channel_id=1, source_target_pairs={{0,2},{1,3},{2,0},{3,1},{4,6},{5,7},{6,4},{7,5},{8,10},{9,11},{10,... | collective-permute-start | bytes 1179656 | tf_op jit(solution)/shard_map/ppermute | solution.py:546
  18.1 23.7 %collective-permute-start.4 = (bf16[256,768]{1,0:T(8,128)(2,1)S(1)}, bf16[256,768]{1,0:T(8,128)(2,1)S(1)}, u32[]{:S(2)}, u32[]{:S(2)}) collective-permute-start(bf16[256,768]{1,0:T(8,128)(2,1)S(1)} %get-tuple-element.30), channel_id=1, source_target_pairs={{0,3},{1,2},{2,1},{3,0},{4,7},{5,6},{6,5},{7,4},{8,11},{9,10},{10,... | collective-permute-start | bytes 1179656 | tf_op jit(solution)/shard_map/ppermute | solution.py:546
  32.4 17.0 %collective-permute-start.8 = (f32[520,128]{1,0:T(8,128)S(1)}, f32[520,128]{1,0:T(8,128)S(1)}, u32[]{:S(2)}, u32[]{:S(2)}) collective-permute-start(f32[520,128]{1,0:T(8,128)S(1)} %get-tuple-element.36), channel_id=1, source_target_pairs={{0,4},{4,8},{8,12},{12,0},{1,5},{5,9},{9,13},{13,1},{2,6},{6,10},{... | collective-permute-start | bytes 798728 | tf_op jit(solution)/shard_map/ppermute | solution.py:556
  34.9 17.1 %collective-permute-start.7 = (f32[520,128]{1,0:T(8,128)S(1)}, f32[520,128]{1,0:T(8,128)S(1)}, u32[]{:S(2)}, u32[]{:S(2)}) collective-permute-start(f32[520,128]{1,0:T(8,128)S(1)} %get-tuple-element.34), channel_id=1, source_target_pairs={{0,4},{4,8},{8,12},{12,0},{1,5},{5,9},{9,13},{13,1},{2,6},{6,10},{... | collective-permute-start | bytes 798728 | tf_op jit(solution)/shard_map/ppermute | solution.py:556
  36.4 18.6 %collective-permute-start.11 = (bf16[256,512]{1,0:T(8,128)(2,1)S(1)}, bf16[256,512]{1,0:T(8,128)(2,1)S(1)}, u32[]{:S(2)}, u32[]{:S(2)}) collective-permute-start(bf16[256,512]{1,0:T(8,128)(2,1)S(1)} %get-tuple-element.43), channel_id=1, source_target_pairs={{0,2},{1,3},{2,0},{3,1},{4,6},{5,7},{6,4},{7,5},{8,10},{9,11},{10,... | collective-permute-start | bytes 786440 | tf_op jit(solution)/shard_map/ppermute | solution.py:546
  37.9 17.7 %collective-permute-start.12 = (bf16[256,512]{1,0:T(8,128)(2,1)S(1)}, bf16[256,512]{1,0:T(8,128)(2,1)S(1)}, u32[]{:S(2)}, u32[]{:S(2)}) collective-permute-start(bf16[256,512]{1,0:T(8,128)(2,1)S(1)} %get-tuple-element.44), channel_id=1, source_target_pairs={{0,3},{1,2},{2,1},{3,0},{4,7},{5,6},{6,5},{7,4},{8,11},{9,10},{10,... | collective-permute-start | bytes 786440 | tf_op jit(solution)/shard_map/ppermute | solution.py:546
  49.5 13.4 %collective-permute-start.15 = (f32[520,128]{1,0:T(8,128)S(1)}, f32[520,128]{1,0:T(8,128)S(1)}, u32[]{:S(2)}, u32[]{:S(2)}) collective-permute-start(f32[520,128]{1,0:T(8,128)S(1)} %add.33), channel_id=1, source_target_pairs={{0,4},{4,8},{8,12},{12,0},{1,5},{5,9},{9,13},{13,1},{2,6},{6,10},{... | collective-permute-start | bytes 798728 | tf_op jit(solution)/shard_map/ppermute | solution.py:556
  52.0 14.7 %collective-permute-start.13 = (f32[520,128]{1,0:T(8,128)S(1)}, f32[520,128]{1,0:T(8,128)S(1)}, u32[]{:S(2)}, u32[]{:S(2)}) collective-permute-start(f32[520,128]{1,0:T(8,128)S(1)} %add.32), channel_id=1, source_target_pairs={{0,4},{4,8},{8,12},{12,0},{1,5},{5,9},{9,13},{13,1},{2,6},{6,10},{... | collective-permute-start | bytes 798728 | tf_op jit(solution)/shard_map/ppermute | solution.py:556
  53.6 13.3 %collective-permute-start.10 = (bf16[256,512]{1,0:T(8,128)(2,1)S(1)}, bf16[256,512]{1,0:T(8,128)(2,1)S(1)}, u32[]{:S(2)}, u32[]{:S(2)}) collective-permute-start(bf16[256,512]{1,0:T(8,128)(2,1)S(1)} %get-tuple-element.38), channel_id=1, source_target_pairs={{0,3},{1,2},{2,1},{3,0},{4,7},{5,6},{6,5},{7,4},{8,11},{9,10},{10,... | collective-permute-start | bytes 786440 | tf_op jit(solution)/shard_map/ppermute | solution.py:546
  55.0 12.8 %collective-permute-start.9 = (bf16[256,512]{1,0:T(8,128)(2,1)S(1)}, bf16[256,512]{1,0:T(8,128)(2,1)S(1)}, u32[]{:S(2)}, u32[]{:S(2)}) collective-permute-start(bf16[256,512]{1,0:T(8,128)(2,1)S(1)} %get-tuple-element.37), channel_id=1, source_target_pairs={{0,2},{1,3},{2,0},{3,1},{4,6},{5,7},{6,4},{7,5},{8,10},{9,11},{10,... | collective-permute-start | bytes 786440 | tf_op jit(solution)/shard_map/ppermute | solution.py:546
  63.0 12.4 %collective-permute-start.16 = (f32[520,128]{1,0:T(8,128)S(1)}, f32[520,128]{1,0:T(8,128)S(1)}, u32[]{:S(2)}, u32[]{:S(2)}) collective-permute-start(f32[520,128]{1,0:T(8,128)S(1)} %add.35), channel_id=1, source_target_pairs={{0,4},{4,8},{8,12},{12,0},{1,5},{5,9},{9,13},{13,1},{2,6},{6,10},{... | collective-permute-start | bytes 798728 | tf_op jit(solution)/shard_map/ppermute | solution.py:556
  66.7 12.0 %collective-permute-start.14 = (f32[520,128]{1,0:T(8,128)S(1)}, f32[520,128]{1,0:T(8,128)S(1)}, u32[]{:S(2)}, u32[]{:S(2)}) collective-permute-start(f32[520,128]{1,0:T(8,128)S(1)} %add.34), channel_id=1, source_target_pairs={{0,4},{4,8},{8,12},{12,0},{1,5},{5,9},{9,13},{13,1},{2,6},{6,10},{... | collective-permute-start | bytes 798728 | tf_op jit(solution)/shard_map/ppermute | solution.py:556
  88.0 14.8 %slice-start = ((s8[8388608]{0:T(1024)(128)(4,1)}), s8[4194304]{0:T(1024)(128)(4,1)S(1)}, s32[]{:S(2)}) async-start(s8[8388608]{0:T(1024)(128)(4,1)} %bitcast.22), calls=%async_computation | async-start | bytes 8388608
  88.1 18.2 %collective-permute-start.22 = (bf16[784,128]{1,0:T(8,128)(2,1)S(1)}, bf16[784,128]{1,0:T(8,128)(2,1)S(1)}, u32[]{:S(2)}, u32[]{:S(2)}) collective-permute-start(bf16[784,128]{1,0:T(8,128)(2,1)S(1)} %get-tuple-element.47.refs_0_), channel_id=1, source_target_pairs={{0,4},{4,0},{8,12},{12,8},{1,5},{5,1},{9,13},{13,9},{2,6},{6,2},{1... | collective-permute-start | bytes 602120 | tf_op jit(solution)/shard_map/ppermute | solution.py:602
  88.6 25.5 %collective-permute-start.17 = (bf16[784,128]{1,0:T(8,128)(2,1)S(1)}, bf16[784,128]{1,0:T(8,128)(2,1)S(1)}, u32[]{:S(2)}, u32[]{:S(2)}) collective-permute-start(bf16[784,128]{1,0:T(8,128)(2,1)S(1)} %get-tuple-element.47.refs_0_), channel_id=1, source_target_pairs={{0,12},{4,8},{8,4},{12,0},{1,13},{5,9},{9,5},{13,1},{2,14},{6,10},... | collective-permute-start | bytes 602120 | tf_op jit(solution)/shard_map/ppermute | solution.py:602
  90.1 24.0 %collective-permute-start.19 = (bf16[784,128]{1,0:T(8,128)(2,1)S(1)}, bf16[784,128]{1,0:T(8,128)(2,1)S(1)}, u32[]{:S(2)}, u32[]{:S(2)}) collective-permute-start(bf16[784,128]{1,0:T(8,128)(2,1)S(1)} %get-tuple-element.47.refs_0_), channel_id=1, source_target_pairs={{0,8},{4,12},{8,0},{12,4},{1,9},{5,13},{9,1},{13,5},{2,10},{6,14},... | collective-permute-start | bytes 602120 | tf_op jit(solution)/shard_map/ppermute | solution.py:602
  91.6 11.2 %slice-start.1 = ((s8[8388608]{0:T(1024)(128)(4,1)}), s8[4194304]{0:T(1024)(128)(4,1)S(1)}, s32[]{:S(2)}) async-start(s8[8388608]{0:T(1024)(128)(4,1)} %bitcast.22), calls=%async_computation.1 | async-start | bytes 8388608
  99.8 9.9 %collective-permute-start.21 = (bf16[272,128]{1,0:T(8,128)(2,1)S(1)}, bf16[272,128]{1,0:T(8,128)(2,1)S(1)}, u32[]{:S(2)}, u32[]{:S(2)}) collective-permute-start(bf16[272,128]{1,0:T(8,128)(2,1)S(1)} %factor_bottom.1.refs_1_), channel_id=1, source_target_pairs={{0,4},{4,0},{8,12},{12,8},{1,5},{5,1},{9,13},{13,9},{2,6},{6,2},{1... | collective-permute-start | bytes 208904 | tf_op jit(solution)/shard_map/ppermute | solution.py:602
  101.3 10.8 %collective-permute-start.18 = (bf16[272,128]{1,0:T(8,128)(2,1)S(1)}, bf16[272,128]{1,0:T(8,128)(2,1)S(1)}, u32[]{:S(2)}, u32[]{:S(2)}) collective-permute-start(bf16[272,128]{1,0:T(8,128)(2,1)S(1)} %factor_bottom.1.refs_1_), channel_id=1, source_target_pairs={{0,12},{4,8},{8,4},{12,0},{1,13},{5,9},{9,5},{13,1},{2,14},{6,10},... | collective-permute-start | bytes 208904 | tf_op jit(solution)/shard_map/ppermute | solution.py:602
  106.3 7.8 %collective-permute-start.20 = (bf16[272,128]{1,0:T(8,128)(2,1)S(1)}, bf16[272,128]{1,0:T(8,128)(2,1)S(1)}, u32[]{:S(2)}, u32[]{:S(2)}) collective-permute-start(bf16[272,128]{1,0:T(8,128)(2,1)S(1)} %factor_bottom.1.refs_1_), channel_id=1, source_target_pairs={{0,8},{4,12},{8,0},{12,4},{1,9},{5,13},{9,1},{13,5},{2,10},{6,14},... | collective-permute-start | bytes 208904 | tf_op jit(solution)/shard_map/ppermute | solution.py:602

commit v10 on v9

--- a/solution.py
+++ b/solution.py
@@ -650,9 +650,8 @@
     result = whiten([tops[0], bottoms[0]], 0, (0, half), None)
     result = whiten(tops[1:2], 1, (0,), result)
     result = whiten(bottoms[1:2], 1, (half,), result)
-    if blocks > 2:
-        rest = [half_block for pair in zip(tops[2:], bottoms[2:]) for half_block in pair]
-        result = whiten(rest, 2, (0, half), result)
+    for i in range(2, blocks):
+        result = whiten([tops[i], bottoms[i]], i, (0, half), result)
     return result
 
 

time: 125 us -> 121 us (0.968)
  waiting for transfers between devices: 16.4 us -> 15.1 us
    pallas_call x4 -> x5, Pallas kernels: 18.1 us -> 15.6 us  [whiten(): pl.pallas_call(functools.partial(whiten_kernel, blocks=count, starts=star...]
    ppermute x6, waiting for transfers between devices: 2 us -> 0.02 us  [shared(): lax.ppermute(array, 'dp', [(z, partner(z, d)) for z in range(ring)])]
    ppermute x6, starting transfers between devices: 10.6 us -> 8.75 us  [shards(): lax.ppermute(part, 'dp', [(z, (z + 1) % ring) for z in range(ring)])]
    pallas_call x4, Pallas kernels: 29.8 us -> 31.4 us  [grams_of(): pl.pallas_call(functools.partial(attention_kernel, chips=chips, spans=spa...]
  transfers between devices with their start and end apart: 23 -> 23, of which waited for: 6 -> 5; matrix products, arithmetic and copies ran while one was open for 3% -> 3% of each run, Pallas kernels for 42% -> 48%
where the time goes in v10:
time: 121 us
  Pallas kernels  70.7 us (58%)
  starting transfers between devices  26.4 us (22%)
  waiting for transfers between devices  15.1 us (12%)
  local copies, waits for them, and re-layouts  7.3 us (6%)
    pallas_call x4, Pallas kernels, grams_of(): pl.pallas_call(functools.partial(attention_kernel, chips=chips, spans=spa...  31.4 us
    pallas_call x5, Pallas kernels, whiten(): pl.pallas_call(functools.partial(whiten_kernel, blocks=count, starts=star...  15.6 us
    ppermute x8, waiting for transfers between devices, shards(): lax.ppermute(part, 'seq', moved(*where))  9.76 us
    pallas_call x1, Pallas kernels, factor_top(): pl.pallas_call(functools.partial(factor_kernel, start=0, stop=half, recei...  9.33 us
    ppermute x6, starting transfers between devices, shards(): lax.ppermute(part, 'dp', [(z, (z + 1) % ring) for z in range(ring)])  8.75 us
    ppermute x8, starting transfers between devices, shards(): lax.ppermute(part, 'seq', moved(*where))  8.63 us
    pallas_call x1, Pallas kernels, factor_bottom(): pl.pallas_call(functools.partial(factor_kernel, start=half, stop=BLOCK_W,...  8.47 us
    ppermute x6, starting transfers between devices, shared(): lax.ppermute(array, 'dp', [(z, partner(z, d)) for z in range(ring)])  8.06 us
  transfers between devices with their start and end apart: 23, of which 5 were waited for; matrix products, arithmetic and copies ran while one was open for 3% of the time, Pallas kernels for 48%

profile of v10, /device:TPU:0, one launch (start us, length us, event | category | flops | bytes accessed | tf_op | source)
XLA Modules:
  0.0 120.9 jit_solution(12259568112042955163)
XLA Ops:
  1.6 2.7 %cut_piece.6 = (bf16[256,768]{1,0:T(8,128)(2,1)}, bf16[256,768]{1,0:T(8,128)(2,1)}) custom-call(s32[3]{0:T(128)} %pad_add_fusion.1.meta, bf16[256,8192]{1,0:T(8,128)(2,1)} %bitcast.25, bf16[256,1024]{1,0:T(8,128)(2,1)} %bitcast.38, bf16[256,1024]{1,0:T(8,128)(2,1)} %bitcast.47, bf16[256,8192]{1,0:T(8,128)(2,1)} %bitcast.26, bf16[256,1024]{1,0:T(8,128)(2,1)} %bitcast.39, ...), custom_call_target="tpu_custom_call" | custom-call | bytes 2097152 | tf_op jit(solution)/shard_map/cut_piece/pallas_call | solution.py:458
  4.3 2.5 %collective-permute-start.5 = (bf16[256,768]{1,0:T(8,128)(2,1)}, bf16[256,768]{1,0:T(8,128)(2,1)S(1)}, u32[]{:S(2)}, u32[]{:S(2)}) collective-permute-start(bf16[256,768]{1,0:T(8,128)(2,1)} %get-tuple-element.31), channel_id=1, source_target_pairs={{0,2},{1,3},{2,0},{3,1},{4,6},{5,7},{6,4},{7,5},{8,10},{9,11},{10,... | collective-permute-start | bytes 1179656 | tf_op jit(solution)/shard_map/ppermute | solution.py:546
  10.2 2.2 %copy-done = bf16[1,256,8192]{2,1,0:T(8,128)(2,1)S(1)} copy-done((bf16[1,256,8192]{2,1,0:T(8,128)(2,1)S(1)}, bf16[1,256,8192]{2,1,0:T(8,128)(2,1)}, u32[]{:S(2)}) %copy-start) | copy-done | bytes 4194328
  12.4 1.0 copy-done.2
  13.4 1.0 copy-done.4
  15.1 1.8 %collective-permute-start.3 = (bf16[256,768]{1,0:T(8,128)(2,1)S(1)}, bf16[256,768]{1,0:T(8,128)(2,1)S(1)}, u32[]{:S(2)}, u32[]{:S(2)}) collective-permute-start(bf16[256,768]{1,0:T(8,128)(2,1)S(1)} %get-tuple-element.29), channel_id=1, source_target_pairs={{0,2},{1,3},{2,0},{3,1},{4,6},{5,7},{6,4},{7,5},{8,10},{9,11},{10,... | collective-permute-start | bytes 1179656 | tf_op jit(solution)/shard_map/ppermute | solution.py:546
  18.9 1.3 %cut_peer.1.refs_1_.refs_6_.refs_7_ = bf16[256,2560]{1,0:T(8,128)(2,1)S(1)} custom-call(s32[1]{0:T(128)} %bitcast.4.meta, bf16[256,8192]{1,0:T(8,128)(2,1)} %collective-permute-done.refs_0_, bf16[256,1024]{1,0:T(8,128)(2,1)S(1)} %collective-permute-done.1.refs_1_.refs_2_.refs_6_, bf16[256,1024]{1,0:T(8,128)(2,1)} %collective-permute-done.2.refs_2_), custom_call_target="tpu_custom_call" | custom-call | bytes 2097152 | tf_op jit(solution)/shard_map/cut_peer/pallas_call | solution.py:458
  20.2 4.8 %collective-permute-done.6.refs_9_.refs_3_ = bf16[256,768]{1,0:T(8,128)(2,1)S(1)} collective-permute-done((bf16[256,768]{1,0:T(8,128)(2,1)}, bf16[256,768]{1,0:T(8,128)(2,1)S(1)}, u32[]{:S(2)}, u32[]{:S(2)}) %collective-permute-start.6) | collective-permute-done | bytes 393248 | tf_op jit(solution)/shard_map/ppermute | solution.py:546
  25.0 7.8 %attention_outer_products.5 = (f32[520,128]{1,0:T(8,128)S(1)}, f32[520,128]{1,0:T(8,128)S(1)}) custom-call(s32[20]{0:T(128)S(1)} %concatenate.14.meta, bf16[256,8192]{1,0:T(8,128)(2,1)S(1)} %bitcast.33, bf16[256,2560]{1,0:T(8,128)(2,1)S(1)} %cut_peer.1.refs_1_.refs_6_.refs_7_, bf16[256,768]{1,0:T(8,128)(2,1)S(1)} %collective-permute-done.5.refs_8_.refs_2_, ...), custom_call_target="tpu_custom_call" | custom-call | flops 14000000000 | bytes 1048576 | tf_op jit(solution)/shard_map/attention_outer_products/pallas_call | solution.py:489
  32.8 1.5 %collective-permute-start.8 = (f32[520,128]{1,0:T(8,128)S(1)}, f32[520,128]{1,0:T(8,128)S(1)}, u32[]{:S(2)}, u32[]{:S(2)}) collective-permute-start(f32[520,128]{1,0:T(8,128)S(1)} %get-tuple-element.36), channel_id=1, source_target_pairs={{0,4},{4,8},{8,12},{12,0},{1,5},{5,9},{9,13},{13,1},{2,6},{6,10},{... | collective-permute-start | bytes 798728 | tf_op jit(solution)/shard_map/ppermute | solution.py:556
  34.3 2.1 %collective-permute-start.7 = (f32[520,128]{1,0:T(8,128)S(1)}, f32[520,128]{1,0:T(8,128)S(1)}, u32[]{:S(2)}, u32[]{:S(2)}) collective-permute-start(f32[520,128]{1,0:T(8,128)S(1)} %get-tuple-element.34), channel_id=1, source_target_pairs={{0,4},{4,8},{8,12},{12,0},{1,5},{5,9},{9,13},{13,1},{2,6},{6,10},{... | collective-permute-start | bytes 798728 | tf_op jit(solution)/shard_map/ppermute | solution.py:556
  36.4 1.5 %collective-permute-start.11 = (bf16[256,512]{1,0:T(8,128)(2,1)S(1)}, bf16[256,512]{1,0:T(8,128)(2,1)S(1)}, u32[]{:S(2)}, u32[]{:S(2)}) collective-permute-start(bf16[256,512]{1,0:T(8,128)(2,1)S(1)} %get-tuple-element.43), channel_id=1, source_target_pairs={{0,2},{1,3},{2,0},{3,1},{4,6},{5,7},{6,4},{7,5},{8,10},{9,11},{10,... | collective-permute-start | bytes 786440 | tf_op jit(solution)/shard_map/ppermute | solution.py:546
  37.9 4.0 %collective-permute-done.4.refs_3_.refs_11_ = bf16[256,768]{1,0:T(8,128)(2,1)S(1)} collective-permute-done((bf16[256,768]{1,0:T(8,128)(2,1)S(1)}, bf16[256,768]{1,0:T(8,128)(2,1)S(1)}, u32[]{:S(2)}, u32[]{:S(2)}) %collective-permute-start.4) | collective-permute-done | bytes 393248 | tf_op jit(solution)/shard_map/ppermute | solution.py:546
  41.9 8.0 %attention_outer_products.4 = (f32[520,128]{1,0:T(8,128)S(1)}, f32[520,128]{1,0:T(8,128)S(1)}) custom-call(s32[20]{0:T(128)S(1)} %concatenate.13.meta, bf16[256,8192]{1,0:T(8,128)(2,1)S(1)} %bitcast.34, bf16[256,2560]{1,0:T(8,128)(2,1)S(1)} %cut_peer.1.refs_1_.refs_6_.refs_7_, bf16[256,768]{1,0:T(8,128)(2,1)S(1)} %collective-permute-done.3.refs_2_.refs_10_, ...), custom_call_target="tpu_custom_call" | custom-call | flops 14000000000 | bytes 1048576 | tf_op jit(solution)/shard_map/attention_outer_products/pallas_call | solution.py:489
  49.9 1.5 %collective-permute-start.15 = (f32[520,128]{1,0:T(8,128)S(1)}, f32[520,128]{1,0:T(8,128)S(1)}, u32[]{:S(2)}, u32[]{:S(2)}) collective-permute-start(f32[520,128]{1,0:T(8,128)S(1)} %add.33), channel_id=1, source_target_pairs={{0,4},{4,8},{8,12},{12,0},{1,5},{5,9},{9,13},{13,1},{2,6},{6,10},{... | collective-permute-start | bytes 798728 | tf_op jit(solution)/shard_map/ppermute | solution.py:556
  51.4 2.2 %collective-permute-start.13 = (f32[520,128]{1,0:T(8,128)S(1)}, f32[520,128]{1,0:T(8,128)S(1)}, u32[]{:S(2)}, u32[]{:S(2)}) collective-permute-start(f32[520,128]{1,0:T(8,128)S(1)} %add.32), channel_id=1, source_target_pairs={{0,4},{4,8},{8,12},{12,0},{1,5},{5,9},{9,13},{13,1},{2,6},{6,10},{... | collective-permute-start | bytes 798728 | tf_op jit(solution)/shard_map/ppermute | solution.py:556
  53.6 1.4 %collective-permute-start.10 = (bf16[256,512]{1,0:T(8,128)(2,1)S(1)}, bf16[256,512]{1,0:T(8,128)(2,1)S(1)}, u32[]{:S(2)}, u32[]{:S(2)}) collective-permute-start(bf16[256,512]{1,0:T(8,128)(2,1)S(1)} %get-tuple-element.38), channel_id=1, source_target_pairs={{0,3},{1,2},{2,1},{3,0},{4,7},{5,6},{6,5},{7,4},{8,11},{9,10},{10,... | collective-permute-start | bytes 786440 | tf_op jit(solution)/shard_map/ppermute | solution.py:546
  55.6 7.7 %attention_outer_products.7 = (f32[520,128]{1,0:T(8,128)S(1)}, f32[520,128]{1,0:T(8,128)S(1)}) custom-call(s32[20]{0:T(128)S(1)} %concatenate.15.meta, bf16[256,8192]{1,0:T(8,128)(2,1)S(1)} %bitcast.35, bf16[256,2560]{1,0:T(8,128)(2,1)S(1)} %cut_peer.1.refs_1_.refs_6_.refs_7_, bf16[256,512]{1,0:T(8,128)(2,1)S(1)} %collective-permute-done.11.refs_2_, ...), custom_call_target="tpu_custom_call" | custom-call | flops 14000000000 | bytes 1048576 | tf_op jit(solution)/shard_map/attention_outer_products/pallas_call | solution.py:489
  63.4 1.4 %collective-permute-start.16 = (f32[520,128]{1,0:T(8,128)S(1)}, f32[520,128]{1,0:T(8,128)S(1)}, u32[]{:S(2)}, u32[]{:S(2)}) collective-permute-start(f32[520,128]{1,0:T(8,128)S(1)} %add.35), channel_id=1, source_target_pairs={{0,4},{4,8},{8,12},{12,0},{1,5},{5,9},{9,13},{13,1},{2,6},{6,10},{... | collective-permute-start | bytes 798728 | tf_op jit(solution)/shard_map/ppermute | solution.py:556
  64.8 1.9 %collective-permute-done.13 = f32[520,128]{1,0:T(8,128)S(1)} collective-permute-done((f32[520,128]{1,0:T(8,128)S(1)}, f32[520,128]{1,0:T(8,128)S(1)}, u32[]{:S(2)}, u32[]{:S(2)}) %collective-permute-start.13) | collective-permute-done | bytes 266272 | tf_op jit(solution)/shard_map/ppermute | solution.py:556
  67.8 8.0 %attention_outer_products.6 = (f32[520,128]{1,0:T(8,128)S(1)}, f32[520,128]{1,0:T(8,128)S(1)}) custom-call(s32[20]{0:T(128)S(1)} %concatenate.12.meta, bf16[256,8192]{1,0:T(8,128)(2,1)S(1)} %bitcast.36, bf16[256,2560]{1,0:T(8,128)(2,1)S(1)} %cut_peer.1.refs_1_.refs_6_.refs_7_, bf16[256,512]{1,0:T(8,128)(2,1)S(1)} %collective-permute-done.9.refs_2_, ...), custom_call_target="tpu_custom_call" | custom-call | flops 14000000000 | bytes 1048576 | tf_op jit(solution)/shard_map/attention_outer_products/pallas_call | solution.py:489
  75.8 3.3 %collective-permute-done.14.refs_2_ = f32[520,128]{1,0:T(8,128)S(1)} collective-permute-done((f32[520,128]{1,0:T(8,128)S(1)}, f32[520,128]{1,0:T(8,128)S(1)}, u32[]{:S(2)}, u32[]{:S(2)}) %collective-permute-start.14) | collective-permute-done | bytes 266272 | tf_op jit(solution)/shard_map/ppermute | solution.py:556
  79.1 9.3 %factor_top.1 = (bf16[784,128]{1,0:T(8,128)(2,1)S(1)}, f32[256,256]{1,0:T(8,128)S(1)}) custom-call(f32[520,128]{1,0:T(8,128)S(1)} %get-tuple-element.39.refs_0_, f32[520,128]{1,0:T(8,128)S(1)} %get-tuple-element.40.refs_1_, f32[520,128]{1,0:T(8,128)S(1)} %collective-permute-done.14.refs_2_, f32[520,128]{1,0:T(8,128)S(1)} %collective-permute-done.16.refs_3_), custom_call_target="tpu_custom_call" | custom-call | flops 10000000000 | bytes 1048576 | tf_op jit(solution)/shard_map/factor_top/pallas_call | solution.py:565
  88.5 1.6 %collective-permute-start.19 = (bf16[784,128]{1,0:T(8,128)(2,1)S(1)}, bf16[784,128]{1,0:T(8,128)(2,1)S(1)}, u32[]{:S(2)}, u32[]{:S(2)}) collective-permute-start(bf16[784,128]{1,0:T(8,128)(2,1)S(1)} %get-tuple-element.47.refs_0_), channel_id=1, source_target_pairs={{0,12},{4,8},{8,4},{12,0},{1,13},{5,9},{9,5},{13,1},{2,14},{6,10},... | collective-permute-start | bytes 602120 | tf_op jit(solution)/shard_map/ppermute | solution.py:602
  90.1 8.5 %factor_bottom.1.refs_1_ = bf16[272,128]{1,0:T(8,128)(2,1)S(1)} custom-call(f32[256,256]{1,0:T(8,128)S(1)} %get-tuple-element.48.refs_0_), custom_call_target="tpu_custom_call" | custom-call | flops 8999999488 | bytes 1048576 | tf_op jit(solution)/shard_map/factor_bottom/pallas_call | solution.py:580
  99.3 2.7 %collective-permute-start.20 = (bf16[272,128]{1,0:T(8,128)(2,1)S(1)}, bf16[272,128]{1,0:T(8,128)(2,1)S(1)}, u32[]{:S(2)}, u32[]{:S(2)}) collective-permute-start(bf16[272,128]{1,0:T(8,128)(2,1)S(1)} %factor_bottom.1.refs_1_), channel_id=1, source_target_pairs={{0,12},{4,8},{8,4},{12,0},{1,13},{5,9},{9,5},{13,1},{2,14},{6,10},... | collective-permute-start | bytes 208904 | tf_op jit(solution)/shard_map/ppermute | solution.py:602
  102.2 3.5 %whiten_top.4.refs_5_ = f32[4,512,2048]{2,1,0:T(8,128)} custom-call(s32[4]{0:T(128)S(1)} %pad_add_fusion.order, bf16[784,128]{1,0:T(8,128)(2,1)S(1)} %get-tuple-element.47.refs_0_, bf16[272,128]{1,0:T(8,128)(2,1)S(1)} %factor_bottom.1.refs_1_, bf16[2048,2048]{1,0:T(8,128)(2,1)S(1)} %bitcast.23, bf16[2048,2048]{1,0:T(8,128)(2,1)S(1)} %bitcast.23, ...), custom_call_target="tpu_custom_call" | custom-call | flops 4000000000 | bytes 1048576 | tf_op jit(solution)/shard_map/whiten_top/pallas_call | solution.py:628
  105.7 2.9 %collective-permute-start.18 = (bf16[272,128]{1,0:T(8,128)(2,1)S(1)}, bf16[272,128]{1,0:T(8,128)(2,1)S(1)}, u32[]{:S(2)}, u32[]{:S(2)}) collective-permute-start(bf16[272,128]{1,0:T(8,128)(2,1)S(1)} %factor_bottom.1.refs_1_), channel_id=1, source_target_pairs={{0,8},{4,12},{8,0},{12,4},{1,9},{5,13},{9,1},{13,5},{2,10},{6,14},... | collective-permute-start | bytes 208904 | tf_op jit(solution)/shard_map/ppermute | solution.py:602
  108.5 2.8 %whiten_top.5.refs_5_ = f32[4,512,2048]{2,1,0:T(8,128)} custom-call(s32[4]{0:T(128)S(1)} %pad_add_fusion.order, bf16[784,128]{1,0:T(8,128)(2,1)S(1)} %collective-permute-done.22.refs_0_, bf16[2048,2048]{1,0:T(8,128)(2,1)S(1)} %bitcast.23, bf16[2048,2048]{1,0:T(8,128)(2,1)S(1)} %bitcast.23, ...), custom_call_target="tpu_custom_call", output_to_operand_aliasing={{}: (6, {})} | custom-call | flops 2000000000 | bytes 1048576 | tf_op jit(solution)/shard_map/whiten_top/pallas_call | solution.py:628
  111.4 2.3 %whiten_bottom.1.refs_6_ = f32[4,512,2048]{2,1,0:T(8,128)} custom-call(s32[4]{0:T(128)S(1)} %pad_add_fusion.order, bf16[272,128]{1,0:T(8,128)(2,1)S(1)} %collective-permute-done.21.refs_0_, bf16[2048,2048]{1,0:T(8,128)(2,1)S(1)} %bitcast.23, bf16[2048,2048]{1,0:T(8,128)(2,1)S(1)} %bitcast.23, ...), custom_call_target="tpu_custom_call", output_to_operand_aliasing={{}: (6, {})} | custom-call | flops 2000000000 | bytes 1048576 | tf_op jit(solution)/shard_map/whiten_bottom/pallas_call | solution.py:628
  113.7 3.5 %whiten_top.6.refs_6_ = f32[4,512,2048]{2,1,0:T(8,128)} custom-call(s32[4]{0:T(128)S(1)} %pad_add_fusion.order, bf16[784,128]{1,0:T(8,128)(2,1)S(1)} %collective-permute-done.19.refs_0_, bf16[272,128]{1,0:T(8,128)(2,1)S(1)} %collective-permute-done.20.refs_1_, bf16[2048,2048]{1,0:T(8,128)(2,1)S(1)} %bitcast.23, ...), custom_call_target="tpu_custom_call", output_to_operand_aliasing={{}: (7, {})} | custom-call | flops 4000000000 | bytes 1048576 | tf_op jit(solution)/shard_map/whiten_top/pallas_call | solution.py:628
  117.2 3.5 %whiten_top.7 = f32[4,512,2048]{2,1,0:T(8,128)} custom-call(s32[4]{0:T(128)S(1)} %pad_add_fusion.order, bf16[784,128]{1,0:T(8,128)(2,1)S(1)} %collective-permute-done.17.refs_0_, bf16[272,128]{1,0:T(8,128)(2,1)S(1)} %collective-permute-done.18.refs_1_, bf16[2048,2048]{1,0:T(8,128)(2,1)S(1)} %bitcast.23, ...), custom_call_target="tpu_custom_call", output_to_operand_aliasing={{}: (7, {})} | custom-call | flops 4000000000 | bytes 1048576 | tf_op jit(solution)/shard_map/whiten_top/pallas_call | solution.py:628
  (59 shorter events, 10.3 us)
Async XLA Ops:
  0.0 18.9 %collective-permute-start = (bf16[256,8192]{1,0:T(8,128)(2,1)}, bf16[256,8192]{1,0:T(8,128)(2,1)}, u32[]{:S(2)}, u32[]{:S(2)}) collective-permute-start(bf16[256,8192]{1,0:T(8,128)(2,1)} %bitcast.24), channel_id=1, source_target_pairs={{0,1},{1,0},{2,3},{3,2},{4,5},{5,4},{6,7},{7,6},{8,9},{9,8},{10,11... | collective-permute-start | bytes 12582920 | tf_op jit(solution)/shard_map/ppermute | solution.py:528
  0.5 9.7 %collective-permute-start.1 = (bf16[256,1024]{1,0:T(8,128)(2,1)}, bf16[256,1024]{1,0:T(8,128)(2,1)S(1)}, u32[]{:S(2)}, u32[]{:S(2)}) collective-permute-start(bf16[256,1024]{1,0:T(8,128)(2,1)} %bitcast.37), channel_id=1, source_target_pairs={{0,1},{1,0},{2,3},{3,2},{4,5},{5,4},{6,7},{7,6},{8,9},{9,8},{10,11... | collective-permute-start | bytes 1572872 | tf_op jit(solution)/shard_map/ppermute | solution.py:528
  0.5 17.6 %collective-permute-start.2 = (bf16[256,1024]{1,0:T(8,128)(2,1)}, bf16[256,1024]{1,0:T(8,128)(2,1)}, u32[]{:S(2)}, u32[]{:S(2)}) collective-permute-start(bf16[256,1024]{1,0:T(8,128)(2,1)} %bitcast.46), channel_id=1, source_target_pairs={{0,1},{1,0},{2,3},{3,2},{4,5},{5,4},{6,7},{7,6},{8,9},{9,8},{10,11... | collective-permute-start | bytes 1572872 | tf_op jit(solution)/shard_map/ppermute | solution.py:528
  4.3 15.9 %collective-permute-start.5 = (bf16[256,768]{1,0:T(8,128)(2,1)}, bf16[256,768]{1,0:T(8,128)(2,1)S(1)}, u32[]{:S(2)}, u32[]{:S(2)}) collective-permute-start(bf16[256,768]{1,0:T(8,128)(2,1)} %get-tuple-element.31), channel_id=1, source_target_pairs={{0,2},{1,3},{2,0},{3,1},{4,6},{5,7},{6,4},{7,5},{8,10},{9,11},{10,... | collective-permute-start | bytes 1179656 | tf_op jit(solution)/shard_map/ppermute | solution.py:546
  6.8 18.2 %collective-permute-start.6 = (bf16[256,768]{1,0:T(8,128)(2,1)}, bf16[256,768]{1,0:T(8,128)(2,1)S(1)}, u32[]{:S(2)}, u32[]{:S(2)}) collective-permute-start(bf16[256,768]{1,0:T(8,128)(2,1)} %get-tuple-element.32), channel_id=1, source_target_pairs={{0,3},{1,2},{2,1},{3,0},{4,7},{5,6},{6,5},{7,4},{8,11},{9,10},{10,... | collective-permute-start | bytes 1179656 | tf_op jit(solution)/shard_map/ppermute | solution.py:546
  10.2 2.2 %copy-start = (bf16[1,256,8192]{2,1,0:T(8,128)(2,1)S(1)}, bf16[1,256,8192]{2,1,0:T(8,128)(2,1)}, u32[]{:S(2)}) copy-start(bf16[1,256,8192]{2,1,0:T(8,128)(2,1)} %param.6) | copy-start | bytes 12582916
  12.4 1.0 copy-start.2
  13.4 1.0 copy-start.4
  14.4 3.1 %copy-start.1 = (bf16[1,256,8192]{2,1,0:T(8,128)(2,1)S(1)}, bf16[1,256,8192]{2,1,0:T(8,128)(2,1)}, u32[]{:S(2)}) copy-start(bf16[1,256,8192]{2,1,0:T(8,128)(2,1)} %param.6) | copy-start | bytes 12582916
  14.4 10.6 %copy-start.3 = (bf16[1,256,1024]{2,1,0:T(8,128)(2,1)S(1)}, bf16[1,256,1024]{2,1,0:T(8,128)(2,1)}, u32[]{:S(2)}) copy-start(bf16[1,256,1024]{2,1,0:T(8,128)(2,1)} %param.7) | copy-start | bytes 1572868
  14.4 10.6 %copy-start.5 = (bf16[1,256,1024]{2,1,0:T(8,128)(2,1)S(1)}, bf16[1,256,1024]{2,1,0:T(8,128)(2,1)}, u32[]{:S(2)}) copy-start(bf16[1,256,1024]{2,1,0:T(8,128)(2,1)} %param.8) | copy-start | bytes 1572868
  15.1 22.7 %collective-permute-start.3 = (bf16[256,768]{1,0:T(8,128)(2,1)S(1)}, bf16[256,768]{1,0:T(8,128)(2,1)S(1)}, u32[]{:S(2)}, u32[]{:S(2)}) collective-permute-start(bf16[256,768]{1,0:T(8,128)(2,1)S(1)} %get-tuple-element.29), channel_id=1, source_target_pairs={{0,2},{1,3},{2,0},{3,1},{4,6},{5,7},{6,4},{7,5},{8,10},{9,11},{10,... | collective-permute-start | bytes 1179656 | tf_op jit(solution)/shard_map/ppermute | solution.py:546
  18.1 23.7 %collective-permute-start.4 = (bf16[256,768]{1,0:T(8,128)(2,1)S(1)}, bf16[256,768]{1,0:T(8,128)(2,1)S(1)}, u32[]{:S(2)}, u32[]{:S(2)}) collective-permute-start(bf16[256,768]{1,0:T(8,128)(2,1)S(1)} %get-tuple-element.30), channel_id=1, source_target_pairs={{0,3},{1,2},{2,1},{3,0},{4,7},{5,6},{6,5},{7,4},{8,11},{9,10},{10,... | collective-permute-start | bytes 1179656 | tf_op jit(solution)/shard_map/ppermute | solution.py:546
  32.8 17.1 %collective-permute-start.8 = (f32[520,128]{1,0:T(8,128)S(1)}, f32[520,128]{1,0:T(8,128)S(1)}, u32[]{:S(2)}, u32[]{:S(2)}) collective-permute-start(f32[520,128]{1,0:T(8,128)S(1)} %get-tuple-element.36), channel_id=1, source_target_pairs={{0,4},{4,8},{8,12},{12,0},{1,5},{5,9},{9,13},{13,1},{2,6},{6,10},{... | collective-permute-start | bytes 798728 | tf_op jit(solution)/shard_map/ppermute | solution.py:556
  34.3 17.1 %collective-permute-start.7 = (f32[520,128]{1,0:T(8,128)S(1)}, f32[520,128]{1,0:T(8,128)S(1)}, u32[]{:S(2)}, u32[]{:S(2)}) collective-permute-start(f32[520,128]{1,0:T(8,128)S(1)} %get-tuple-element.34), channel_id=1, source_target_pairs={{0,4},{4,8},{8,12},{12,0},{1,5},{5,9},{9,13},{13,1},{2,6},{6,10},{... | collective-permute-start | bytes 798728 | tf_op jit(solution)/shard_map/ppermute | solution.py:556
  36.4 18.6 %collective-permute-start.11 = (bf16[256,512]{1,0:T(8,128)(2,1)S(1)}, bf16[256,512]{1,0:T(8,128)(2,1)S(1)}, u32[]{:S(2)}, u32[]{:S(2)}) collective-permute-start(bf16[256,512]{1,0:T(8,128)(2,1)S(1)} %get-tuple-element.43), channel_id=1, source_target_pairs={{0,2},{1,3},{2,0},{3,1},{4,6},{5,7},{6,4},{7,5},{8,10},{9,11},{10,... | collective-permute-start | bytes 786440 | tf_op jit(solution)/shard_map/ppermute | solution.py:546
  37.9 17.7 %collective-permute-start.12 = (bf16[256,512]{1,0:T(8,128)(2,1)S(1)}, bf16[256,512]{1,0:T(8,128)(2,1)S(1)}, u32[]{:S(2)}, u32[]{:S(2)}) collective-permute-start(bf16[256,512]{1,0:T(8,128)(2,1)S(1)} %get-tuple-element.44), channel_id=1, source_target_pairs={{0,3},{1,2},{2,1},{3,0},{4,7},{5,6},{6,5},{7,4},{8,11},{9,10},{10,... | collective-permute-start | bytes 786440 | tf_op jit(solution)/shard_map/ppermute | solution.py:546
  49.9 13.4 %collective-permute-start.15 = (f32[520,128]{1,0:T(8,128)S(1)}, f32[520,128]{1,0:T(8,128)S(1)}, u32[]{:S(2)}, u32[]{:S(2)}) collective-permute-start(f32[520,128]{1,0:T(8,128)S(1)} %add.33), channel_id=1, source_target_pairs={{0,4},{4,8},{8,12},{12,0},{1,5},{5,9},{9,13},{13,1},{2,6},{6,10},{... | collective-permute-start | bytes 798728 | tf_op jit(solution)/shard_map/ppermute | solution.py:556
  51.4 15.3 %collective-permute-start.13 = (f32[520,128]{1,0:T(8,128)S(1)}, f32[520,128]{1,0:T(8,128)S(1)}, u32[]{:S(2)}, u32[]{:S(2)}) collective-permute-start(f32[520,128]{1,0:T(8,128)S(1)} %add.32), channel_id=1, source_target_pairs={{0,4},{4,8},{8,12},{12,0},{1,5},{5,9},{9,13},{13,1},{2,6},{6,10},{... | collective-permute-start | bytes 798728 | tf_op jit(solution)/shard_map/ppermute | solution.py:556
  53.6 13.2 %collective-permute-start.10 = (bf16[256,512]{1,0:T(8,128)(2,1)S(1)}, bf16[256,512]{1,0:T(8,128)(2,1)S(1)}, u32[]{:S(2)}, u32[]{:S(2)}) collective-permute-start(bf16[256,512]{1,0:T(8,128)(2,1)S(1)} %get-tuple-element.38), channel_id=1, source_target_pairs={{0,3},{1,2},{2,1},{3,0},{4,7},{5,6},{6,5},{7,4},{8,11},{9,10},{10,... | collective-permute-start | bytes 786440 | tf_op jit(solution)/shard_map/ppermute | solution.py:546
  55.0 12.8 %collective-permute-start.9 = (bf16[256,512]{1,0:T(8,128)(2,1)S(1)}, bf16[256,512]{1,0:T(8,128)(2,1)S(1)}, u32[]{:S(2)}, u32[]{:S(2)}) collective-permute-start(bf16[256,512]{1,0:T(8,128)(2,1)S(1)} %get-tuple-element.37), channel_id=1, source_target_pairs={{0,2},{1,3},{2,0},{3,1},{4,6},{5,7},{6,4},{7,5},{8,10},{9,11},{10,... | collective-permute-start | bytes 786440 | tf_op jit(solution)/shard_map/ppermute | solution.py:546
  63.4 12.4 %collective-permute-start.16 = (f32[520,128]{1,0:T(8,128)S(1)}, f32[520,128]{1,0:T(8,128)S(1)}, u32[]{:S(2)}, u32[]{:S(2)}) collective-permute-start(f32[520,128]{1,0:T(8,128)S(1)} %add.35), channel_id=1, source_target_pairs={{0,4},{4,8},{8,12},{12,0},{1,5},{5,9},{9,13},{13,1},{2,6},{6,10},{... | collective-permute-start | bytes 798728 | tf_op jit(solution)/shard_map/ppermute | solution.py:556
  66.7 12.4 %collective-permute-start.14 = (f32[520,128]{1,0:T(8,128)S(1)}, f32[520,128]{1,0:T(8,128)S(1)}, u32[]{:S(2)}, u32[]{:S(2)}) collective-permute-start(f32[520,128]{1,0:T(8,128)S(1)} %add.34), channel_id=1, source_target_pairs={{0,4},{4,8},{8,12},{12,0},{1,5},{5,9},{9,13},{13,1},{2,6},{6,10},{... | collective-permute-start | bytes 798728 | tf_op jit(solution)/shard_map/ppermute | solution.py:556
  88.4 13.7 %slice-start = ((s8[8388608]{0:T(1024)(128)(4,1)}), s8[4194304]{0:T(1024)(128)(4,1)S(1)}, s32[]{:S(2)}) async-start(s8[8388608]{0:T(1024)(128)(4,1)} %bitcast.22), calls=%async_computation | async-start | bytes 8388608
  88.5 17.2 %collective-permute-start.22 = (bf16[784,128]{1,0:T(8,128)(2,1)S(1)}, bf16[784,128]{1,0:T(8,128)(2,1)S(1)}, u32[]{:S(2)}, u32[]{:S(2)}) collective-permute-start(bf16[784,128]{1,0:T(8,128)(2,1)S(1)} %get-tuple-element.47.refs_0_), channel_id=1, source_target_pairs={{0,4},{4,0},{8,12},{12,8},{1,5},{5,1},{9,13},{13,9},{2,6},{6,2},{1... | collective-permute-start | bytes 602120 | tf_op jit(solution)/shard_map/ppermute | solution.py:602
  88.5 25.2 %collective-permute-start.19 = (bf16[784,128]{1,0:T(8,128)(2,1)S(1)}, bf16[784,128]{1,0:T(8,128)(2,1)S(1)}, u32[]{:S(2)}, u32[]{:S(2)}) collective-permute-start(bf16[784,128]{1,0:T(8,128)(2,1)S(1)} %get-tuple-element.47.refs_0_), channel_id=1, source_target_pairs={{0,12},{4,8},{8,4},{12,0},{1,13},{5,9},{9,5},{13,1},{2,14},{6,10},... | collective-permute-start | bytes 602120 | tf_op jit(solution)/shard_map/ppermute | solution.py:602
  90.1 12.0 %slice-start.1 = ((s8[8388608]{0:T(1024)(128)(4,1)}), s8[4194304]{0:T(1024)(128)(4,1)S(1)}, s32[]{:S(2)}) async-start(s8[8388608]{0:T(1024)(128)(4,1)} %bitcast.22), calls=%async_computation.1 | async-start | bytes 8388608
  98.6 12.8 %collective-permute-start.21 = (bf16[272,128]{1,0:T(8,128)(2,1)S(1)}, bf16[272,128]{1,0:T(8,128)(2,1)S(1)}, u32[]{:S(2)}, u32[]{:S(2)}) collective-permute-start(bf16[272,128]{1,0:T(8,128)(2,1)S(1)} %factor_bottom.1.refs_1_), channel_id=1, source_target_pairs={{0,4},{4,0},{8,12},{12,8},{1,5},{5,1},{9,13},{13,9},{2,6},{6,2},{1... | collective-permute-start | bytes 208904 | tf_op jit(solution)/shard_map/ppermute | solution.py:602
  99.3 14.4 %collective-permute-start.20 = (bf16[272,128]{1,0:T(8,128)(2,1)S(1)}, bf16[272,128]{1,0:T(8,128)(2,1)S(1)}, u32[]{:S(2)}, u32[]{:S(2)}) collective-permute-start(bf16[272,128]{1,0:T(8,128)(2,1)S(1)} %factor_bottom.1.refs_1_), channel_id=1, source_target_pairs={{0,12},{4,8},{8,4},{12,0},{1,13},{5,9},{9,5},{13,1},{2,14},{6,10},... | collective-permute-start | bytes 208904 | tf_op jit(solution)/shard_map/ppermute | solution.py:602
  102.0 15.2 %collective-permute-start.17 = (bf16[784,128]{1,0:T(8,128)(2,1)S(1)}, bf16[784,128]{1,0:T(8,128)(2,1)S(1)}, u32[]{:S(2)}, u32[]{:S(2)}) collective-permute-start(bf16[784,128]{1,0:T(8,128)(2,1)S(1)} %get-tuple-element.47.refs_0_), channel_id=1, source_target_pairs={{0,8},{4,12},{8,0},{12,4},{1,9},{5,13},{9,1},{13,5},{2,10},{6,14},... | collective-permute-start | bytes 602120 | tf_op jit(solution)/shard_map/ppermute | solution.py:602
  105.7 11.5 %collective-permute-start.18 = (bf16[272,128]{1,0:T(8,128)(2,1)S(1)}, bf16[272,128]{1,0:T(8,128)(2,1)S(1)}, u32[]{:S(2)}, u32[]{:S(2)}) collective-permute-start(bf16[272,128]{1,0:T(8,128)(2,1)S(1)} %factor_bottom.1.refs_1_), channel_id=1, source_target_pairs={{0,8},{4,12},{8,0},{12,4},{1,9},{5,13},{9,1},{13,5},{2,10},{6,14},... | collective-permute-start | bytes 208904 | tf_op jit(solution)/shard_map/ppermute | solution.py:602
